TPU v7x, 32 devices: a whole 2x2x4 slice. The times are simulated.
32 devices in a mesh: probe: 4 (over x, core), tile: 4 (over z), level: 2 (over y).
Axes of the slice: x: 2, y: 2, z: 4, core: 2. Of those that a mesh axis runs over, the one named last changes fastest.
Arguments:
- probe_bits: int32 [4, 64, 32, 256], P('probe', 'level', 'tile'), may hold values from 0 to 1
- kappa_sq: float32 [64, 32, 256], P('level', 'tile'), may hold values from 0.25 to 4
- observed: float32 [64, 32, 256], P('level', 'tile'), may hold values from -0.6 to 0.6
Outputs:
- gradient: float32 [64, 32, 256], P('level', 'tile', 'probe')
Inputs may be any that keep to these rules, and one draw needn't show every extreme that they name: `probe_bits`: a probe's sign is 2 times its bit minus 1.
All inputs are finite; a program needn't handle non-finite values.
Results may differ from a plain program's by a relative error of at most 0.0003.
Values sent between devices are 32-bit elements; how exact they have to be, the bound alone decides.
No kernel may reach another device: no remote copies, remote signals or barrier semaphores. Data moves between devices by JAX's collectives and lax.ppermute only.
A program may use at most 64 MiB of HBM per device.

v0:
```python
import jax
import jax.numpy as jnp
from jax import lax
from jax.sharding import PartitionSpec as P

ITERS = 4


VERTICAL = 2.0


def with_halo(cells, sides, width):
    for axis, dim in sides:
        count = lax.axis_size(axis)
        ends = count - 1
        head = lax.slice_in_dim(cells, 0, width, axis=dim)
        tail = lax.slice_in_dim(cells, cells.shape[dim] - width, cells.shape[dim], axis=dim)
        cells = jnp.concatenate(
            [
                lax.ppermute(tail, axis, [(i, (i + 1) % count) for i in range(ends)]),
                cells,
                lax.ppermute(head, axis, [((i + 1) % count, i) for i in range(ends)]),
            ],
            axis=dim,
        )
    return cells


def shift_levels(values, stride, level_dim, fill_value):
    level_count = values.shape[level_dim]
    widths = [(0, 0)] * values.ndim
    if stride > 0:
        widths[level_dim] = (stride, 0)
        padded = jnp.pad(values, widths, constant_values=fill_value)
        return lax.slice_in_dim(padded, 0, level_count, axis=level_dim)
    widths[level_dim] = (0, -stride)
    padded = jnp.pad(values, widths, constant_values=fill_value)
    return lax.slice_in_dim(padded, -stride, level_count - stride, axis=level_dim)


def reduction_tables(kappa_sq):
    level_count = kappa_sq.shape[0]
    level_ids = lax.broadcasted_iota(jnp.int32, kappa_sq.shape, 0)
    diagonal = kappa_sq + (4.0 + 2.0 * VERTICAL)
    lower = jnp.where(level_ids > 0, -VERTICAL, 0.0).astype(jnp.float32)
    upper = jnp.where(level_ids < level_count - 1, -VERTICAL, 0.0).astype(jnp.float32)
    tables = []
    stride = 1
    while stride < level_count:
        lower_ratio = -lower / shift_levels(diagonal, stride, 0, 1.0)
        upper_ratio = -upper / shift_levels(diagonal, -stride, 0, 1.0)
        new_diagonal = (
            diagonal
            + lower_ratio * shift_levels(upper, stride, 0, 0.0)
            + upper_ratio * shift_levels(lower, -stride, 0, 0.0)
        )
        new_lower = lower_ratio * shift_levels(lower, stride, 0, 0.0)
        upper = upper_ratio * shift_levels(upper, -stride, 0, 0.0)
        lower = new_lower
        diagonal = new_diagonal
        tables.append((lower_ratio, upper_ratio, stride))
        stride = stride * 2
    return (tables, 1.0 / diagonal)


def vertical_solve(values, tables, inverse_diagonal):
    for lower_ratio, upper_ratio, stride in tables:
        values = (
            values
            + lower_ratio * shift_levels(values, stride, 1, 0.0)
            + upper_ratio * shift_levels(values, -stride, 1, 0.0)
        )
    return values * inverse_diagonal


def stencil(padded, values, kappa_sq):
    beside_x = padded[:, 1:-1, 2:, 1:-1] + padded[:, 1:-1, :-2, 1:-1]
    beside_y = padded[:, 1:-1, 1:-1, 2:] + padded[:, 1:-1, 1:-1, :-2]
    beside_z = padded[:, 2:, 1:-1, 1:-1] + padded[:, :-2, 1:-1, 1:-1]
    return (kappa_sq + (4.0 + 2.0 * VERTICAL)) * values - beside_x - beside_y - VERTICAL * beside_z


def slab_apply(values, kappa_sq):
    extended = with_halo(values, (("tile", 2), ("level", 1)), 1)
    padded = jnp.pad(extended, ((0, 0), (0, 0), (0, 0), (1, 1)))
    return stencil(padded, values, kappa_sq)


def local_dots(first, second):
    return jnp.sum(first * second, axis=(1, 2, 3))


def paired_totals(residual, precond, image_field):
    return lax.psum(
        (local_dots(residual, precond), local_dots(image_field, precond)), ("tile", "level")
    )


def conjugate_solve(right_side, apply_q, apply_m):
    shaped = (right_side.shape[0], 1, 1, 1)
    solution = jnp.zeros_like(right_side)
    residual = right_side
    precond = apply_m(residual)
    image_field = apply_q(precond)
    rho_now, curv_total = paired_totals(residual, precond, image_field)
    step_size = rho_now / curv_total
    direction = precond
    along_q = image_field
    for iteration in range(ITERS):
        solution = solution + step_size.reshape(shaped) * direction
        if iteration + 1 < ITERS:
            residual = residual - step_size.reshape(shaped) * along_q
            precond = apply_m(residual)
            image_field = apply_q(precond)
            rho_next, curv_total = paired_totals(residual, precond, image_field)
            beta_ratio = rho_next / rho_now
            step_size = rho_next / (curv_total - beta_ratio * rho_next / step_size)
            direction = precond + beta_ratio.reshape(shaped) * direction
            along_q = image_field + beta_ratio.reshape(shaped) * along_q
            rho_now = rho_next
    return solution


def body(probe_bits, kappa_sq, observed):
    sign_field = (2 * probe_bits - 1).astype(jnp.float32)
    stacked = jnp.concatenate([sign_field, observed[None]], axis=0)
    extended = with_halo(stacked, (("tile", 2), ("level", 1)), 1)
    padded = jnp.pad(extended, ((0, 0), (0, 0), (0, 0), (1, 1)))
    k_stacked = stencil(padded, stacked, kappa_sq)
    k_signs = k_stacked[:-1]
    data_term = 2.0 * observed * k_stacked[-1]
    kappa_cols = lax.all_to_all(kappa_sq[None], "level", split_axis=3, concat_axis=1, tiled=True)[0]
    tables, inverse_diagonal = reduction_tables(kappa_cols)

    def solve_columns(columns):
        solved = vertical_solve(
            vertical_solve(columns, tables, inverse_diagonal), tables, inverse_diagonal
        )
        return lax.all_to_all(solved, "level", split_axis=1, concat_axis=3, tiled=True)

    def apply_m(values):
        return solve_columns(
            lax.all_to_all(values, "level", split_axis=3, concat_axis=1, tiled=True)
        )

    def apply_q(values):
        return slab_apply(slab_apply(values, kappa_sq), kappa_sq)

    solution = conjugate_solve(sign_field, apply_q, apply_m)
    probe_partial = jnp.sum(
        solution * k_signs + slab_apply(solution, kappa_sq) * sign_field, axis=0
    )
    summed = lax.psum_scatter(probe_partial, "probe", scatter_dimension=2, tiled=True)
    y_width = summed.shape[2]
    offset = lax.axis_index("probe") * y_width
    kappa_part = lax.dynamic_slice_in_dim(kappa_sq, offset, y_width, 2)
    data_part = lax.dynamic_slice_in_dim(data_term, offset, y_width, 2)
    probe_count = probe_bits.shape[0] * lax.axis_size("probe")
    return kappa_part * (summed / probe_count - data_part)


def solution(mesh):
    in_specs = (
        P("probe", "level", "tile", None),
        P("level", "tile", None),
        P("level", "tile", None),
    )
    out_specs = P("level", "tile", "probe")
    return jax.shard_map(body, mesh=mesh, in_specs=in_specs, out_specs=out_specs, check_vma=False)
```

profile of v0, /device:TPU:0, one launch (start us, length us, event | category | flops | bytes accessed | tf_op | source)
XLA Modules:
  0.0 430.8 jit_solution(11291845997502162646)
XLA Ops:
  9.2 4.2 all-to-all-start.1
  15.1 4.2 all-to-all-done.1
  19.3 3.4 all-to-all-start
  25.7 2.2 all-to-all-done
  32.5 7.7 %all_to_all.165 = f32[1,64,8,128]{3,2,0,1:T(8,128)S(1)} all-to-all(f32[1,64,8,128]{3,2,0,1:T(8,128)S(1)} %fusion.226), channel_id=1, replica_groups=mesh['probe'=4,'tile'=4,'level'=2] {'level'}, dimensions={1} | all-to-all | bytes 524288 | tf_op jit(solution)/shard_map/all_to_all | solution.py:139
  41.6 4.5 %collective-permute-start.1 = (f32[1,32,1,256]{3,2,1,0:T(1,128)S(1)}, f32[1,32,1,256]{3,2,1,0:T(1,128)S(1)}, u32[]{:S(2)}, u32[]{:S(2)}) collective-permute-start(f32[1,32,1,256]{3,2,1,0:T(1,128)S(1)} %get-tuple-element.90), channel_id=1, source_target_pairs={{0,2},{2,4},{4,6},{1,3},{3,5},{5,7},{8,10},{10,12},{12,14},{9,11},... | collective-permute-start | bytes 98312 | tf_op jit(solution)/shard_map/ppermute | solution.py:20
  47.7 1.9 collective-permute-start.2
  51.1 4.2 collective-permute-done.3
  57.5 4.9 %collective-permute-start.5 = (f32[1,32,1,256]{3,2,1,0:T(1,128)S(1)}, f32[1,32,1,256]{3,2,1,0:T(1,128)S(1)}, u32[]{:S(2)}, u32[]{:S(2)}) collective-permute-start(f32[1,32,1,256]{3,2,1,0:T(1,128)S(1)} %get-tuple-element.88), channel_id=1, source_target_pairs={{0,2},{2,4},{4,6},{1,3},{3,5},{5,7},{8,10},{10,12},{12,14},{9,11},... | collective-permute-start | bytes 98312 | tf_op jit(solution)/shard_map/ppermute | solution.py:20
  63.9 1.6 collective-permute-start.6
  67.0 4.2 collective-permute-done.7
  71.8 1.6 multiply_reduce_fusion.5
  73.4 22.0 %all-reduce.143 = (f32[1]{0:T(128)}, f32[1]{0:T(128)}) all-reduce(f32[1]{0:T(128)} %bitcast.26, f32[1]{0:T(128)} %bitcast.30), channel_id=1, replica_groups=mesh['probe'=4,'tile'=4,'level'=2] {'tile','level'}, use_global_device_ids=true, to_apply=%region_1.2 | all-reduce | flops 2 | bytes 16 | tf_op jit(solution)/shard_map/psum | solution.py:94
  96.7 1.8 multiply_subtract_fusion.2
  98.4 2.3 copy.53
  100.7 2.4 reshape.155
  103.1 9.4 %all_to_all.166 = f32[2,1,32768]{2,1,0:T(1,128)} all-to-all(f32[2,1,32768]{2,1,0:T(1,128)} %reshape.155), channel_id=1, replica_groups=mesh['probe'=4,'tile'=4,'level'=2] {'level'}, dimensions={0} | all-to-all | bytes 524288 | tf_op jit(solution)/shard_map/all_to_all | solution.py:143
  112.5 3.0 reduce.10
  115.5 2.4 reshape.156
  117.9 2.2 copy.54
  122.2 7.7 %all_to_all.167 = f32[1,64,8,128]{3,2,0,1:T(8,128)S(1)} all-to-all(f32[1,64,8,128]{3,2,0,1:T(8,128)S(1)} %fusion.237), channel_id=1, replica_groups=mesh['probe'=4,'tile'=4,'level'=2] {'level'}, dimensions={1} | all-to-all | bytes 524288 | tf_op jit(solution)/shard_map/all_to_all | solution.py:139
  131.3 4.5 %collective-permute-start.9 = (f32[1,32,1,256]{3,2,1,0:T(1,128)S(1)}, f32[1,32,1,256]{3,2,1,0:T(1,128)S(1)}, u32[]{:S(2)}, u32[]{:S(2)}) collective-permute-start(f32[1,32,1,256]{3,2,1,0:T(1,128)S(1)} %get-tuple-element.86), channel_id=1, source_target_pairs={{0,2},{2,4},{4,6},{1,3},{3,5},{5,7},{8,10},{10,12},{12,14},{9,11},... | collective-permute-start | bytes 98312 | tf_op jit(solution)/shard_map/ppermute | solution.py:20
  137.4 1.7 collective-permute-start.10
  140.6 4.2 collective-permute-done.11
  147.0 4.9 %collective-permute-start.13 = (f32[1,32,1,256]{3,2,1,0:T(1,128)S(1)}, f32[1,32,1,256]{3,2,1,0:T(1,128)S(1)}, u32[]{:S(2)}, u32[]{:S(2)}) collective-permute-start(f32[1,32,1,256]{3,2,1,0:T(1,128)S(1)} %get-tuple-element.84), channel_id=1, source_target_pairs={{0,2},{2,4},{4,6},{1,3},{3,5},{5,7},{8,10},{10,12},{12,14},{9,11},... | collective-permute-start | bytes 98312 | tf_op jit(solution)/shard_map/ppermute | solution.py:20
  156.5 4.2 collective-permute-done.15
  161.3 1.7 multiply_reduce_fusion.3
  162.9 20.3 %all-reduce.142 = (f32[1]{0:T(128)}, f32[1]{0:T(128)}) all-reduce(f32[1]{0:T(128)} %bitcast.39, f32[1]{0:T(128)} %bitcast.42), channel_id=1, replica_groups=mesh['probe'=4,'tile'=4,'level'=2] {'tile','level'}, use_global_device_ids=true, to_apply=%region_5.6 | all-reduce | flops 2 | bytes 16 | tf_op jit(solution)/shard_map/psum | solution.py:94
  187.7 1.9 multiply_subtract_fusion.1
  189.6 2.3 copy.59
  191.9 2.4 reshape.157
  194.3 9.4 %all_to_all.168 = f32[2,1,32768]{2,1,0:T(1,128)} all-to-all(f32[2,1,32768]{2,1,0:T(1,128)} %reshape.157), channel_id=1, replica_groups=mesh['probe'=4,'tile'=4,'level'=2] {'level'}, dimensions={0} | all-to-all | bytes 524288 | tf_op jit(solution)/shard_map/all_to_all | solution.py:143
  203.6 3.1 reduce.11
  206.7 2.4 reshape.158
  209.1 2.3 copy.60
  213.4 7.6 %all_to_all.169 = f32[1,64,8,128]{3,2,0,1:T(8,128)S(1)} all-to-all(f32[1,64,8,128]{3,2,0,1:T(8,128)S(1)} %fusion.248), channel_id=1, replica_groups=mesh['probe'=4,'tile'=4,'level'=2] {'level'}, dimensions={1} | all-to-all | bytes 524288 | tf_op jit(solution)/shard_map/all_to_all | solution.py:139
  222.3 4.5 %collective-permute-start.17 = (f32[1,32,1,256]{3,2,1,0:T(1,128)S(1)}, f32[1,32,1,256]{3,2,1,0:T(1,128)S(1)}, u32[]{:S(2)}, u32[]{:S(2)}) collective-permute-start(f32[1,32,1,256]{3,2,1,0:T(1,128)S(1)} %get-tuple-element.82), channel_id=1, source_target_pairs={{0,2},{2,4},{4,6},{1,3},{3,5},{5,7},{8,10},{10,12},{12,14},{9,11},... | collective-permute-start | bytes 98312 | tf_op jit(solution)/shard_map/ppermute | solution.py:20
  228.5 1.9 collective-permute-start.18
  231.8 4.2 collective-permute-done.19
  238.2 4.9 %collective-permute-start.21 = (f32[1,32,1,256]{3,2,1,0:T(1,128)S(1)}, f32[1,32,1,256]{3,2,1,0:T(1,128)S(1)}, u32[]{:S(2)}, u32[]{:S(2)}) collective-permute-start(f32[1,32,1,256]{3,2,1,0:T(1,128)S(1)} %get-tuple-element.80), channel_id=1, source_target_pairs={{0,2},{2,4},{4,6},{1,3},{3,5},{5,7},{8,10},{10,12},{12,14},{9,11},... | collective-permute-start | bytes 98312 | tf_op jit(solution)/shard_map/ppermute | solution.py:20
  244.6 1.6 collective-permute-start.22
  247.7 4.2 collective-permute-done.23
  252.5 1.7 multiply_reduce_fusion.1
  254.1 20.1 %all-reduce.141 = (f32[1]{0:T(128)}, f32[1]{0:T(128)}) all-reduce(f32[1]{0:T(128)} %bitcast.52, f32[1]{0:T(128)} %bitcast.55), channel_id=1, replica_groups=mesh['probe'=4,'tile'=4,'level'=2] {'tile','level'}, use_global_device_ids=true, to_apply=%region_9.10 | all-reduce | flops 2 | bytes 16 | tf_op jit(solution)/shard_map/psum | solution.py:94
  278.0 2.0 multiply_subtract_fusion
  280.0 2.3 copy.65
  282.3 2.4 reshape.159
  284.7 9.4 %all_to_all.170 = f32[2,1,32768]{2,1,0:T(1,128)} all-to-all(f32[2,1,32768]{2,1,0:T(1,128)} %reshape.159), channel_id=1, replica_groups=mesh['probe'=4,'tile'=4,'level'=2] {'level'}, dimensions={0} | all-to-all | bytes 524288 | tf_op jit(solution)/shard_map/all_to_all | solution.py:143
  294.0 3.1 reduce.12
  297.1 2.4 reshape.160
  299.5 2.2 copy.66
  303.8 7.7 %all_to_all.171 = f32[1,64,8,128]{3,2,0,1:T(8,128)S(1)} all-to-all(f32[1,64,8,128]{3,2,0,1:T(8,128)S(1)} %fusion.259), channel_id=1, replica_groups=mesh['probe'=4,'tile'=4,'level'=2] {'level'}, dimensions={1} | all-to-all | bytes 524288 | tf_op jit(solution)/shard_map/all_to_all | solution.py:139
  312.8 4.5 %collective-permute-start.25 = (f32[1,32,1,256]{3,2,1,0:T(1,128)S(1)}, f32[1,32,1,256]{3,2,1,0:T(1,128)S(1)}, u32[]{:S(2)}, u32[]{:S(2)}) collective-permute-start(f32[1,32,1,256]{3,2,1,0:T(1,128)S(1)} %get-tuple-element.78), channel_id=1, source_target_pairs={{0,2},{2,4},{4,6},{1,3},{3,5},{5,7},{8,10},{10,12},{12,14},{9,11},... | collective-permute-start | bytes 98312 | tf_op jit(solution)/shard_map/ppermute | solution.py:20
  319.0 2.0 collective-permute-start.26
  323.7 4.9 %collective-permute-start.33 = (f32[2,32,1,256]{3,2,1,0:T(1,128)S(1)}, f32[2,32,1,256]{3,2,1,0:T(1,128)S(1)}, u32[]{:S(2)}, u32[]{:S(2)}) collective-permute-start(f32[2,32,1,256]{3,2,1,0:T(1,128)S(1)} %get-tuple-element.54), channel_id=1, source_target_pairs={{0,2},{2,4},{4,6},{1,3},{3,5},{5,7},{8,10},{10,12},{12,14},{9,11},... | collective-permute-start | bytes 196616 | tf_op jit(solution)/shard_map/ppermute | solution.py:20
  330.9 4.5 %collective-permute-start.29 = (f32[1,32,1,256]{3,2,1,0:T(1,128)S(1)}, f32[1,32,1,256]{3,2,1,0:T(1,128)S(1)}, u32[]{:S(2)}, u32[]{:S(2)}) collective-permute-start(f32[1,32,1,256]{3,2,1,0:T(1,128)S(1)} %get-tuple-element.76), channel_id=1, source_target_pairs={{0,2},{2,4},{4,6},{1,3},{3,5},{5,7},{8,10},{10,12},{12,14},{9,11},... | collective-permute-start | bytes 98312 | tf_op jit(solution)/shard_map/ppermute | solution.py:20
  337.0 4.5 %collective-permute-start.30 = (f32[1,1,10,256]{3,2,1,0:T(8,128)S(1)}, f32[1,1,10,256]{3,2,1,0:T(8,128)S(1)}, u32[]{:S(2)}, u32[]{:S(2)}) collective-permute-start(f32[1,1,10,256]{3,2,1,0:T(8,128)S(1)} %get-tuple-element.59), channel_id=1, source_target_pairs={{0,1},{2,3},{4,5},{6,7},{8,9},{10,11},{12,13},{14,15},{16,17},{18,... | collective-permute-start | bytes 30728 | tf_op jit(solution)/shard_map/ppermute | solution.py:20
  343.1 4.5 %collective-permute-start.34 = (f32[2,1,10,256]{3,2,1,0:T(8,128)S(1)}, f32[2,1,10,256]{3,2,1,0:T(8,128)S(1)}, u32[]{:S(2)}, u32[]{:S(2)}) collective-permute-start(f32[2,1,10,256]{3,2,1,0:T(8,128)S(1)} %get-tuple-element.47), channel_id=1, source_target_pairs={{0,1},{2,3},{4,5},{6,7},{8,9},{10,11},{12,13},{14,15},{16,17},{18,... | collective-permute-start | bytes 61448 | tf_op jit(solution)/shard_map/ppermute | solution.py:20
  350.5 23.0 %all-reduce.140 = (f32[1]{0:T(128)}, f32[1]{0:T(128)}) all-reduce(f32[1]{0:T(128)} %bitcast.65, f32[1]{0:T(128)} %bitcast.68), channel_id=1, replica_groups=mesh['probe'=4,'tile'=4,'level'=2] {'tile','level'}, use_global_device_ids=true, to_apply=%region_13.14 | all-reduce | flops 2 | bytes 16 | tf_op jit(solution)/shard_map/psum | solution.py:94
  378.7 4.5 %collective-permute-start.37 = (f32[1,32,1,256]{3,2,1,0:T(1,128)S(1)}, f32[1,32,1,256]{3,2,1,0:T(1,128)S(1)}, u32[]{:S(2)}, u32[]{:S(2)}) collective-permute-start(f32[1,32,1,256]{3,2,1,0:T(1,128)S(1)} %get-tuple-element.74), channel_id=1, source_target_pairs={{0,2},{2,4},{4,6},{1,3},{3,5},{5,7},{8,10},{10,12},{12,14},{9,11},... | collective-permute-start | bytes 98312 | tf_op jit(solution)/shard_map/ppermute | solution.py:20
  388.1 3.8 collective-permute-done.39
  392.9 4.4 %copy.71 = f32[32,8,256]{1,0,2:T(8,128)} copy(f32[32,8,256]{2,1,0:T(8,128)S(1)} %fusion.266) | data formatting | bytes 524288
  397.2 4.7 %reshape.149 = f32[256,256]{1,0:T(8,128)} reshape(f32[256,32,8]{2,1,0:T(8,128)} %bitcast.303) | data formatting | bytes 524288
  402.0 19.2 %reduce-scatter.4.cloned.1.call-done = f32[64,256]{1,0:T(8,128)} async-done(((f32[256,256]{1,0:T(8,128)}), f32[64,256]{1,0:T(8,128)}) %reduce-scatter.4.cloned.1.call-update) | async-done | bytes 65552
  (213 shorter events, 72.9 us)
Async XLA Ops:
  7.9 5.5 %copy-start.12 = (s32[1,32,8,256]{3,2,1,0:T(8,128)S(1)}, s32[1,32,8,256]{3,2,1,0:T(8,128)}, u32[]{:S(2)}) copy-start(s32[1,32,8,256]{3,2,1,0:T(8,128)} %param.3) | copy-start | bytes 786436
  9.2 10.1 %all-to-all-start.1 = ((f32[2,1,32768]{2,1,0:T(1,128)}), f32[2,1,32768]{2,1,0:T(1,128)S(1)}, u32[]{:S(2)}, u32[]{:S(2)}) async-start(f32[2,1,32768]{2,1,0:T(1,128)} %reshape.151), calls=%async_computation.1 | async-start | bytes 524288 | tf_op jit(solution)/shard_map/all_to_all | solution.py:132
  13.4 11.3 %copy-start.1 = (f32[1,32,8,256]{3,2,1,0:T(8,128)}, f32[1,32,8,256]{3,2,1,0:T(8,128)S(1)}, u32[]{:S(2)}) copy-start(f32[1,32,8,256]{3,2,1,0:T(8,128)S(1)} %add_convert_fusion) | copy-start | bytes 786436
  19.3 8.6 %all-to-all-start = ((f32[2,1,32768]{2,1,0:T(1,128)}), f32[2,1,32768]{2,1,0:T(1,128)S(1)}, u32[]{:S(2)}, u32[]{:S(2)}) async-start(f32[2,1,32768]{2,1,0:T(1,128)} %reshape.153), calls=%async_computation | async-start | bytes 524288 | tf_op jit(solution)/shard_map/all_to_all | solution.py:143
  22.7 398.4 %reduce-scatter.4.cloned.1.call-start = ((), (), s32[]{:S(2)}) async-start(), calls=%async_computation.10 | async-start | bytes 327680
  32.5 23.3 %copy-start = (f32[32,8,256]{2,1,0:T(8,128)S(1)}, f32[32,8,256]{2,1,0:T(8,128)}, u32[]{:S(2)}) copy-start(f32[32,8,256]{2,1,0:T(8,128)} %param.4) | copy-start | bytes 786436
  40.2 31.5 %copy-start.3 = (f32[1,64,8,128]{3,2,0,1:T(8,128)}, f32[1,64,8,128]{3,2,0,1:T(8,128)S(1)}, u32[]{:S(2)}) copy-start(f32[1,64,8,128]{3,2,0,1:T(8,128)S(1)} %all_to_all.165) | copy-start | bytes 786436
  40.3 5.9 %collective-permute-start = (f32[1,32,1,256]{3,2,1,0:T(1,128)S(1)}, f32[1,32,1,256]{3,2,1,0:T(1,128)S(1)}, u32[]{:S(2)}, u32[]{:S(2)}) collective-permute-start(f32[1,32,1,256]{3,2,1,0:T(1,128)S(1)} %get-tuple-element.91), channel_id=1, source_target_pairs={{2,0},{4,2},{6,4},{3,1},{5,3},{7,5},{10,8},{12,10},{14,12},{11,9},... | collective-permute-start | bytes 98312 | tf_op jit(solution)/shard_map/ppermute | solution.py:22
  41.6 6.1 %collective-permute-start.1 = (f32[1,32,1,256]{3,2,1,0:T(1,128)S(1)}, f32[1,32,1,256]{3,2,1,0:T(1,128)S(1)}, u32[]{:S(2)}, u32[]{:S(2)}) collective-permute-start(f32[1,32,1,256]{3,2,1,0:T(1,128)S(1)} %get-tuple-element.90), channel_id=1, source_target_pairs={{0,2},{2,4},{4,6},{1,3},{3,5},{5,7},{8,10},{10,12},{12,14},{9,11},... | collective-permute-start | bytes 98312 | tf_op jit(solution)/shard_map/ppermute | solution.py:20
  47.7 3.4 collective-permute-start.2
  49.7 5.6 %collective-permute-start.3 = (f32[1,1,10,256]{3,2,1,0:T(8,128)S(1)}, f32[1,1,10,256]{3,2,1,0:T(8,128)S(1)}, u32[]{:S(2)}, u32[]{:S(2)}) collective-permute-start(f32[1,1,10,256]{3,2,1,0:T(8,128)S(1)} %get-tuple-element.72), channel_id=1, source_target_pairs={{1,0},{3,2},{5,4},{7,6},{9,8},{11,10},{13,12},{15,14},{17,16},{19,... | collective-permute-start | bytes 30728 | tf_op jit(solution)/shard_map/ppermute | solution.py:22
  55.8 15.9 %copy-start.13 = (s32[1,32,8,256]{3,2,1,0:T(8,128)S(1)}, s32[1,32,8,256]{3,2,1,0:T(8,128)}, u32[]{:S(2)}) copy-start(s32[1,32,8,256]{3,2,1,0:T(8,128)} %param.3) | copy-start | bytes 786436
  56.2 6.2 %collective-permute-start.4 = (f32[1,32,1,256]{3,2,1,0:T(1,128)S(1)}, f32[1,32,1,256]{3,2,1,0:T(1,128)S(1)}, u32[]{:S(2)}, u32[]{:S(2)}) collective-permute-start(f32[1,32,1,256]{3,2,1,0:T(1,128)S(1)} %get-tuple-element.89), channel_id=1, source_target_pairs={{2,0},{4,2},{6,4},{3,1},{5,3},{7,5},{10,8},{12,10},{14,12},{11,9},... | collective-permute-start | bytes 98312 | tf_op jit(solution)/shard_map/ppermute | solution.py:22
  57.5 6.4 %collective-permute-start.5 = (f32[1,32,1,256]{3,2,1,0:T(1,128)S(1)}, f32[1,32,1,256]{3,2,1,0:T(1,128)S(1)}, u32[]{:S(2)}, u32[]{:S(2)}) collective-permute-start(f32[1,32,1,256]{3,2,1,0:T(1,128)S(1)} %get-tuple-element.88), channel_id=1, source_target_pairs={{0,2},{2,4},{4,6},{1,3},{3,5},{5,7},{8,10},{10,12},{12,14},{9,11},... | collective-permute-start | bytes 98312 | tf_op jit(solution)/shard_map/ppermute | solution.py:20
  63.9 3.1 collective-permute-start.6
  65.6 5.6 %collective-permute-start.7 = (f32[1,1,10,256]{3,2,1,0:T(8,128)S(1)}, f32[1,1,10,256]{3,2,1,0:T(8,128)S(1)}, u32[]{:S(2)}, u32[]{:S(2)}) collective-permute-start(f32[1,1,10,256]{3,2,1,0:T(8,128)S(1)} %get-tuple-element.70), channel_id=1, source_target_pairs={{1,0},{3,2},{5,4},{7,6},{9,8},{11,10},{13,12},{15,14},{17,16},{19,... | collective-permute-start | bytes 30728 | tf_op jit(solution)/shard_map/ppermute | solution.py:22
  129.9 31.3 %copy-start.5 = (f32[1,64,8,128]{3,2,0,1:T(8,128)}, f32[1,64,8,128]{3,2,0,1:T(8,128)S(1)}, u32[]{:S(2)}) copy-start(f32[1,64,8,128]{3,2,0,1:T(8,128)S(1)} %all_to_all.167) | copy-start | bytes 786436
  130.0 5.9 %collective-permute-start.8 = (f32[1,32,1,256]{3,2,1,0:T(1,128)S(1)}, f32[1,32,1,256]{3,2,1,0:T(1,128)S(1)}, u32[]{:S(2)}, u32[]{:S(2)}) collective-permute-start(f32[1,32,1,256]{3,2,1,0:T(1,128)S(1)} %get-tuple-element.87), channel_id=1, source_target_pairs={{2,0},{4,2},{6,4},{3,1},{5,3},{7,5},{10,8},{12,10},{14,12},{11,9},... | collective-permute-start | bytes 98312 | tf_op jit(solution)/shard_map/ppermute | solution.py:22
  131.3 6.1 %collective-permute-start.9 = (f32[1,32,1,256]{3,2,1,0:T(1,128)S(1)}, f32[1,32,1,256]{3,2,1,0:T(1,128)S(1)}, u32[]{:S(2)}, u32[]{:S(2)}) collective-permute-start(f32[1,32,1,256]{3,2,1,0:T(1,128)S(1)} %get-tuple-element.86), channel_id=1, source_target_pairs={{0,2},{2,4},{4,6},{1,3},{3,5},{5,7},{8,10},{10,12},{12,14},{9,11},... | collective-permute-start | bytes 98312 | tf_op jit(solution)/shard_map/ppermute | solution.py:20
  137.4 3.2 collective-permute-start.10
  139.2 5.6 %collective-permute-start.11 = (f32[1,1,10,256]{3,2,1,0:T(8,128)S(1)}, f32[1,1,10,256]{3,2,1,0:T(8,128)S(1)}, u32[]{:S(2)}, u32[]{:S(2)}) collective-permute-start(f32[1,1,10,256]{3,2,1,0:T(8,128)S(1)} %get-tuple-element.68), channel_id=1, source_target_pairs={{1,0},{3,2},{5,4},{7,6},{9,8},{11,10},{13,12},{15,14},{17,16},{19,... | collective-permute-start | bytes 30728 | tf_op jit(solution)/shard_map/ppermute | solution.py:22
  145.3 15.9 %copy-start.11 = (f32[1,32,8,256]{3,2,1,0:T(8,128)S(1)}, f32[1,32,8,256]{3,2,1,0:T(8,128)}, u32[]{:S(2)}) copy-start(f32[1,32,8,256]{3,2,1,0:T(8,128)} %multiply_subtract_fusion.2) | copy-start | bytes 786436
  145.7 6.2 %collective-permute-start.12 = (f32[1,32,1,256]{3,2,1,0:T(1,128)S(1)}, f32[1,32,1,256]{3,2,1,0:T(1,128)S(1)}, u32[]{:S(2)}, u32[]{:S(2)}) collective-permute-start(f32[1,32,1,256]{3,2,1,0:T(1,128)S(1)} %get-tuple-element.85), channel_id=1, source_target_pairs={{2,0},{4,2},{6,4},{3,1},{5,3},{7,5},{10,8},{12,10},{14,12},{11,9},... | collective-permute-start | bytes 98312 | tf_op jit(solution)/shard_map/ppermute | solution.py:22
  147.0 6.4 %collective-permute-start.13 = (f32[1,32,1,256]{3,2,1,0:T(1,128)S(1)}, f32[1,32,1,256]{3,2,1,0:T(1,128)S(1)}, u32[]{:S(2)}, u32[]{:S(2)}) collective-permute-start(f32[1,32,1,256]{3,2,1,0:T(1,128)S(1)} %get-tuple-element.84), channel_id=1, source_target_pairs={{0,2},{2,4},{4,6},{1,3},{3,5},{5,7},{8,10},{10,12},{12,14},{9,11},... | collective-permute-start | bytes 98312 | tf_op jit(solution)/shard_map/ppermute | solution.py:20
  153.4 3.1 collective-permute-start.14
  155.1 5.6 %collective-permute-start.15 = (f32[1,1,10,256]{3,2,1,0:T(8,128)S(1)}, f32[1,1,10,256]{3,2,1,0:T(8,128)S(1)}, u32[]{:S(2)}, u32[]{:S(2)}) collective-permute-start(f32[1,1,10,256]{3,2,1,0:T(8,128)S(1)} %get-tuple-element.66), channel_id=1, source_target_pairs={{1,0},{3,2},{5,4},{7,6},{9,8},{11,10},{13,12},{15,14},{17,16},{19,... | collective-permute-start | bytes 30728 | tf_op jit(solution)/shard_map/ppermute | solution.py:22
  220.9 31.5 %copy-start.7 = (f32[1,64,8,128]{3,2,0,1:T(8,128)}, f32[1,64,8,128]{3,2,0,1:T(8,128)S(1)}, u32[]{:S(2)}) copy-start(f32[1,64,8,128]{3,2,0,1:T(8,128)S(1)} %all_to_all.169) | copy-start | bytes 786436
  221.0 5.9 %collective-permute-start.16 = (f32[1,32,1,256]{3,2,1,0:T(1,128)S(1)}, f32[1,32,1,256]{3,2,1,0:T(1,128)S(1)}, u32[]{:S(2)}, u32[]{:S(2)}) collective-permute-start(f32[1,32,1,256]{3,2,1,0:T(1,128)S(1)} %get-tuple-element.83), channel_id=1, source_target_pairs={{2,0},{4,2},{6,4},{3,1},{5,3},{7,5},{10,8},{12,10},{14,12},{11,9},... | collective-permute-start | bytes 98312 | tf_op jit(solution)/shard_map/ppermute | solution.py:22
  222.3 6.1 %collective-permute-start.17 = (f32[1,32,1,256]{3,2,1,0:T(1,128)S(1)}, f32[1,32,1,256]{3,2,1,0:T(1,128)S(1)}, u32[]{:S(2)}, u32[]{:S(2)}) collective-permute-start(f32[1,32,1,256]{3,2,1,0:T(1,128)S(1)} %get-tuple-element.82), channel_id=1, source_target_pairs={{0,2},{2,4},{4,6},{1,3},{3,5},{5,7},{8,10},{10,12},{12,14},{9,11},... | collective-permute-start | bytes 98312 | tf_op jit(solution)/shard_map/ppermute | solution.py:20
  228.5 3.4 collective-permute-start.18
  230.4 5.6 %collective-permute-start.19 = (f32[1,1,10,256]{3,2,1,0:T(8,128)S(1)}, f32[1,1,10,256]{3,2,1,0:T(8,128)S(1)}, u32[]{:S(2)}, u32[]{:S(2)}) collective-permute-start(f32[1,1,10,256]{3,2,1,0:T(8,128)S(1)} %get-tuple-element.64), channel_id=1, source_target_pairs={{1,0},{3,2},{5,4},{7,6},{9,8},{11,10},{13,12},{15,14},{17,16},{19,... | collective-permute-start | bytes 30728 | tf_op jit(solution)/shard_map/ppermute | solution.py:22
  236.6 15.9 %copy-start.10 = (f32[1,32,8,256]{3,2,1,0:T(8,128)S(1)}, f32[1,32,8,256]{3,2,1,0:T(8,128)}, u32[]{:S(2)}) copy-start(f32[1,32,8,256]{3,2,1,0:T(8,128)} %multiply_subtract_fusion.1) | copy-start | bytes 786436
  236.9 6.2 %collective-permute-start.20 = (f32[1,32,1,256]{3,2,1,0:T(1,128)S(1)}, f32[1,32,1,256]{3,2,1,0:T(1,128)S(1)}, u32[]{:S(2)}, u32[]{:S(2)}) collective-permute-start(f32[1,32,1,256]{3,2,1,0:T(1,128)S(1)} %get-tuple-element.81), channel_id=1, source_target_pairs={{2,0},{4,2},{6,4},{3,1},{5,3},{7,5},{10,8},{12,10},{14,12},{11,9},... | collective-permute-start | bytes 98312 | tf_op jit(solution)/shard_map/ppermute | solution.py:22
  238.2 6.4 %collective-permute-start.21 = (f32[1,32,1,256]{3,2,1,0:T(1,128)S(1)}, f32[1,32,1,256]{3,2,1,0:T(1,128)S(1)}, u32[]{:S(2)}, u32[]{:S(2)}) collective-permute-start(f32[1,32,1,256]{3,2,1,0:T(1,128)S(1)} %get-tuple-element.80), channel_id=1, source_target_pairs={{0,2},{2,4},{4,6},{1,3},{3,5},{5,7},{8,10},{10,12},{12,14},{9,11},... | collective-permute-start | bytes 98312 | tf_op jit(solution)/shard_map/ppermute | solution.py:20
  244.6 3.1 collective-permute-start.22
  246.3 5.6 %collective-permute-start.23 = (f32[1,1,10,256]{3,2,1,0:T(8,128)S(1)}, f32[1,1,10,256]{3,2,1,0:T(8,128)S(1)}, u32[]{:S(2)}, u32[]{:S(2)}) collective-permute-start(f32[1,1,10,256]{3,2,1,0:T(8,128)S(1)} %get-tuple-element.62), channel_id=1, source_target_pairs={{1,0},{3,2},{5,4},{7,6},{9,8},{11,10},{13,12},{15,14},{17,16},{19,... | collective-permute-start | bytes 30728 | tf_op jit(solution)/shard_map/ppermute | solution.py:22
  303.7 18.6 %copy-start.2 = (f32[1,32,8,256]{3,2,1,0:T(8,128)S(1)}, f32[1,32,8,256]{3,2,1,0:T(8,128)}, u32[]{:S(2)}) copy-start(f32[1,32,8,256]{3,2,1,0:T(8,128)} %copy-done.1) | copy-start | bytes 786436
  303.7 18.6 %copy-start.9 = (f32[32,8,256]{2,1,0:T(8,128)S(1)}, f32[32,8,256]{2,1,0:T(8,128)}, u32[]{:S(2)}) copy-start(f32[32,8,256]{2,1,0:T(8,128)} %param.5) | copy-start | bytes 786436
  311.5 5.9 %collective-permute-start.24 = (f32[1,32,1,256]{3,2,1,0:T(1,128)S(1)}, f32[1,32,1,256]{3,2,1,0:T(1,128)S(1)}, u32[]{:S(2)}, u32[]{:S(2)}) collective-permute-start(f32[1,32,1,256]{3,2,1,0:T(1,128)S(1)} %get-tuple-element.79), channel_id=1, source_target_pairs={{2,0},{4,2},{6,4},{3,1},{5,3},{7,5},{10,8},{12,10},{14,12},{11,9},... | collective-permute-start | bytes 98312 | tf_op jit(solution)/shard_map/ppermute | solution.py:22
  312.8 6.1 %collective-permute-start.25 = (f32[1,32,1,256]{3,2,1,0:T(1,128)S(1)}, f32[1,32,1,256]{3,2,1,0:T(1,128)S(1)}, u32[]{:S(2)}, u32[]{:S(2)}) collective-permute-start(f32[1,32,1,256]{3,2,1,0:T(1,128)S(1)} %get-tuple-element.78), channel_id=1, source_target_pairs={{0,2},{2,4},{4,6},{1,3},{3,5},{5,7},{8,10},{10,12},{12,14},{9,11},... | collective-permute-start | bytes 98312 | tf_op jit(solution)/shard_map/ppermute | solution.py:20
  319.0 9.6 %collective-permute-start.26 = (f32[1,1,10,256]{3,2,1,0:T(8,128)S(1)}, f32[1,1,10,256]{3,2,1,0:T(8,128)S(1)}, u32[]{:S(2)}, u32[]{:S(2)}) collective-permute-start(f32[1,1,10,256]{3,2,1,0:T(8,128)S(1)} %get-tuple-element.61), channel_id=1, source_target_pairs={{0,1},{2,3},{4,5},{6,7},{8,9},{10,11},{12,13},{14,15},{16,17},{18,... | collective-permute-start | bytes 30728 | tf_op jit(solution)/shard_map/ppermute | solution.py:20
  321.0 7.6 %collective-permute-start.27 = (f32[1,1,10,256]{3,2,1,0:T(8,128)S(1)}, f32[1,1,10,256]{3,2,1,0:T(8,128)S(1)}, u32[]{:S(2)}, u32[]{:S(2)}) collective-permute-start(f32[1,1,10,256]{3,2,1,0:T(8,128)S(1)} %get-tuple-element.60), channel_id=1, source_target_pairs={{1,0},{3,2},{5,4},{7,6},{9,8},{11,10},{13,12},{15,14},{17,16},{19,... | collective-permute-start | bytes 30728 | tf_op jit(solution)/shard_map/ppermute | solution.py:22
  322.4 20.6 %collective-permute-start.32 = (f32[2,32,1,256]{3,2,1,0:T(1,128)S(1)}, f32[2,32,1,256]{3,2,1,0:T(1,128)S(1)}, u32[]{:S(2)}, u32[]{:S(2)}) collective-permute-start(f32[2,32,1,256]{3,2,1,0:T(1,128)S(1)} %get-tuple-element.55), channel_id=1, source_target_pairs={{2,0},{4,2},{6,4},{3,1},{5,3},{7,5},{10,8},{12,10},{14,12},{11,9},... | collective-permute-start | bytes 196616 | tf_op jit(solution)/shard_map/ppermute | solution.py:22
  323.7 19.4 %collective-permute-start.33 = (f32[2,32,1,256]{3,2,1,0:T(1,128)S(1)}, f32[2,32,1,256]{3,2,1,0:T(1,128)S(1)}, u32[]{:S(2)}, u32[]{:S(2)}) collective-permute-start(f32[2,32,1,256]{3,2,1,0:T(1,128)S(1)} %get-tuple-element.54), channel_id=1, source_target_pairs={{0,2},{2,4},{4,6},{1,3},{3,5},{5,7},{8,10},{10,12},{12,14},{9,11},... | collective-permute-start | bytes 196616 | tf_op jit(solution)/shard_map/ppermute | solution.py:20
  329.4 20.1 %copy-start.15 = (f32[1,32,8,256]{3,2,1,0:T(8,128)S(1)}, f32[1,32,8,256]{3,2,1,0:T(8,128)}, u32[]{:S(2)}) copy-start(f32[1,32,8,256]{3,2,1,0:T(8,128)} %multiply_subtract_fusion) | copy-start | bytes 786436
  329.4 6.0 %collective-permute-start.28 = (f32[1,32,1,256]{3,2,1,0:T(1,128)S(1)}, f32[1,32,1,256]{3,2,1,0:T(1,128)S(1)}, u32[]{:S(2)}, u32[]{:S(2)}) collective-permute-start(f32[1,32,1,256]{3,2,1,0:T(1,128)S(1)} %get-tuple-element.77), channel_id=1, source_target_pairs={{2,0},{4,2},{6,4},{3,1},{5,3},{7,5},{10,8},{12,10},{14,12},{11,9},... | collective-permute-start | bytes 98312 | tf_op jit(solution)/shard_map/ppermute | solution.py:22
  330.9 6.1 %collective-permute-start.29 = (f32[1,32,1,256]{3,2,1,0:T(1,128)S(1)}, f32[1,32,1,256]{3,2,1,0:T(1,128)S(1)}, u32[]{:S(2)}, u32[]{:S(2)}) collective-permute-start(f32[1,32,1,256]{3,2,1,0:T(1,128)S(1)} %get-tuple-element.76), channel_id=1, source_target_pairs={{0,2},{2,4},{4,6},{1,3},{3,5},{5,7},{8,10},{10,12},{12,14},{9,11},... | collective-permute-start | bytes 98312 | tf_op jit(solution)/shard_map/ppermute | solution.py:20
  337.0 11.9 %collective-permute-start.30 = (f32[1,1,10,256]{3,2,1,0:T(8,128)S(1)}, f32[1,1,10,256]{3,2,1,0:T(8,128)S(1)}, u32[]{:S(2)}, u32[]{:S(2)}) collective-permute-start(f32[1,1,10,256]{3,2,1,0:T(8,128)S(1)} %get-tuple-element.59), channel_id=1, source_target_pairs={{0,1},{2,3},{4,5},{6,7},{8,9},{10,11},{12,13},{14,15},{16,17},{18,... | collective-permute-start | bytes 30728 | tf_op jit(solution)/shard_map/ppermute | solution.py:20
  341.6 35.6 %copy-start.4 = (f32[1,64,8,128]{3,2,0,1:T(8,128)S(1)}, f32[1,64,8,128]{3,2,0,1:T(8,128)}, u32[]{:S(2)}) copy-start(f32[1,64,8,128]{3,2,0,1:T(8,128)} %copy-done.3) | copy-start | bytes 786436
  341.6 35.6 %copy-start.6 = (f32[1,64,8,128]{3,2,0,1:T(8,128)S(1)}, f32[1,64,8,128]{3,2,0,1:T(8,128)}, u32[]{:S(2)}) copy-start(f32[1,64,8,128]{3,2,0,1:T(8,128)} %copy-done.5) | copy-start | bytes 786436
  341.6 35.6 %copy-start.8 = (f32[1,64,8,128]{3,2,0,1:T(8,128)S(1)}, f32[1,64,8,128]{3,2,0,1:T(8,128)}, u32[]{:S(2)}) copy-start(f32[1,64,8,128]{3,2,0,1:T(8,128)} %copy-done.7) | copy-start | bytes 786436
  341.6 7.3 %collective-permute-start.31 = (f32[1,1,10,256]{3,2,1,0:T(8,128)S(1)}, f32[1,1,10,256]{3,2,1,0:T(8,128)S(1)}, u32[]{:S(2)}, u32[]{:S(2)}) collective-permute-start(f32[1,1,10,256]{3,2,1,0:T(8,128)S(1)} %get-tuple-element.58), channel_id=1, source_target_pairs={{1,0},{3,2},{5,4},{7,6},{9,8},{11,10},{13,12},{15,14},{17,16},{19,... | collective-permute-start | bytes 30728 | tf_op jit(solution)/shard_map/ppermute | solution.py:22
  343.1 40.2 %collective-permute-start.34 = (f32[2,1,10,256]{3,2,1,0:T(8,128)S(1)}, f32[2,1,10,256]{3,2,1,0:T(8,128)S(1)}, u32[]{:S(2)}, u32[]{:S(2)}) collective-permute-start(f32[2,1,10,256]{3,2,1,0:T(8,128)S(1)} %get-tuple-element.47), channel_id=1, source_target_pairs={{0,1},{2,3},{4,5},{6,7},{8,9},{10,11},{12,13},{14,15},{16,17},{18,... | collective-permute-start | bytes 61448 | tf_op jit(solution)/shard_map/ppermute | solution.py:20
  347.6 35.6 %collective-permute-start.35 = (f32[2,1,10,256]{3,2,1,0:T(8,128)S(1)}, f32[2,1,10,256]{3,2,1,0:T(8,128)S(1)}, u32[]{:S(2)}, u32[]{:S(2)}) collective-permute-start(f32[2,1,10,256]{3,2,1,0:T(8,128)S(1)} %get-tuple-element.46), channel_id=1, source_target_pairs={{1,0},{3,2},{5,4},{7,6},{9,8},{11,10},{13,12},{15,14},{17,16},{19,... | collective-permute-start | bytes 61448 | tf_op jit(solution)/shard_map/ppermute | solution.py:22
  377.4 6.9 %collective-permute-start.36 = (f32[1,32,1,256]{3,2,1,0:T(1,128)S(1)}, f32[1,32,1,256]{3,2,1,0:T(1,128)S(1)}, u32[]{:S(2)}, u32[]{:S(2)}) collective-permute-start(f32[1,32,1,256]{3,2,1,0:T(1,128)S(1)} %get-tuple-element.75), channel_id=1, source_target_pairs={{2,0},{4,2},{6,4},{3,1},{5,3},{7,5},{10,8},{12,10},{14,12},{11,9},... | collective-permute-start | bytes 98312 | tf_op jit(solution)/shard_map/ppermute | solution.py:22
  378.7 6.1 %collective-permute-start.37 = (f32[1,32,1,256]{3,2,1,0:T(1,128)S(1)}, f32[1,32,1,256]{3,2,1,0:T(1,128)S(1)}, u32[]{:S(2)}, u32[]{:S(2)}) collective-permute-start(f32[1,32,1,256]{3,2,1,0:T(1,128)S(1)} %get-tuple-element.74), channel_id=1, source_target_pairs={{0,2},{2,4},{4,6},{1,3},{3,5},{5,7},{8,10},{10,12},{12,14},{9,11},... | collective-permute-start | bytes 98312 | tf_op jit(solution)/shard_map/ppermute | solution.py:20
  384.8 3.3 collective-permute-start.38
  386.1 6.3 %copy-start.14 = (s32[1,32,8,256]{3,2,1,0:T(8,128)S(1)}, s32[1,32,8,256]{3,2,1,0:T(8,128)}, u32[]{:S(2)}) copy-start(s32[1,32,8,256]{3,2,1,0:T(8,128)} %param.3) | copy-start | bytes 786436
  386.1 5.8 %collective-permute-start.39 = (f32[1,1,10,256]{3,2,1,0:T(8,128)S(1)}, f32[1,1,10,256]{3,2,1,0:T(8,128)S(1)}, u32[]{:S(2)}, u32[]{:S(2)}) collective-permute-start(f32[1,1,10,256]{3,2,1,0:T(8,128)S(1)} %get-tuple-element.56), channel_id=1, source_target_pairs={{1,0},{3,2},{5,4},{7,6},{9,8},{11,10},{13,12},{15,14},{17,16},{19,... | collective-permute-start | bytes 30728 | tf_op jit(solution)/shard_map/ppermute | solution.py:22
Sparse Core Ops, SparseCore 0:
  402.1 19.0 reduce-scatter.3
where the time goes:
time: 433 us; the launch traced here: 431 us
  blocking collectives  144 us (33%)
  starting transfers between devices  104 us (24%)
  waiting for transfers between devices  68.5 us (16%)
  local copies, waits for them, and re-layouts  49.2 us (11%)
  other arithmetic  37.5 us (9%)
  between operations  28 us (6%)
    psum x4, blocking collectives, paired_totals(): lax.psum((local_dots(residual, precond), local_dots(image_field, precond)...  85.4 us
    ppermute x20, starting transfers between devices, with_halo(): lax.ppermute(tail, axis, [(i, (i + 1) % count) for i in range(ends)])  69.6 us
    all_to_all x4, blocking collectives, solve_columns(): lax.all_to_all(solved, 'level', split_axis=1, concat_axis=3, tiled=True)  30.7 us
    unnamed x48, local copies, waits for them, and re-layouts  30.2 us
    ppermute x20, waiting for transfers between devices, with_halo(): lax.ppermute(head, axis, [((i + 1) % count, i) for i in range(ends)])  29.1 us
    all_to_all x3, blocking collectives, apply_m(): lax.all_to_all(values, 'level', split_axis=3, concat_axis=1, tiled=True)  28.1 us
    ppermute x20, starting transfers between devices, with_halo(): lax.ppermute(head, axis, [((i + 1) % count, i) for i in range(ends)])  26.2 us
    unnamed x2, waiting for transfers between devices  19.2 us
  transfers between devices with their start and end apart: 43, of which 25 were waited for; matrix products, arithmetic and copies ran while one was open for 2% of the time, Pallas kernels for 0%

commit v1 on v0

v1 whole, which is shorter than its diff:
```python
import functools

import jax
import jax.numpy as jnp
from jax import lax
from jax.experimental import pallas as pl
from jax.experimental.pallas import tpu as pltpu
from jax.sharding import PartitionSpec as P

ITERS = 4
VERTICAL = 2.0
LANES = 128
ROWS = 8
EDGE = 8
GROUP = 4
SHIFTS = (1.0, 0.0, -2.0)
PAIRS = [(i, j) for j in range(ITERS) for i in range(j + 1)]
COUNT = len(PAIRS) + ITERS
SLOTS = 16


def two_sum(a, b):
    total = a + b
    part = total - a
    return total, (a - (total - part)) + (b - part)


def two_product(a, b):
    def split(v):
        big = v * 4097.0
        high = big - (big - v)
        return high, v - high

    product = a * b
    a_high, a_low = split(a)
    b_high, b_low = split(b)
    return product, ((a_high * b_high - product) + a_high * b_low + a_low * b_high) + a_low * b_low


def pair_add(first, second):
    total, rest = two_sum(first[0], second[0])
    rest = rest + (first[1] + second[1])
    high = total + rest
    return high, rest - (high - total)


def lane_ids(shape):
    return lax.broadcasted_iota(jnp.int32, shape, len(shape) - 1)


def row_ids(shape):
    return lax.broadcasted_iota(jnp.int32, shape, len(shape) - 2)


def pack_kernel(depth, bits_ref, kappa_ref, observed_ref, up_ref, down_ref, cross_ref):
    level = lax.axis_index("level")
    first = level == 0
    per_tile = LANES // EDGE
    tiles = depth // per_tile
    lanes = lane_ids((ROWS, LANES))

    def write(refs, offset, tile):
        for ref in refs:
            ref[offset] = tile

    for which, source in enumerate((bits_ref, kappa_ref)):
        base = which * (depth + tiles)

        def tile_loop(tile, unused, source=source, base=base, which=which):
            def step(slot, packed):
                z = tile * per_tile + slot
                value = source[z]
                if which == 0:
                    value = (2 * value - 1).astype(jnp.float32)
                low, high = value[:, :LANES], value[:, LANES:]
                same = jnp.where(first, low, high)
                cross = jnp.where(first, high, low)
                write((up_ref, down_ref), base + z, same)
                cross_ref[base + z] = cross
                here = lanes // EDGE == slot
                shift = lax.rem(EDGE * slot + EDGE * level, LANES)
                cross_shift = lax.rem(EDGE * slot + EDGE * (1 - level), LANES)
                return (
                    jnp.where(here, pltpu.roll(cross, shift, 1), packed[0]),
                    jnp.where(here, pltpu.roll(same, cross_shift, 1), packed[1]),
                )

            zero = jnp.zeros((ROWS, LANES), jnp.float32)
            packed = lax.fori_loop(0, per_tile, step, (zero, zero), unroll=4)
            write((up_ref, down_ref), base + depth + tile, packed[0])
            cross_ref[base + depth + tile] = packed[1]
            return unused

        lax.fori_loop(0, tiles, tile_loop, 0)
    base = 2 * (depth + tiles)
    in_low = lax.axis_index("probe") < lax.axis_size("probe") // 2

    def half(value):
        return jnp.where(in_low, value[..., :LANES], value[..., LANES:])

    top = half(observed_ref[:, ROWS - 1, :])
    bottom = half(observed_ref[:, 0, :])
    for tile in range(depth // ROWS):
        up_ref[base + tile] = top[tile * ROWS : (tile + 1) * ROWS]
        down_ref[base + tile] = bottom[tile * ROWS : (tile + 1) * ROWS]
    cross_ref[base] = jnp.where(first, half(observed_ref[depth - 1]), half(observed_ref[0]))


def beside(values):
    rows, columns = values.shape
    return (pltpu.roll(values, 1, 0) + pltpu.roll(values, rows - 1, 0)) + (
        pltpu.roll(values, 1, 1) + pltpu.roll(values, columns - 1, 1)
    )


def basis_kernel(
    depth,
    own_ref,
    own_far_ref,
    left_ref,
    left_far_ref,
    right_ref,
    right_far_ref,
    terms_ref,
    gram_ref,
    signs,
    half_diag,
    lower,
    upper,
    basis,
    forward,
    sides,
    backward,
    k_signs,
    k_basis,
    sums,
):
    levels = 2 * depth
    rows, columns = 3 * ROWS, 2 * LANES
    shape = (rows, columns)
    level = lax.axis_index("level")
    tile = lax.axis_index("tile")
    last_tile = lax.axis_size("tile") - 1
    per_tile = LANES // EDGE
    tiles = depth // per_tile
    lanes, ids = lane_ids(shape), row_ids(shape)
    near = jnp.where(level == 0, LANES, 2 * LANES - EDGE)
    inside = (lanes < LANES) | ((lanes >= near) & (lanes < near + EDGE))
    inside = inside & (ids >= jnp.where(tile > 0, 0, ROWS))
    inside = inside & (ids < jnp.where(tile < last_tile, 3 * ROWS, 2 * ROWS))
    mask = jnp.where(inside, 1.0, 0.0)
    zero = jnp.zeros(shape, jnp.float32)
    own = (slice(ROWS, 2 * ROWS), slice(0, LANES))
    own_zero = jnp.zeros((ROWS, LANES), jnp.float32)

    signs[0] = zero
    signs[levels + 1] = zero
    backward[levels] = zero
    upper[levels] = zero
    basis[levels] = zero
    for far, pieces in enumerate(
        ((left_ref, own_ref, right_ref), (left_far_ref, own_far_ref, right_far_ref))
    ):
        start = depth * (level if far == 0 else 1 - level)

        def unpack(z, unused, pieces=pieces, start=start):
            group = z // per_tile
            shift = lax.rem(2 * LANES - EDGE * lax.rem(z, per_tile) - EDGE * level, LANES)

            def gather(base):
                main = jnp.concatenate([piece[base + z] for piece in pieces], axis=0)
                edge = jnp.concatenate([piece[base + depth + group] for piece in pieces], axis=0)
                return jnp.concatenate([main, pltpu.roll(edge, shift, 1)], axis=1)

            signs[start + z + 1] = gather(0) * mask
            half_diag[start + z] = 0.5 * gather(depth + tiles) + (2.0 + VERTICAL)
            return unused

        lax.fori_loop(0, depth, unpack, 0, unroll=2)

    def start_down(k, carry):
        ratio, value = carry
        ratio = mask / (half_diag[k] - ratio)
        value = ratio * (signs[k + 1] + value)
        lower[k] = ratio
        forward[k] = value
        return ratio, value

    lax.fori_loop(0, levels, start_down, (zero, zero), unroll=GROUP)

    def start_up(step, carry):
        k = levels - 1 - step
        ratio, solved, value = carry
        ratio = mask / (half_diag[k] - ratio)
        solved = forward[k] + lower[k] * solved
        value = ratio * (solved + value)
        upper[k] = ratio
        backward[k] = value
        return ratio, solved, value

    lax.fori_loop(0, levels, start_up, (zero, zero, zero), unroll=GROUP)

    def k_of_signs(k, unused):
        value = signs[k + 1]
        image = half_diag[k] * value - (signs[k] + signs[k + 2]) - 0.5 * beside(value)
        k_signs[k] = image[own]
        return unused

    lax.fori_loop(0, levels, k_of_signs, 0, unroll=GROUP)

    place = 0
    for index in range(ITERS):
        final = index + 1 == ITERS

        def next_basis(k, previous, index=index):
            solved = backward[k] + upper[k] * previous
            if index == 0:
                value = solved
            elif SHIFTS[index - 1] == 0.0:
                value = -solved
            else:
                value = SHIFTS[index - 1] * basis[k] - solved
            return solved, value

        def down(group, carry, index=index, final=final, next_basis=next_basis):
            solved, above, here, value, *totals = carry
            products = []
            for step in range(GROUP):
                k = group * GROUP + step
                solved, below = next_basis(k + 1, solved)
                if not final:
                    basis[k + 1] = below
                side = beside(here)
                image = half_diag[k] * here - (above + below) - 0.5 * side
                if not final:
                    value = lower[k] * (beside(image * mask) + value)
                    forward[k] = value
                    sides[k] = side
                my_sign, my_basis, my_image = signs[k + 1][own], here[own], image[own]
                terms_ref[index, k] = my_basis * k_signs[k] + my_image * my_sign
                if not final:
                    k_basis[index, k] = my_image
                products.append(
                    [k_basis[other, k] * my_image for other in range(index)]
                    + [my_image * my_image, my_basis * my_sign]
                )
                above, here = here, below
            for slot in range(index + 2):
                added = (products[0][slot] + products[1][slot]) + (
                    products[2][slot] + products[3][slot]
                )
                totals[2 * slot], rest = two_sum(totals[2 * slot], added)
                totals[2 * slot + 1] = totals[2 * slot + 1] + rest
            return (solved, above, here, value, *totals)

        solved, here = next_basis(0, zero)
        if not final:
            basis[0] = here
        carry = lax.fori_loop(
            0,
            levels // GROUP,
            down,
            (solved, zero, here, zero) + (own_zero,) * (2 * (index + 2)),
        )
        totals = carry[4:]
        for slot in range(index + 1):
            sums[2 * (place + slot)] = totals[2 * slot]
            sums[2 * (place + slot) + 1] = totals[2 * slot + 1]
        place += index + 1
        sums[2 * (len(PAIRS) + index)] = totals[2 * index + 2]
        sums[2 * (len(PAIRS) + index) + 1] = totals[2 * index + 3]
        if final:
            break

        def up(step, carry):
            k = levels - 1 - step
            solved, value = carry
            solved = forward[k] + lower[k] * solved
            value = upper[k] * ((sides[k] + solved) + value)
            backward[k] = value
            return solved, value

        lax.fori_loop(0, levels, up, (zero, zero), unroll=GROUP)

    ids = row_ids((ROWS, LANES))
    for block in range(SLOTS // ROWS):
        high, low = own_zero, own_zero
        for slot in range(block * ROWS, min((block + 1) * ROWS, COUNT)):
            pair = (sums[2 * slot], sums[2 * slot + 1])
            for axis, shift in ((0, 4), (0, 2), (0, 1), (1, 64), (1, 32), (1, 16), (1, 8), (1, 4), (1, 2), (1, 1)):
                pair = pair_add(pair, tuple(pltpu.roll(part, shift, axis) for part in pair))
            here = ids == slot - block * ROWS
            high, low = jnp.where(here, pair[0], high), jnp.where(here, pair[1], low)
        gram_ref[block * ROWS : (block + 1) * ROWS] = high
        gram_ref[SLOTS + block * ROWS : SLOTS + (block + 1) * ROWS] = low


def solve_small(high, low):
    def entry(index):
        return tuple(jnp.broadcast_to(part[index : index + 1], (ROWS, LANES)) for part in (high, low))

    gram = {}
    for place, (i, j) in enumerate(PAIRS):
        gram[i, j] = gram[j, i] = entry(place)
    right = [entry(len(PAIRS) + j) for j in range(ITERS)]
    work = {key: pair[0] for key, pair in gram.items()}
    ratios, inverses = {}, []
    for i in range(ITERS):
        pivot = work[i, i]
        good = pivot > 1e-7 * gram[i, i][0]
        inverses.append(jnp.where(good, 1.0 / jnp.where(good, pivot, 1.0), 0.0))
        for r in range(i + 1, ITERS):
            ratios[r, i] = work[r, i] * inverses[i]
        for r in range(i + 1, ITERS):
            for c in range(i + 1, r + 1):
                work[r, c] = work[c, r] = work[r, c] - ratios[r, i] * work[c, i]

    def solve(values):
        values = list(values)
        for i in range(ITERS):
            for r in range(i + 1, ITERS):
                values[r] = values[r] - ratios[r, i] * values[i]
        values = [value * inverse for value, inverse in zip(values, inverses)]
        for i in reversed(range(ITERS)):
            for r in range(i):
                values[r] = values[r] - ratios[i, r] * values[i]
        return values

    found = solve([pair[0] for pair in right])
    for unused in range(2):
        rest = []
        for i in range(ITERS):
            total = right[i]
            for j in range(ITERS):
                product, error = two_product(gram[i, j][0], found[j])
                total = pair_add(total, (-product, -(error + gram[i, j][1] * found[j])))
            rest.append(total[0] + total[1])
        found = [a + b for a, b in zip(found, solve(rest))]
    return found


def combine_kernel(depth, terms_ref, *refs):
    gram_refs, (keep_ref, send_ref) = refs[:-2], refs[-2:]
    pairs = []
    for ref in gram_refs:
        for start in range(0, ref.shape[0], 2 * SLOTS):
            pairs.append((ref[start : start + SLOTS], ref[start + SLOTS : start + 2 * SLOTS]))
    while len(pairs) > 1:
        merged = [pair_add(pairs[i], pairs[i + 1]) for i in range(0, len(pairs) - 1, 2)]
        pairs = merged + pairs[2 * len(merged) :]
    found = solve_small(*pairs[0])
    core = lax.rem(lax.axis_index("probe"), 2)
    width = LANES // 2
    lower_lanes = lane_ids((ROWS, LANES)) < width
    pairs_deep = depth // 2

    def step(z, unused):
        for half in range(2):
            def total(k):
                value = found[0] * terms_ref[0, k]
                for j in range(1, ITERS):
                    value = value + found[j] * terms_ref[j, k]
                return value

            one = total(half * depth + z)
            two = total(half * depth + pairs_deep + z)
            low = jnp.where(lower_lanes, one, pltpu.roll(two, width, 1))
            high = jnp.where(lower_lanes, pltpu.roll(one, width, 1), two)
            keep_ref[half, z] = jnp.where(core == 0, low, high)
            send_ref[half, z] = jnp.where(core == 0, high, low)
        return unused

    lax.fori_loop(0, pairs_deep, step, 0, unroll=2)


def gradient_kernel(
    depth, probes, trace_a_ref, trace_b_ref, kappa_ref, observed_ref, left_ref, right_ref, far_ref, out_ref
):
    level = lax.axis_index("level")
    tile = lax.axis_index("tile")
    last_tile = lax.axis_size("tile") - 1
    probe = lax.axis_index("probe")
    in_low = probe < probes // 2
    even = lax.rem(probe, 2) == 0
    width = LANES // 2
    lanes = lane_ids((ROWS, 2 * LANES))
    ids = row_ids((ROWS, LANES))
    base = left_ref.shape[0] - depth // ROWS

    def half(value):
        return jnp.where(in_low, value[..., :LANES], value[..., LANES:])

    def take(value):
        return jnp.where(even, value, pltpu.roll(value, width, 1))[:, :width]

    far_edge = far_ref[far_ref.shape[0] - 1]
    for z in range(depth):
        value = observed_ref[z]
        mine = half(value)
        y_sides = jnp.where(lanes > 0, pltpu.roll(value, 1, 1), 0.0) + jnp.where(
            lanes < 2 * LANES - 1, pltpu.roll(value, 2 * LANES - 1, 1), 0.0
        )
        left = left_ref[base + z // ROWS, z % ROWS : z % ROWS + 1, :]
        right = right_ref[base + z // ROWS, z % ROWS : z % ROWS + 1, :]
        before = jnp.where(ids > 0, pltpu.roll(mine, 1, 0), jnp.where(tile > 0, left, 0.0))
        after = jnp.where(
            ids < ROWS - 1, pltpu.roll(mine, ROWS - 1, 0), jnp.where(tile < last_tile, right, 0.0)
        )
        above = half(observed_ref[z - 1]) if z > 0 else jnp.where(level > 0, far_edge, 0.0)
        below = half(observed_ref[z + 1]) if z < depth - 1 else jnp.where(level == 0, far_edge, 0.0)
        kappa = half(kappa_ref[z])
        k_observed = (
            (kappa + (4.0 + 2.0 * VERTICAL)) * mine
            - (before + after)
            - half(y_sides)
            - VERTICAL * (above + below)
        )
        data_part = take(2.0 * mine * k_observed)
        trace = trace_a_ref[z % (depth // 2)] + trace_b_ref[z % (depth // 2)]
        trace = trace[:, :width] if z < depth // 2 else pltpu.roll(trace, width, 1)[:, :width]
        out_ref[z] = take(kappa) * (trace * (0.5 / probes) - data_part)


def whole(count):
    return [pl.BlockSpec(memory_space=pltpu.VMEM)] * count


def body(probe_bits, kappa_sq, observed):
    probes, tile_count = lax.axis_size("probe"), lax.axis_size("tile")
    unused, depth, rows, columns = probe_bits.shape
    assert probe_bits.shape[0] == 1 and lax.axis_size("level") == 2 and probes == 4
    assert rows == ROWS and columns == 2 * LANES and depth % (LANES // EDGE) == 0
    params = pltpu.CompilerParams(vmem_limit_bytes=48 * 1024 * 1024)
    f32 = jnp.float32
    tiles = depth * EDGE // LANES
    field = 2 * (depth + tiles)
    near_shape = jax.ShapeDtypeStruct((field + depth // ROWS, ROWS, LANES), f32)
    far_shape = jax.ShapeDtypeStruct((field + 1, ROWS, LANES), f32)

    up_block, down_block, cross_block = pl.pallas_call(
        functools.partial(pack_kernel, depth),
        out_shape=(near_shape, near_shape, far_shape),
        in_specs=whole(3),
        out_specs=tuple(whole(3)),
        compiler_params=params,
        name="pack",
    )(probe_bits[0], kappa_sq, observed)

    up_pairs = [(i, i + 1) for i in range(tile_count - 1)]
    down_pairs = [(i + 1, i) for i in range(tile_count - 1)]
    own_far = lax.ppermute(cross_block, "level", [(0, 1), (1, 0)])
    left = lax.ppermute(up_block, "tile", up_pairs)
    right = lax.ppermute(down_block, "tile", down_pairs)
    left_far = lax.ppermute(own_far, "tile", up_pairs)
    right_far = lax.ppermute(
        cross_block,
        ("tile", "level"),
        [(2 * a + level, 2 * b + 1 - level) for a, b in down_pairs for level in range(2)],
    )

    levels = 2 * depth
    padded = pltpu.VMEM((levels + 1, 3 * ROWS, 2 * LANES), f32)
    plain = pltpu.VMEM((levels, 3 * ROWS, 2 * LANES), f32)
    terms, gram = pl.pallas_call(
        functools.partial(basis_kernel, depth),
        out_shape=(
            jax.ShapeDtypeStruct((ITERS, levels, ROWS, LANES), f32),
            jax.ShapeDtypeStruct((2 * SLOTS, LANES), f32),
        ),
        in_specs=whole(6),
        out_specs=tuple(whole(2)),
        scratch_shapes=[
            pltpu.VMEM((levels + 2, 3 * ROWS, 2 * LANES), f32),
            plain,
            plain,
            padded,
            padded,
            plain,
            plain,
            padded,
            pltpu.VMEM((levels, ROWS, LANES), f32),
            pltpu.VMEM((ITERS - 1, levels, ROWS, LANES), f32),
            pltpu.VMEM((2 * SLOTS, ROWS, LANES), f32),
        ],
        compiler_params=params,
        name="basis",
    )(up_block, own_far, left, left_far, right, right_far)

    both = jnp.concatenate([gram, lax.ppermute(gram, "level", [(0, 1), (1, 0)])], axis=0)
    if tile_count <= 4:
        partials = [both] + [
            lax.ppermute(both, "tile", [(i, (i + k) % tile_count) for i in range(tile_count)])
            for k in range(1, tile_count)
        ]
    else:
        partials = [lax.all_gather(both, "tile", axis=0, tiled=True)]
    piece = jax.ShapeDtypeStruct((2, depth // 2, ROWS, LANES), f32)
    keep, send = pl.pallas_call(
        functools.partial(combine_kernel, depth),
        out_shape=(piece, piece),
        in_specs=whole(1 + len(partials)),
        out_specs=tuple(whole(2)),
        compiler_params=params,
        name="combine",
    )(terms, *partials)

    summed = keep + lax.ppermute(send, "probe", [(0, 1), (1, 0), (2, 3), (3, 2)])
    half = lax.axis_index("probe") // 2
    straight = lax.dynamic_index_in_dim(summed, half, 0, keepdims=False)
    turned = lax.dynamic_index_in_dim(summed, 1 - half, 0, keepdims=False)

    def routes(flip):
        pairs = []
        for x in range(2):
            for core in range(2):
                for level in range(2):
                    target = x if not flip else 1 - x
                    pairs.append(((2 * x + core) * 2 + level, (2 * level + core) * 2 + target))
        return pairs

    trace_a = lax.ppermute(straight, ("probe", "level"), routes(False))
    trace_b = lax.ppermute(turned, ("probe", "level"), routes(True))
    return pl.pallas_call(
        functools.partial(gradient_kernel, depth, probes),
        out_shape=jax.ShapeDtypeStruct((depth, ROWS, columns // probes), f32),
        in_specs=whole(7),
        out_specs=pl.BlockSpec(memory_space=pltpu.VMEM),
        compiler_params=params,
        name="gradient",
    )(trace_a, trace_b, kappa_sq, observed, left, right, own_far)


def solution(mesh):
    in_specs = (
        P("probe", "level", "tile", None),
        P("level", "tile", None),
        P("level", "tile", None),
    )
    out_specs = P("level", "tile", "probe")
    return jax.shard_map(body, mesh=mesh, in_specs=in_specs, out_specs=out_specs, check_vma=False)
```

time: 433 us -> 70.1 us (0.16)
  blocking collectives: 144 us -> 0 us
  starting transfers between devices: 104 us -> 25.9 us
  waiting for transfers between devices: 68.5 us -> 17.5 us
  local copies, waits for them, and re-layouts: 49.2 us -> 2.88 us
  other arithmetic: 37.5 us -> 0.02 us
  between operations: 28 us -> 0.12 us
  Pallas kernels: 0 us -> 23.4 us
    psum x4 -> x0, blocking collectives: 85.4 us -> none  [paired_totals(): lax.psum((local_dots(residual, precond), local_dots(image_field, precond)...]
    ppermute x40 -> x12, starting transfers between devices: 95.8 us -> 25.9 us  [the longest x3 5.5 us: body(): lax.ppermute(both, 'tile', [(i, (i + k) % tile_count) for i in range(tile...]
    all_to_all x7 -> x0, blocking collectives: 58.8 us -> none  [the longest x4 30.7 us: solve_columns(): lax.all_to_all(solved, 'level', split_axis=1, concat_axis=3, tiled=True)]
    unnamed x48 -> x11, local copies, waits for them, and re-layouts: 30.2 us -> 2.86 us
    ppermute x40 -> x12, waiting for transfers between devices: 42.9 us -> 17.5 us  [the longest x1 8.27 us: body(): lax.ppermute(cross_block, ('tile', 'level'), [(2 * a + level, 2 * b + 1 -...]
    pallas_call x0 -> x4, Pallas kernels: none -> 23.4 us  [the longest x1 19.4 us: body(): pl.pallas_call(functools.partial(basis_kernel, depth), out_shape=(jax.Sha...]
    unnamed x2 -> x0, waiting for transfers between devices: 19.2 us -> none
    all_to_all x5 -> x0, other arithmetic: 12.1 us -> none  [the longest x4 10.6 us: apply_m(): lax.all_to_all(values, 'level', split_axis=3, concat_axis=1, tiled=True)]
  transfers between devices with their start and end apart: 43 -> 12, of which waited for: 25 -> 8; matrix products, arithmetic and copies ran while one was open for 2% -> 0% of each run, Pallas kernels for 0% -> 0%
where the time goes in v1:
time: 70.1 us; the launch traced here: 69.8 us
  starting transfers between devices  25.9 us (37%)
  Pallas kernels  23.4 us (33%)
  waiting for transfers between devices  17.5 us (25%)
  local copies, waits for them, and re-layouts  2.88 us (4%)
    pallas_call x1, Pallas kernels, body(): pl.pallas_call(functools.partial(basis_kernel, depth), out_shape=(jax.Sha...  19.4 us
    ppermute x1, waiting for transfers between devices, body(): lax.ppermute(cross_block, ('tile', 'level'), [(2 * a + level, 2 * b + 1 -...  8.27 us
    ppermute x3, starting transfers between devices, body(): lax.ppermute(both, 'tile', [(i, (i + k) % tile_count) for i in range(tile...  5.5 us
    ppermute x1, starting transfers between devices, body(): left_far = lax.ppermute(own_far, 'tile', up_pairs)  4.55 us
    ppermute x1, starting transfers between devices, body(): trace_b = lax.ppermute(turned, ('probe', 'level'), routes(True))  4.25 us
    ppermute x1, starting transfers between devices, body(): left = lax.ppermute(up_block, 'tile', up_pairs)  3.49 us
    ppermute x1, waiting for transfers between devices, body(): trace_b = lax.ppermute(turned, ('probe', 'level'), routes(True))  3.48 us
    ppermute x1, starting transfers between devices, body(): own_far = lax.ppermute(cross_block, 'level', [(0, 1), (1, 0)])  3.03 us
  transfers between devices with their start and end apart: 12, of which 8 were waited for; matrix products, arithmetic and copies ran while one was open for 0% of the time, Pallas kernels for 0%

profile of v1, /device:TPU:0, one launch (start us, length us, event | category | flops | bytes accessed | tf_op | source)
XLA Modules:
  0.0 69.8 jit_solution(13718945311505385230)
XLA Ops:
  0.0 0.0 copy-start
  0.0 0.9 %copy-done = f32[32,8,256]{2,1,0:T(8,128)S(1)} copy-done((f32[32,8,256]{2,1,0:T(8,128)S(1)}, f32[32,8,256]{2,1,0:T(8,128)}, u32[]{:S(2)}) %copy-start) | copy-done | bytes 262168
  1.0 0.0 copy-start.2
  1.0 0.9 %copy-done.2 = f32[32,8,256]{2,1,0:T(8,128)S(1)} copy-done((f32[32,8,256]{2,1,0:T(8,128)S(1)}, f32[32,8,256]{2,1,0:T(8,128)}, u32[]{:S(2)}) %copy-start.2) | copy-done | bytes 262168
  1.9 0.0 copy-start.4
  1.9 0.9 %copy-done.4 = s32[1,32,8,256]{3,2,1,0:T(8,128)S(1)} copy-done((s32[1,32,8,256]{3,2,1,0:T(8,128)S(1)}, s32[1,32,8,256]{3,2,1,0:T(8,128)}, u32[]{:S(2)}) %copy-start.4) | copy-done | bytes 262168
  2.9 1.4 %pack.1 = (f32[72,8,128]{2,1,0:T(8,128)S(1)}, f32[72,8,128]{2,1,0:T(8,128)S(1)}, f32[69,8,128]{2,1,0:T(8,128)S(1)}) custom-call(s32[32,8,256]{2,1,0:T(8,128)S(1)} %bitcast.5, f32[32,8,256]{2,1,0:T(8,128)S(1)} %copy-done, f32[32,8,256]{2,1,0:T(8,128)S(1)} %copy-done.2), custom_call_target="tpu_custom_call" | custom-call | tf_op jit(solution)/shard_map/pack/pallas_call | solution.py:440
  4.2 3.0 %collective-permute-start = (f32[69,8,128]{2,1,0:T(8,128)S(1)}, f32[69,8,128]{2,1,0:T(8,128)S(1)}, u32[]{:S(2)}, u32[]{:S(2)}) collective-permute-start(f32[69,8,128]{2,1,0:T(8,128)S(1)} %get-tuple-element.13), channel_id=1, source_target_pairs={{0,1},{1,0},{2,3},{3,2},{4,5},{5,4},{6,7},{7,6},{8,9},{9,8},{10,11... | collective-permute-start | bytes 847880 | tf_op jit(solution)/shard_map/ppermute | solution.py:451
  7.3 3.5 %collective-permute-start.1 = (f32[72,8,128]{2,1,0:T(8,128)S(1)}, f32[72,8,128]{2,1,0:T(8,128)S(1)}, u32[]{:S(2)}, u32[]{:S(2)}) collective-permute-start(f32[72,8,128]{2,1,0:T(8,128)S(1)} %get-tuple-element.12.own_ref), channel_id=1, source_target_pairs={{0,2},{2,4},{4,6},{1,3},{3,5},{5,7},{8,10},{10,12},{12,14},{9,11},... | collective-permute-start | bytes 884744 | tf_op jit(solution)/shard_map/ppermute | solution.py:452
  10.8 1.3 %collective-permute-start.3 = (f32[72,8,128]{2,1,0:T(8,128)S(1)}, f32[72,8,128]{2,1,0:T(8,128)S(1)}, u32[]{:S(2)}, u32[]{:S(2)}) collective-permute-start(f32[72,8,128]{2,1,0:T(8,128)S(1)} %get-tuple-element.14), channel_id=1, source_target_pairs={{2,0},{4,2},{6,4},{3,1},{5,3},{7,5},{10,8},{12,10},{14,12},{11,9},... | collective-permute-start | bytes 884744 | tf_op jit(solution)/shard_map/ppermute | solution.py:453
  12.1 1.3 %collective-permute-start.4 = (f32[69,8,128]{2,1,0:T(8,128)S(1)}, f32[69,8,128]{2,1,0:T(8,128)S(1)}, u32[]{:S(2)}, u32[]{:S(2)}) collective-permute-start(f32[69,8,128]{2,1,0:T(8,128)S(1)} %get-tuple-element.13), channel_id=1, source_target_pairs={{2,1},{3,0},{4,3},{5,2},{6,5},{7,4},{10,9},{11,8},{12,11},{13,10},... | collective-permute-start | bytes 847880 | tf_op jit(solution)/shard_map/ppermute | solution.py:455
  13.4 0.7 collective-permute-done.own_far_ref.far_ref
  14.0 4.6 %collective-permute-start.2 = (f32[69,8,128]{2,1,0:T(8,128)S(1)}, f32[69,8,128]{2,1,0:T(8,128)S(1)}, u32[]{:S(2)}, u32[]{:S(2)}) collective-permute-start(f32[69,8,128]{2,1,0:T(8,128)S(1)} %collective-permute-done.own_far_ref.far_ref), channel_id=1, source_target_pairs={{0,2},{2,4},{4,6},{1,3},{3,5},{5,7},{8,10},{10,12},{12,14},{9,11},... | collective-permute-start | bytes 847880 | tf_op jit(solution)/shard_map/ppermute | solution.py:454
  18.6 8.3 %collective-permute-done.4.right_far_ref = f32[69,8,128]{2,1,0:T(8,128)S(1)} collective-permute-done((f32[69,8,128]{2,1,0:T(8,128)S(1)}, f32[69,8,128]{2,1,0:T(8,128)S(1)}, u32[]{:S(2)}, u32[]{:S(2)}) %collective-permute-start.4) | collective-permute-done | bytes 282656 | tf_op jit(solution)/shard_map/ppermute | solution.py:455
  26.9 0.0 collective-permute-done.1.left_ref
  26.9 0.0 collective-permute-done.3.right_ref
  26.9 0.0 collective-permute-done.2.left_far_ref
  26.9 19.4 %basis.1 = (f32[4,64,8,128]{3,2,1,0:T(8,128)S(1)}, f32[32,128]{1,0:T(8,128)S(1)}) custom-call(f32[72,8,128]{2,1,0:T(8,128)S(1)} %get-tuple-element.12.own_ref, f32[69,8,128]{2,1,0:T(8,128)S(1)} %collective-permute-done.own_far_ref.far_ref, f32[72,8,128]{2,1,0:T(8,128)S(1)} %collective-permute-done.1.left_ref, ...), custom_call_target="tpu_custom_call" | custom-call | tf_op jit(solution)/shard_map/basis/pallas_call | solution.py:464
  46.3 1.6 %collective-permute-start.5 = (f32[32,128]{1,0:T(8,128)S(1)}, f32[32,128]{1,0:T(8,128)S(1)}, u32[]{:S(2)}, u32[]{:S(2)}) collective-permute-start(f32[32,128]{1,0:T(8,128)S(1)} %get-tuple-element.16), channel_id=1, source_target_pairs={{0,1},{1,0},{2,3},{3,2},{4,5},{5,4},{6,7},{7,6},{8,9},{9,8},{10,11... | collective-permute-start | bytes 49160 | tf_op jit(solution)/shard_map/ppermute | solution.py:489
  47.9 2.2 %collective-permute-done.5 = f32[32,128]{1,0:T(8,128)S(1)} collective-permute-done((f32[32,128]{1,0:T(8,128)S(1)}, f32[32,128]{1,0:T(8,128)S(1)}, u32[]{:S(2)}, u32[]{:S(2)}) %collective-permute-start.5) | collective-permute-done | bytes 16416 | tf_op jit(solution)/shard_map/ppermute | solution.py:489
  50.1 1.6 %collective-permute-start.6 = (f32[64,128]{1,0:T(8,128)S(1)}, f32[64,128]{1,0:T(8,128)S(1)}, u32[]{:S(2)}, u32[]{:S(2)}) collective-permute-start(f32[64,128]{1,0:T(8,128)S(1)} %constant_dynamic-update-slice_fusion.refs_0_), channel_id=1, source_target_pairs={{0,2},{2,4},{4,6},{6,0},{1,3},{3,5},{5,7},{7,1},{8,10},{10,12},{12... | collective-permute-start | bytes 98312 | tf_op jit(solution)/shard_map/ppermute | solution.py:492
  51.6 1.0 %collective-permute-start.7 = (f32[64,128]{1,0:T(8,128)S(1)}, f32[64,128]{1,0:T(8,128)S(1)}, u32[]{:S(2)}, u32[]{:S(2)}) collective-permute-start(f32[64,128]{1,0:T(8,128)S(1)} %constant_dynamic-update-slice_fusion.refs_0_), channel_id=1, source_target_pairs={{0,4},{2,6},{4,0},{6,2},{1,5},{3,7},{5,1},{7,3},{8,12},{10,14},{12... | collective-permute-start | bytes 98312 | tf_op jit(solution)/shard_map/ppermute | solution.py:492
  52.7 2.9 %collective-permute-start.8 = (f32[64,128]{1,0:T(8,128)S(1)}, f32[64,128]{1,0:T(8,128)S(1)}, u32[]{:S(2)}, u32[]{:S(2)}) collective-permute-start(f32[64,128]{1,0:T(8,128)S(1)} %constant_dynamic-update-slice_fusion.refs_0_), channel_id=1, source_target_pairs={{0,6},{2,0},{4,2},{6,4},{1,7},{3,1},{5,3},{7,5},{8,14},{10,8},{12,... | collective-permute-start | bytes 98312 | tf_op jit(solution)/shard_map/ppermute | solution.py:492
  55.6 0.2 collective-permute-done.6.refs_1_
  55.8 0.7 collective-permute-done.7.refs_2_
  56.5 0.7 %collective-permute-done.8.refs_3_ = f32[64,128]{1,0:T(8,128)S(1)} collective-permute-done((f32[64,128]{1,0:T(8,128)S(1)}, f32[64,128]{1,0:T(8,128)S(1)}, u32[]{:S(2)}, u32[]{:S(2)}) %collective-permute-start.8) | collective-permute-done | bytes 32800 | tf_op jit(solution)/shard_map/ppermute | solution.py:492
  57.2 0.9 %combine.1 = (f32[2,16,8,128]{3,2,1,0:T(8,128)S(1)}, f32[2,16,8,128]{3,2,1,0:T(8,128)S(1)}) custom-call(f32[4,64,8,128]{3,2,1,0:T(8,128)S(1)} %get-tuple-element.15.terms_ref, f32[64,128]{1,0:T(8,128)S(1)} %constant_dynamic-update-slice_fusion.refs_0_, f32[64,128]{1,0:T(8,128)S(1)} %collective-permute-done.6.refs_1_, ...), custom_call_target="tpu_custom_call" | custom-call | tf_op jit(solution)/shard_map/combine/pallas_call | solution.py:498
  58.1 0.1 collective-permute-start.9
  58.2 1.3 %collective-permute-done.9 = f32[2,16,8,128]{3,2,1,0:T(8,128)S(1)} collective-permute-done((f32[2,16,8,128]{3,2,1,0:T(8,128)S(1)}, f32[2,16,8,128]{3,2,1,0:T(8,128)S(1)}, u32[]{:S(2)}, u32[]{:S(2)}) %collective-permute-start.9) | collective-permute-done | bytes 131104 | tf_op jit(solution)/shard_map/ppermute | solution.py:507
  59.5 0.0 copy-start.1
  59.5 0.0 copy-start.3
  59.5 0.8 %collective-permute-start.10 = (f32[16,8,128]{2,1,0:T(8,128)S(1)}, f32[16,8,128]{2,1,0:T(8,128)S(1)}, u32[]{:S(2)}, u32[]{:S(2)}) collective-permute-start(f32[16,8,128]{2,1,0:T(8,128)S(1)} %get-tuple-element.20), channel_id=1, source_target_pairs={{0,0},{1,16},{8,8},{9,24},{16,1},{17,17},{24,9},{25,25},{2,2},{3,1... | collective-permute-start | bytes 196616 | tf_op jit(solution)/shard_map/ppermute | solution.py:521
  60.4 4.2 %collective-permute-start.11 = (f32[16,8,128]{2,1,0:T(8,128)S(1)}, f32[16,8,128]{2,1,0:T(8,128)S(1)}, u32[]{:S(2)}, u32[]{:S(2)}) collective-permute-start(f32[16,8,128]{2,1,0:T(8,128)S(1)} %get-tuple-element.19), channel_id=1, source_target_pairs={{0,1},{1,17},{8,9},{9,25},{16,0},{17,16},{24,8},{25,24},{2,3},{3,1... | collective-permute-start | bytes 196616 | tf_op jit(solution)/shard_map/ppermute | solution.py:522
  64.6 0.0 collective-permute-done.10.trace_a_ref
  64.6 3.5 %collective-permute-done.11.trace_b_ref = f32[16,8,128]{2,1,0:T(8,128)S(1)} collective-permute-done((f32[16,8,128]{2,1,0:T(8,128)S(1)}, f32[16,8,128]{2,1,0:T(8,128)S(1)}, u32[]{:S(2)}, u32[]{:S(2)}) %collective-permute-start.11) | collective-permute-done | bytes 65568 | tf_op jit(solution)/shard_map/ppermute | solution.py:522
  68.1 0.0 copy-done.1
  68.1 0.0 copy-done.3
  68.1 1.7 %gradient.1 = f32[32,8,64]{2,1,0:T(8,128)} custom-call(f32[16,8,128]{2,1,0:T(8,128)S(1)} %collective-permute-done.10.trace_a_ref, f32[16,8,128]{2,1,0:T(8,128)S(1)} %collective-permute-done.11.trace_b_ref, f32[32,8,256]{2,1,0:T(8,128)S(1)} %copy-done.1, f32[32,8,256]{2,1,0:T(8,128)S(1)} %copy-done.3, f32[72,8,128]{2,1,0:T(8,128)S(1)} %collective-permute-done.1.left_ref, ...), custom_call_target="tpu_custom_call" | custom-call | tf_op jit(solution)/shard_map/gradient/pallas_call | solution.py:523
  (4 shorter events, 0.0 us)
Async XLA Ops:
  0.0 0.9 %copy-start = (f32[32,8,256]{2,1,0:T(8,128)S(1)}, f32[32,8,256]{2,1,0:T(8,128)}, u32[]{:S(2)}) copy-start(f32[32,8,256]{2,1,0:T(8,128)} %kappa_ref.3) | copy-start | bytes 786436
  1.0 0.9 %copy-start.2 = (f32[32,8,256]{2,1,0:T(8,128)S(1)}, f32[32,8,256]{2,1,0:T(8,128)}, u32[]{:S(2)}) copy-start(f32[32,8,256]{2,1,0:T(8,128)} %observed_ref.3) | copy-start | bytes 786436
  1.9 0.9 %copy-start.4 = (s32[1,32,8,256]{3,2,1,0:T(8,128)S(1)}, s32[1,32,8,256]{3,2,1,0:T(8,128)}, u32[]{:S(2)}) copy-start(s32[1,32,8,256]{3,2,1,0:T(8,128)} %param.3) | copy-start | bytes 786436
  4.2 9.8 %collective-permute-start = (f32[69,8,128]{2,1,0:T(8,128)S(1)}, f32[69,8,128]{2,1,0:T(8,128)S(1)}, u32[]{:S(2)}, u32[]{:S(2)}) collective-permute-start(f32[69,8,128]{2,1,0:T(8,128)S(1)} %get-tuple-element.13), channel_id=1, source_target_pairs={{0,1},{1,0},{2,3},{3,2},{4,5},{5,4},{6,7},{7,6},{8,9},{9,8},{10,11... | collective-permute-start | bytes 847880 | tf_op jit(solution)/shard_map/ppermute | solution.py:451
  7.3 19.6 %collective-permute-start.1 = (f32[72,8,128]{2,1,0:T(8,128)S(1)}, f32[72,8,128]{2,1,0:T(8,128)S(1)}, u32[]{:S(2)}, u32[]{:S(2)}) collective-permute-start(f32[72,8,128]{2,1,0:T(8,128)S(1)} %get-tuple-element.12.own_ref), channel_id=1, source_target_pairs={{0,2},{2,4},{4,6},{1,3},{3,5},{5,7},{8,10},{10,12},{12,14},{9,11},... | collective-permute-start | bytes 884744 | tf_op jit(solution)/shard_map/ppermute | solution.py:452
  10.8 16.1 %collective-permute-start.3 = (f32[72,8,128]{2,1,0:T(8,128)S(1)}, f32[72,8,128]{2,1,0:T(8,128)S(1)}, u32[]{:S(2)}, u32[]{:S(2)}) collective-permute-start(f32[72,8,128]{2,1,0:T(8,128)S(1)} %get-tuple-element.14), channel_id=1, source_target_pairs={{2,0},{4,2},{6,4},{3,1},{5,3},{7,5},{10,8},{12,10},{14,12},{11,9},... | collective-permute-start | bytes 884744 | tf_op jit(solution)/shard_map/ppermute | solution.py:453
  12.1 14.8 %collective-permute-start.4 = (f32[69,8,128]{2,1,0:T(8,128)S(1)}, f32[69,8,128]{2,1,0:T(8,128)S(1)}, u32[]{:S(2)}, u32[]{:S(2)}) collective-permute-start(f32[69,8,128]{2,1,0:T(8,128)S(1)} %get-tuple-element.13), channel_id=1, source_target_pairs={{2,1},{3,0},{4,3},{5,2},{6,5},{7,4},{10,9},{11,8},{12,11},{13,10},... | collective-permute-start | bytes 847880 | tf_op jit(solution)/shard_map/ppermute | solution.py:455
  14.0 12.8 %collective-permute-start.2 = (f32[69,8,128]{2,1,0:T(8,128)S(1)}, f32[69,8,128]{2,1,0:T(8,128)S(1)}, u32[]{:S(2)}, u32[]{:S(2)}) collective-permute-start(f32[69,8,128]{2,1,0:T(8,128)S(1)} %collective-permute-done.own_far_ref.far_ref), channel_id=1, source_target_pairs={{0,2},{2,4},{4,6},{1,3},{3,5},{5,7},{8,10},{10,12},{12,14},{9,11},... | collective-permute-start | bytes 847880 | tf_op jit(solution)/shard_map/ppermute | solution.py:454
  46.3 3.8 %collective-permute-start.5 = (f32[32,128]{1,0:T(8,128)S(1)}, f32[32,128]{1,0:T(8,128)S(1)}, u32[]{:S(2)}, u32[]{:S(2)}) collective-permute-start(f32[32,128]{1,0:T(8,128)S(1)} %get-tuple-element.16), channel_id=1, source_target_pairs={{0,1},{1,0},{2,3},{3,2},{4,5},{5,4},{6,7},{7,6},{8,9},{9,8},{10,11... | collective-permute-start | bytes 49160 | tf_op jit(solution)/shard_map/ppermute | solution.py:489
  50.1 5.7 %collective-permute-start.6 = (f32[64,128]{1,0:T(8,128)S(1)}, f32[64,128]{1,0:T(8,128)S(1)}, u32[]{:S(2)}, u32[]{:S(2)}) collective-permute-start(f32[64,128]{1,0:T(8,128)S(1)} %constant_dynamic-update-slice_fusion.refs_0_), channel_id=1, source_target_pairs={{0,2},{2,4},{4,6},{6,0},{1,3},{3,5},{5,7},{7,1},{8,10},{10,12},{12... | collective-permute-start | bytes 98312 | tf_op jit(solution)/shard_map/ppermute | solution.py:492
  51.6 4.8 %collective-permute-start.7 = (f32[64,128]{1,0:T(8,128)S(1)}, f32[64,128]{1,0:T(8,128)S(1)}, u32[]{:S(2)}, u32[]{:S(2)}) collective-permute-start(f32[64,128]{1,0:T(8,128)S(1)} %constant_dynamic-update-slice_fusion.refs_0_), channel_id=1, source_target_pairs={{0,4},{2,6},{4,0},{6,2},{1,5},{3,7},{5,1},{7,3},{8,12},{10,14},{12... | collective-permute-start | bytes 98312 | tf_op jit(solution)/shard_map/ppermute | solution.py:492
  52.7 4.5 %collective-permute-start.8 = (f32[64,128]{1,0:T(8,128)S(1)}, f32[64,128]{1,0:T(8,128)S(1)}, u32[]{:S(2)}, u32[]{:S(2)}) collective-permute-start(f32[64,128]{1,0:T(8,128)S(1)} %constant_dynamic-update-slice_fusion.refs_0_), channel_id=1, source_target_pairs={{0,6},{2,0},{4,2},{6,4},{1,7},{3,1},{5,3},{7,5},{8,14},{10,8},{12,... | collective-permute-start | bytes 98312 | tf_op jit(solution)/shard_map/ppermute | solution.py:492
  58.1 1.4 %collective-permute-start.9 = (f32[2,16,8,128]{3,2,1,0:T(8,128)S(1)}, f32[2,16,8,128]{3,2,1,0:T(8,128)S(1)}, u32[]{:S(2)}, u32[]{:S(2)}) collective-permute-start(f32[2,16,8,128]{3,2,1,0:T(8,128)S(1)} %get-tuple-element.18), channel_id=1, source_target_pairs={{0,8},{8,0},{16,24},{24,16},{1,9},{9,1},{17,25},{25,17},{2,10},{10... | collective-permute-start | bytes 393224 | tf_op jit(solution)/shard_map/ppermute | solution.py:507
  59.5 8.6 %copy-start.1 = (f32[32,8,256]{2,1,0:T(8,128)S(1)}, f32[32,8,256]{2,1,0:T(8,128)}, u32[]{:S(2)}) copy-start(f32[32,8,256]{2,1,0:T(8,128)} %kappa_ref.3) | copy-start | bytes 786436
  59.5 8.6 %copy-start.3 = (f32[32,8,256]{2,1,0:T(8,128)S(1)}, f32[32,8,256]{2,1,0:T(8,128)}, u32[]{:S(2)}) copy-start(f32[32,8,256]{2,1,0:T(8,128)} %observed_ref.3) | copy-start | bytes 786436
  59.5 5.1 %collective-permute-start.10 = (f32[16,8,128]{2,1,0:T(8,128)S(1)}, f32[16,8,128]{2,1,0:T(8,128)S(1)}, u32[]{:S(2)}, u32[]{:S(2)}) collective-permute-start(f32[16,8,128]{2,1,0:T(8,128)S(1)} %get-tuple-element.20), channel_id=1, source_target_pairs={{0,0},{1,16},{8,8},{9,24},{16,1},{17,17},{24,9},{25,25},{2,2},{3,1... | collective-permute-start | bytes 196616 | tf_op jit(solution)/shard_map/ppermute | solution.py:521
  60.4 7.7 %collective-permute-start.11 = (f32[16,8,128]{2,1,0:T(8,128)S(1)}, f32[16,8,128]{2,1,0:T(8,128)S(1)}, u32[]{:S(2)}, u32[]{:S(2)}) collective-permute-start(f32[16,8,128]{2,1,0:T(8,128)S(1)} %get-tuple-element.19), channel_id=1, source_target_pairs={{0,1},{1,17},{8,9},{9,25},{16,0},{17,16},{24,8},{25,24},{2,3},{3,1... | collective-permute-start | bytes 196616 | tf_op jit(solution)/shard_map/ppermute | solution.py:522

commit v2 on v1

--- a/solution.py
+++ b/solution.py
@@ -52,46 +52,81 @@
     return lax.broadcasted_iota(jnp.int32, shape, len(shape) - 2)
 
 
-def pack_kernel(depth, bits_ref, kappa_ref, observed_ref, up_ref, down_ref, cross_ref):
+def split_three(values):
+    high = values.astype(jnp.bfloat16)
+    rest = values - high.astype(jnp.float32)
+    middle = rest.astype(jnp.bfloat16)
+    low = (rest - middle.astype(jnp.float32)).astype(jnp.bfloat16)
+    return high, middle, low
+
+
+def pick(values, chosen):
+    high, middle, low = (
+        jnp.dot(part, chosen, preferred_element_type=jnp.float32) for part in split_three(values)
+    )
+    return high + (middle + low)
+
+
+def columns_of(half):
+    shape = (2 * LANES, 2 * LANES)
+    ids, lane = row_ids(shape), lane_ids(shape)
+    odd = (lane // (LANES // 2)) % 2
+    main = LANES * half + 2 * (lane % (LANES // 2)) + odd
+    edge = LANES - EDGE * half + 2 * (lane % (EDGE // 2)) + odd
+    wanted = jnp.where(lane < LANES, main, edge)
+    return jnp.where(ids == wanted, 1.0, 0.0).astype(jnp.bfloat16)
+
+
+def pack_kernel(
+    depth,
+    bits_hbm,
+    kappa_hbm,
+    observed_hbm,
+    up_ref,
+    down_ref,
+    cross_ref,
+    bits_ref,
+    kappa_ref,
+    observed_ref,
+    arrived,
+):
+    copies = [
+        pltpu.make_async_copy(source, target, arrived.at[place])
+        for place, (source, target) in enumerate(
+            ((bits_hbm, bits_ref), (kappa_hbm, kappa_ref), (observed_hbm, observed_ref))
+        )
+    ]
+    for copy in copies:
+        copy.start()
     level = lax.axis_index("level")
     first = level == 0
     per_tile = LANES // EDGE
     tiles = depth // per_tile
-    lanes = lane_ids((ROWS, LANES))
-
-    def write(refs, offset, tile):
-        for ref in refs:
-            ref[offset] = tile
-
-    for which, source in enumerate((bits_ref, kappa_ref)):
+    slot_ids = (lane_ids((ROWS, LANES)) % (LANES // 2)) // (EDGE // 2)
+    same_columns, cross_columns = columns_of(level), columns_of(1 - level)
+    for which in range(2):
         base = which * (depth + tiles)
-
-        def tile_loop(tile, unused, source=source, base=base, which=which):
-            def step(slot, packed):
-                z = tile * per_tile + slot
-                value = source[z]
-                if which == 0:
-                    value = (2 * value - 1).astype(jnp.float32)
-                low, high = value[:, :LANES], value[:, LANES:]
-                same = jnp.where(first, low, high)
-                cross = jnp.where(first, high, low)
-                write((up_ref, down_ref), base + z, same)
-                cross_ref[base + z] = cross
-                here = lanes // EDGE == slot
-                shift = lax.rem(EDGE * slot + EDGE * level, LANES)
-                cross_shift = lax.rem(EDGE * slot + EDGE * (1 - level), LANES)
-                return (
-                    jnp.where(here, pltpu.roll(cross, shift, 1), packed[0]),
-                    jnp.where(here, pltpu.roll(same, cross_shift, 1), packed[1]),
+        copies[which].wait()
+        for refs, chosen in (((up_ref, down_ref), same_columns), ((cross_ref,), cross_columns)):
+            if which == 0:
+                values = (2 * bits_ref[...] - 1).astype(jnp.float32).reshape(depth * ROWS, 2 * LANES)
+                picked = jnp.dot(
+                    values.astype(jnp.bfloat16), chosen, preferred_element_type=jnp.float32
                 )
-
-            zero = jnp.zeros((ROWS, LANES), jnp.float32)
-            packed = lax.fori_loop(0, per_tile, step, (zero, zero), unroll=4)
-            write((up_ref, down_ref), base + depth + tile, packed[0])
-            cross_ref[base + depth + tile] = packed[1]
-            return unused
-
-        lax.fori_loop(0, tiles, tile_loop, 0)
+            else:
+                picked = pick(kappa_ref[...].reshape(depth * ROWS, 2 * LANES), chosen)
+            picked = picked.reshape(depth, ROWS, 2 * LANES)
+            for ref in refs:
+                ref[base : base + depth] = picked[:, :, :LANES]
+            for tile in range(tiles):
+                packed = picked[tile * per_tile, :, LANES:]
+                for slot in range(1, per_tile):
+                    packed = jnp.where(
+                        slot_ids == slot, picked[tile * per_tile + slot, :, LANES:], packed
+                    )
+                for ref in refs:
+                    ref[base + depth + tile] = packed
+    copies[2].wait()
     base = 2 * (depth + tiles)
     in_low = lax.axis_index("probe") < lax.axis_size("probe") // 2
 
@@ -107,10 +142,12 @@
 
 
 def beside(values):
-    rows, columns = values.shape
-    return (pltpu.roll(values, 1, 0) + pltpu.roll(values, rows - 1, 0)) + (
-        pltpu.roll(values, 1, 1) + pltpu.roll(values, columns - 1, 1)
+    rows = values.shape[0]
+    even, odd = values[:, :LANES], values[:, LANES:]
+    y_sides = jnp.concatenate(
+        [odd + pltpu.roll(odd, 1, 1), even + pltpu.roll(even, LANES - 1, 1)], axis=1
     )
+    return (pltpu.roll(values, 1, 0) + pltpu.roll(values, rows - 1, 0)) + y_sides
 
 
 def basis_kernel(
@@ -144,13 +181,16 @@
     per_tile = LANES // EDGE
     tiles = depth // per_tile
     lanes, ids = lane_ids(shape), row_ids(shape)
-    near = jnp.where(level == 0, LANES, 2 * LANES - EDGE)
-    inside = (lanes < LANES) | ((lanes >= near) & (lanes < near + EDGE))
+    half = LANES // 2
+    lanes = lanes % LANES
+    near = jnp.where(level == 0, half, LANES - EDGE // 2)
+    inside = (lanes < half) | ((lanes >= near) & (lanes < near + EDGE // 2))
     inside = inside & (ids >= jnp.where(tile > 0, 0, ROWS))
     inside = inside & (ids < jnp.where(tile < last_tile, 3 * ROWS, 2 * ROWS))
     mask = jnp.where(inside, 1.0, 0.0)
     zero = jnp.zeros(shape, jnp.float32)
-    own = (slice(ROWS, 2 * ROWS), slice(0, LANES))
+    own = (slice(ROWS, 2 * ROWS), slice(0, 2 * LANES))
+    mine = lane_ids((ROWS, LANES)) < half
     own_zero = jnp.zeros((ROWS, LANES), jnp.float32)
 
     signs[0] = zero
@@ -165,12 +205,19 @@
 
         def unpack(z, unused, pieces=pieces, start=start):
             group = z // per_tile
-            shift = lax.rem(2 * LANES - EDGE * lax.rem(z, per_tile) - EDGE * level, LANES)
+            shift = half + (half - EDGE // 2) * level - (EDGE // 2) * lax.rem(z, per_tile)
+            shift = lax.rem(shift + LANES, LANES)
 
             def gather(base):
-                main = jnp.concatenate([piece[base + z] for piece in pieces], axis=0)
-                edge = jnp.concatenate([piece[base + depth + group] for piece in pieces], axis=0)
-                return jnp.concatenate([main, pltpu.roll(edge, shift, 1)], axis=1)
+                evens, odds = [], []
+                for piece in pieces:
+                    main = piece[base + z]
+                    edge = pltpu.roll(piece[base + depth + group], shift, 1)
+                    evens.append(jnp.where(mine, main, edge))
+                    odds.append(pltpu.roll(jnp.where(mine, edge, main), half, 1))
+                return jnp.concatenate(
+                    [jnp.concatenate(evens, axis=0), jnp.concatenate(odds, axis=0)], axis=1
+                )
 
             signs[start + z + 1] = gather(0) * mask
             half_diag[start + z] = 0.5 * gather(depth + tiles) + (2.0 + VERTICAL)
@@ -179,34 +226,30 @@
         lax.fori_loop(0, depth, unpack, 0, unroll=2)
 
     def start_down(k, carry):
-        ratio, value = carry
+        ratio, value, from_end = carry
         ratio = mask / (half_diag[k] - ratio)
-        value = ratio * (signs[k + 1] + value)
+        here = signs[k + 1]
+        value = ratio * (here + value)
         lower[k] = ratio
         forward[k] = value
-        return ratio, value
-
-    lax.fori_loop(0, levels, start_down, (zero, zero), unroll=GROUP)
+        other = levels - 1 - k
+        from_end = mask / (half_diag[other] - from_end)
+        upper[other] = from_end
+        image = half_diag[k] * here - (signs[k] + signs[k + 2]) - 0.5 * beside(here)
+        k_signs[k] = image[own]
+        return ratio, value, from_end
+
+    lax.fori_loop(0, levels, start_down, (zero, zero, zero), unroll=GROUP)
 
     def start_up(step, carry):
         k = levels - 1 - step
-        ratio, solved, value = carry
-        ratio = mask / (half_diag[k] - ratio)
+        solved, value = carry
         solved = forward[k] + lower[k] * solved
-        value = ratio * (solved + value)
-        upper[k] = ratio
+        value = upper[k] * (solved + value)
         backward[k] = value
-        return ratio, solved, value
-
-    lax.fori_loop(0, levels, start_up, (zero, zero, zero), unroll=GROUP)
-
-    def k_of_signs(k, unused):
-        value = signs[k + 1]
-        image = half_diag[k] * value - (signs[k] + signs[k + 2]) - 0.5 * beside(value)
-        k_signs[k] = image[own]
-        return unused
-
-    lax.fori_loop(0, levels, k_of_signs, 0, unroll=GROUP)
+        return solved, value
+
+    lax.fori_loop(0, levels, start_up, (zero, zero), unroll=GROUP)
 
     place = 0
     for index in range(ITERS):
@@ -237,12 +280,16 @@
                     forward[k] = value
                     sides[k] = side
                 my_sign, my_basis, my_image = signs[k + 1][own], here[own], image[own]
-                terms_ref[index, k] = my_basis * k_signs[k] + my_image * my_sign
+                term = my_basis * k_signs[k] + my_image * my_sign
+                terms_ref[index, k] = jnp.where(
+                    mine, term[:, :LANES], pltpu.roll(term[:, LANES:], half, 1)
+                )
                 if not final:
                     k_basis[index, k] = my_image
+                factors = [(k_basis[other, k], my_image) for other in range(index)]
+                factors += [(my_image, my_image), (my_basis, my_sign)]
                 products.append(
-                    [k_basis[other, k] * my_image for other in range(index)]
-                    + [my_image * my_image, my_basis * my_sign]
+                    [a[:, :LANES] * b[:, :LANES] + a[:, LANES:] * b[:, LANES:] for a, b in factors]
                 )
                 above, here = here, below
             for slot in range(index + 2):
@@ -262,7 +309,7 @@
             down,
             (solved, zero, here, zero) + (own_zero,) * (2 * (index + 2)),
         )
-        totals = carry[4:]
+        totals = [jnp.where(mine, total, 0.0) for total in carry[4:]]
         for slot in range(index + 1):
             sums[2 * (place + slot)] = totals[2 * slot]
             sums[2 * (place + slot) + 1] = totals[2 * slot + 1]
@@ -350,8 +397,8 @@
         pairs = merged + pairs[2 * len(merged) :]
     found = solve_small(*pairs[0])
     core = lax.rem(lax.axis_index("probe"), 2)
-    width = LANES // 2
-    lower_lanes = lane_ids((ROWS, LANES)) < width
+    width = LANES // 4
+    first_lanes = lane_ids((ROWS, LANES)) % (2 * width) < width
     pairs_deep = depth // 2
 
     def step(z, unused):
@@ -364,8 +411,8 @@
 
             one = total(half * depth + z)
             two = total(half * depth + pairs_deep + z)
-            low = jnp.where(lower_lanes, one, pltpu.roll(two, width, 1))
-            high = jnp.where(lower_lanes, pltpu.roll(one, width, 1), two)
+            low = jnp.where(first_lanes, one, pltpu.roll(two, width, 1))
+            high = jnp.where(first_lanes, pltpu.roll(one, LANES - width, 1), two)
             keep_ref[half, z] = jnp.where(core == 0, low, high)
             send_ref[half, z] = jnp.where(core == 0, high, low)
         return unused
@@ -394,6 +441,12 @@
         return jnp.where(even, value, pltpu.roll(value, width, 1))[:, :width]
 
     far_edge = far_ref[far_ref.shape[0] - 1]
+    square = (LANES, LANES)
+    lane = lane_ids(square)
+    source = (width // 2) * (lane // width) + (lane % width) // 2 + width * (lane % 2)
+    chosen = jnp.where(row_ids(square) == source, 1.0, 0.0).astype(jnp.bfloat16)
+    traces = pick((trace_a_ref[...] + trace_b_ref[...]).reshape(-1, LANES), chosen)
+    traces = traces.reshape(depth // 2, ROWS, LANES)
     for z in range(depth):
         value = observed_ref[z]
         mine = half(value)
@@ -416,7 +469,7 @@
             - VERTICAL * (above + below)
         )
         data_part = take(2.0 * mine * k_observed)
-        trace = trace_a_ref[z % (depth // 2)] + trace_b_ref[z % (depth // 2)]
+        trace = traces[z % (depth // 2)]
         trace = trace[:, :width] if z < depth // 2 else pltpu.roll(trace, width, 1)[:, :width]
         out_ref[z] = take(kappa) * (trace * (0.5 / probes) - data_part)
 
@@ -440,8 +493,14 @@
     up_block, down_block, cross_block = pl.pallas_call(
         functools.partial(pack_kernel, depth),
         out_shape=(near_shape, near_shape, far_shape),
-        in_specs=whole(3),
+        in_specs=[pl.BlockSpec(memory_space=pl.ANY)] * 3,
         out_specs=tuple(whole(3)),
+        scratch_shapes=[
+            pltpu.VMEM((depth, rows, columns), jnp.int32),
+            pltpu.VMEM((depth, rows, columns), f32),
+            pltpu.VMEM((depth, rows, columns), f32),
+            pltpu.SemaphoreType.DMA((3,)),
+        ],
         compiler_params=params,
         name="pack",
     )(probe_bits[0], kappa_sq, observed)
@@ -478,8 +537,8 @@
             plain,
             plain,
             padded,
-            pltpu.VMEM((levels, ROWS, LANES), f32),
-            pltpu.VMEM((ITERS - 1, levels, ROWS, LANES), f32),
+            pltpu.VMEM((levels, ROWS, 2 * LANES), f32),
+            pltpu.VMEM((ITERS - 1, levels, ROWS, 2 * LANES), f32),
             pltpu.VMEM((2 * SLOTS, ROWS, LANES), f32),
         ],
         compiler_params=params,

time: 70.1 us -> 70.1 us (level)
  no operation moved by 1% of the time
where the time goes in v2:
time: 70.1 us; the launch traced here: 69.8 us
  starting transfers between devices  25.8 us (37%)
  Pallas kernels  23.4 us (33%)
  waiting for transfers between devices  17.5 us (25%)
  local copies, waits for them, and re-layouts  2.88 us (4%)
    pallas_call x1, Pallas kernels, body(): pl.pallas_call(functools.partial(basis_kernel, depth), out_shape=(jax.Sha...  20 us
    ppermute x1, waiting for transfers between devices, body(): lax.ppermute(cross_block, ('tile', 'level'), [(2 * a + level, 2 * b + 1 -...  8.26 us
    ppermute x3, starting transfers between devices, body(): lax.ppermute(both, 'tile', [(i, (i + k) % tile_count) for i in range(tile...  5.5 us
    ppermute x1, starting transfers between devices, body(): left_far = lax.ppermute(own_far, 'tile', up_pairs)  4.55 us
    ppermute x1, starting transfers between devices, body(): trace_b = lax.ppermute(turned, ('probe', 'level'), routes(True))  4.25 us
    ppermute x1, starting transfers between devices, body(): left = lax.ppermute(up_block, 'tile', up_pairs)  3.49 us
    ppermute x1, waiting for transfers between devices, body(): trace_b = lax.ppermute(turned, ('probe', 'level'), routes(True))  3.48 us
    ppermute x1, starting transfers between devices, body(): own_far = lax.ppermute(cross_block, 'level', [(0, 1), (1, 0)])  3.03 us
  transfers between devices with their start and end apart: 12, of which 8 were waited for; matrix products, arithmetic and copies ran while one was open for 0% of the time, Pallas kernels for 0%

profile of v2, /device:TPU:0, one launch (start us, length us, event | category | flops | bytes accessed | tf_op | source)
XLA Modules:
  0.0 69.8 jit_solution(14017802466805730651)
XLA Ops:
  0.0 0.0 copy-start
  0.0 0.9 %copy-done = f32[32,8,256]{2,1,0:T(8,128)S(1)} copy-done((f32[32,8,256]{2,1,0:T(8,128)S(1)}, f32[32,8,256]{2,1,0:T(8,128)}, u32[]{:S(2)}) %copy-start) | copy-done | bytes 262168
  1.0 0.0 copy-start.2
  1.0 0.9 %copy-done.2 = f32[32,8,256]{2,1,0:T(8,128)S(1)} copy-done((f32[32,8,256]{2,1,0:T(8,128)S(1)}, f32[32,8,256]{2,1,0:T(8,128)}, u32[]{:S(2)}) %copy-start.2) | copy-done | bytes 262168
  1.9 0.0 copy-start.4
  1.9 0.9 %copy-done.4 = s32[1,32,8,256]{3,2,1,0:T(8,128)S(1)} copy-done((s32[1,32,8,256]{3,2,1,0:T(8,128)S(1)}, s32[1,32,8,256]{3,2,1,0:T(8,128)}, u32[]{:S(2)}) %copy-start.4) | copy-done | bytes 262168
  2.9 0.8 %pack.1 = (f32[72,8,128]{2,1,0:T(8,128)S(1)}, f32[72,8,128]{2,1,0:T(8,128)S(1)}, f32[69,8,128]{2,1,0:T(8,128)S(1)}) custom-call(s32[32,8,256]{2,1,0:T(8,128)S(1)} %bitcast.5, f32[32,8,256]{2,1,0:T(8,128)S(1)} %copy-done, f32[32,8,256]{2,1,0:T(8,128)S(1)} %copy-done.2), custom_call_target="tpu_custom_call" | custom-call | tf_op jit(solution)/shard_map/pack/pallas_call | solution.py:493
  3.7 3.0 %collective-permute-start = (f32[69,8,128]{2,1,0:T(8,128)S(1)}, f32[69,8,128]{2,1,0:T(8,128)S(1)}, u32[]{:S(2)}, u32[]{:S(2)}) collective-permute-start(f32[69,8,128]{2,1,0:T(8,128)S(1)} %get-tuple-element.13), channel_id=1, source_target_pairs={{0,1},{1,0},{2,3},{3,2},{4,5},{5,4},{6,7},{7,6},{8,9},{9,8},{10,11... | collective-permute-start | bytes 847880 | tf_op jit(solution)/shard_map/ppermute | solution.py:510
  6.7 3.5 %collective-permute-start.1 = (f32[72,8,128]{2,1,0:T(8,128)S(1)}, f32[72,8,128]{2,1,0:T(8,128)S(1)}, u32[]{:S(2)}, u32[]{:S(2)}) collective-permute-start(f32[72,8,128]{2,1,0:T(8,128)S(1)} %get-tuple-element.12.own_ref), channel_id=1, source_target_pairs={{0,2},{2,4},{4,6},{1,3},{3,5},{5,7},{8,10},{10,12},{12,14},{9,11},... | collective-permute-start | bytes 884744 | tf_op jit(solution)/shard_map/ppermute | solution.py:511
  10.2 1.3 %collective-permute-start.3 = (f32[72,8,128]{2,1,0:T(8,128)S(1)}, f32[72,8,128]{2,1,0:T(8,128)S(1)}, u32[]{:S(2)}, u32[]{:S(2)}) collective-permute-start(f32[72,8,128]{2,1,0:T(8,128)S(1)} %get-tuple-element.14), channel_id=1, source_target_pairs={{2,0},{4,2},{6,4},{3,1},{5,3},{7,5},{10,8},{12,10},{14,12},{11,9},... | collective-permute-start | bytes 884744 | tf_op jit(solution)/shard_map/ppermute | solution.py:512
  11.5 1.3 %collective-permute-start.4 = (f32[69,8,128]{2,1,0:T(8,128)S(1)}, f32[69,8,128]{2,1,0:T(8,128)S(1)}, u32[]{:S(2)}, u32[]{:S(2)}) collective-permute-start(f32[69,8,128]{2,1,0:T(8,128)S(1)} %get-tuple-element.13), channel_id=1, source_target_pairs={{2,1},{3,0},{4,3},{5,2},{6,5},{7,4},{10,9},{11,8},{12,11},{13,10},... | collective-permute-start | bytes 847880 | tf_op jit(solution)/shard_map/ppermute | solution.py:514
  12.8 0.7 collective-permute-done.own_far_ref.far_ref
  13.5 4.5 %collective-permute-start.2 = (f32[69,8,128]{2,1,0:T(8,128)S(1)}, f32[69,8,128]{2,1,0:T(8,128)S(1)}, u32[]{:S(2)}, u32[]{:S(2)}) collective-permute-start(f32[69,8,128]{2,1,0:T(8,128)S(1)} %collective-permute-done.own_far_ref.far_ref), channel_id=1, source_target_pairs={{0,2},{2,4},{4,6},{1,3},{3,5},{5,7},{8,10},{10,12},{12,14},{9,11},... | collective-permute-start | bytes 847880 | tf_op jit(solution)/shard_map/ppermute | solution.py:513
  18.0 8.3 %collective-permute-done.4.right_far_ref = f32[69,8,128]{2,1,0:T(8,128)S(1)} collective-permute-done((f32[69,8,128]{2,1,0:T(8,128)S(1)}, f32[69,8,128]{2,1,0:T(8,128)S(1)}, u32[]{:S(2)}, u32[]{:S(2)}) %collective-permute-start.4) | collective-permute-done | bytes 282656 | tf_op jit(solution)/shard_map/ppermute | solution.py:514
  26.3 0.0 collective-permute-done.1.left_ref
  26.3 0.0 collective-permute-done.3.right_ref
  26.3 0.0 collective-permute-done.2.left_far_ref
  26.3 20.0 %basis.1 = (f32[4,64,8,128]{3,2,1,0:T(8,128)S(1)}, f32[32,128]{1,0:T(8,128)S(1)}) custom-call(f32[72,8,128]{2,1,0:T(8,128)S(1)} %get-tuple-element.12.own_ref, f32[69,8,128]{2,1,0:T(8,128)S(1)} %collective-permute-done.own_far_ref.far_ref, f32[72,8,128]{2,1,0:T(8,128)S(1)} %collective-permute-done.1.left_ref, ...), custom_call_target="tpu_custom_call" | custom-call | tf_op jit(solution)/shard_map/basis/pallas_call | solution.py:523
  46.3 1.6 %collective-permute-start.5 = (f32[32,128]{1,0:T(8,128)S(1)}, f32[32,128]{1,0:T(8,128)S(1)}, u32[]{:S(2)}, u32[]{:S(2)}) collective-permute-start(f32[32,128]{1,0:T(8,128)S(1)} %get-tuple-element.16), channel_id=1, source_target_pairs={{0,1},{1,0},{2,3},{3,2},{4,5},{5,4},{6,7},{7,6},{8,9},{9,8},{10,11... | collective-permute-start | bytes 49160 | tf_op jit(solution)/shard_map/ppermute | solution.py:548
  47.9 2.2 %collective-permute-done.5 = f32[32,128]{1,0:T(8,128)S(1)} collective-permute-done((f32[32,128]{1,0:T(8,128)S(1)}, f32[32,128]{1,0:T(8,128)S(1)}, u32[]{:S(2)}, u32[]{:S(2)}) %collective-permute-start.5) | collective-permute-done | bytes 16416 | tf_op jit(solution)/shard_map/ppermute | solution.py:548
  50.1 1.6 %collective-permute-start.6 = (f32[64,128]{1,0:T(8,128)S(1)}, f32[64,128]{1,0:T(8,128)S(1)}, u32[]{:S(2)}, u32[]{:S(2)}) collective-permute-start(f32[64,128]{1,0:T(8,128)S(1)} %constant_dynamic-update-slice_fusion.refs_0_), channel_id=1, source_target_pairs={{0,2},{2,4},{4,6},{6,0},{1,3},{3,5},{5,7},{7,1},{8,10},{10,12},{12... | collective-permute-start | bytes 98312 | tf_op jit(solution)/shard_map/ppermute | solution.py:551
  51.6 1.0 %collective-permute-start.7 = (f32[64,128]{1,0:T(8,128)S(1)}, f32[64,128]{1,0:T(8,128)S(1)}, u32[]{:S(2)}, u32[]{:S(2)}) collective-permute-start(f32[64,128]{1,0:T(8,128)S(1)} %constant_dynamic-update-slice_fusion.refs_0_), channel_id=1, source_target_pairs={{0,4},{2,6},{4,0},{6,2},{1,5},{3,7},{5,1},{7,3},{8,12},{10,14},{12... | collective-permute-start | bytes 98312 | tf_op jit(solution)/shard_map/ppermute | solution.py:551
  52.7 2.9 %collective-permute-start.8 = (f32[64,128]{1,0:T(8,128)S(1)}, f32[64,128]{1,0:T(8,128)S(1)}, u32[]{:S(2)}, u32[]{:S(2)}) collective-permute-start(f32[64,128]{1,0:T(8,128)S(1)} %constant_dynamic-update-slice_fusion.refs_0_), channel_id=1, source_target_pairs={{0,6},{2,0},{4,2},{6,4},{1,7},{3,1},{5,3},{7,5},{8,14},{10,8},{12,... | collective-permute-start | bytes 98312 | tf_op jit(solution)/shard_map/ppermute | solution.py:551
  55.6 0.2 collective-permute-done.6.refs_1_
  55.8 0.7 collective-permute-done.7.refs_2_
  56.5 0.7 %collective-permute-done.8.refs_3_ = f32[64,128]{1,0:T(8,128)S(1)} collective-permute-done((f32[64,128]{1,0:T(8,128)S(1)}, f32[64,128]{1,0:T(8,128)S(1)}, u32[]{:S(2)}, u32[]{:S(2)}) %collective-permute-start.8) | collective-permute-done | bytes 32800 | tf_op jit(solution)/shard_map/ppermute | solution.py:551
  57.2 0.9 %combine.1 = (f32[2,16,8,128]{3,2,1,0:T(8,128)S(1)}, f32[2,16,8,128]{3,2,1,0:T(8,128)S(1)}) custom-call(f32[4,64,8,128]{3,2,1,0:T(8,128)S(1)} %get-tuple-element.15.terms_ref, f32[64,128]{1,0:T(8,128)S(1)} %constant_dynamic-update-slice_fusion.refs_0_, f32[64,128]{1,0:T(8,128)S(1)} %collective-permute-done.6.refs_1_, ...), custom_call_target="tpu_custom_call" | custom-call | tf_op jit(solution)/shard_map/combine/pallas_call | solution.py:557
  58.1 0.1 collective-permute-start.9
  58.2 1.3 %collective-permute-done.9 = f32[2,16,8,128]{3,2,1,0:T(8,128)S(1)} collective-permute-done((f32[2,16,8,128]{3,2,1,0:T(8,128)S(1)}, f32[2,16,8,128]{3,2,1,0:T(8,128)S(1)}, u32[]{:S(2)}, u32[]{:S(2)}) %collective-permute-start.9) | collective-permute-done | bytes 131104 | tf_op jit(solution)/shard_map/ppermute | solution.py:566
  59.5 0.0 copy-start.1
  59.5 0.0 copy-start.3
  59.6 0.8 %collective-permute-start.10 = (f32[16,8,128]{2,1,0:T(8,128)S(1)}, f32[16,8,128]{2,1,0:T(8,128)S(1)}, u32[]{:S(2)}, u32[]{:S(2)}) collective-permute-start(f32[16,8,128]{2,1,0:T(8,128)S(1)} %get-tuple-element.20), channel_id=1, source_target_pairs={{0,0},{1,16},{8,8},{9,24},{16,1},{17,17},{24,9},{25,25},{2,2},{3,1... | collective-permute-start | bytes 196616 | tf_op jit(solution)/shard_map/ppermute | solution.py:580
  60.4 4.2 %collective-permute-start.11 = (f32[16,8,128]{2,1,0:T(8,128)S(1)}, f32[16,8,128]{2,1,0:T(8,128)S(1)}, u32[]{:S(2)}, u32[]{:S(2)}) collective-permute-start(f32[16,8,128]{2,1,0:T(8,128)S(1)} %get-tuple-element.19), channel_id=1, source_target_pairs={{0,1},{1,17},{8,9},{9,25},{16,0},{17,16},{24,8},{25,24},{2,3},{3,1... | collective-permute-start | bytes 196616 | tf_op jit(solution)/shard_map/ppermute | solution.py:581
  64.6 0.0 collective-permute-done.10.trace_a_ref
  64.6 3.5 %collective-permute-done.11.trace_b_ref = f32[16,8,128]{2,1,0:T(8,128)S(1)} collective-permute-done((f32[16,8,128]{2,1,0:T(8,128)S(1)}, f32[16,8,128]{2,1,0:T(8,128)S(1)}, u32[]{:S(2)}, u32[]{:S(2)}) %collective-permute-start.11) | collective-permute-done | bytes 65568 | tf_op jit(solution)/shard_map/ppermute | solution.py:581
  68.1 0.0 copy-done.1
  68.1 0.0 copy-done.3
  68.1 1.7 %gradient.1 = f32[32,8,64]{2,1,0:T(8,128)} custom-call(f32[16,8,128]{2,1,0:T(8,128)S(1)} %collective-permute-done.10.trace_a_ref, f32[16,8,128]{2,1,0:T(8,128)S(1)} %collective-permute-done.11.trace_b_ref, f32[32,8,256]{2,1,0:T(8,128)S(1)} %copy-done.1, f32[32,8,256]{2,1,0:T(8,128)S(1)} %copy-done.3, f32[72,8,128]{2,1,0:T(8,128)S(1)} %collective-permute-done.1.left_ref, ...), custom_call_target="tpu_custom_call" | custom-call | tf_op jit(solution)/shard_map/gradient/pallas_call | solution.py:582
  (4 shorter events, 0.0 us)
Async XLA Ops:
  0.0 0.9 %copy-start = (f32[32,8,256]{2,1,0:T(8,128)S(1)}, f32[32,8,256]{2,1,0:T(8,128)}, u32[]{:S(2)}) copy-start(f32[32,8,256]{2,1,0:T(8,128)} %kappa_ref.1) | copy-start | bytes 786436
  1.0 0.9 %copy-start.2 = (f32[32,8,256]{2,1,0:T(8,128)S(1)}, f32[32,8,256]{2,1,0:T(8,128)}, u32[]{:S(2)}) copy-start(f32[32,8,256]{2,1,0:T(8,128)} %observed_ref.1) | copy-start | bytes 786436
  1.9 0.9 %copy-start.4 = (s32[1,32,8,256]{3,2,1,0:T(8,128)S(1)}, s32[1,32,8,256]{3,2,1,0:T(8,128)}, u32[]{:S(2)}) copy-start(s32[1,32,8,256]{3,2,1,0:T(8,128)} %param.3) | copy-start | bytes 786436
  3.7 9.8 %collective-permute-start = (f32[69,8,128]{2,1,0:T(8,128)S(1)}, f32[69,8,128]{2,1,0:T(8,128)S(1)}, u32[]{:S(2)}, u32[]{:S(2)}) collective-permute-start(f32[69,8,128]{2,1,0:T(8,128)S(1)} %get-tuple-element.13), channel_id=1, source_target_pairs={{0,1},{1,0},{2,3},{3,2},{4,5},{5,4},{6,7},{7,6},{8,9},{9,8},{10,11... | collective-permute-start | bytes 847880 | tf_op jit(solution)/shard_map/ppermute | solution.py:510
  6.7 19.6 %collective-permute-start.1 = (f32[72,8,128]{2,1,0:T(8,128)S(1)}, f32[72,8,128]{2,1,0:T(8,128)S(1)}, u32[]{:S(2)}, u32[]{:S(2)}) collective-permute-start(f32[72,8,128]{2,1,0:T(8,128)S(1)} %get-tuple-element.12.own_ref), channel_id=1, source_target_pairs={{0,2},{2,4},{4,6},{1,3},{3,5},{5,7},{8,10},{10,12},{12,14},{9,11},... | collective-permute-start | bytes 884744 | tf_op jit(solution)/shard_map/ppermute | solution.py:511
  10.2 16.1 %collective-permute-start.3 = (f32[72,8,128]{2,1,0:T(8,128)S(1)}, f32[72,8,128]{2,1,0:T(8,128)S(1)}, u32[]{:S(2)}, u32[]{:S(2)}) collective-permute-start(f32[72,8,128]{2,1,0:T(8,128)S(1)} %get-tuple-element.14), channel_id=1, source_target_pairs={{2,0},{4,2},{6,4},{3,1},{5,3},{7,5},{10,8},{12,10},{14,12},{11,9},... | collective-permute-start | bytes 884744 | tf_op jit(solution)/shard_map/ppermute | solution.py:512
  11.5 14.8 %collective-permute-start.4 = (f32[69,8,128]{2,1,0:T(8,128)S(1)}, f32[69,8,128]{2,1,0:T(8,128)S(1)}, u32[]{:S(2)}, u32[]{:S(2)}) collective-permute-start(f32[69,8,128]{2,1,0:T(8,128)S(1)} %get-tuple-element.13), channel_id=1, source_target_pairs={{2,1},{3,0},{4,3},{5,2},{6,5},{7,4},{10,9},{11,8},{12,11},{13,10},... | collective-permute-start | bytes 847880 | tf_op jit(solution)/shard_map/ppermute | solution.py:514
  13.5 12.8 %collective-permute-start.2 = (f32[69,8,128]{2,1,0:T(8,128)S(1)}, f32[69,8,128]{2,1,0:T(8,128)S(1)}, u32[]{:S(2)}, u32[]{:S(2)}) collective-permute-start(f32[69,8,128]{2,1,0:T(8,128)S(1)} %collective-permute-done.own_far_ref.far_ref), channel_id=1, source_target_pairs={{0,2},{2,4},{4,6},{1,3},{3,5},{5,7},{8,10},{10,12},{12,14},{9,11},... | collective-permute-start | bytes 847880 | tf_op jit(solution)/shard_map/ppermute | solution.py:513
  46.3 3.8 %collective-permute-start.5 = (f32[32,128]{1,0:T(8,128)S(1)}, f32[32,128]{1,0:T(8,128)S(1)}, u32[]{:S(2)}, u32[]{:S(2)}) collective-permute-start(f32[32,128]{1,0:T(8,128)S(1)} %get-tuple-element.16), channel_id=1, source_target_pairs={{0,1},{1,0},{2,3},{3,2},{4,5},{5,4},{6,7},{7,6},{8,9},{9,8},{10,11... | collective-permute-start | bytes 49160 | tf_op jit(solution)/shard_map/ppermute | solution.py:548
  50.1 5.7 %collective-permute-start.6 = (f32[64,128]{1,0:T(8,128)S(1)}, f32[64,128]{1,0:T(8,128)S(1)}, u32[]{:S(2)}, u32[]{:S(2)}) collective-permute-start(f32[64,128]{1,0:T(8,128)S(1)} %constant_dynamic-update-slice_fusion.refs_0_), channel_id=1, source_target_pairs={{0,2},{2,4},{4,6},{6,0},{1,3},{3,5},{5,7},{7,1},{8,10},{10,12},{12... | collective-permute-start | bytes 98312 | tf_op jit(solution)/shard_map/ppermute | solution.py:551
  51.6 4.8 %collective-permute-start.7 = (f32[64,128]{1,0:T(8,128)S(1)}, f32[64,128]{1,0:T(8,128)S(1)}, u32[]{:S(2)}, u32[]{:S(2)}) collective-permute-start(f32[64,128]{1,0:T(8,128)S(1)} %constant_dynamic-update-slice_fusion.refs_0_), channel_id=1, source_target_pairs={{0,4},{2,6},{4,0},{6,2},{1,5},{3,7},{5,1},{7,3},{8,12},{10,14},{12... | collective-permute-start | bytes 98312 | tf_op jit(solution)/shard_map/ppermute | solution.py:551
  52.7 4.5 %collective-permute-start.8 = (f32[64,128]{1,0:T(8,128)S(1)}, f32[64,128]{1,0:T(8,128)S(1)}, u32[]{:S(2)}, u32[]{:S(2)}) collective-permute-start(f32[64,128]{1,0:T(8,128)S(1)} %constant_dynamic-update-slice_fusion.refs_0_), channel_id=1, source_target_pairs={{0,6},{2,0},{4,2},{6,4},{1,7},{3,1},{5,3},{7,5},{8,14},{10,8},{12,... | collective-permute-start | bytes 98312 | tf_op jit(solution)/shard_map/ppermute | solution.py:551
  58.1 1.4 %collective-permute-start.9 = (f32[2,16,8,128]{3,2,1,0:T(8,128)S(1)}, f32[2,16,8,128]{3,2,1,0:T(8,128)S(1)}, u32[]{:S(2)}, u32[]{:S(2)}) collective-permute-start(f32[2,16,8,128]{3,2,1,0:T(8,128)S(1)} %get-tuple-element.18), channel_id=1, source_target_pairs={{0,8},{8,0},{16,24},{24,16},{1,9},{9,1},{17,25},{25,17},{2,10},{10... | collective-permute-start | bytes 393224 | tf_op jit(solution)/shard_map/ppermute | solution.py:566
  59.5 8.6 %copy-start.1 = (f32[32,8,256]{2,1,0:T(8,128)S(1)}, f32[32,8,256]{2,1,0:T(8,128)}, u32[]{:S(2)}) copy-start(f32[32,8,256]{2,1,0:T(8,128)} %kappa_ref.1) | copy-start | bytes 786436
  59.5 8.6 %copy-start.3 = (f32[32,8,256]{2,1,0:T(8,128)S(1)}, f32[32,8,256]{2,1,0:T(8,128)}, u32[]{:S(2)}) copy-start(f32[32,8,256]{2,1,0:T(8,128)} %observed_ref.1) | copy-start | bytes 786436
  59.6 5.1 %collective-permute-start.10 = (f32[16,8,128]{2,1,0:T(8,128)S(1)}, f32[16,8,128]{2,1,0:T(8,128)S(1)}, u32[]{:S(2)}, u32[]{:S(2)}) collective-permute-start(f32[16,8,128]{2,1,0:T(8,128)S(1)} %get-tuple-element.20), channel_id=1, source_target_pairs={{0,0},{1,16},{8,8},{9,24},{16,1},{17,17},{24,9},{25,25},{2,2},{3,1... | collective-permute-start | bytes 196616 | tf_op jit(solution)/shard_map/ppermute | solution.py:580
  60.4 7.7 %collective-permute-start.11 = (f32[16,8,128]{2,1,0:T(8,128)S(1)}, f32[16,8,128]{2,1,0:T(8,128)S(1)}, u32[]{:S(2)}, u32[]{:S(2)}) collective-permute-start(f32[16,8,128]{2,1,0:T(8,128)S(1)} %get-tuple-element.19), channel_id=1, source_target_pairs={{0,1},{1,17},{8,9},{9,25},{16,0},{17,16},{24,8},{25,24},{2,3},{3,1... | collective-permute-start | bytes 196616 | tf_op jit(solution)/shard_map/ppermute | solution.py:581

commit v3 on v2

--- a/solution.py
+++ b/solution.py
@@ -12,7 +12,7 @@
 LANES = 128
 ROWS = 8
 EDGE = 8
-GROUP = 4
+GROUP = 8
 SHIFTS = (1.0, 0.0, -2.0)
 PAIRS = [(i, j) for j in range(ITERS) for i in range(j + 1)]
 COUNT = len(PAIRS) + ITERS
@@ -188,6 +188,7 @@
     inside = inside & (ids >= jnp.where(tile > 0, 0, ROWS))
     inside = inside & (ids < jnp.where(tile < last_tile, 3 * ROWS, 2 * ROWS))
     mask = jnp.where(inside, 1.0, 0.0)
+    half_mask = 0.5 * mask
     zero = jnp.zeros(shape, jnp.float32)
     own = (slice(ROWS, 2 * ROWS), slice(0, 2 * LANES))
     mine = lane_ids((ROWS, LANES)) < half
@@ -223,7 +224,7 @@
             half_diag[start + z] = 0.5 * gather(depth + tiles) + (2.0 + VERTICAL)
             return unused
 
-        lax.fori_loop(0, depth, unpack, 0, unroll=2)
+        lax.fori_loop(0, depth, unpack, 0, unroll=per_tile)
 
     def start_down(k, carry):
         ratio, value, from_end = carry
@@ -274,9 +275,9 @@
                 if not final:
                     basis[k + 1] = below
                 side = beside(here)
-                image = half_diag[k] * here - (above + below) - 0.5 * side
+                image = half_diag[k] * here - (above + below) - half_mask * side
                 if not final:
-                    value = lower[k] * (beside(image * mask) + value)
+                    value = lower[k] * (beside(image) + value)
                     forward[k] = value
                     sides[k] = side
                 my_sign, my_basis, my_image = signs[k + 1][own], here[own], image[own]
@@ -293,11 +294,12 @@
                 )
                 above, here = here, below
             for slot in range(index + 2):
-                added = (products[0][slot] + products[1][slot]) + (
-                    products[2][slot] + products[3][slot]
-                )
-                totals[2 * slot], rest = two_sum(totals[2 * slot], added)
-                totals[2 * slot + 1] = totals[2 * slot + 1] + rest
+                for four in range(0, GROUP, 4):
+                    added = (products[four][slot] + products[four + 1][slot]) + (
+                        products[four + 2][slot] + products[four + 3][slot]
+                    )
+                    totals[2 * slot], rest = two_sum(totals[2 * slot], added)
+                    totals[2 * slot + 1] = totals[2 * slot + 1] + rest
             return (solved, above, here, value, *totals)
 
         solved, here = next_basis(0, zero)
@@ -334,12 +336,21 @@
         high, low = own_zero, own_zero
         for slot in range(block * ROWS, min((block + 1) * ROWS, COUNT)):
             pair = (sums[2 * slot], sums[2 * slot + 1])
-            for axis, shift in ((0, 4), (0, 2), (0, 1), (1, 64), (1, 32), (1, 16), (1, 8), (1, 4), (1, 2), (1, 1)):
-                pair = pair_add(pair, tuple(pltpu.roll(part, shift, axis) for part in pair))
+            for shift in (4, 2, 1):
+                pair = pair_add(pair, tuple(pltpu.roll(part, shift, 0) for part in pair))
             here = ids == slot - block * ROWS
             high, low = jnp.where(here, pair[0], high), jnp.where(here, pair[1], low)
         gram_ref[block * ROWS : (block + 1) * ROWS] = high
         gram_ref[SLOTS + block * ROWS : SLOTS + (block + 1) * ROWS] = low
+    ones = jnp.ones((LANES, LANES), jnp.bfloat16)
+
+    def lane_sum(part):
+        return jnp.dot(part, ones, preferred_element_type=jnp.float32)
+
+    high, middle, low = (lane_sum(part) for part in split_three(gram_ref[:SLOTS]))
+    high, rest = two_sum(high, middle)
+    gram_ref[:SLOTS] = high
+    gram_ref[SLOTS:] = rest + (low + lane_sum(gram_ref[SLOTS:].astype(jnp.bfloat16)))
 
 
 def solve_small(high, low):
@@ -420,8 +431,8 @@
     lax.fori_loop(0, pairs_deep, step, 0, unroll=2)
 
 
-def gradient_kernel(
-    depth, probes, trace_a_ref, trace_b_ref, kappa_ref, observed_ref, left_ref, right_ref, far_ref, out_ref
+def observed_kernel(
+    depth, probes, kappa_ref, observed_ref, left_ref, right_ref, far_ref, factor_ref, data_ref
 ):
     level = lax.axis_index("level")
     tile = lax.axis_index("tile")
@@ -441,12 +452,6 @@
         return jnp.where(even, value, pltpu.roll(value, width, 1))[:, :width]
 
     far_edge = far_ref[far_ref.shape[0] - 1]
-    square = (LANES, LANES)
-    lane = lane_ids(square)
-    source = (width // 2) * (lane // width) + (lane % width) // 2 + width * (lane % 2)
-    chosen = jnp.where(row_ids(square) == source, 1.0, 0.0).astype(jnp.bfloat16)
-    traces = pick((trace_a_ref[...] + trace_b_ref[...]).reshape(-1, LANES), chosen)
-    traces = traces.reshape(depth // 2, ROWS, LANES)
     for z in range(depth):
         value = observed_ref[z]
         mine = half(value)
@@ -468,10 +473,23 @@
             - half(y_sides)
             - VERTICAL * (above + below)
         )
-        data_part = take(2.0 * mine * k_observed)
-        trace = traces[z % (depth // 2)]
-        trace = trace[:, :width] if z < depth // 2 else pltpu.roll(trace, width, 1)[:, :width]
-        out_ref[z] = take(kappa) * (trace * (0.5 / probes) - data_part)
+        factor_ref[z] = take(kappa * (0.5 / probes))
+        data_ref[z] = take(kappa * (2.0 * mine * k_observed))
+
+
+def gradient_kernel(depth, trace_a_ref, trace_b_ref, factor_ref, data_ref, out_ref):
+    width = LANES // 2
+    square = (LANES, LANES)
+    lane = lane_ids(square)
+    source = (width // 2) * (lane // width) + (lane % width) // 2 + width * (lane % 2)
+    chosen = jnp.where(row_ids(square) == source, 1.0, 0.0).astype(jnp.bfloat16)
+    traces = pick((trace_a_ref[...] + trace_b_ref[...]).reshape(-1, LANES), chosen)
+    traces = traces.reshape(depth // 2, ROWS, LANES)
+    for z in range(depth // 2):
+        out_ref[z] = factor_ref[z] * traces[z, :, :width] - data_ref[z]
+        later = depth // 2 + z
+        second = pltpu.roll(traces[z], width, 1)[:, :width]
+        out_ref[later] = factor_ref[later] * second - data_ref[later]
 
 
 def whole(count):
@@ -493,7 +511,7 @@
     up_block, down_block, cross_block = pl.pallas_call(
         functools.partial(pack_kernel, depth),
         out_shape=(near_shape, near_shape, far_shape),
-        in_specs=[pl.BlockSpec(memory_space=pl.ANY)] * 3,
+        in_specs=[pl.BlockSpec(memory_space=pltpu.HBM)] * 3,
         out_specs=tuple(whole(3)),
         scratch_shapes=[
             pltpu.VMEM((depth, rows, columns), jnp.int32),
@@ -516,6 +534,16 @@
         ("tile", "level"),
         [(2 * a + level, 2 * b + 1 - level) for a, b in down_pairs for level in range(2)],
     )
+
+    quarter = jax.ShapeDtypeStruct((depth, ROWS, columns // probes), f32)
+    factor, data = pl.pallas_call(
+        functools.partial(observed_kernel, depth, probes),
+        out_shape=(quarter, quarter),
+        in_specs=whole(5),
+        out_specs=tuple(whole(2)),
+        compiler_params=params,
+        name="observed",
+    )(kappa_sq, observed, left, right, own_far)
 
     levels = 2 * depth
     padded = pltpu.VMEM((levels + 1, 3 * ROWS, 2 * LANES), f32)
@@ -580,13 +608,13 @@
     trace_a = lax.ppermute(straight, ("probe", "level"), routes(False))
     trace_b = lax.ppermute(turned, ("probe", "level"), routes(True))
     return pl.pallas_call(
-        functools.partial(gradient_kernel, depth, probes),
-        out_shape=jax.ShapeDtypeStruct((depth, ROWS, columns // probes), f32),
-        in_specs=whole(7),
+        functools.partial(gradient_kernel, depth),
+        out_shape=quarter,
+        in_specs=whole(4),
         out_specs=pl.BlockSpec(memory_space=pltpu.VMEM),
         compiler_params=params,
         name="gradient",
-    )(trace_a, trace_b, kappa_sq, observed, left, right, own_far)
+    )(trace_a, trace_b, factor, data)
 
 
 def solution(mesh):

time: 70.1 us -> 60.7 us (0.87)
  Pallas kernels: 23.4 us -> 15 us
  waiting for transfers between devices: 17.5 us -> 16.6 us
    pallas_call x1, Pallas kernels: 20 us -> 11.4 us  [body(): pl.pallas_call(functools.partial(basis_kernel, depth), out_shape=(jax.Sha...]
    ppermute x1, waiting for transfers between devices: 3.48 us -> 2.5 us  [body(): trace_b = lax.ppermute(turned, ('probe', 'level'), routes(True))]
    pallas_call x1 -> x2, Pallas kernels: 1.73 us -> 1.88 us  [the longest x1 0.97 us: body(): pl.pallas_call(functools.partial(observed_kernel, depth, probes), out_sha...]
  transfers between devices with their start and end apart: 12 -> 12, of which waited for: 8 -> 8; matrix products, arithmetic and copies ran while one was open for 0% -> 0% of each run, Pallas kernels for 0% -> 2%
where the time goes in v3:
time: 60.7 us; the launch traced here: 60.4 us
  starting transfers between devices  25.9 us (43%)
  waiting for transfers between devices  16.6 us (27%)
  Pallas kernels  15 us (25%)
  local copies, waits for them, and re-layouts  2.88 us (5%)
    pallas_call x1, Pallas kernels, body(): pl.pallas_call(functools.partial(basis_kernel, depth), out_shape=(jax.Sha...  11.4 us
    ppermute x1, waiting for transfers between devices, body(): lax.ppermute(cross_block, ('tile', 'level'), [(2 * a + level, 2 * b + 1 -...  8.26 us
    ppermute x3, starting transfers between devices, body(): lax.ppermute(both, 'tile', [(i, (i + k) % tile_count) for i in range(tile...  5.5 us
    ppermute x1, starting transfers between devices, body(): left_far = lax.ppermute(own_far, 'tile', up_pairs)  4.55 us
    ppermute x1, starting transfers between devices, body(): trace_b = lax.ppermute(turned, ('probe', 'level'), routes(True))  4.25 us
    ppermute x1, starting transfers between devices, body(): left = lax.ppermute(up_block, 'tile', up_pairs)  3.49 us
    ppermute x1, starting transfers between devices, body(): own_far = lax.ppermute(cross_block, 'level', [(0, 1), (1, 0)])  3.03 us
    unnamed x11, local copies, waits for them, and re-layouts  2.86 us
  transfers between devices with their start and end apart: 12, of which 8 were waited for; matrix products, arithmetic and copies ran while one was open for 0% of the time, Pallas kernels for 2%

profile of v3, /device:TPU:0, one launch (start us, length us, event | category | flops | bytes accessed | tf_op | source)
XLA Modules:
  0.0 60.4 jit_solution(8058105445892651295)
XLA Ops:
  0.0 0.0 copy-start
  0.0 0.9 %copy-done = f32[32,8,256]{2,1,0:T(8,128)S(1)} copy-done((f32[32,8,256]{2,1,0:T(8,128)S(1)}, f32[32,8,256]{2,1,0:T(8,128)}, u32[]{:S(2)}) %copy-start) | copy-done | bytes 262168
  1.0 0.0 copy-start.2
  1.0 0.9 %copy-done.2 = f32[32,8,256]{2,1,0:T(8,128)S(1)} copy-done((f32[32,8,256]{2,1,0:T(8,128)S(1)}, f32[32,8,256]{2,1,0:T(8,128)}, u32[]{:S(2)}) %copy-start.2) | copy-done | bytes 262168
  1.9 0.0 copy-start.4
  1.9 0.9 %copy-done.4 = s32[1,32,8,256]{3,2,1,0:T(8,128)S(1)} copy-done((s32[1,32,8,256]{3,2,1,0:T(8,128)S(1)}, s32[1,32,8,256]{3,2,1,0:T(8,128)}, u32[]{:S(2)}) %copy-start.4) | copy-done | bytes 262168
  2.9 0.8 %pack.1 = (f32[72,8,128]{2,1,0:T(8,128)S(1)}, f32[72,8,128]{2,1,0:T(8,128)S(1)}, f32[69,8,128]{2,1,0:T(8,128)S(1)}) custom-call(s32[32,8,256]{2,1,0:T(8,128)S(1)} %bitcast.5, f32[32,8,256]{2,1,0:T(8,128)S(1)} %copy-done, f32[32,8,256]{2,1,0:T(8,128)S(1)} %copy-done.2), custom_call_target="tpu_custom_call" | custom-call | tf_op jit(solution)/shard_map/pack/pallas_call | solution.py:511
  3.7 3.0 %collective-permute-start = (f32[69,8,128]{2,1,0:T(8,128)S(1)}, f32[69,8,128]{2,1,0:T(8,128)S(1)}, u32[]{:S(2)}, u32[]{:S(2)}) collective-permute-start(f32[69,8,128]{2,1,0:T(8,128)S(1)} %get-tuple-element.15), channel_id=1, source_target_pairs={{0,1},{1,0},{2,3},{3,2},{4,5},{5,4},{6,7},{7,6},{8,9},{9,8},{10,11... | collective-permute-start | bytes 847880 | tf_op jit(solution)/shard_map/ppermute | solution.py:528
  6.7 3.5 %collective-permute-start.1 = (f32[72,8,128]{2,1,0:T(8,128)S(1)}, f32[72,8,128]{2,1,0:T(8,128)S(1)}, u32[]{:S(2)}, u32[]{:S(2)}) collective-permute-start(f32[72,8,128]{2,1,0:T(8,128)S(1)} %get-tuple-element.14.own_ref), channel_id=1, source_target_pairs={{0,2},{2,4},{4,6},{1,3},{3,5},{5,7},{8,10},{10,12},{12,14},{9,11},... | collective-permute-start | bytes 884744 | tf_op jit(solution)/shard_map/ppermute | solution.py:529
  10.2 1.3 %collective-permute-start.3 = (f32[72,8,128]{2,1,0:T(8,128)S(1)}, f32[72,8,128]{2,1,0:T(8,128)S(1)}, u32[]{:S(2)}, u32[]{:S(2)}) collective-permute-start(f32[72,8,128]{2,1,0:T(8,128)S(1)} %get-tuple-element.16), channel_id=1, source_target_pairs={{2,0},{4,2},{6,4},{3,1},{5,3},{7,5},{10,8},{12,10},{14,12},{11,9},... | collective-permute-start | bytes 884744 | tf_op jit(solution)/shard_map/ppermute | solution.py:530
  11.5 1.3 %collective-permute-start.4 = (f32[69,8,128]{2,1,0:T(8,128)S(1)}, f32[69,8,128]{2,1,0:T(8,128)S(1)}, u32[]{:S(2)}, u32[]{:S(2)}) collective-permute-start(f32[69,8,128]{2,1,0:T(8,128)S(1)} %get-tuple-element.15), channel_id=1, source_target_pairs={{2,1},{3,0},{4,3},{5,2},{6,5},{7,4},{10,9},{11,8},{12,11},{13,10},... | collective-permute-start | bytes 847880 | tf_op jit(solution)/shard_map/ppermute | solution.py:532
  12.8 0.7 %collective-permute-done.own_far_ref.far_ref = f32[69,8,128]{2,1,0:T(8,128)S(1)} collective-permute-done((f32[69,8,128]{2,1,0:T(8,128)S(1)}, f32[69,8,128]{2,1,0:T(8,128)S(1)}, u32[]{:S(2)}, u32[]{:S(2)}) %collective-permute-start) | collective-permute-done | bytes 282656 | tf_op jit(solution)/shard_map/ppermute | solution.py:528
  13.5 4.5 %collective-permute-start.2 = (f32[69,8,128]{2,1,0:T(8,128)S(1)}, f32[69,8,128]{2,1,0:T(8,128)S(1)}, u32[]{:S(2)}, u32[]{:S(2)}) collective-permute-start(f32[69,8,128]{2,1,0:T(8,128)S(1)} %collective-permute-done.own_far_ref.far_ref), channel_id=1, source_target_pairs={{0,2},{2,4},{4,6},{1,3},{3,5},{5,7},{8,10},{10,12},{12,14},{9,11},... | collective-permute-start | bytes 847880 | tf_op jit(solution)/shard_map/ppermute | solution.py:531
  18.0 8.3 %collective-permute-done.4.right_far_ref = f32[69,8,128]{2,1,0:T(8,128)S(1)} collective-permute-done((f32[69,8,128]{2,1,0:T(8,128)S(1)}, f32[69,8,128]{2,1,0:T(8,128)S(1)}, u32[]{:S(2)}, u32[]{:S(2)}) %collective-permute-start.4) | collective-permute-done | bytes 282656 | tf_op jit(solution)/shard_map/ppermute | solution.py:532
  26.3 0.0 collective-permute-done.1.left_ref
  26.3 0.0 collective-permute-done.3.right_ref
  26.3 0.0 collective-permute-done.2.left_far_ref
  26.3 11.4 %basis.1 = (f32[4,64,8,128]{3,2,1,0:T(8,128)S(1)}, f32[32,128]{1,0:T(8,128)S(1)}) custom-call(f32[72,8,128]{2,1,0:T(8,128)S(1)} %get-tuple-element.14.own_ref, f32[69,8,128]{2,1,0:T(8,128)S(1)} %collective-permute-done.own_far_ref.far_ref, f32[72,8,128]{2,1,0:T(8,128)S(1)} %collective-permute-done.1.left_ref, ...), custom_call_target="tpu_custom_call" | custom-call | tf_op jit(solution)/shard_map/basis/pallas_call | solution.py:551
  37.7 1.6 %collective-permute-start.5 = (f32[32,128]{1,0:T(8,128)S(1)}, f32[32,128]{1,0:T(8,128)S(1)}, u32[]{:S(2)}, u32[]{:S(2)}) collective-permute-start(f32[32,128]{1,0:T(8,128)S(1)} %get-tuple-element.18), channel_id=1, source_target_pairs={{0,1},{1,0},{2,3},{3,2},{4,5},{5,4},{6,7},{7,6},{8,9},{9,8},{10,11... | collective-permute-start | bytes 49160 | tf_op jit(solution)/shard_map/ppermute | solution.py:576
  39.3 2.2 %collective-permute-done.5 = f32[32,128]{1,0:T(8,128)S(1)} collective-permute-done((f32[32,128]{1,0:T(8,128)S(1)}, f32[32,128]{1,0:T(8,128)S(1)}, u32[]{:S(2)}, u32[]{:S(2)}) %collective-permute-start.5) | collective-permute-done | bytes 16416 | tf_op jit(solution)/shard_map/ppermute | solution.py:576
  41.5 1.6 %collective-permute-start.6 = (f32[64,128]{1,0:T(8,128)S(1)}, f32[64,128]{1,0:T(8,128)S(1)}, u32[]{:S(2)}, u32[]{:S(2)}) collective-permute-start(f32[64,128]{1,0:T(8,128)S(1)} %constant_dynamic-update-slice_fusion.refs_0_), channel_id=1, source_target_pairs={{0,2},{2,4},{4,6},{6,0},{1,3},{3,5},{5,7},{7,1},{8,10},{10,12},{12... | collective-permute-start | bytes 98312 | tf_op jit(solution)/shard_map/ppermute | solution.py:579
  43.1 1.0 %collective-permute-start.7 = (f32[64,128]{1,0:T(8,128)S(1)}, f32[64,128]{1,0:T(8,128)S(1)}, u32[]{:S(2)}, u32[]{:S(2)}) collective-permute-start(f32[64,128]{1,0:T(8,128)S(1)} %constant_dynamic-update-slice_fusion.refs_0_), channel_id=1, source_target_pairs={{0,4},{2,6},{4,0},{6,2},{1,5},{3,7},{5,1},{7,3},{8,12},{10,14},{12... | collective-permute-start | bytes 98312 | tf_op jit(solution)/shard_map/ppermute | solution.py:579
  44.1 2.9 %collective-permute-start.8 = (f32[64,128]{1,0:T(8,128)S(1)}, f32[64,128]{1,0:T(8,128)S(1)}, u32[]{:S(2)}, u32[]{:S(2)}) collective-permute-start(f32[64,128]{1,0:T(8,128)S(1)} %constant_dynamic-update-slice_fusion.refs_0_), channel_id=1, source_target_pairs={{0,6},{2,0},{4,2},{6,4},{1,7},{3,1},{5,3},{7,5},{8,14},{10,8},{12,... | collective-permute-start | bytes 98312 | tf_op jit(solution)/shard_map/ppermute | solution.py:579
  47.0 0.2 collective-permute-done.6.refs_1_
  47.2 0.7 %collective-permute-done.7.refs_2_ = f32[64,128]{1,0:T(8,128)S(1)} collective-permute-done((f32[64,128]{1,0:T(8,128)S(1)}, f32[64,128]{1,0:T(8,128)S(1)}, u32[]{:S(2)}, u32[]{:S(2)}) %collective-permute-start.7) | collective-permute-done | bytes 32800 | tf_op jit(solution)/shard_map/ppermute | solution.py:579
  47.9 0.7 %collective-permute-done.8.refs_3_ = f32[64,128]{1,0:T(8,128)S(1)} collective-permute-done((f32[64,128]{1,0:T(8,128)S(1)}, f32[64,128]{1,0:T(8,128)S(1)}, u32[]{:S(2)}, u32[]{:S(2)}) %collective-permute-start.8) | collective-permute-done | bytes 32800 | tf_op jit(solution)/shard_map/ppermute | solution.py:579
  48.6 0.9 %combine.1 = (f32[2,16,8,128]{3,2,1,0:T(8,128)S(1)}, f32[2,16,8,128]{3,2,1,0:T(8,128)S(1)}) custom-call(f32[4,64,8,128]{3,2,1,0:T(8,128)S(1)} %get-tuple-element.17.terms_ref, f32[64,128]{1,0:T(8,128)S(1)} %constant_dynamic-update-slice_fusion.refs_0_, f32[64,128]{1,0:T(8,128)S(1)} %collective-permute-done.6.refs_1_, ...), custom_call_target="tpu_custom_call" | custom-call | tf_op jit(solution)/shard_map/combine/pallas_call | solution.py:585
  49.5 0.1 collective-permute-start.9
  49.6 1.3 %collective-permute-done.9 = f32[2,16,8,128]{3,2,1,0:T(8,128)S(1)} collective-permute-done((f32[2,16,8,128]{3,2,1,0:T(8,128)S(1)}, f32[2,16,8,128]{3,2,1,0:T(8,128)S(1)}, u32[]{:S(2)}, u32[]{:S(2)}) %collective-permute-start.9) | collective-permute-done | bytes 131104 | tf_op jit(solution)/shard_map/ppermute | solution.py:594
  50.9 0.0 copy-start.1
  50.9 0.0 copy-start.3
  51.0 0.8 %collective-permute-start.10 = (f32[16,8,128]{2,1,0:T(8,128)S(1)}, f32[16,8,128]{2,1,0:T(8,128)S(1)}, u32[]{:S(2)}, u32[]{:S(2)}) collective-permute-start(f32[16,8,128]{2,1,0:T(8,128)S(1)} %get-tuple-element.24), channel_id=1, source_target_pairs={{0,0},{1,16},{8,8},{9,24},{16,1},{17,17},{24,9},{25,25},{2,2},{3,1... | collective-permute-start | bytes 196616 | tf_op jit(solution)/shard_map/ppermute | solution.py:608
  51.8 4.2 %collective-permute-start.11 = (f32[16,8,128]{2,1,0:T(8,128)S(1)}, f32[16,8,128]{2,1,0:T(8,128)S(1)}, u32[]{:S(2)}, u32[]{:S(2)}) collective-permute-start(f32[16,8,128]{2,1,0:T(8,128)S(1)} %get-tuple-element.23), channel_id=1, source_target_pairs={{0,1},{1,17},{8,9},{9,25},{16,0},{17,16},{24,8},{25,24},{2,3},{3,1... | collective-permute-start | bytes 196616 | tf_op jit(solution)/shard_map/ppermute | solution.py:609
  56.0 0.0 copy-done.1
  56.0 0.0 copy-done.3
  56.0 1.0 %observed.1 = (f32[32,8,64]{2,1,0:T(8,128)S(1)}, f32[32,8,64]{2,1,0:T(8,128)S(1)}) custom-call(f32[32,8,256]{2,1,0:T(8,128)S(1)} %copy-done.1, f32[32,8,256]{2,1,0:T(8,128)S(1)} %copy-done.3, f32[72,8,128]{2,1,0:T(8,128)S(1)} %collective-permute-done.1.left_ref, f32[72,8,128]{2,1,0:T(8,128)S(1)} %collective-permute-done.3.right_ref, ...), custom_call_target="tpu_custom_call" | custom-call | tf_op jit(solution)/shard_map/observed/pallas_call | solution.py:539
  57.0 0.0 collective-permute-done.10.trace_a_ref
  57.0 2.5 %collective-permute-done.11.trace_b_ref = f32[16,8,128]{2,1,0:T(8,128)S(1)} collective-permute-done((f32[16,8,128]{2,1,0:T(8,128)S(1)}, f32[16,8,128]{2,1,0:T(8,128)S(1)}, u32[]{:S(2)}, u32[]{:S(2)}) %collective-permute-start.11) | collective-permute-done | bytes 65568 | tf_op jit(solution)/shard_map/ppermute | solution.py:609
  59.5 0.9 %gradient.1 = f32[32,8,64]{2,1,0:T(8,128)} custom-call(f32[16,8,128]{2,1,0:T(8,128)S(1)} %collective-permute-done.10.trace_a_ref, f32[16,8,128]{2,1,0:T(8,128)S(1)} %collective-permute-done.11.trace_b_ref, f32[32,8,64]{2,1,0:T(8,128)S(1)} %get-tuple-element.21.factor_ref, f32[32,8,64]{2,1,0:T(8,128)S(1)} %get-tuple-element.22.data_ref), custom_call_target="tpu_custom_call" | custom-call | tf_op jit(solution)/shard_map/gradient/pallas_call | solution.py:610
  (4 shorter events, 0.0 us)
Async XLA Ops:
  0.0 0.9 %copy-start = (f32[32,8,256]{2,1,0:T(8,128)S(1)}, f32[32,8,256]{2,1,0:T(8,128)}, u32[]{:S(2)}) copy-start(f32[32,8,256]{2,1,0:T(8,128)} %kappa_ref.1) | copy-start | bytes 786436
  1.0 0.9 %copy-start.2 = (f32[32,8,256]{2,1,0:T(8,128)S(1)}, f32[32,8,256]{2,1,0:T(8,128)}, u32[]{:S(2)}) copy-start(f32[32,8,256]{2,1,0:T(8,128)} %observed_ref.1) | copy-start | bytes 786436
  1.9 0.9 %copy-start.4 = (s32[1,32,8,256]{3,2,1,0:T(8,128)S(1)}, s32[1,32,8,256]{3,2,1,0:T(8,128)}, u32[]{:S(2)}) copy-start(s32[1,32,8,256]{3,2,1,0:T(8,128)} %param.3) | copy-start | bytes 786436
  3.7 9.8 %collective-permute-start = (f32[69,8,128]{2,1,0:T(8,128)S(1)}, f32[69,8,128]{2,1,0:T(8,128)S(1)}, u32[]{:S(2)}, u32[]{:S(2)}) collective-permute-start(f32[69,8,128]{2,1,0:T(8,128)S(1)} %get-tuple-element.15), channel_id=1, source_target_pairs={{0,1},{1,0},{2,3},{3,2},{4,5},{5,4},{6,7},{7,6},{8,9},{9,8},{10,11... | collective-permute-start | bytes 847880 | tf_op jit(solution)/shard_map/ppermute | solution.py:528
  6.7 19.6 %collective-permute-start.1 = (f32[72,8,128]{2,1,0:T(8,128)S(1)}, f32[72,8,128]{2,1,0:T(8,128)S(1)}, u32[]{:S(2)}, u32[]{:S(2)}) collective-permute-start(f32[72,8,128]{2,1,0:T(8,128)S(1)} %get-tuple-element.14.own_ref), channel_id=1, source_target_pairs={{0,2},{2,4},{4,6},{1,3},{3,5},{5,7},{8,10},{10,12},{12,14},{9,11},... | collective-permute-start | bytes 884744 | tf_op jit(solution)/shard_map/ppermute | solution.py:529
  10.2 16.1 %collective-permute-start.3 = (f32[72,8,128]{2,1,0:T(8,128)S(1)}, f32[72,8,128]{2,1,0:T(8,128)S(1)}, u32[]{:S(2)}, u32[]{:S(2)}) collective-permute-start(f32[72,8,128]{2,1,0:T(8,128)S(1)} %get-tuple-element.16), channel_id=1, source_target_pairs={{2,0},{4,2},{6,4},{3,1},{5,3},{7,5},{10,8},{12,10},{14,12},{11,9},... | collective-permute-start | bytes 884744 | tf_op jit(solution)/shard_map/ppermute | solution.py:530
  11.5 14.8 %collective-permute-start.4 = (f32[69,8,128]{2,1,0:T(8,128)S(1)}, f32[69,8,128]{2,1,0:T(8,128)S(1)}, u32[]{:S(2)}, u32[]{:S(2)}) collective-permute-start(f32[69,8,128]{2,1,0:T(8,128)S(1)} %get-tuple-element.15), channel_id=1, source_target_pairs={{2,1},{3,0},{4,3},{5,2},{6,5},{7,4},{10,9},{11,8},{12,11},{13,10},... | collective-permute-start | bytes 847880 | tf_op jit(solution)/shard_map/ppermute | solution.py:532
  13.5 12.8 %collective-permute-start.2 = (f32[69,8,128]{2,1,0:T(8,128)S(1)}, f32[69,8,128]{2,1,0:T(8,128)S(1)}, u32[]{:S(2)}, u32[]{:S(2)}) collective-permute-start(f32[69,8,128]{2,1,0:T(8,128)S(1)} %collective-permute-done.own_far_ref.far_ref), channel_id=1, source_target_pairs={{0,2},{2,4},{4,6},{1,3},{3,5},{5,7},{8,10},{10,12},{12,14},{9,11},... | collective-permute-start | bytes 847880 | tf_op jit(solution)/shard_map/ppermute | solution.py:531
  37.7 3.8 %collective-permute-start.5 = (f32[32,128]{1,0:T(8,128)S(1)}, f32[32,128]{1,0:T(8,128)S(1)}, u32[]{:S(2)}, u32[]{:S(2)}) collective-permute-start(f32[32,128]{1,0:T(8,128)S(1)} %get-tuple-element.18), channel_id=1, source_target_pairs={{0,1},{1,0},{2,3},{3,2},{4,5},{5,4},{6,7},{7,6},{8,9},{9,8},{10,11... | collective-permute-start | bytes 49160 | tf_op jit(solution)/shard_map/ppermute | solution.py:576
  41.5 5.7 %collective-permute-start.6 = (f32[64,128]{1,0:T(8,128)S(1)}, f32[64,128]{1,0:T(8,128)S(1)}, u32[]{:S(2)}, u32[]{:S(2)}) collective-permute-start(f32[64,128]{1,0:T(8,128)S(1)} %constant_dynamic-update-slice_fusion.refs_0_), channel_id=1, source_target_pairs={{0,2},{2,4},{4,6},{6,0},{1,3},{3,5},{5,7},{7,1},{8,10},{10,12},{12... | collective-permute-start | bytes 98312 | tf_op jit(solution)/shard_map/ppermute | solution.py:579
  43.1 4.8 %collective-permute-start.7 = (f32[64,128]{1,0:T(8,128)S(1)}, f32[64,128]{1,0:T(8,128)S(1)}, u32[]{:S(2)}, u32[]{:S(2)}) collective-permute-start(f32[64,128]{1,0:T(8,128)S(1)} %constant_dynamic-update-slice_fusion.refs_0_), channel_id=1, source_target_pairs={{0,4},{2,6},{4,0},{6,2},{1,5},{3,7},{5,1},{7,3},{8,12},{10,14},{12... | collective-permute-start | bytes 98312 | tf_op jit(solution)/shard_map/ppermute | solution.py:579
  44.1 4.5 %collective-permute-start.8 = (f32[64,128]{1,0:T(8,128)S(1)}, f32[64,128]{1,0:T(8,128)S(1)}, u32[]{:S(2)}, u32[]{:S(2)}) collective-permute-start(f32[64,128]{1,0:T(8,128)S(1)} %constant_dynamic-update-slice_fusion.refs_0_), channel_id=1, source_target_pairs={{0,6},{2,0},{4,2},{6,4},{1,7},{3,1},{5,3},{7,5},{8,14},{10,8},{12,... | collective-permute-start | bytes 98312 | tf_op jit(solution)/shard_map/ppermute | solution.py:579
  49.5 1.4 %collective-permute-start.9 = (f32[2,16,8,128]{3,2,1,0:T(8,128)S(1)}, f32[2,16,8,128]{3,2,1,0:T(8,128)S(1)}, u32[]{:S(2)}, u32[]{:S(2)}) collective-permute-start(f32[2,16,8,128]{3,2,1,0:T(8,128)S(1)} %get-tuple-element.20), channel_id=1, source_target_pairs={{0,8},{8,0},{16,24},{24,16},{1,9},{9,1},{17,25},{25,17},{2,10},{10... | collective-permute-start | bytes 393224 | tf_op jit(solution)/shard_map/ppermute | solution.py:594
  50.9 5.1 %copy-start.1 = (f32[32,8,256]{2,1,0:T(8,128)S(1)}, f32[32,8,256]{2,1,0:T(8,128)}, u32[]{:S(2)}) copy-start(f32[32,8,256]{2,1,0:T(8,128)} %kappa_ref.1) | copy-start | bytes 786436
  50.9 5.1 %copy-start.3 = (f32[32,8,256]{2,1,0:T(8,128)S(1)}, f32[32,8,256]{2,1,0:T(8,128)}, u32[]{:S(2)}) copy-start(f32[32,8,256]{2,1,0:T(8,128)} %observed_ref.1) | copy-start | bytes 786436
  51.0 6.0 %collective-permute-start.10 = (f32[16,8,128]{2,1,0:T(8,128)S(1)}, f32[16,8,128]{2,1,0:T(8,128)S(1)}, u32[]{:S(2)}, u32[]{:S(2)}) collective-permute-start(f32[16,8,128]{2,1,0:T(8,128)S(1)} %get-tuple-element.24), channel_id=1, source_target_pairs={{0,0},{1,16},{8,8},{9,24},{16,1},{17,17},{24,9},{25,25},{2,2},{3,1... | collective-permute-start | bytes 196616 | tf_op jit(solution)/shard_map/ppermute | solution.py:608
  51.8 7.7 %collective-permute-start.11 = (f32[16,8,128]{2,1,0:T(8,128)S(1)}, f32[16,8,128]{2,1,0:T(8,128)S(1)}, u32[]{:S(2)}, u32[]{:S(2)}) collective-permute-start(f32[16,8,128]{2,1,0:T(8,128)S(1)} %get-tuple-element.23), channel_id=1, source_target_pairs={{0,1},{1,17},{8,9},{9,25},{16,0},{17,16},{24,8},{25,24},{2,3},{3,1... | collective-permute-start | bytes 196616 | tf_op jit(solution)/shard_map/ppermute | solution.py:609

commit v4 on v3

--- a/solution.py
+++ b/solution.py
@@ -82,8 +82,8 @@
     bits_hbm,
     kappa_hbm,
     observed_hbm,
-    up_ref,
-    down_ref,
+    even_ref,
+    odd_ref,
     cross_ref,
     bits_ref,
     kappa_ref,
@@ -107,7 +107,7 @@
     for which in range(2):
         base = which * (depth + tiles)
         copies[which].wait()
-        for refs, chosen in (((up_ref, down_ref), same_columns), ((cross_ref,), cross_columns)):
+        for refs, chosen in (((even_ref, odd_ref), same_columns), ((cross_ref,), cross_columns)):
             if which == 0:
                 values = (2 * bits_ref[...] - 1).astype(jnp.float32).reshape(depth * ROWS, 2 * LANES)
                 picked = jnp.dot(
@@ -135,9 +135,11 @@
 
     top = half(observed_ref[:, ROWS - 1, :])
     bottom = half(observed_ref[:, 0, :])
+    goes_up = lax.rem(lax.axis_index("tile"), 2) == 0
     for tile in range(depth // ROWS):
-        up_ref[base + tile] = top[tile * ROWS : (tile + 1) * ROWS]
-        down_ref[base + tile] = bottom[tile * ROWS : (tile + 1) * ROWS]
+        here = slice(tile * ROWS, (tile + 1) * ROWS)
+        even_ref[base + tile] = jnp.where(goes_up, top[here], bottom[here])
+        odd_ref[base + tile] = jnp.where(goes_up, bottom[here], top[here])
     cross_ref[base] = jnp.where(first, half(observed_ref[depth - 1]), half(observed_ref[0]))
 
 
@@ -154,10 +156,10 @@
     depth,
     own_ref,
     own_far_ref,
-    left_ref,
-    left_far_ref,
-    right_ref,
-    right_far_ref,
+    even_ref,
+    even_far_ref,
+    odd_ref,
+    odd_far_ref,
     terms_ref,
     gram_ref,
     signs,
@@ -199,8 +201,9 @@
     backward[levels] = zero
     upper[levels] = zero
     basis[levels] = zero
+    from_even = lax.rem(tile, 2) == 1
     for far, pieces in enumerate(
-        ((left_ref, own_ref, right_ref), (left_far_ref, own_far_ref, right_far_ref))
+        ((even_ref, own_ref, odd_ref), (even_far_ref, own_far_ref, odd_far_ref))
     ):
         start = depth * (level if far == 0 else 1 - level)
 
@@ -211,9 +214,13 @@
 
             def gather(base):
                 evens, odds = [], []
-                for piece in pieces:
-                    main = piece[base + z]
-                    edge = pltpu.roll(piece[base + depth + group], shift, 1)
+                first, second, third = [
+                    (piece[base + z], piece[base + depth + group]) for piece in pieces
+                ]
+                left = [jnp.where(from_even, a, b) for a, b in zip(first, third)]
+                right = [jnp.where(from_even, b, a) for a, b in zip(first, third)]
+                for main, edge in (left, second, right):
+                    edge = pltpu.roll(edge, shift, 1)
                     evens.append(jnp.where(mine, main, edge))
                     odds.append(pltpu.roll(jnp.where(mine, edge, main), half, 1))
                 return jnp.concatenate(
@@ -432,7 +439,7 @@
 
 
 def observed_kernel(
-    depth, probes, kappa_ref, observed_ref, left_ref, right_ref, far_ref, factor_ref, data_ref
+    depth, probes, kappa_ref, observed_ref, even_ref, odd_ref, far_ref, factor_ref, data_ref
 ):
     level = lax.axis_index("level")
     tile = lax.axis_index("tile")
@@ -443,7 +450,8 @@
     width = LANES // 2
     lanes = lane_ids((ROWS, 2 * LANES))
     ids = row_ids((ROWS, LANES))
-    base = left_ref.shape[0] - depth // ROWS
+    base = even_ref.shape[0] - depth // ROWS
+    from_even = lax.rem(tile, 2) == 1
 
     def half(value):
         return jnp.where(in_low, value[..., :LANES], value[..., LANES:])
@@ -458,8 +466,9 @@
         y_sides = jnp.where(lanes > 0, pltpu.roll(value, 1, 1), 0.0) + jnp.where(
             lanes < 2 * LANES - 1, pltpu.roll(value, 2 * LANES - 1, 1), 0.0
         )
-        left = left_ref[base + z // ROWS, z % ROWS : z % ROWS + 1, :]
-        right = right_ref[base + z // ROWS, z % ROWS : z % ROWS + 1, :]
+        first = even_ref[base + z // ROWS, z % ROWS : z % ROWS + 1, :]
+        second = odd_ref[base + z // ROWS, z % ROWS : z % ROWS + 1, :]
+        left, right = jnp.where(from_even, first, second), jnp.where(from_even, second, first)
         before = jnp.where(ids > 0, pltpu.roll(mine, 1, 0), jnp.where(tile > 0, left, 0.0))
         after = jnp.where(
             ids < ROWS - 1, pltpu.roll(mine, ROWS - 1, 0), jnp.where(tile < last_tile, right, 0.0)
@@ -508,7 +517,7 @@
     near_shape = jax.ShapeDtypeStruct((field + depth // ROWS, ROWS, LANES), f32)
     far_shape = jax.ShapeDtypeStruct((field + 1, ROWS, LANES), f32)
 
-    up_block, down_block, cross_block = pl.pallas_call(
+    even_block, odd_block, cross_block = pl.pallas_call(
         functools.partial(pack_kernel, depth),
         out_shape=(near_shape, near_shape, far_shape),
         in_specs=[pl.BlockSpec(memory_space=pltpu.HBM)] * 3,
@@ -521,18 +530,26 @@
         ],
         compiler_params=params,
         name="pack",
-    )(probe_bits[0], kappa_sq, observed)
-
-    up_pairs = [(i, i + 1) for i in range(tile_count - 1)]
-    down_pairs = [(i + 1, i) for i in range(tile_count - 1)]
-    own_far = lax.ppermute(cross_block, "level", [(0, 1), (1, 0)])
-    left = lax.ppermute(up_block, "tile", up_pairs)
-    right = lax.ppermute(down_block, "tile", down_pairs)
-    left_far = lax.ppermute(own_far, "tile", up_pairs)
-    right_far = lax.ppermute(
+    )(
+        *(
+            pltpu.with_memory_space_constraint(value, pltpu.HBM)
+            for value in (probe_bits[0], kappa_sq, observed)
+        )
+    )
+
+    def swaps(pairs):
+        return [way for a, b in pairs for way in ((a, b), (b, a))]
+
+    even_pairs = [(i, i + 1) for i in range(0, tile_count - 1, 2)]
+    odd_pairs = [(i, i + 1) for i in range(1, tile_count - 1, 2)]
+    own_far = lax.ppermute(cross_block, "level", swaps([(0, 1)]))
+    even = lax.ppermute(even_block, "tile", swaps(even_pairs))
+    odd = lax.ppermute(odd_block, "tile", swaps(odd_pairs))
+    odd_far = lax.ppermute(own_far, "tile", swaps(odd_pairs))
+    even_far = lax.ppermute(
         cross_block,
         ("tile", "level"),
-        [(2 * a + level, 2 * b + 1 - level) for a, b in down_pairs for level in range(2)],
+        swaps([(2 * a + level, 2 * b + 1 - level) for a, b in even_pairs for level in range(2)]),
     )
 
     quarter = jax.ShapeDtypeStruct((depth, ROWS, columns // probes), f32)
@@ -543,7 +560,7 @@
         out_specs=tuple(whole(2)),
         compiler_params=params,
         name="observed",
-    )(kappa_sq, observed, left, right, own_far)
+    )(kappa_sq, observed, even, odd, own_far)
 
     levels = 2 * depth
     padded = pltpu.VMEM((levels + 1, 3 * ROWS, 2 * LANES), f32)
@@ -571,12 +588,12 @@
         ],
         compiler_params=params,
         name="basis",
-    )(up_block, own_far, left, left_far, right, right_far)
+    )(even_block, own_far, even, even_far, odd, odd_far)
 
     both = jnp.concatenate([gram, lax.ppermute(gram, "level", [(0, 1), (1, 0)])], axis=0)
-    if tile_count <= 4:
+    if tile_count in (2, 4):
         partials = [both] + [
-            lax.ppermute(both, "tile", [(i, (i + k) % tile_count) for i in range(tile_count)])
+            lax.ppermute(both, "tile", [(i, i ^ k) for i in range(tile_count)])
             for k in range(1, tile_count)
         ]
     else:

time: 60.7 us -> 56.9 us (0.937)
  local copies, waits for them, and re-layouts: 2.88 us -> 0.03 us
  starting transfers between devices: 25.9 us -> 24.6 us
  Pallas kernels: 15 us -> 15.8 us
    unnamed x11 -> x5, local copies, waits for them, and re-layouts: 2.86 us -> 0.01 us
    ppermute x8, starting transfers between devices: 19.2 us -> 17.7 us  [the longest x3 7.41 us: body(): lax.ppermute(both, 'tile', [(i, i ^ k) for i in range(tile_count)])]
    ppermute x1, waiting for transfers between devices: 2.5 us -> 1.48 us  [body(): trace_b = lax.ppermute(turned, ('probe', 'level'), routes(True))]
    pallas_call x1, Pallas kernels: 0.81 us -> 1.62 us  [body(): pl.pallas_call(functools.partial(pack_kernel, depth), out_shape=(near_sha...]
    ppermute x8, waiting for transfers between devices: 10.5 us -> 11.3 us  [the longest x1 6.9 us: body(): lax.ppermute(cross_block, ('tile', 'level'), swaps([(2 * a + level, 2 * b...]
  transfers between devices with their start and end apart: 12 -> 12, of which waited for: 8 -> 7; matrix products, arithmetic and copies ran while one was open for 0% -> 0% of each run, Pallas kernels for 2% -> 2%
where the time goes in v4:
time: 56.9 us; the launch traced here: 56.7 us
  starting transfers between devices  24.6 us (43%)
  waiting for transfers between devices  16.1 us (28%)
  Pallas kernels  15.8 us (28%)
    pallas_call x1, Pallas kernels, body(): pl.pallas_call(functools.partial(basis_kernel, depth), out_shape=(jax.Sha...  11.4 us
    ppermute x3, starting transfers between devices, body(): lax.ppermute(both, 'tile', [(i, i ^ k) for i in range(tile_count)])  7.41 us
    ppermute x1, waiting for transfers between devices, body(): lax.ppermute(cross_block, ('tile', 'level'), swaps([(2 * a + level, 2 * b...  6.9 us
    ppermute x1, starting transfers between devices, body(): lax.ppermute(cross_block, ('tile', 'level'), swaps([(2 * a + level, 2 * b...  4.38 us
    ppermute x3, waiting for transfers between devices, body(): lax.ppermute(both, 'tile', [(i, i ^ k) for i in range(tile_count)])  4.26 us
    ppermute x1, starting transfers between devices, body(): trace_b = lax.ppermute(turned, ('probe', 'level'), routes(True))  4.26 us
    ppermute x1, starting transfers between devices, body(): own_far = lax.ppermute(cross_block, 'level', swaps([(0, 1)]))  3.03 us
    ppermute x1, waiting for transfers between devices, body(): lax.ppermute(gram, 'level', [(0, 1), (1, 0)])  2.07 us
  transfers between devices with their start and end apart: 12, of which 7 were waited for; matrix products, arithmetic and copies ran while one was open for 0% of the time, Pallas kernels for 2%

profile of v4, /device:TPU:0, one launch (start us, length us, event | category | flops | bytes accessed | tf_op | source)
XLA Modules:
  0.0 56.7 jit_solution(14890056081303630748)
XLA Ops:
  0.0 1.6 %pack.1 = (f32[72,8,128]{2,1,0:T(8,128)S(1)}, f32[72,8,128]{2,1,0:T(8,128)S(1)}, f32[69,8,128]{2,1,0:T(8,128)S(1)}) custom-call(s32[32,8,256]{2,1,0:T(8,128)} %bitcast.5, f32[32,8,256]{2,1,0:T(8,128)} %kappa_ref.1, f32[32,8,256]{2,1,0:T(8,128)} %observed_ref.1), custom_call_target="tpu_custom_call" | custom-call | tf_op jit(solution)/shard_map/pack/pallas_call | solution.py:520
  1.6 3.0 %collective-permute-start = (f32[69,8,128]{2,1,0:T(8,128)S(1)}, f32[69,8,128]{2,1,0:T(8,128)S(1)}, u32[]{:S(2)}, u32[]{:S(2)}) collective-permute-start(f32[69,8,128]{2,1,0:T(8,128)S(1)} %get-tuple-element.15), channel_id=1, source_target_pairs={{0,1},{1,0},{2,3},{3,2},{4,5},{5,4},{6,7},{7,6},{8,9},{9,8},{10,11... | collective-permute-start | bytes 847880 | tf_op jit(solution)/shard_map/ppermute | solution.py:545
  4.7 1.6 %collective-permute-start.1 = (f32[72,8,128]{2,1,0:T(8,128)S(1)}, f32[72,8,128]{2,1,0:T(8,128)S(1)}, u32[]{:S(2)}, u32[]{:S(2)}) collective-permute-start(f32[72,8,128]{2,1,0:T(8,128)S(1)} %get-tuple-element.14.own_ref), channel_id=1, source_target_pairs={{0,2},{2,0},{4,6},{6,4},{1,3},{3,1},{5,7},{7,5},{8,10},{10,8},{12,... | collective-permute-start | bytes 884744 | tf_op jit(solution)/shard_map/ppermute | solution.py:546
  6.2 0.7 %collective-permute-start.3 = (f32[72,8,128]{2,1,0:T(8,128)S(1)}, f32[72,8,128]{2,1,0:T(8,128)S(1)}, u32[]{:S(2)}, u32[]{:S(2)}) collective-permute-start(f32[72,8,128]{2,1,0:T(8,128)S(1)} %get-tuple-element.16), channel_id=1, source_target_pairs={{2,4},{4,2},{3,5},{5,3},{10,12},{12,10},{11,13},{13,11},{18,20},{2... | collective-permute-start | bytes 884744 | tf_op jit(solution)/shard_map/ppermute | solution.py:547
  6.9 4.4 %collective-permute-start.2 = (f32[69,8,128]{2,1,0:T(8,128)S(1)}, f32[69,8,128]{2,1,0:T(8,128)S(1)}, u32[]{:S(2)}, u32[]{:S(2)}) collective-permute-start(f32[69,8,128]{2,1,0:T(8,128)S(1)} %get-tuple-element.15), channel_id=1, source_target_pairs={{0,3},{3,0},{1,2},{2,1},{4,7},{7,4},{5,6},{6,5},{8,11},{11,8},{9,1... | collective-permute-start | bytes 847880 | tf_op jit(solution)/shard_map/ppermute | solution.py:549
  11.3 0.1 collective-permute-done.own_far_ref.far_ref
  11.4 0.7 %collective-permute-start.4 = (f32[69,8,128]{2,1,0:T(8,128)S(1)}, f32[69,8,128]{2,1,0:T(8,128)S(1)}, u32[]{:S(2)}, u32[]{:S(2)}) collective-permute-start(f32[69,8,128]{2,1,0:T(8,128)S(1)} %collective-permute-done.own_far_ref.far_ref), channel_id=1, source_target_pairs={{2,4},{4,2},{3,5},{5,3},{10,12},{12,10},{11,13},{13,11},{18,20},{2... | collective-permute-start | bytes 847880 | tf_op jit(solution)/shard_map/ppermute | solution.py:548
  12.1 6.9 %collective-permute-done.2.even_far_ref = f32[69,8,128]{2,1,0:T(8,128)S(1)} collective-permute-done((f32[69,8,128]{2,1,0:T(8,128)S(1)}, f32[69,8,128]{2,1,0:T(8,128)S(1)}, u32[]{:S(2)}, u32[]{:S(2)}) %collective-permute-start.2) | collective-permute-done | bytes 282656 | tf_op jit(solution)/shard_map/ppermute | solution.py:549
  19.0 0.0 collective-permute-done.1.even_ref
  19.0 0.0 collective-permute-done.3.odd_ref
  19.0 0.0 collective-permute-done.4.odd_far_ref
  19.0 11.4 %basis.1 = (f32[4,64,8,128]{3,2,1,0:T(8,128)S(1)}, f32[32,128]{1,0:T(8,128)S(1)}) custom-call(f32[72,8,128]{2,1,0:T(8,128)S(1)} %get-tuple-element.14.own_ref, f32[69,8,128]{2,1,0:T(8,128)S(1)} %collective-permute-done.own_far_ref.far_ref, f32[72,8,128]{2,1,0:T(8,128)S(1)} %collective-permute-done.1.even_ref, ...), custom_call_target="tpu_custom_call" | custom-call | tf_op jit(solution)/shard_map/basis/pallas_call | solution.py:568
  30.4 1.7 %collective-permute-start.5 = (f32[32,128]{1,0:T(8,128)S(1)}, f32[32,128]{1,0:T(8,128)S(1)}, u32[]{:S(2)}, u32[]{:S(2)}) collective-permute-start(f32[32,128]{1,0:T(8,128)S(1)} %get-tuple-element.18), channel_id=1, source_target_pairs={{0,1},{1,0},{2,3},{3,2},{4,5},{5,4},{6,7},{7,6},{8,9},{9,8},{10,11... | collective-permute-start | bytes 49160 | tf_op jit(solution)/shard_map/ppermute | solution.py:593
  32.1 2.1 %collective-permute-done.5 = f32[32,128]{1,0:T(8,128)S(1)} collective-permute-done((f32[32,128]{1,0:T(8,128)S(1)}, f32[32,128]{1,0:T(8,128)S(1)}, u32[]{:S(2)}, u32[]{:S(2)}) %collective-permute-start.5) | collective-permute-done | bytes 16416 | tf_op jit(solution)/shard_map/ppermute | solution.py:593
  34.2 4.8 %collective-permute-start.6 = (f32[64,128]{1,0:T(8,128)S(1)}, f32[64,128]{1,0:T(8,128)S(1)}, u32[]{:S(2)}, u32[]{:S(2)}) collective-permute-start(f32[64,128]{1,0:T(8,128)S(1)} %constant_dynamic-update-slice_fusion.refs_0_), channel_id=1, source_target_pairs={{0,2},{2,0},{4,6},{6,4},{1,3},{3,1},{5,7},{7,5},{8,10},{10,8},{12,... | collective-permute-start | bytes 98312 | tf_op jit(solution)/shard_map/ppermute | solution.py:596
  39.0 1.2 %collective-permute-start.7 = (f32[64,128]{1,0:T(8,128)S(1)}, f32[64,128]{1,0:T(8,128)S(1)}, u32[]{:S(2)}, u32[]{:S(2)}) collective-permute-start(f32[64,128]{1,0:T(8,128)S(1)} %constant_dynamic-update-slice_fusion.refs_0_), channel_id=1, source_target_pairs={{0,4},{2,6},{4,0},{6,2},{1,5},{3,7},{5,1},{7,3},{8,12},{10,14},{12... | collective-permute-start | bytes 98312 | tf_op jit(solution)/shard_map/ppermute | solution.py:596
  40.2 1.5 %collective-permute-start.8 = (f32[64,128]{1,0:T(8,128)S(1)}, f32[64,128]{1,0:T(8,128)S(1)}, u32[]{:S(2)}, u32[]{:S(2)}) collective-permute-start(f32[64,128]{1,0:T(8,128)S(1)} %constant_dynamic-update-slice_fusion.refs_0_), channel_id=1, source_target_pairs={{0,6},{2,4},{4,2},{6,0},{1,7},{3,5},{5,3},{7,1},{8,14},{10,12},{12... | collective-permute-start | bytes 98312 | tf_op jit(solution)/shard_map/ppermute | solution.py:596
  41.6 0.0 collective-permute-done.6.refs_1_
  41.6 2.5 %collective-permute-done.7.refs_2_ = f32[64,128]{1,0:T(8,128)S(1)} collective-permute-done((f32[64,128]{1,0:T(8,128)S(1)}, f32[64,128]{1,0:T(8,128)S(1)}, u32[]{:S(2)}, u32[]{:S(2)}) %collective-permute-start.7) | collective-permute-done | bytes 32800 | tf_op jit(solution)/shard_map/ppermute | solution.py:596
  44.2 1.7 %collective-permute-done.8.refs_3_ = f32[64,128]{1,0:T(8,128)S(1)} collective-permute-done((f32[64,128]{1,0:T(8,128)S(1)}, f32[64,128]{1,0:T(8,128)S(1)}, u32[]{:S(2)}, u32[]{:S(2)}) %collective-permute-start.8) | collective-permute-done | bytes 32800 | tf_op jit(solution)/shard_map/ppermute | solution.py:596
  45.9 0.9 %combine.1 = (f32[2,16,8,128]{3,2,1,0:T(8,128)S(1)}, f32[2,16,8,128]{3,2,1,0:T(8,128)S(1)}) custom-call(f32[4,64,8,128]{3,2,1,0:T(8,128)S(1)} %get-tuple-element.17.terms_ref, f32[64,128]{1,0:T(8,128)S(1)} %constant_dynamic-update-slice_fusion.refs_0_, f32[64,128]{1,0:T(8,128)S(1)} %collective-permute-done.6.refs_1_, ...), custom_call_target="tpu_custom_call" | custom-call | tf_op jit(solution)/shard_map/combine/pallas_call | solution.py:602
  46.8 0.1 collective-permute-start.9
  46.9 1.3 %collective-permute-done.9 = f32[2,16,8,128]{3,2,1,0:T(8,128)S(1)} collective-permute-done((f32[2,16,8,128]{3,2,1,0:T(8,128)S(1)}, f32[2,16,8,128]{3,2,1,0:T(8,128)S(1)}, u32[]{:S(2)}, u32[]{:S(2)}) %collective-permute-start.9) | collective-permute-done | bytes 131104 | tf_op jit(solution)/shard_map/ppermute | solution.py:611
  48.2 0.0 copy-start
  48.2 0.0 copy-start.1
  48.3 0.8 %collective-permute-start.10 = (f32[16,8,128]{2,1,0:T(8,128)S(1)}, f32[16,8,128]{2,1,0:T(8,128)S(1)}, u32[]{:S(2)}, u32[]{:S(2)}) collective-permute-start(f32[16,8,128]{2,1,0:T(8,128)S(1)} %get-tuple-element.24), channel_id=1, source_target_pairs={{0,0},{1,16},{8,8},{9,24},{16,1},{17,17},{24,9},{25,25},{2,2},{3,1... | collective-permute-start | bytes 196616 | tf_op jit(solution)/shard_map/ppermute | solution.py:625
  49.1 4.3 %collective-permute-start.11 = (f32[16,8,128]{2,1,0:T(8,128)S(1)}, f32[16,8,128]{2,1,0:T(8,128)S(1)}, u32[]{:S(2)}, u32[]{:S(2)}) collective-permute-start(f32[16,8,128]{2,1,0:T(8,128)S(1)} %get-tuple-element.23), channel_id=1, source_target_pairs={{0,1},{1,17},{8,9},{9,25},{16,0},{17,16},{24,8},{25,24},{2,3},{3,1... | collective-permute-start | bytes 196616 | tf_op jit(solution)/shard_map/ppermute | solution.py:626
  53.3 0.0 copy-done
  53.3 0.0 copy-done.1
  53.3 1.0 %observed.1 = (f32[32,8,64]{2,1,0:T(8,128)S(1)}, f32[32,8,64]{2,1,0:T(8,128)S(1)}) custom-call(f32[32,8,256]{2,1,0:T(8,128)S(1)} %copy-done, f32[32,8,256]{2,1,0:T(8,128)S(1)} %copy-done.1, f32[72,8,128]{2,1,0:T(8,128)S(1)} %collective-permute-done.1.even_ref, f32[72,8,128]{2,1,0:T(8,128)S(1)} %collective-permute-done.3.odd_ref, ...), custom_call_target="tpu_custom_call" | custom-call | tf_op jit(solution)/shard_map/observed/pallas_call | solution.py:556
  54.3 0.0 collective-permute-done.10.trace_a_ref
  54.3 1.5 %collective-permute-done.11.trace_b_ref = f32[16,8,128]{2,1,0:T(8,128)S(1)} collective-permute-done((f32[16,8,128]{2,1,0:T(8,128)S(1)}, f32[16,8,128]{2,1,0:T(8,128)S(1)}, u32[]{:S(2)}, u32[]{:S(2)}) %collective-permute-start.11) | collective-permute-done | bytes 65568 | tf_op jit(solution)/shard_map/ppermute | solution.py:626
  55.8 0.9 %gradient.1 = f32[32,8,64]{2,1,0:T(8,128)} custom-call(f32[16,8,128]{2,1,0:T(8,128)S(1)} %collective-permute-done.10.trace_a_ref, f32[16,8,128]{2,1,0:T(8,128)S(1)} %collective-permute-done.11.trace_b_ref, f32[32,8,64]{2,1,0:T(8,128)S(1)} %get-tuple-element.21.factor_ref, f32[32,8,64]{2,1,0:T(8,128)S(1)} %get-tuple-element.22.data_ref), custom_call_target="tpu_custom_call" | custom-call | tf_op jit(solution)/shard_map/gradient/pallas_call | solution.py:627
  (4 shorter events, 0.0 us)
Async XLA Ops:
  1.6 9.8 %collective-permute-start = (f32[69,8,128]{2,1,0:T(8,128)S(1)}, f32[69,8,128]{2,1,0:T(8,128)S(1)}, u32[]{:S(2)}, u32[]{:S(2)}) collective-permute-start(f32[69,8,128]{2,1,0:T(8,128)S(1)} %get-tuple-element.15), channel_id=1, source_target_pairs={{0,1},{1,0},{2,3},{3,2},{4,5},{5,4},{6,7},{7,6},{8,9},{9,8},{10,11... | collective-permute-start | bytes 847880 | tf_op jit(solution)/shard_map/ppermute | solution.py:545
  4.7 14.3 %collective-permute-start.1 = (f32[72,8,128]{2,1,0:T(8,128)S(1)}, f32[72,8,128]{2,1,0:T(8,128)S(1)}, u32[]{:S(2)}, u32[]{:S(2)}) collective-permute-start(f32[72,8,128]{2,1,0:T(8,128)S(1)} %get-tuple-element.14.own_ref), channel_id=1, source_target_pairs={{0,2},{2,0},{4,6},{6,4},{1,3},{3,1},{5,7},{7,5},{8,10},{10,8},{12,... | collective-permute-start | bytes 884744 | tf_op jit(solution)/shard_map/ppermute | solution.py:546
  6.2 12.7 %collective-permute-start.3 = (f32[72,8,128]{2,1,0:T(8,128)S(1)}, f32[72,8,128]{2,1,0:T(8,128)S(1)}, u32[]{:S(2)}, u32[]{:S(2)}) collective-permute-start(f32[72,8,128]{2,1,0:T(8,128)S(1)} %get-tuple-element.16), channel_id=1, source_target_pairs={{2,4},{4,2},{3,5},{5,3},{10,12},{12,10},{11,13},{13,11},{18,20},{2... | collective-permute-start | bytes 884744 | tf_op jit(solution)/shard_map/ppermute | solution.py:547
  6.9 12.1 %collective-permute-start.2 = (f32[69,8,128]{2,1,0:T(8,128)S(1)}, f32[69,8,128]{2,1,0:T(8,128)S(1)}, u32[]{:S(2)}, u32[]{:S(2)}) collective-permute-start(f32[69,8,128]{2,1,0:T(8,128)S(1)} %get-tuple-element.15), channel_id=1, source_target_pairs={{0,3},{3,0},{1,2},{2,1},{4,7},{7,4},{5,6},{6,5},{8,11},{11,8},{9,1... | collective-permute-start | bytes 847880 | tf_op jit(solution)/shard_map/ppermute | solution.py:549
  11.4 7.6 %collective-permute-start.4 = (f32[69,8,128]{2,1,0:T(8,128)S(1)}, f32[69,8,128]{2,1,0:T(8,128)S(1)}, u32[]{:S(2)}, u32[]{:S(2)}) collective-permute-start(f32[69,8,128]{2,1,0:T(8,128)S(1)} %collective-permute-done.own_far_ref.far_ref), channel_id=1, source_target_pairs={{2,4},{4,2},{3,5},{5,3},{10,12},{12,10},{11,13},{13,11},{18,20},{2... | collective-permute-start | bytes 847880 | tf_op jit(solution)/shard_map/ppermute | solution.py:548
  30.4 3.8 %collective-permute-start.5 = (f32[32,128]{1,0:T(8,128)S(1)}, f32[32,128]{1,0:T(8,128)S(1)}, u32[]{:S(2)}, u32[]{:S(2)}) collective-permute-start(f32[32,128]{1,0:T(8,128)S(1)} %get-tuple-element.18), channel_id=1, source_target_pairs={{0,1},{1,0},{2,3},{3,2},{4,5},{5,4},{6,7},{7,6},{8,9},{9,8},{10,11... | collective-permute-start | bytes 49160 | tf_op jit(solution)/shard_map/ppermute | solution.py:593
  34.2 7.4 %collective-permute-start.6 = (f32[64,128]{1,0:T(8,128)S(1)}, f32[64,128]{1,0:T(8,128)S(1)}, u32[]{:S(2)}, u32[]{:S(2)}) collective-permute-start(f32[64,128]{1,0:T(8,128)S(1)} %constant_dynamic-update-slice_fusion.refs_0_), channel_id=1, source_target_pairs={{0,2},{2,0},{4,6},{6,4},{1,3},{3,1},{5,7},{7,5},{8,10},{10,8},{12,... | collective-permute-start | bytes 98312 | tf_op jit(solution)/shard_map/ppermute | solution.py:596
  39.0 5.2 %collective-permute-start.7 = (f32[64,128]{1,0:T(8,128)S(1)}, f32[64,128]{1,0:T(8,128)S(1)}, u32[]{:S(2)}, u32[]{:S(2)}) collective-permute-start(f32[64,128]{1,0:T(8,128)S(1)} %constant_dynamic-update-slice_fusion.refs_0_), channel_id=1, source_target_pairs={{0,4},{2,6},{4,0},{6,2},{1,5},{3,7},{5,1},{7,3},{8,12},{10,14},{12... | collective-permute-start | bytes 98312 | tf_op jit(solution)/shard_map/ppermute | solution.py:596
  40.2 5.7 %collective-permute-start.8 = (f32[64,128]{1,0:T(8,128)S(1)}, f32[64,128]{1,0:T(8,128)S(1)}, u32[]{:S(2)}, u32[]{:S(2)}) collective-permute-start(f32[64,128]{1,0:T(8,128)S(1)} %constant_dynamic-update-slice_fusion.refs_0_), channel_id=1, source_target_pairs={{0,6},{2,4},{4,2},{6,0},{1,7},{3,5},{5,3},{7,1},{8,14},{10,12},{12... | collective-permute-start | bytes 98312 | tf_op jit(solution)/shard_map/ppermute | solution.py:596
  46.8 1.4 %collective-permute-start.9 = (f32[2,16,8,128]{3,2,1,0:T(8,128)S(1)}, f32[2,16,8,128]{3,2,1,0:T(8,128)S(1)}, u32[]{:S(2)}, u32[]{:S(2)}) collective-permute-start(f32[2,16,8,128]{3,2,1,0:T(8,128)S(1)} %get-tuple-element.20), channel_id=1, source_target_pairs={{0,8},{8,0},{16,24},{24,16},{1,9},{9,1},{17,25},{25,17},{2,10},{10... | collective-permute-start | bytes 393224 | tf_op jit(solution)/shard_map/ppermute | solution.py:611
  48.2 5.1 %copy-start = (f32[32,8,256]{2,1,0:T(8,128)S(1)}, f32[32,8,256]{2,1,0:T(8,128)}, u32[]{:S(2)}) copy-start(f32[32,8,256]{2,1,0:T(8,128)} %kappa_ref.1) | copy-start | bytes 786436
  48.2 5.1 %copy-start.1 = (f32[32,8,256]{2,1,0:T(8,128)S(1)}, f32[32,8,256]{2,1,0:T(8,128)}, u32[]{:S(2)}) copy-start(f32[32,8,256]{2,1,0:T(8,128)} %observed_ref.1) | copy-start | bytes 786436
  48.3 6.0 %collective-permute-start.10 = (f32[16,8,128]{2,1,0:T(8,128)S(1)}, f32[16,8,128]{2,1,0:T(8,128)S(1)}, u32[]{:S(2)}, u32[]{:S(2)}) collective-permute-start(f32[16,8,128]{2,1,0:T(8,128)S(1)} %get-tuple-element.24), channel_id=1, source_target_pairs={{0,0},{1,16},{8,8},{9,24},{16,1},{17,17},{24,9},{25,25},{2,2},{3,1... | collective-permute-start | bytes 196616 | tf_op jit(solution)/shard_map/ppermute | solution.py:625
  49.1 6.7 %collective-permute-start.11 = (f32[16,8,128]{2,1,0:T(8,128)S(1)}, f32[16,8,128]{2,1,0:T(8,128)S(1)}, u32[]{:S(2)}, u32[]{:S(2)}) collective-permute-start(f32[16,8,128]{2,1,0:T(8,128)S(1)} %get-tuple-element.23), channel_id=1, source_target_pairs={{0,1},{1,17},{8,9},{9,25},{16,0},{17,16},{24,8},{25,24},{2,3},{3,1... | collective-permute-start | bytes 196616 | tf_op jit(solution)/shard_map/ppermute | solution.py:626

commit v5 on v4

--- a/solution.py
+++ b/solution.py
@@ -82,6 +82,7 @@
     bits_hbm,
     kappa_hbm,
     observed_hbm,
+    own_ref,
     even_ref,
     odd_ref,
     cross_ref,
@@ -100,34 +101,45 @@
         copy.start()
     level = lax.axis_index("level")
     first = level == 0
+    in_first_core = lax.rem(lax.axis_index("probe"), 2) == 0
     per_tile = LANES // EDGE
     tiles = depth // per_tile
+    field = depth + tiles
     slot_ids = (lane_ids((ROWS, LANES)) % (LANES // 2)) // (EDGE // 2)
     same_columns, cross_columns = columns_of(level), columns_of(1 - level)
-    for which in range(2):
-        base = which * (depth + tiles)
-        copies[which].wait()
-        for refs, chosen in (((even_ref, odd_ref), same_columns), ((cross_ref,), cross_columns)):
-            if which == 0:
-                values = (2 * bits_ref[...] - 1).astype(jnp.float32).reshape(depth * ROWS, 2 * LANES)
-                picked = jnp.dot(
-                    values.astype(jnp.bfloat16), chosen, preferred_element_type=jnp.float32
-                )
-            else:
-                picked = pick(kappa_ref[...].reshape(depth * ROWS, 2 * LANES), chosen)
-            picked = picked.reshape(depth, ROWS, 2 * LANES)
+
+    def blocks(picked):
+        picked = picked.reshape(depth, ROWS, 2 * LANES)
+        edges = []
+        for tile in range(tiles):
+            packed = picked[tile * per_tile, :, LANES:]
+            for slot in range(1, per_tile):
+                packed = jnp.where(slot_ids == slot, picked[tile * per_tile + slot, :, LANES:], packed)
+            edges.append(packed)
+        return [picked[z, :, :LANES] for z in range(depth)], edges
+
+    def write(refs, base, values):
+        for place, value in enumerate(values):
             for ref in refs:
-                ref[base : base + depth] = picked[:, :, :LANES]
-            for tile in range(tiles):
-                packed = picked[tile * per_tile, :, LANES:]
-                for slot in range(1, per_tile):
-                    packed = jnp.where(
-                        slot_ids == slot, picked[tile * per_tile + slot, :, LANES:], packed
-                    )
-                for ref in refs:
-                    ref[base + depth + tile] = packed
+                ref[base + place] = value
+
+    copies[0].wait()
+    signs = (2 * bits_ref[...] - 1).astype(jnp.float32).reshape(depth * ROWS, 2 * LANES)
+    signs = signs.astype(jnp.bfloat16)
+    for refs, chosen in (((own_ref, even_ref, odd_ref), same_columns), ((cross_ref,), cross_columns)):
+        main, edges = blocks(jnp.dot(signs, chosen, preferred_element_type=jnp.float32))
+        write(refs, 0, main + edges)
+    copies[1].wait()
+    kappa = kappa_ref[...].reshape(depth * ROWS, 2 * LANES)
+    for refs, chosen in (((even_ref, odd_ref), same_columns), ((cross_ref,), cross_columns)):
+        main, edges = blocks(pick(kappa, chosen))
+        if len(refs) == 2:
+            write((own_ref,), field, main + edges)
+        low = main[: depth // 2] + edges[: tiles // 2]
+        high = main[depth // 2 :] + edges[tiles // 2 :]
+        write(refs, field, [jnp.where(in_first_core, a, b) for a, b in zip(low, high)])
     copies[2].wait()
-    base = 2 * (depth + tiles)
+    base = field + field // 2
     in_low = lax.axis_index("probe") < lax.axis_size("probe") // 2
 
     def half(value):
@@ -152,116 +164,205 @@
     return (pltpu.roll(values, 1, 0) + pltpu.roll(values, rows - 1, 0)) + y_sides
 
 
+def inside_mask():
+    shape = (3 * ROWS, 2 * LANES)
+    tile = lax.axis_index("tile")
+    half = LANES // 2
+    lanes, ids = lane_ids(shape) % LANES, row_ids(shape)
+    near = jnp.where(lax.axis_index("level") == 0, half, LANES - EDGE // 2)
+    inside = (lanes < half) | ((lanes >= near) & (lanes < near + EDGE // 2))
+    inside = inside & (ids >= jnp.where(tile > 0, 0, ROWS))
+    inside = inside & (ids < jnp.where(tile < lax.axis_size("tile") - 1, 3 * ROWS, 2 * ROWS))
+    return jnp.where(inside, 1.0, 0.0)
+
+
+def join(z, even, own, odd):
+    half, short = LANES // 2, EDGE // 2
+    level = lax.axis_index("level")
+    from_even = lax.rem(lax.axis_index("tile"), 2) == 1
+    mine = lane_ids((ROWS, LANES)) < half
+    shift = half + (half - short) * level - short * lax.rem(z, LANES // EDGE)
+    shift = lax.rem(shift + LANES, LANES)
+    left = [jnp.where(from_even, a, b) for a, b in zip(even, odd)]
+    right = [jnp.where(from_even, b, a) for a, b in zip(even, odd)]
+    evens, odds = [], []
+    for main, edge in (left, own, right):
+        edge = pltpu.roll(edge, shift, 1)
+        evens.append(jnp.where(mine, main, edge))
+        odds.append(pltpu.roll(jnp.where(mine, edge, main), half, 1))
+    return jnp.concatenate([jnp.concatenate(evens, axis=0), jnp.concatenate(odds, axis=0)], axis=1)
+
+
+def unpack(depth, signs, half_diag, mask, sign_pieces, kappa_pieces):
+    level = lax.axis_index("level")
+    per_tile = LANES // EDGE
+
+    def place(z):
+        return jnp.where(level == 0, z, depth - 1 - z)
+
+    def sign_level(z, unused):
+        pieces = [(ref[z], ref[depth + z // per_tile]) for ref in sign_pieces]
+        signs[place(z) + 1] = join(z, *pieces) * mask
+        return unused
+
+    lax.fori_loop(0, depth, sign_level, 0, unroll=per_tile)
+    core = lax.rem(lax.axis_index("probe"), 2)
+    for start, pieces in zip((core, 1 - core), kappa_pieces):
+        start = start * (depth // 2)
+
+        def kappa_level(step, unused, start=start, pieces=pieces):
+            z = start + step
+            tiles = []
+            for ref, base, whole_field in pieces:
+                if whole_field:
+                    tiles.append((ref[base + z], ref[base + depth + z // per_tile]))
+                else:
+                    tiles.append((ref[base + step], ref[base + depth // 2 + step // per_tile]))
+            half_diag[place(z)] = 0.5 * join(z, *tiles) + (2.0 + VERTICAL)
+            return unused
+
+        lax.fori_loop(0, depth // 2, kappa_level, 0, unroll=per_tile)
+
+
+OWN_ROWS = slice(ROWS, 2 * ROWS)
+
+
+def near_kernel(
+    depth,
+    own_ref,
+    even_ref,
+    odd_ref,
+    swapped_ref,
+    half_diag,
+    lower,
+    forward,
+    own_signs,
+    k_signs,
+    signs,
+):
+    field = own_ref.shape[0] // 2
+    mask = inside_mask()
+    zero = jnp.zeros(mask.shape, jnp.float32)
+    signs[0] = zero
+    signs[depth + 1] = zero
+    kappa_pieces = (
+        ((even_ref, field, False), (own_ref, field, True), (odd_ref, field, False)),
+        ((swapped_ref, 0, False), (own_ref, field, True), (swapped_ref, field // 2, False)),
+    )
+    unpack(depth, signs, half_diag, mask, (even_ref, own_ref, odd_ref), kappa_pieces)
+
+    def down(k, carry):
+        ratio, value = carry
+        ratio = mask / (half_diag[k] - ratio)
+        here = signs[k + 1]
+        value = ratio * (here + value)
+        lower[k] = ratio
+        forward[k] = value
+        image = half_diag[k] * here - (signs[k] + signs[k + 2]) - 0.5 * beside(here)
+        own_signs[k] = here[OWN_ROWS]
+        k_signs[k] = image[OWN_ROWS]
+        return ratio, value
+
+    lax.fori_loop(0, depth, down, (zero, zero), unroll=GROUP)
+
+
 def basis_kernel(
     depth,
-    own_ref,
+    near_diag,
+    near_lower,
+    near_forward,
+    near_signs,
     own_far_ref,
-    even_ref,
     even_far_ref,
-    odd_ref,
     odd_far_ref,
-    terms_ref,
+    swapped_ref,
+    swapped_far_ref,
+    basis_ref,
+    image_ref,
+    far_signs,
+    far_k_signs,
     gram_ref,
     signs,
-    half_diag,
-    lower,
+    far_diag,
+    far_lower,
     upper,
     basis,
     forward,
     sides,
     backward,
-    k_signs,
-    k_basis,
     sums,
 ):
     levels = 2 * depth
-    rows, columns = 3 * ROWS, 2 * LANES
-    shape = (rows, columns)
-    level = lax.axis_index("level")
-    tile = lax.axis_index("tile")
-    last_tile = lax.axis_size("tile") - 1
-    per_tile = LANES // EDGE
-    tiles = depth // per_tile
-    lanes, ids = lane_ids(shape), row_ids(shape)
-    half = LANES // 2
-    lanes = lanes % LANES
-    near = jnp.where(level == 0, half, LANES - EDGE // 2)
-    inside = (lanes < half) | ((lanes >= near) & (lanes < near + EDGE // 2))
-    inside = inside & (ids >= jnp.where(tile > 0, 0, ROWS))
-    inside = inside & (ids < jnp.where(tile < last_tile, 3 * ROWS, 2 * ROWS))
-    mask = jnp.where(inside, 1.0, 0.0)
+    mask = inside_mask()
     half_mask = 0.5 * mask
-    zero = jnp.zeros(shape, jnp.float32)
-    own = (slice(ROWS, 2 * ROWS), slice(0, 2 * LANES))
-    mine = lane_ids((ROWS, LANES)) < half
+    zero = jnp.zeros(mask.shape, jnp.float32)
     own_zero = jnp.zeros((ROWS, LANES), jnp.float32)
-
+    mine = lane_ids((ROWS, LANES)) < LANES // 2
+    field = swapped_ref.shape[0] // 3 * 2
     signs[0] = zero
-    signs[levels + 1] = zero
+    signs[0, OWN_ROWS] = near_signs[depth - 1]
+    signs[depth + 1] = zero
     backward[levels] = zero
     upper[levels] = zero
     basis[levels] = zero
-    from_even = lax.rem(tile, 2) == 1
-    for far, pieces in enumerate(
-        ((even_ref, own_ref, odd_ref), (even_far_ref, own_far_ref, odd_far_ref))
-    ):
-        start = depth * (level if far == 0 else 1 - level)
-
-        def unpack(z, unused, pieces=pieces, start=start):
-            group = z // per_tile
-            shift = half + (half - EDGE // 2) * level - (EDGE // 2) * lax.rem(z, per_tile)
-            shift = lax.rem(shift + LANES, LANES)
-
-            def gather(base):
-                evens, odds = [], []
-                first, second, third = [
-                    (piece[base + z], piece[base + depth + group]) for piece in pieces
-                ]
-                left = [jnp.where(from_even, a, b) for a, b in zip(first, third)]
-                right = [jnp.where(from_even, b, a) for a, b in zip(first, third)]
-                for main, edge in (left, second, right):
-                    edge = pltpu.roll(edge, shift, 1)
-                    evens.append(jnp.where(mine, main, edge))
-                    odds.append(pltpu.roll(jnp.where(mine, edge, main), half, 1))
-                return jnp.concatenate(
-                    [jnp.concatenate(evens, axis=0), jnp.concatenate(odds, axis=0)], axis=1
-                )
-
-            signs[start + z + 1] = gather(0) * mask
-            half_diag[start + z] = 0.5 * gather(depth + tiles) + (2.0 + VERTICAL)
-            return unused
-
-        lax.fori_loop(0, depth, unpack, 0, unroll=per_tile)
+    kappa_pieces = (
+        tuple((ref, field, False) for ref in (even_far_ref, own_far_ref, odd_far_ref)),
+        (
+            (swapped_far_ref, 0, False),
+            (swapped_ref, field, False),
+            (swapped_far_ref, field // 2, False),
+        ),
+    )
+    unpack(depth, signs, far_diag, mask, (even_far_ref, own_far_ref, odd_far_ref), kappa_pieces)
 
     def start_down(k, carry):
         ratio, value, from_end = carry
-        ratio = mask / (half_diag[k] - ratio)
+        ratio = mask / (far_diag[k] - ratio)
         here = signs[k + 1]
         value = ratio * (here + value)
-        lower[k] = ratio
-        forward[k] = value
-        other = levels - 1 - k
-        from_end = mask / (half_diag[other] - from_end)
-        upper[other] = from_end
-        image = half_diag[k] * here - (signs[k] + signs[k + 2]) - 0.5 * beside(here)
-        k_signs[k] = image[own]
+        far_lower[k] = ratio
+        forward[depth + k] = value
+        other = depth - 1 - k
+        from_end = mask / (far_diag[other] - from_end)
+        upper[depth + other] = from_end
+        image = far_diag[k] * here - (signs[k] + signs[k + 2]) - 0.5 * beside(here)
+        far_signs[k] = here[OWN_ROWS]
+        far_k_signs[k] = image[OWN_ROWS]
         return ratio, value, from_end
 
-    lax.fori_loop(0, levels, start_down, (zero, zero, zero), unroll=GROUP)
-
-    def start_up(step, carry):
-        k = levels - 1 - step
+    start = (near_lower[depth - 1], near_forward[depth - 1], zero)
+    carry = lax.fori_loop(0, depth, start_down, start, unroll=GROUP)
+
+    def start_up_far(step, carry):
+        k = depth - 1 - step
         solved, value = carry
-        solved = forward[k] + lower[k] * solved
-        value = upper[k] * (solved + value)
+        solved = forward[depth + k] + far_lower[k] * solved
+        value = upper[depth + k] * (solved + value)
+        backward[depth + k] = value
+        return solved, value
+
+    solved, value = lax.fori_loop(0, depth, start_up_far, (zero, zero), unroll=GROUP)
+
+    def start_up_near(step, carry):
+        k = depth - 1 - step
+        ratio, solved, value = carry
+        ratio = mask / (near_diag[k] - ratio)
+        solved = near_forward[k] + near_lower[k] * solved
+        value = ratio * (solved + value)
+        upper[k] = ratio
         backward[k] = value
-        return solved, value
-
-    lax.fori_loop(0, levels, start_up, (zero, zero), unroll=GROUP)
-
+        return ratio, solved, value
+
+    lax.fori_loop(0, depth, start_up_near, (carry[2], solved, value), unroll=GROUP)
+
+    parts = (
+        (0, near_diag, near_lower, lambda k: near_signs[k]),
+        (depth, far_diag, far_lower, lambda k: signs[k + 1, OWN_ROWS]),
+    )
     place = 0
     for index in range(ITERS):
         final = index + 1 == ITERS
+        group_size = 2 * GROUP if final else GROUP
 
         def next_basis(k, previous, index=index):
             solved = backward[k] + upper[k] * previous
@@ -273,51 +374,45 @@
                 value = SHIFTS[index - 1] * basis[k] - solved
             return solved, value
 
-        def down(group, carry, index=index, final=final, next_basis=next_basis):
-            solved, above, here, value, *totals = carry
-            products = []
-            for step in range(GROUP):
-                k = group * GROUP + step
-                solved, below = next_basis(k + 1, solved)
-                if not final:
-                    basis[k + 1] = below
-                side = beside(here)
-                image = half_diag[k] * here - (above + below) - half_mask * side
-                if not final:
-                    value = lower[k] * (beside(image) + value)
-                    forward[k] = value
-                    sides[k] = side
-                my_sign, my_basis, my_image = signs[k + 1][own], here[own], image[own]
-                term = my_basis * k_signs[k] + my_image * my_sign
-                terms_ref[index, k] = jnp.where(
-                    mine, term[:, :LANES], pltpu.roll(term[:, LANES:], half, 1)
-                )
-                if not final:
-                    k_basis[index, k] = my_image
-                factors = [(k_basis[other, k], my_image) for other in range(index)]
-                factors += [(my_image, my_image), (my_basis, my_sign)]
-                products.append(
-                    [a[:, :LANES] * b[:, :LANES] + a[:, LANES:] * b[:, LANES:] for a, b in factors]
-                )
-                above, here = here, below
-            for slot in range(index + 2):
-                for four in range(0, GROUP, 4):
-                    added = (products[four][slot] + products[four + 1][slot]) + (
-                        products[four + 2][slot] + products[four + 3][slot]
-                    )
-                    totals[2 * slot], rest = two_sum(totals[2 * slot], added)
-                    totals[2 * slot + 1] = totals[2 * slot + 1] + rest
-            return (solved, above, here, value, *totals)
-
         solved, here = next_basis(0, zero)
         if not final:
             basis[0] = here
-        carry = lax.fori_loop(
-            0,
-            levels // GROUP,
-            down,
-            (solved, zero, here, zero) + (own_zero,) * (2 * (index + 2)),
-        )
+        carry = (solved, zero, here, zero) + (own_zero,) * (2 * (index + 2))
+        for offset, half_diag, lower, sign_of in parts:
+
+            def down(group, carry):
+                solved, above, here, value, *totals = carry
+                products = []
+                for step in range(group_size):
+                    k = group * group_size + step
+                    solved, below = next_basis(offset + k + 1, solved)
+                    if not final:
+                        basis[offset + k + 1] = below
+                    side = beside(here)
+                    image = half_diag[k] * here - (above + below) - half_mask * side
+                    if not final:
+                        value = lower[k] * (beside(image) + value)
+                        forward[offset + k] = value
+                        sides[offset + k] = side
+                    my_basis, my_image = here[OWN_ROWS], image[OWN_ROWS]
+                    basis_ref[index, offset + k] = my_basis
+                    image_ref[index, offset + k] = my_image
+                    factors = [(image_ref[other, offset + k], my_image) for other in range(index)]
+                    factors += [(my_image, my_image), (my_basis, sign_of(k))]
+                    products.append(
+                        [a[:, :LANES] * b[:, :LANES] + a[:, LANES:] * b[:, LANES:] for a, b in factors]
+                    )
+                    above, here = here, below
+                for slot in range(index + 2):
+                    for four in range(0, group_size, 4):
+                        added = (products[four][slot] + products[four + 1][slot]) + (
+                            products[four + 2][slot] + products[four + 3][slot]
+                        )
+                        totals[2 * slot], rest = two_sum(totals[2 * slot], added)
+                        totals[2 * slot + 1] = totals[2 * slot + 1] + rest
+                return (solved, above, here, value, *totals)
+
+            carry = lax.fori_loop(0, depth // group_size, down, carry)
         totals = [jnp.where(mine, total, 0.0) for total in carry[4:]]
         for slot in range(index + 1):
             sums[2 * (place + slot)] = totals[2 * slot]
@@ -327,16 +422,18 @@
         sums[2 * (len(PAIRS) + index) + 1] = totals[2 * index + 3]
         if final:
             break
-
-        def up(step, carry):
-            k = levels - 1 - step
-            solved, value = carry
-            solved = forward[k] + lower[k] * solved
-            value = upper[k] * ((sides[k] + solved) + value)
-            backward[k] = value
-            return solved, value
-
-        lax.fori_loop(0, levels, up, (zero, zero), unroll=GROUP)
+        carry = (zero, zero)
+        for offset, half_diag, lower, sign_of in reversed(parts):
+
+            def up(step, carry):
+                k = depth - 1 - step
+                solved, value = carry
+                solved = forward[offset + k] + lower[k] * solved
+                value = upper[offset + k] * ((sides[offset + k] + solved) + value)
+                backward[offset + k] = value
+                return solved, value
+
+            carry = lax.fori_loop(0, depth, up, carry, unroll=GROUP)
 
     ids = row_ids((ROWS, LANES))
     for block in range(SLOTS // ROWS):
@@ -358,6 +455,38 @@
     high, rest = two_sum(high, middle)
     gram_ref[:SLOTS] = high
     gram_ref[SLOTS:] = rest + (low + lane_sum(gram_ref[SLOTS:].astype(jnp.bfloat16)))
+
+
+def terms_kernel(
+    depth, basis_ref, image_ref, near_signs, near_k_signs, far_signs, far_k_signs, terms_ref
+):
+    level = lax.axis_index("level")
+    half = LANES // 2
+    mine = lane_ids((ROWS, LANES)) < half
+    for offset, signs, k_signs in ((0, near_signs, near_k_signs), (depth, far_signs, far_k_signs)):
+
+        def step(k, unused, offset=offset, signs=signs, k_signs=k_signs):
+            z = offset + k
+            target = jnp.where(level == 0, z, 2 * depth - 1 - z)
+            sign, image = signs[k], k_signs[k]
+            for index in range(ITERS):
+                term = basis_ref[index, z] * image + image_ref[index, z] * sign
+                terms_ref[index, target] = jnp.where(
+                    mine, term[:, :LANES], pltpu.roll(term[:, LANES:], half, 1)
+                )
+            return unused
+
+        if offset == 0:
+            lax.fori_loop(0, depth - 1, step, 0, unroll=GROUP)
+            sign, image = signs[depth - 1], k_signs[depth - 1] - far_signs[0]
+            target = jnp.where(level == 0, depth - 1, depth)
+            for index in range(ITERS):
+                term = basis_ref[index, depth - 1] * image + image_ref[index, depth - 1] * sign
+                terms_ref[index, target] = jnp.where(
+                    mine, term[:, :LANES], pltpu.roll(term[:, LANES:], half, 1)
+                )
+        else:
+            lax.fori_loop(0, depth, step, 0, unroll=GROUP)
 
 
 def solve_small(high, low):
@@ -509,19 +638,21 @@
     probes, tile_count = lax.axis_size("probe"), lax.axis_size("tile")
     unused, depth, rows, columns = probe_bits.shape
     assert probe_bits.shape[0] == 1 and lax.axis_size("level") == 2 and probes == 4
-    assert rows == ROWS and columns == 2 * LANES and depth % (LANES // EDGE) == 0
+    assert rows == ROWS and columns == 2 * LANES and depth % (2 * LANES // EDGE) == 0
     params = pltpu.CompilerParams(vmem_limit_bytes=48 * 1024 * 1024)
     f32 = jnp.float32
     tiles = depth * EDGE // LANES
-    field = 2 * (depth + tiles)
-    near_shape = jax.ShapeDtypeStruct((field + depth // ROWS, ROWS, LANES), f32)
-    far_shape = jax.ShapeDtypeStruct((field + 1, ROWS, LANES), f32)
-
-    even_block, odd_block, cross_block = pl.pallas_call(
+    field = depth + tiles
+    sent = field + field // 2
+    own_shape = jax.ShapeDtypeStruct((2 * field, ROWS, LANES), f32)
+    near_shape = jax.ShapeDtypeStruct((sent + depth // ROWS, ROWS, LANES), f32)
+    far_shape = jax.ShapeDtypeStruct((sent + 1, ROWS, LANES), f32)
+
+    own_block, even_block, odd_block, cross_block = pl.pallas_call(
         functools.partial(pack_kernel, depth),
-        out_shape=(near_shape, near_shape, far_shape),
+        out_shape=(own_shape, near_shape, near_shape, far_shape),
         in_specs=[pl.BlockSpec(memory_space=pltpu.HBM)] * 3,
-        out_specs=tuple(whole(3)),
+        out_specs=tuple(whole(4)),
         scratch_shapes=[
             pltpu.VMEM((depth, rows, columns), jnp.int32),
             pltpu.VMEM((depth, rows, columns), f32),
@@ -562,33 +693,72 @@
         name="observed",
     )(kappa_sq, observed, even, odd, own_far)
 
+    def core_swap(*pieces):
+        kappa = jnp.concatenate([piece[field:sent] for piece in pieces], axis=0)
+        return lax.ppermute(kappa, "probe", swaps([(0, 1), (2, 3)]))
+
+    swapped = core_swap(even, odd, own_far)
     levels = 2 * depth
+    part = jax.ShapeDtypeStruct((depth, 3 * ROWS, 2 * LANES), f32)
+    own_part = jax.ShapeDtypeStruct((depth, ROWS, 2 * LANES), f32)
+    near_diag, near_lower, near_forward, near_signs, near_k_signs = pl.pallas_call(
+        functools.partial(near_kernel, depth),
+        out_shape=(part, part, part, own_part, own_part),
+        in_specs=whole(4),
+        out_specs=tuple(whole(5)),
+        scratch_shapes=[pltpu.VMEM((depth + 2, 3 * ROWS, 2 * LANES), f32)],
+        compiler_params=params,
+        name="near",
+    )(own_block, even, odd, swapped)
+
+    swapped_far = core_swap(even_far, odd_far)
     padded = pltpu.VMEM((levels + 1, 3 * ROWS, 2 * LANES), f32)
     plain = pltpu.VMEM((levels, 3 * ROWS, 2 * LANES), f32)
-    terms, gram = pl.pallas_call(
+    short = pltpu.VMEM((depth, 3 * ROWS, 2 * LANES), f32)
+    fields = jax.ShapeDtypeStruct((ITERS, levels, ROWS, 2 * LANES), f32)
+    basis, images, far_signs, far_k_signs, gram = pl.pallas_call(
         functools.partial(basis_kernel, depth),
         out_shape=(
-            jax.ShapeDtypeStruct((ITERS, levels, ROWS, LANES), f32),
+            fields,
+            fields,
+            own_part,
+            own_part,
             jax.ShapeDtypeStruct((2 * SLOTS, LANES), f32),
         ),
-        in_specs=whole(6),
-        out_specs=tuple(whole(2)),
+        in_specs=whole(9),
+        out_specs=tuple(whole(5)),
         scratch_shapes=[
-            pltpu.VMEM((levels + 2, 3 * ROWS, 2 * LANES), f32),
-            plain,
-            plain,
+            pltpu.VMEM((depth + 2, 3 * ROWS, 2 * LANES), f32),
+            short,
+            short,
             padded,
             padded,
             plain,
             plain,
             padded,
-            pltpu.VMEM((levels, ROWS, 2 * LANES), f32),
-            pltpu.VMEM((ITERS - 1, levels, ROWS, 2 * LANES), f32),
             pltpu.VMEM((2 * SLOTS, ROWS, LANES), f32),
         ],
         compiler_params=params,
         name="basis",
-    )(even_block, own_far, even, even_far, odd, odd_far)
+    )(
+        near_diag,
+        near_lower,
+        near_forward,
+        near_signs,
+        own_far,
+        even_far,
+        odd_far,
+        swapped,
+        swapped_far,
+    )
+    terms = pl.pallas_call(
+        functools.partial(terms_kernel, depth),
+        out_shape=jax.ShapeDtypeStruct((ITERS, levels, ROWS, LANES), f32),
+        in_specs=whole(6),
+        out_specs=pl.BlockSpec(memory_space=pltpu.VMEM),
+        compiler_params=params,
+        name="terms",
+    )(basis, images, near_signs, near_k_signs, far_signs, far_k_signs)
 
     both = jnp.concatenate([gram, lax.ppermute(gram, "level", [(0, 1), (1, 0)])], axis=0)
     if tile_count in (2, 4):

time: 56.9 us -> 53.8 us (0.946)
  the two profiles are of different devices: /device:TPU:0 before, /device:TPU:28 now
where the time goes in v5:
time: 53.8 us; the launch traced here: 53.6 us
  Pallas kernels  20 us (37%)
  waiting for transfers between devices  15.9 us (30%)
  starting transfers between devices  15.7 us (29%)
  local copies, waits for them, and re-layouts  1.65 us (3%)
    pallas_call x1, Pallas kernels, body(): pl.pallas_call(functools.partial(basis_kernel, depth), out_shape=(fields,...  11.3 us
    ppermute x1, waiting for transfers between devices, body(): lax.ppermute(cross_block, ('tile', 'level'), swaps([(2 * a + level, 2 * b...  5.29 us
    ppermute x3, starting transfers between devices, body(): lax.ppermute(both, 'tile', [(i, i ^ k) for i in range(tile_count)])  4.39 us
    ppermute x1, starting transfers between devices, body(): lax.ppermute(cross_block, ('tile', 'level'), swaps([(2 * a + level, 2 * b...  3.84 us
    ppermute x1, waiting for transfers between devices, body(): trace_a = lax.ppermute(straight, ('probe', 'level'), routes(False))  3.67 us
    ppermute x1, waiting for transfers between devices, body(): lax.ppermute(gram, 'level', [(0, 1), (1, 0)])  3.22 us
    pallas_call x1, Pallas kernels, body(): pl.pallas_call(functools.partial(terms_kernel, depth), out_shape=jax.Shap...  2.93 us
    ppermute x1, starting transfers between devices, body(): trace_a = lax.ppermute(straight, ('probe', 'level'), routes(False))  2.37 us
  transfers between devices with their start and end apart: 14, of which 6 were waited for; matrix products, arithmetic and copies ran while one was open for 0% of the time, Pallas kernels for 10%

profile of v5, /device:TPU:28, one launch (start us, length us, event | category | flops | bytes accessed | tf_op | source)
XLA Modules:
  0.0 53.6 jit_solution(13510150660937469652)
XLA Ops:
  0.0 1.6 %pack.1 = (f32[68,8,128]{2,1,0:T(8,128)S(1)}, f32[55,8,128]{2,1,0:T(8,128)S(1)}, f32[55,8,128]{2,1,0:T(8,128)S(1)}, f32[52,8,128]{2,1,0:T(8,128)S(1)}) custom-call(s32[32,8,256]{2,1,0:T(8,128)} %bitcast.5, f32[32,8,256]{2,1,0:T(8,128)} %kappa_ref.1, f32[32,8,256]{2,1,0:T(8,128)} %observed_ref.1), custom_call_target="tpu_custom_call" | custom-call | tf_op jit(solution)/shard_map/pack/pallas_call | solution.py:651
  1.6 0.6 %collective-permute-start.2 = (f32[52,8,128]{2,1,0:T(8,128)S(1)}, f32[52,8,128]{2,1,0:T(8,128)S(1)}, u32[]{:S(2)}, u32[]{:S(2)}) collective-permute-start(f32[52,8,128]{2,1,0:T(8,128)S(1)} %get-tuple-element.26), channel_id=1, source_target_pairs={{0,1},{1,0},{2,3},{3,2},{4,5},{5,4},{6,7},{7,6},{8,9},{9,8},{10,11... | collective-permute-start | bytes 638984 | tf_op jit(solution)/shard_map/ppermute | solution.py:676
  2.2 0.5 collective-permute-start
  2.7 0.7 %collective-permute-start.1 = (f32[55,8,128]{2,1,0:T(8,128)S(1)}, f32[55,8,128]{2,1,0:T(8,128)S(1)}, u32[]{:S(2)}, u32[]{:S(2)}) collective-permute-start(f32[55,8,128]{2,1,0:T(8,128)S(1)} %get-tuple-element.25), channel_id=1, source_target_pairs={{2,4},{4,2},{3,5},{5,3},{10,12},{12,10},{11,13},{13,11},{18,20},{2... | collective-permute-start | bytes 675848 | tf_op jit(solution)/shard_map/ppermute | solution.py:678
  3.3 3.8 %collective-permute-start.4 = (f32[52,8,128]{2,1,0:T(8,128)S(1)}, f32[52,8,128]{2,1,0:T(8,128)S(1)}, u32[]{:S(2)}, u32[]{:S(2)}) collective-permute-start(f32[52,8,128]{2,1,0:T(8,128)S(1)} %get-tuple-element.26), channel_id=1, source_target_pairs={{0,3},{3,0},{1,2},{2,1},{4,7},{7,4},{5,6},{6,5},{8,11},{11,8},{9,1... | collective-permute-start | bytes 638984 | tf_op jit(solution)/shard_map/ppermute | solution.py:680
  7.2 1.5 %collective-permute-done.2.own_far_ref.far_ref = f32[52,8,128]{2,1,0:T(8,128)S(1)} collective-permute-done((f32[52,8,128]{2,1,0:T(8,128)S(1)}, f32[52,8,128]{2,1,0:T(8,128)S(1)}, u32[]{:S(2)}, u32[]{:S(2)}) %collective-permute-start.2) | collective-permute-done | bytes 213024 | tf_op jit(solution)/shard_map/ppermute | solution.py:676
  8.7 0.7 %collective-permute-start.5 = (f32[52,8,128]{2,1,0:T(8,128)S(1)}, f32[52,8,128]{2,1,0:T(8,128)S(1)}, u32[]{:S(2)}, u32[]{:S(2)}) collective-permute-start(f32[52,8,128]{2,1,0:T(8,128)S(1)} %collective-permute-done.2.own_far_ref.far_ref), channel_id=1, source_target_pairs={{2,4},{4,2},{3,5},{5,3},{10,12},{12,10},{11,13},{13,11},{18,20},{2... | collective-permute-start | bytes 638984 | tf_op jit(solution)/shard_map/ppermute | solution.py:679
  9.4 5.3 %collective-permute-done.4.even_far_ref = f32[52,8,128]{2,1,0:T(8,128)S(1)} collective-permute-done((f32[52,8,128]{2,1,0:T(8,128)S(1)}, f32[52,8,128]{2,1,0:T(8,128)S(1)}, u32[]{:S(2)}, u32[]{:S(2)}) %collective-permute-start.4) | collective-permute-done | bytes 213024 | tf_op jit(solution)/shard_map/ppermute | solution.py:680
  14.7 0.0 collective-permute-done.even_ref
  14.7 0.0 collective-permute-done.1.odd_ref
  14.8 0.1 collective-permute-start.3
  14.8 0.0 collective-permute-done.5.odd_far_ref
  14.9 0.5 %collective-permute-start.6 = (f32[34,8,128]{2,1,0:T(8,128)S(1)}, f32[34,8,128]{2,1,0:T(8,128)S(1)}, u32[]{:S(2)}, u32[]{:S(2)}) collective-permute-start(f32[34,8,128]{2,1,0:T(8,128)S(1)} %pad_maximum_fusion.1), channel_id=1, source_target_pairs={{0,8},{8,0},{16,24},{24,16},{1,9},{9,1},{17,25},{25,17},{2,10},{10... | collective-permute-start | bytes 417800 | tf_op jit(solution)/shard_map/ppermute | solution.py:698
  15.4 0.9 %collective-permute-done.3.swapped_ref = f32[51,8,128]{2,1,0:T(8,128)S(1)} collective-permute-done((f32[51,8,128]{2,1,0:T(8,128)S(1)}, f32[51,8,128]{2,1,0:T(8,128)S(1)}, u32[]{:S(2)}, u32[]{:S(2)}) %collective-permute-start.3) | collective-permute-done | bytes 208928 | tf_op jit(solution)/shard_map/ppermute | solution.py:698
  16.3 1.3 %near.1 = (f32[32,24,256]{2,1,0:T(8,128)S(1)}, f32[32,24,256]{2,1,0:T(8,128)S(1)}, f32[32,24,256]{2,1,0:T(8,128)S(1)}, f32[32,8,256]{2,1,0:T(8,128)S(1)}, f32[32,8,256]{2,1,0:T(8,128)S(1)}) custom-call(f32[68,8,128]{2,1,0:T(8,128)S(1)} %get-tuple-element.23.own_ref, f32[55,8,128]{2,1,0:T(8,128)S(1)} %collective-permute-done.even_ref, ...), custom_call_target="tpu_custom_call" | custom-call | tf_op jit(solution)/shard_map/near/pallas_call | solution.py:704
  17.6 0.0 collective-permute-done.6.swapped_far_ref
  17.6 11.3 %basis.1 = (f32[4,64,8,256]{3,2,1,0:T(8,128)}, f32[4,64,8,256]{3,2,1,0:T(8,128)}, f32[32,8,256]{2,1,0:T(8,128)S(1)}, f32[32,8,256]{2,1,0:T(8,128)S(1)}, f32[32,128]{1,0:T(8,128)S(1)}) custom-call(f32[32,24,256]{2,1,0:T(8,128)S(1)} %get-tuple-element.27.near_diag, f32[32,24,256]{2,1,0:T(8,128)S(1)} %get-tuple-element.28.near_lower, ...), custom_call_target="tpu_custom_call" | custom-call | tf_op jit(solution)/shard_map/basis/pallas_call | solution.py:719
  29.0 0.5 collective-permute-start.7
  29.5 3.2 %collective-permute-done.7 = f32[32,128]{1,0:T(8,128)S(1)} collective-permute-done((f32[32,128]{1,0:T(8,128)S(1)}, f32[32,128]{1,0:T(8,128)S(1)}, u32[]{:S(2)}, u32[]{:S(2)}) %collective-permute-start.7) | collective-permute-done | bytes 16416 | tf_op jit(solution)/shard_map/ppermute | solution.py:763
  32.7 0.2 collective-permute-start.10
  33.0 2.4 %collective-permute-start.9 = (f32[64,128]{1,0:T(8,128)S(1)}, f32[64,128]{1,0:T(8,128)S(1)}, u32[]{:S(2)}, u32[]{:S(2)}) collective-permute-start(f32[64,128]{1,0:T(8,128)S(1)} %constant_dynamic-update-slice_fusion.refs_0_), channel_id=1, source_target_pairs={{0,4},{2,6},{4,0},{6,2},{1,5},{3,7},{5,1},{7,3},{8,12},{10,14},{12... | collective-permute-start | bytes 98312 | tf_op jit(solution)/shard_map/ppermute | solution.py:766
  35.4 1.7 %collective-permute-start.8 = (f32[64,128]{1,0:T(8,128)S(1)}, f32[64,128]{1,0:T(8,128)S(1)}, u32[]{:S(2)}, u32[]{:S(2)}) collective-permute-start(f32[64,128]{1,0:T(8,128)S(1)} %constant_dynamic-update-slice_fusion.refs_0_), channel_id=1, source_target_pairs={{0,2},{2,0},{4,6},{6,4},{1,3},{3,1},{5,7},{7,5},{8,10},{10,8},{12,... | collective-permute-start | bytes 98312 | tf_op jit(solution)/shard_map/ppermute | solution.py:766
  37.1 0.0 copy-start
  37.1 1.6 %copy-done = f32[4,64,8,256]{3,2,1,0:T(8,128)S(1)} copy-done((f32[4,64,8,256]{3,2,1,0:T(8,128)S(1)}, f32[4,64,8,256]{3,2,1,0:T(8,128)}, u32[]{:S(2)}) %copy-start) | copy-done | bytes 2097176
  38.7 0.0 copy-start.1
  38.7 0.0 copy-start.2
  38.7 2.9 %terms.1.terms_ref = f32[4,64,8,128]{3,2,1,0:T(8,128)S(1)} custom-call(f32[4,64,8,256]{3,2,1,0:T(8,128)S(1)} %copy-done, f32[4,64,8,256]{3,2,1,0:T(8,128)} %get-tuple-element.32.image_ref, f32[32,8,256]{2,1,0:T(8,128)S(1)} %get-tuple-element.30.near_signs, f32[32,8,256]{2,1,0:T(8,128)S(1)} %get-tuple-element.33.near_k_signs, ...), custom_call_target="tpu_custom_call" | custom-call | tf_op jit(solution)/shard_map/terms/pallas_call | solution.py:754
  41.7 0.0 collective-permute-done.10.refs_3_
  41.7 0.0 collective-permute-done.9.refs_2_
  41.7 0.0 collective-permute-done.8.refs_1_
  41.7 0.9 %combine.1 = (f32[2,16,8,128]{3,2,1,0:T(8,128)S(1)}, f32[2,16,8,128]{3,2,1,0:T(8,128)S(1)}) custom-call(f32[4,64,8,128]{3,2,1,0:T(8,128)S(1)} %terms.1.terms_ref, f32[64,128]{1,0:T(8,128)S(1)} %constant_dynamic-update-slice_fusion.refs_0_, f32[64,128]{1,0:T(8,128)S(1)} %collective-permute-done.8.refs_1_, f32[64,128]{1,0:T(8,128)S(1)} %collective-permute-done.9.refs_2_, ...), custom_call_target="tpu_custom_call" | custom-call | tf_op jit(solution)/shard_map/combine/pallas_call | solution.py:772
  42.6 0.1 collective-permute-start.11
  42.7 1.3 %collective-permute-done.11 = f32[2,16,8,128]{3,2,1,0:T(8,128)S(1)} collective-permute-done((f32[2,16,8,128]{3,2,1,0:T(8,128)S(1)}, f32[2,16,8,128]{3,2,1,0:T(8,128)S(1)}, u32[]{:S(2)}, u32[]{:S(2)}) %collective-permute-start.11) | collective-permute-done | bytes 131104 | tf_op jit(solution)/shard_map/ppermute | solution.py:781
  44.1 1.6 %collective-permute-start.13 = (f32[16,8,128]{2,1,0:T(8,128)S(1)}, f32[16,8,128]{2,1,0:T(8,128)S(1)}, u32[]{:S(2)}, u32[]{:S(2)}) collective-permute-start(f32[16,8,128]{2,1,0:T(8,128)S(1)} %get-tuple-element.41), channel_id=1, source_target_pairs={{0,1},{1,17},{8,9},{9,25},{16,0},{17,16},{24,8},{25,24},{2,3},{3,1... | collective-permute-start | bytes 196616 | tf_op jit(solution)/shard_map/ppermute | solution.py:796
  45.6 2.4 %collective-permute-start.12 = (f32[16,8,128]{2,1,0:T(8,128)S(1)}, f32[16,8,128]{2,1,0:T(8,128)S(1)}, u32[]{:S(2)}, u32[]{:S(2)}) collective-permute-start(f32[16,8,128]{2,1,0:T(8,128)S(1)} %get-tuple-element.42), channel_id=1, source_target_pairs={{0,0},{1,16},{8,8},{9,24},{16,1},{17,17},{24,9},{25,25},{2,2},{3,1... | collective-permute-start | bytes 196616 | tf_op jit(solution)/shard_map/ppermute | solution.py:795
  48.0 0.0 copy-done.1
  48.0 0.0 copy-done.2
  48.0 1.0 %observed.1 = (f32[32,8,64]{2,1,0:T(8,128)S(1)}, f32[32,8,64]{2,1,0:T(8,128)S(1)}) custom-call(f32[32,8,256]{2,1,0:T(8,128)S(1)} %copy-done.1, f32[32,8,256]{2,1,0:T(8,128)S(1)} %copy-done.2, f32[55,8,128]{2,1,0:T(8,128)S(1)} %collective-permute-done.even_ref, f32[55,8,128]{2,1,0:T(8,128)S(1)} %collective-permute-done.1.odd_ref, ...), custom_call_target="tpu_custom_call" | custom-call | tf_op jit(solution)/shard_map/observed/pallas_call | solution.py:687
  49.0 0.0 collective-permute-done.13.trace_b_ref
  49.0 3.7 %collective-permute-done.12.trace_a_ref = f32[16,8,128]{2,1,0:T(8,128)S(1)} collective-permute-done((f32[16,8,128]{2,1,0:T(8,128)S(1)}, f32[16,8,128]{2,1,0:T(8,128)S(1)}, u32[]{:S(2)}, u32[]{:S(2)}) %collective-permute-start.12) | collective-permute-done | bytes 65568 | tf_op jit(solution)/shard_map/ppermute | solution.py:795
  52.7 0.9 %gradient.1 = f32[32,8,64]{2,1,0:T(8,128)} custom-call(f32[16,8,128]{2,1,0:T(8,128)S(1)} %collective-permute-done.12.trace_a_ref, f32[16,8,128]{2,1,0:T(8,128)S(1)} %collective-permute-done.13.trace_b_ref, f32[32,8,64]{2,1,0:T(8,128)S(1)} %get-tuple-element.39.factor_ref, f32[32,8,64]{2,1,0:T(8,128)S(1)} %get-tuple-element.40.data_ref), custom_call_target="tpu_custom_call" | custom-call | tf_op jit(solution)/shard_map/gradient/pallas_call | solution.py:797
  (11 shorter events, 0.1 us)
Async XLA Ops:
  1.6 7.1 %collective-permute-start.2 = (f32[52,8,128]{2,1,0:T(8,128)S(1)}, f32[52,8,128]{2,1,0:T(8,128)S(1)}, u32[]{:S(2)}, u32[]{:S(2)}) collective-permute-start(f32[52,8,128]{2,1,0:T(8,128)S(1)} %get-tuple-element.26), channel_id=1, source_target_pairs={{0,1},{1,0},{2,3},{3,2},{4,5},{5,4},{6,7},{7,6},{8,9},{9,8},{10,11... | collective-permute-start | bytes 638984 | tf_op jit(solution)/shard_map/ppermute | solution.py:676
  2.2 12.5 %collective-permute-start = (f32[55,8,128]{2,1,0:T(8,128)S(1)}, f32[55,8,128]{2,1,0:T(8,128)S(1)}, u32[]{:S(2)}, u32[]{:S(2)}) collective-permute-start(f32[55,8,128]{2,1,0:T(8,128)S(1)} %get-tuple-element.24), channel_id=1, source_target_pairs={{0,2},{2,0},{4,6},{6,4},{1,3},{3,1},{5,7},{7,5},{8,10},{10,8},{12,... | collective-permute-start | bytes 675848 | tf_op jit(solution)/shard_map/ppermute | solution.py:677
  2.7 12.1 %collective-permute-start.1 = (f32[55,8,128]{2,1,0:T(8,128)S(1)}, f32[55,8,128]{2,1,0:T(8,128)S(1)}, u32[]{:S(2)}, u32[]{:S(2)}) collective-permute-start(f32[55,8,128]{2,1,0:T(8,128)S(1)} %get-tuple-element.25), channel_id=1, source_target_pairs={{2,4},{4,2},{3,5},{5,3},{10,12},{12,10},{11,13},{13,11},{18,20},{2... | collective-permute-start | bytes 675848 | tf_op jit(solution)/shard_map/ppermute | solution.py:678
  3.3 11.4 %collective-permute-start.4 = (f32[52,8,128]{2,1,0:T(8,128)S(1)}, f32[52,8,128]{2,1,0:T(8,128)S(1)}, u32[]{:S(2)}, u32[]{:S(2)}) collective-permute-start(f32[52,8,128]{2,1,0:T(8,128)S(1)} %get-tuple-element.26), channel_id=1, source_target_pairs={{0,3},{3,0},{1,2},{2,1},{4,7},{7,4},{5,6},{6,5},{8,11},{11,8},{9,1... | collective-permute-start | bytes 638984 | tf_op jit(solution)/shard_map/ppermute | solution.py:680
  8.7 6.1 %collective-permute-start.5 = (f32[52,8,128]{2,1,0:T(8,128)S(1)}, f32[52,8,128]{2,1,0:T(8,128)S(1)}, u32[]{:S(2)}, u32[]{:S(2)}) collective-permute-start(f32[52,8,128]{2,1,0:T(8,128)S(1)} %collective-permute-done.2.own_far_ref.far_ref), channel_id=1, source_target_pairs={{2,4},{4,2},{3,5},{5,3},{10,12},{12,10},{11,13},{13,11},{18,20},{2... | collective-permute-start | bytes 638984 | tf_op jit(solution)/shard_map/ppermute | solution.py:679
  14.8 1.5 %collective-permute-start.3 = (f32[51,8,128]{2,1,0:T(8,128)S(1)}, f32[51,8,128]{2,1,0:T(8,128)S(1)}, u32[]{:S(2)}, u32[]{:S(2)}) collective-permute-start(f32[51,8,128]{2,1,0:T(8,128)S(1)} %pad_maximum_fusion), channel_id=1, source_target_pairs={{0,8},{8,0},{16,24},{24,16},{1,9},{9,1},{17,25},{25,17},{2,10},{10... | collective-permute-start | bytes 626696 | tf_op jit(solution)/shard_map/ppermute | solution.py:698
  14.9 2.7 %collective-permute-start.6 = (f32[34,8,128]{2,1,0:T(8,128)S(1)}, f32[34,8,128]{2,1,0:T(8,128)S(1)}, u32[]{:S(2)}, u32[]{:S(2)}) collective-permute-start(f32[34,8,128]{2,1,0:T(8,128)S(1)} %pad_maximum_fusion.1), channel_id=1, source_target_pairs={{0,8},{8,0},{16,24},{24,16},{1,9},{9,1},{17,25},{25,17},{2,10},{10... | collective-permute-start | bytes 417800 | tf_op jit(solution)/shard_map/ppermute | solution.py:698
  29.0 3.7 %collective-permute-start.7 = (f32[32,128]{1,0:T(8,128)S(1)}, f32[32,128]{1,0:T(8,128)S(1)}, u32[]{:S(2)}, u32[]{:S(2)}) collective-permute-start(f32[32,128]{1,0:T(8,128)S(1)} %get-tuple-element.36), channel_id=1, source_target_pairs={{0,1},{1,0},{2,3},{3,2},{4,5},{5,4},{6,7},{7,6},{8,9},{9,8},{10,11... | collective-permute-start | bytes 49160 | tf_op jit(solution)/shard_map/ppermute | solution.py:763
  32.7 8.9 %collective-permute-start.10 = (f32[64,128]{1,0:T(8,128)S(1)}, f32[64,128]{1,0:T(8,128)S(1)}, u32[]{:S(2)}, u32[]{:S(2)}) collective-permute-start(f32[64,128]{1,0:T(8,128)S(1)} %constant_dynamic-update-slice_fusion.refs_0_), channel_id=1, source_target_pairs={{0,6},{2,4},{4,2},{6,0},{1,7},{3,5},{5,3},{7,1},{8,14},{10,12},{12... | collective-permute-start | bytes 98312 | tf_op jit(solution)/shard_map/ppermute | solution.py:766
  33.0 8.7 %collective-permute-start.9 = (f32[64,128]{1,0:T(8,128)S(1)}, f32[64,128]{1,0:T(8,128)S(1)}, u32[]{:S(2)}, u32[]{:S(2)}) collective-permute-start(f32[64,128]{1,0:T(8,128)S(1)} %constant_dynamic-update-slice_fusion.refs_0_), channel_id=1, source_target_pairs={{0,4},{2,6},{4,0},{6,2},{1,5},{3,7},{5,1},{7,3},{8,12},{10,14},{12... | collective-permute-start | bytes 98312 | tf_op jit(solution)/shard_map/ppermute | solution.py:766
  35.4 6.3 %collective-permute-start.8 = (f32[64,128]{1,0:T(8,128)S(1)}, f32[64,128]{1,0:T(8,128)S(1)}, u32[]{:S(2)}, u32[]{:S(2)}) collective-permute-start(f32[64,128]{1,0:T(8,128)S(1)} %constant_dynamic-update-slice_fusion.refs_0_), channel_id=1, source_target_pairs={{0,2},{2,0},{4,6},{6,4},{1,3},{3,1},{5,7},{7,5},{8,10},{10,8},{12,... | collective-permute-start | bytes 98312 | tf_op jit(solution)/shard_map/ppermute | solution.py:766
  37.1 1.6 %copy-start = (f32[4,64,8,256]{3,2,1,0:T(8,128)S(1)}, f32[4,64,8,256]{3,2,1,0:T(8,128)}, u32[]{:S(2)}) copy-start(f32[4,64,8,256]{3,2,1,0:T(8,128)} %get-tuple-element.31.basis_ref) | copy-start | bytes 6291460
  38.7 9.3 %copy-start.1 = (f32[32,8,256]{2,1,0:T(8,128)S(1)}, f32[32,8,256]{2,1,0:T(8,128)}, u32[]{:S(2)}) copy-start(f32[32,8,256]{2,1,0:T(8,128)} %kappa_ref.1) | copy-start | bytes 786436
  38.7 9.3 %copy-start.2 = (f32[32,8,256]{2,1,0:T(8,128)S(1)}, f32[32,8,256]{2,1,0:T(8,128)}, u32[]{:S(2)}) copy-start(f32[32,8,256]{2,1,0:T(8,128)} %observed_ref.1) | copy-start | bytes 786436
  42.6 1.4 %collective-permute-start.11 = (f32[2,16,8,128]{3,2,1,0:T(8,128)S(1)}, f32[2,16,8,128]{3,2,1,0:T(8,128)S(1)}, u32[]{:S(2)}, u32[]{:S(2)}) collective-permute-start(f32[2,16,8,128]{3,2,1,0:T(8,128)S(1)} %get-tuple-element.38), channel_id=1, source_target_pairs={{0,8},{8,0},{16,24},{24,16},{1,9},{9,1},{17,25},{25,17},{2,10},{10... | collective-permute-start | bytes 393224 | tf_op jit(solution)/shard_map/ppermute | solution.py:781
  44.1 4.9 %collective-permute-start.13 = (f32[16,8,128]{2,1,0:T(8,128)S(1)}, f32[16,8,128]{2,1,0:T(8,128)S(1)}, u32[]{:S(2)}, u32[]{:S(2)}) collective-permute-start(f32[16,8,128]{2,1,0:T(8,128)S(1)} %get-tuple-element.41), channel_id=1, source_target_pairs={{0,1},{1,17},{8,9},{9,25},{16,0},{17,16},{24,8},{25,24},{2,3},{3,1... | collective-permute-start | bytes 196616 | tf_op jit(solution)/shard_map/ppermute | solution.py:796
  45.6 7.0 %collective-permute-start.12 = (f32[16,8,128]{2,1,0:T(8,128)S(1)}, f32[16,8,128]{2,1,0:T(8,128)S(1)}, u32[]{:S(2)}, u32[]{:S(2)}) collective-permute-start(f32[16,8,128]{2,1,0:T(8,128)S(1)} %get-tuple-element.42), channel_id=1, source_target_pairs={{0,0},{1,16},{8,8},{9,24},{16,1},{17,17},{24,9},{25,25},{2,2},{3,1... | collective-permute-start | bytes 196616 | tf_op jit(solution)/shard_map/ppermute | solution.py:795

commit v6 on v5

--- a/solution.py
+++ b/solution.py
@@ -639,7 +639,7 @@
     unused, depth, rows, columns = probe_bits.shape
     assert probe_bits.shape[0] == 1 and lax.axis_size("level") == 2 and probes == 4
     assert rows == ROWS and columns == 2 * LANES and depth % (2 * LANES // EDGE) == 0
-    params = pltpu.CompilerParams(vmem_limit_bytes=48 * 1024 * 1024)
+    params = pltpu.CompilerParams(vmem_limit_bytes=24 * 1024 * 1024)
     f32 = jnp.float32
     tiles = depth * EDGE // LANES
     field = depth + tiles

time: 53.8 us -> 51.8 us (0.963)
  the two profiles are of different devices: /device:TPU:28 before, /device:TPU:4 now
where the time goes in v6:
time: 51.8 us; the launch traced here: 51.6 us
  starting transfers between devices  18.6 us (36%)
  Pallas kernels  16.9 us (33%)
  waiting for transfers between devices  15.8 us (31%)
    pallas_call x1, Pallas kernels, body(): pl.pallas_call(functools.partial(basis_kernel, depth), out_shape=(fields,...  9.75 us
    ppermute x1, starting transfers between devices, body(): lax.ppermute(cross_block, ('tile', 'level'), swaps([(2 * a + level, 2 * b...  5.41 us
    ppermute x3, starting transfers between devices, body(): lax.ppermute(both, 'tile', [(i, i ^ k) for i in range(tile_count)])  4.39 us
    ppermute x1, waiting for transfers between devices, body(): lax.ppermute(cross_block, ('tile', 'level'), swaps([(2 * a + level, 2 * b...  4.14 us
    ppermute x1, waiting for transfers between devices, body(): trace_a = lax.ppermute(straight, ('probe', 'level'), routes(False))  3.4 us
    ppermute x1, waiting for transfers between devices, body(): lax.ppermute(gram, 'level', [(0, 1), (1, 0)])  3.38 us
    ppermute x3, waiting for transfers between devices, body(): lax.ppermute(both, 'tile', [(i, i ^ k) for i in range(tile_count)])  2.73 us
    ppermute x1, starting transfers between devices, body(): trace_a = lax.ppermute(straight, ('probe', 'level'), routes(False))  2.64 us
  transfers between devices with their start and end apart: 14, of which 6 were waited for; matrix products, arithmetic and copies ran while one was open for 0% of the time, Pallas kernels for 7%

profile of v6, /device:TPU:4, one launch (start us, length us, event | category | flops | bytes accessed | tf_op | source)
XLA Modules:
  0.0 51.6 jit_solution(2017788394792219739)
XLA Ops:
  0.0 1.6 %pack.1 = (f32[68,8,128]{2,1,0:T(8,128)S(1)}, f32[55,8,128]{2,1,0:T(8,128)S(1)}, f32[55,8,128]{2,1,0:T(8,128)S(1)}, f32[52,8,128]{2,1,0:T(8,128)S(1)}) custom-call(s32[32,8,256]{2,1,0:T(8,128)} %bitcast.5, f32[32,8,256]{2,1,0:T(8,128)} %kappa_ref.1, f32[32,8,256]{2,1,0:T(8,128)} %observed_ref.1), custom_call_target="tpu_custom_call" | custom-call | tf_op jit(solution)/shard_map/pack/pallas_call | solution.py:651
  1.6 0.1 collective-permute-start.2
  1.7 2.1 %collective-permute-start = (f32[55,8,128]{2,1,0:T(8,128)S(1)}, f32[55,8,128]{2,1,0:T(8,128)S(1)}, u32[]{:S(2)}, u32[]{:S(2)}) collective-permute-start(f32[55,8,128]{2,1,0:T(8,128)S(1)} %get-tuple-element.24), channel_id=1, source_target_pairs={{0,2},{2,0},{4,6},{6,4},{1,3},{3,1},{5,7},{7,5},{8,10},{10,8},{12,... | collective-permute-start | bytes 675848 | tf_op jit(solution)/shard_map/ppermute | solution.py:677
  3.8 0.7 %collective-permute-start.1 = (f32[55,8,128]{2,1,0:T(8,128)S(1)}, f32[55,8,128]{2,1,0:T(8,128)S(1)}, u32[]{:S(2)}, u32[]{:S(2)}) collective-permute-start(f32[55,8,128]{2,1,0:T(8,128)S(1)} %get-tuple-element.25), channel_id=1, source_target_pairs={{2,4},{4,2},{3,5},{5,3},{10,12},{12,10},{11,13},{13,11},{18,20},{2... | collective-permute-start | bytes 675848 | tf_op jit(solution)/shard_map/ppermute | solution.py:678
  4.4 5.4 %collective-permute-start.4 = (f32[52,8,128]{2,1,0:T(8,128)S(1)}, f32[52,8,128]{2,1,0:T(8,128)S(1)}, u32[]{:S(2)}, u32[]{:S(2)}) collective-permute-start(f32[52,8,128]{2,1,0:T(8,128)S(1)} %get-tuple-element.26), channel_id=1, source_target_pairs={{0,3},{3,0},{1,2},{2,1},{4,7},{7,4},{5,6},{6,5},{8,11},{11,8},{9,1... | collective-permute-start | bytes 638984 | tf_op jit(solution)/shard_map/ppermute | solution.py:680
  9.9 0.0 collective-permute-done.2.own_far_ref.far_ref
  9.9 0.7 %collective-permute-start.5 = (f32[52,8,128]{2,1,0:T(8,128)S(1)}, f32[52,8,128]{2,1,0:T(8,128)S(1)}, u32[]{:S(2)}, u32[]{:S(2)}) collective-permute-start(f32[52,8,128]{2,1,0:T(8,128)S(1)} %collective-permute-done.2.own_far_ref.far_ref), channel_id=1, source_target_pairs={{2,4},{4,2},{3,5},{5,3},{10,12},{12,10},{11,13},{13,11},{18,20},{2... | collective-permute-start | bytes 638984 | tf_op jit(solution)/shard_map/ppermute | solution.py:679
  10.6 4.1 %collective-permute-done.4.even_far_ref = f32[52,8,128]{2,1,0:T(8,128)S(1)} collective-permute-done((f32[52,8,128]{2,1,0:T(8,128)S(1)}, f32[52,8,128]{2,1,0:T(8,128)S(1)}, u32[]{:S(2)}, u32[]{:S(2)}) %collective-permute-start.4) | collective-permute-done | bytes 213024 | tf_op jit(solution)/shard_map/ppermute | solution.py:680
  14.7 0.0 collective-permute-done.even_ref
  14.7 0.0 collective-permute-done.1.odd_ref
  14.8 0.1 collective-permute-start.3
  14.9 0.0 collective-permute-done.5.odd_far_ref
  14.9 0.5 %collective-permute-start.6 = (f32[34,8,128]{2,1,0:T(8,128)S(1)}, f32[34,8,128]{2,1,0:T(8,128)S(1)}, u32[]{:S(2)}, u32[]{:S(2)}) collective-permute-start(f32[34,8,128]{2,1,0:T(8,128)S(1)} %pad_maximum_fusion.1), channel_id=1, source_target_pairs={{0,8},{8,0},{16,24},{24,16},{1,9},{9,1},{17,25},{25,17},{2,10},{10... | collective-permute-start | bytes 417800 | tf_op jit(solution)/shard_map/ppermute | solution.py:698
  15.4 0.9 %collective-permute-done.3.swapped_ref = f32[51,8,128]{2,1,0:T(8,128)S(1)} collective-permute-done((f32[51,8,128]{2,1,0:T(8,128)S(1)}, f32[51,8,128]{2,1,0:T(8,128)S(1)}, u32[]{:S(2)}, u32[]{:S(2)}) %collective-permute-start.3) | collective-permute-done | bytes 208928 | tf_op jit(solution)/shard_map/ppermute | solution.py:698
  16.3 1.3 %near.1 = (f32[32,24,256]{2,1,0:T(8,128)S(1)}, f32[32,24,256]{2,1,0:T(8,128)S(1)}, f32[32,24,256]{2,1,0:T(8,128)S(1)}, f32[32,8,256]{2,1,0:T(8,128)S(1)}, f32[32,8,256]{2,1,0:T(8,128)S(1)}) custom-call(f32[68,8,128]{2,1,0:T(8,128)S(1)} %get-tuple-element.23.own_ref, f32[55,8,128]{2,1,0:T(8,128)S(1)} %collective-permute-done.even_ref, ...), custom_call_target="tpu_custom_call" | custom-call | tf_op jit(solution)/shard_map/near/pallas_call | solution.py:704
  17.6 0.0 collective-permute-done.6.swapped_far_ref
  17.7 9.8 %basis.1 = (f32[4,64,8,256]{3,2,1,0:T(8,128)S(1)}, f32[4,64,8,256]{3,2,1,0:T(8,128)S(1)}, f32[32,8,256]{2,1,0:T(8,128)S(1)}, f32[32,8,256]{2,1,0:T(8,128)S(1)}, f32[32,128]{1,0:T(8,128)S(1)}) custom-call(f32[32,24,256]{2,1,0:T(8,128)S(1)} %get-tuple-element.27.near_diag, f32[32,24,256]{2,1,0:T(8,128)S(1)} %get-tuple-element.28.near_lower, ...), custom_call_target="tpu_custom_call" | custom-call | tf_op jit(solution)/shard_map/basis/pallas_call | solution.py:719
  27.4 0.4 collective-permute-start.7
  27.8 3.4 %collective-permute-done.7 = f32[32,128]{1,0:T(8,128)S(1)} collective-permute-done((f32[32,128]{1,0:T(8,128)S(1)}, f32[32,128]{1,0:T(8,128)S(1)}, u32[]{:S(2)}, u32[]{:S(2)}) %collective-permute-start.7) | collective-permute-done | bytes 16416 | tf_op jit(solution)/shard_map/ppermute | solution.py:763
  31.2 3.6 %collective-permute-start.10 = (f32[64,128]{1,0:T(8,128)S(1)}, f32[64,128]{1,0:T(8,128)S(1)}, u32[]{:S(2)}, u32[]{:S(2)}) collective-permute-start(f32[64,128]{1,0:T(8,128)S(1)} %constant_dynamic-update-slice_fusion.refs_0_), channel_id=1, source_target_pairs={{0,6},{2,4},{4,2},{6,0},{1,7},{3,5},{5,3},{7,1},{8,14},{10,12},{12... | collective-permute-start | bytes 98312 | tf_op jit(solution)/shard_map/ppermute | solution.py:766
  34.8 0.0 collective-permute-start.9
  34.8 0.8 %collective-permute-start.8 = (f32[64,128]{1,0:T(8,128)S(1)}, f32[64,128]{1,0:T(8,128)S(1)}, u32[]{:S(2)}, u32[]{:S(2)}) collective-permute-start(f32[64,128]{1,0:T(8,128)S(1)} %constant_dynamic-update-slice_fusion.refs_0_), channel_id=1, source_target_pairs={{0,2},{2,0},{4,6},{6,4},{1,3},{3,1},{5,7},{7,5},{8,10},{10,8},{12,... | collective-permute-start | bytes 98312 | tf_op jit(solution)/shard_map/ppermute | solution.py:766
  35.6 0.0 copy-start
  35.6 0.0 copy-start.1
  35.6 1.4 %terms.1.terms_ref = f32[4,64,8,128]{3,2,1,0:T(8,128)S(1)} custom-call(f32[4,64,8,256]{3,2,1,0:T(8,128)S(1)} %get-tuple-element.31.basis_ref, f32[4,64,8,256]{3,2,1,0:T(8,128)S(1)} %get-tuple-element.32.image_ref, f32[32,8,256]{2,1,0:T(8,128)S(1)} %get-tuple-element.30.near_signs, f32[32,8,256]{2,1,0:T(8,128)S(1)} %get-tuple-element.33.near_k_signs, ...), custom_call_target="tpu_custom_call" | custom-call | tf_op jit(solution)/shard_map/terms/pallas_call | solution.py:754
  37.0 0.0 collective-permute-done.10.refs_3_
  37.0 2.7 %collective-permute-done.9.refs_2_ = f32[64,128]{1,0:T(8,128)S(1)} collective-permute-done((f32[64,128]{1,0:T(8,128)S(1)}, f32[64,128]{1,0:T(8,128)S(1)}, u32[]{:S(2)}, u32[]{:S(2)}) %collective-permute-start.9) | collective-permute-done | bytes 32800 | tf_op jit(solution)/shard_map/ppermute | solution.py:766
  39.7 0.0 collective-permute-done.8.refs_1_
  39.7 0.9 %combine.1 = (f32[2,16,8,128]{3,2,1,0:T(8,128)S(1)}, f32[2,16,8,128]{3,2,1,0:T(8,128)S(1)}) custom-call(f32[4,64,8,128]{3,2,1,0:T(8,128)S(1)} %terms.1.terms_ref, f32[64,128]{1,0:T(8,128)S(1)} %constant_dynamic-update-slice_fusion.refs_0_, f32[64,128]{1,0:T(8,128)S(1)} %collective-permute-done.8.refs_1_, f32[64,128]{1,0:T(8,128)S(1)} %collective-permute-done.9.refs_2_, ...), custom_call_target="tpu_custom_call" | custom-call | tf_op jit(solution)/shard_map/combine/pallas_call | solution.py:772
  40.6 0.1 collective-permute-start.11
  40.7 1.3 %collective-permute-done.11 = f32[2,16,8,128]{3,2,1,0:T(8,128)S(1)} collective-permute-done((f32[2,16,8,128]{3,2,1,0:T(8,128)S(1)}, f32[2,16,8,128]{3,2,1,0:T(8,128)S(1)}, u32[]{:S(2)}, u32[]{:S(2)}) %collective-permute-start.11) | collective-permute-done | bytes 131104 | tf_op jit(solution)/shard_map/ppermute | solution.py:781
  42.1 1.5 %collective-permute-start.13 = (f32[16,8,128]{2,1,0:T(8,128)S(1)}, f32[16,8,128]{2,1,0:T(8,128)S(1)}, u32[]{:S(2)}, u32[]{:S(2)}) collective-permute-start(f32[16,8,128]{2,1,0:T(8,128)S(1)} %get-tuple-element.41), channel_id=1, source_target_pairs={{0,1},{1,17},{8,9},{9,25},{16,0},{17,16},{24,8},{25,24},{2,3},{3,1... | collective-permute-start | bytes 196616 | tf_op jit(solution)/shard_map/ppermute | solution.py:796
  43.6 2.6 %collective-permute-start.12 = (f32[16,8,128]{2,1,0:T(8,128)S(1)}, f32[16,8,128]{2,1,0:T(8,128)S(1)}, u32[]{:S(2)}, u32[]{:S(2)}) collective-permute-start(f32[16,8,128]{2,1,0:T(8,128)S(1)} %get-tuple-element.42), channel_id=1, source_target_pairs={{0,0},{1,16},{8,8},{9,24},{16,1},{17,17},{24,9},{25,25},{2,2},{3,1... | collective-permute-start | bytes 196616 | tf_op jit(solution)/shard_map/ppermute | solution.py:795
  46.3 0.0 copy-done
  46.3 0.0 copy-done.1
  46.3 1.0 %observed.1 = (f32[32,8,64]{2,1,0:T(8,128)S(1)}, f32[32,8,64]{2,1,0:T(8,128)S(1)}) custom-call(f32[32,8,256]{2,1,0:T(8,128)S(1)} %copy-done, f32[32,8,256]{2,1,0:T(8,128)S(1)} %copy-done.1, f32[55,8,128]{2,1,0:T(8,128)S(1)} %collective-permute-done.even_ref, f32[55,8,128]{2,1,0:T(8,128)S(1)} %collective-permute-done.1.odd_ref, ...), custom_call_target="tpu_custom_call" | custom-call | tf_op jit(solution)/shard_map/observed/pallas_call | solution.py:687
  47.3 0.0 collective-permute-done.13.trace_b_ref
  47.3 3.4 %collective-permute-done.12.trace_a_ref = f32[16,8,128]{2,1,0:T(8,128)S(1)} collective-permute-done((f32[16,8,128]{2,1,0:T(8,128)S(1)}, f32[16,8,128]{2,1,0:T(8,128)S(1)}, u32[]{:S(2)}, u32[]{:S(2)}) %collective-permute-start.12) | collective-permute-done | bytes 65568 | tf_op jit(solution)/shard_map/ppermute | solution.py:795
  50.7 0.9 %gradient.1 = f32[32,8,64]{2,1,0:T(8,128)} custom-call(f32[16,8,128]{2,1,0:T(8,128)S(1)} %collective-permute-done.12.trace_a_ref, f32[16,8,128]{2,1,0:T(8,128)S(1)} %collective-permute-done.13.trace_b_ref, f32[32,8,64]{2,1,0:T(8,128)S(1)} %get-tuple-element.39.factor_ref, f32[32,8,64]{2,1,0:T(8,128)S(1)} %get-tuple-element.40.data_ref), custom_call_target="tpu_custom_call" | custom-call | tf_op jit(solution)/shard_map/gradient/pallas_call | solution.py:797
  (11 shorter events, 0.1 us)
Async XLA Ops:
  1.6 8.2 %collective-permute-start.2 = (f32[52,8,128]{2,1,0:T(8,128)S(1)}, f32[52,8,128]{2,1,0:T(8,128)S(1)}, u32[]{:S(2)}, u32[]{:S(2)}) collective-permute-start(f32[52,8,128]{2,1,0:T(8,128)S(1)} %get-tuple-element.26), channel_id=1, source_target_pairs={{0,1},{1,0},{2,3},{3,2},{4,5},{5,4},{6,7},{7,6},{8,9},{9,8},{10,11... | collective-permute-start | bytes 638984 | tf_op jit(solution)/shard_map/ppermute | solution.py:676
  1.7 13.0 %collective-permute-start = (f32[55,8,128]{2,1,0:T(8,128)S(1)}, f32[55,8,128]{2,1,0:T(8,128)S(1)}, u32[]{:S(2)}, u32[]{:S(2)}) collective-permute-start(f32[55,8,128]{2,1,0:T(8,128)S(1)} %get-tuple-element.24), channel_id=1, source_target_pairs={{0,2},{2,0},{4,6},{6,4},{1,3},{3,1},{5,7},{7,5},{8,10},{10,8},{12,... | collective-permute-start | bytes 675848 | tf_op jit(solution)/shard_map/ppermute | solution.py:677
  3.8 10.9 %collective-permute-start.1 = (f32[55,8,128]{2,1,0:T(8,128)S(1)}, f32[55,8,128]{2,1,0:T(8,128)S(1)}, u32[]{:S(2)}, u32[]{:S(2)}) collective-permute-start(f32[55,8,128]{2,1,0:T(8,128)S(1)} %get-tuple-element.25), channel_id=1, source_target_pairs={{2,4},{4,2},{3,5},{5,3},{10,12},{12,10},{11,13},{13,11},{18,20},{2... | collective-permute-start | bytes 675848 | tf_op jit(solution)/shard_map/ppermute | solution.py:678
  4.4 10.2 %collective-permute-start.4 = (f32[52,8,128]{2,1,0:T(8,128)S(1)}, f32[52,8,128]{2,1,0:T(8,128)S(1)}, u32[]{:S(2)}, u32[]{:S(2)}) collective-permute-start(f32[52,8,128]{2,1,0:T(8,128)S(1)} %get-tuple-element.26), channel_id=1, source_target_pairs={{0,3},{3,0},{1,2},{2,1},{4,7},{7,4},{5,6},{6,5},{8,11},{11,8},{9,1... | collective-permute-start | bytes 638984 | tf_op jit(solution)/shard_map/ppermute | solution.py:680
  9.9 5.0 %collective-permute-start.5 = (f32[52,8,128]{2,1,0:T(8,128)S(1)}, f32[52,8,128]{2,1,0:T(8,128)S(1)}, u32[]{:S(2)}, u32[]{:S(2)}) collective-permute-start(f32[52,8,128]{2,1,0:T(8,128)S(1)} %collective-permute-done.2.own_far_ref.far_ref), channel_id=1, source_target_pairs={{2,4},{4,2},{3,5},{5,3},{10,12},{12,10},{11,13},{13,11},{18,20},{2... | collective-permute-start | bytes 638984 | tf_op jit(solution)/shard_map/ppermute | solution.py:679
  14.8 1.5 %collective-permute-start.3 = (f32[51,8,128]{2,1,0:T(8,128)S(1)}, f32[51,8,128]{2,1,0:T(8,128)S(1)}, u32[]{:S(2)}, u32[]{:S(2)}) collective-permute-start(f32[51,8,128]{2,1,0:T(8,128)S(1)} %pad_maximum_fusion), channel_id=1, source_target_pairs={{0,8},{8,0},{16,24},{24,16},{1,9},{9,1},{17,25},{25,17},{2,10},{10... | collective-permute-start | bytes 626696 | tf_op jit(solution)/shard_map/ppermute | solution.py:698
  14.9 2.7 %collective-permute-start.6 = (f32[34,8,128]{2,1,0:T(8,128)S(1)}, f32[34,8,128]{2,1,0:T(8,128)S(1)}, u32[]{:S(2)}, u32[]{:S(2)}) collective-permute-start(f32[34,8,128]{2,1,0:T(8,128)S(1)} %pad_maximum_fusion.1), channel_id=1, source_target_pairs={{0,8},{8,0},{16,24},{24,16},{1,9},{9,1},{17,25},{25,17},{2,10},{10... | collective-permute-start | bytes 417800 | tf_op jit(solution)/shard_map/ppermute | solution.py:698
  27.4 3.8 %collective-permute-start.7 = (f32[32,128]{1,0:T(8,128)S(1)}, f32[32,128]{1,0:T(8,128)S(1)}, u32[]{:S(2)}, u32[]{:S(2)}) collective-permute-start(f32[32,128]{1,0:T(8,128)S(1)} %get-tuple-element.36), channel_id=1, source_target_pairs={{0,1},{1,0},{2,3},{3,2},{4,5},{5,4},{6,7},{7,6},{8,9},{9,8},{10,11... | collective-permute-start | bytes 49160 | tf_op jit(solution)/shard_map/ppermute | solution.py:763
  31.2 5.8 %collective-permute-start.10 = (f32[64,128]{1,0:T(8,128)S(1)}, f32[64,128]{1,0:T(8,128)S(1)}, u32[]{:S(2)}, u32[]{:S(2)}) collective-permute-start(f32[64,128]{1,0:T(8,128)S(1)} %constant_dynamic-update-slice_fusion.refs_0_), channel_id=1, source_target_pairs={{0,6},{2,4},{4,2},{6,0},{1,7},{3,5},{5,3},{7,1},{8,14},{10,12},{12... | collective-permute-start | bytes 98312 | tf_op jit(solution)/shard_map/ppermute | solution.py:766
  34.8 4.9 %collective-permute-start.9 = (f32[64,128]{1,0:T(8,128)S(1)}, f32[64,128]{1,0:T(8,128)S(1)}, u32[]{:S(2)}, u32[]{:S(2)}) collective-permute-start(f32[64,128]{1,0:T(8,128)S(1)} %constant_dynamic-update-slice_fusion.refs_0_), channel_id=1, source_target_pairs={{0,4},{2,6},{4,0},{6,2},{1,5},{3,7},{5,1},{7,3},{8,12},{10,14},{12... | collective-permute-start | bytes 98312 | tf_op jit(solution)/shard_map/ppermute | solution.py:766
  34.8 4.9 %collective-permute-start.8 = (f32[64,128]{1,0:T(8,128)S(1)}, f32[64,128]{1,0:T(8,128)S(1)}, u32[]{:S(2)}, u32[]{:S(2)}) collective-permute-start(f32[64,128]{1,0:T(8,128)S(1)} %constant_dynamic-update-slice_fusion.refs_0_), channel_id=1, source_target_pairs={{0,2},{2,0},{4,6},{6,4},{1,3},{3,1},{5,7},{7,5},{8,10},{10,8},{12,... | collective-permute-start | bytes 98312 | tf_op jit(solution)/shard_map/ppermute | solution.py:766
  35.6 10.7 %copy-start = (f32[32,8,256]{2,1,0:T(8,128)S(1)}, f32[32,8,256]{2,1,0:T(8,128)}, u32[]{:S(2)}) copy-start(f32[32,8,256]{2,1,0:T(8,128)} %kappa_ref.1) | copy-start | bytes 786436
  35.6 10.7 %copy-start.1 = (f32[32,8,256]{2,1,0:T(8,128)S(1)}, f32[32,8,256]{2,1,0:T(8,128)}, u32[]{:S(2)}) copy-start(f32[32,8,256]{2,1,0:T(8,128)} %observed_ref.1) | copy-start | bytes 786436
  40.6 1.4 %collective-permute-start.11 = (f32[2,16,8,128]{3,2,1,0:T(8,128)S(1)}, f32[2,16,8,128]{3,2,1,0:T(8,128)S(1)}, u32[]{:S(2)}, u32[]{:S(2)}) collective-permute-start(f32[2,16,8,128]{3,2,1,0:T(8,128)S(1)} %get-tuple-element.38), channel_id=1, source_target_pairs={{0,8},{8,0},{16,24},{24,16},{1,9},{9,1},{17,25},{25,17},{2,10},{10... | collective-permute-start | bytes 393224 | tf_op jit(solution)/shard_map/ppermute | solution.py:781
  42.1 5.2 %collective-permute-start.13 = (f32[16,8,128]{2,1,0:T(8,128)S(1)}, f32[16,8,128]{2,1,0:T(8,128)S(1)}, u32[]{:S(2)}, u32[]{:S(2)}) collective-permute-start(f32[16,8,128]{2,1,0:T(8,128)S(1)} %get-tuple-element.41), channel_id=1, source_target_pairs={{0,1},{1,17},{8,9},{9,25},{16,0},{17,16},{24,8},{25,24},{2,3},{3,1... | collective-permute-start | bytes 196616 | tf_op jit(solution)/shard_map/ppermute | solution.py:796
  43.6 7.0 %collective-permute-start.12 = (f32[16,8,128]{2,1,0:T(8,128)S(1)}, f32[16,8,128]{2,1,0:T(8,128)S(1)}, u32[]{:S(2)}, u32[]{:S(2)}) collective-permute-start(f32[16,8,128]{2,1,0:T(8,128)S(1)} %get-tuple-element.42), channel_id=1, source_target_pairs={{0,0},{1,16},{8,8},{9,24},{16,1},{17,17},{24,9},{25,25},{2,2},{3,1... | collective-permute-start | bytes 196616 | tf_op jit(solution)/shard_map/ppermute | solution.py:795

commit v7 on v6

--- a/solution.py
+++ b/solution.py
@@ -65,6 +65,10 @@
         jnp.dot(part, chosen, preferred_element_type=jnp.float32) for part in split_three(values)
     )
     return high + (middle + low)
+
+
+def y_half():
+    return lax.rem(lax.axis_index("level") + lax.axis_index("probe") // 2, 2)
 
 
 def columns_of(half):
@@ -106,7 +110,7 @@
     tiles = depth // per_tile
     field = depth + tiles
     slot_ids = (lane_ids((ROWS, LANES)) % (LANES // 2)) // (EDGE // 2)
-    same_columns, cross_columns = columns_of(level), columns_of(1 - level)
+    same_columns, cross_columns = columns_of(y_half()), columns_of(1 - y_half())
 
     def blocks(picked):
         picked = picked.reshape(depth, ROWS, 2 * LANES)
@@ -169,7 +173,7 @@
     tile = lax.axis_index("tile")
     half = LANES // 2
     lanes, ids = lane_ids(shape) % LANES, row_ids(shape)
-    near = jnp.where(lax.axis_index("level") == 0, half, LANES - EDGE // 2)
+    near = jnp.where(y_half() == 0, half, LANES - EDGE // 2)
     inside = (lanes < half) | ((lanes >= near) & (lanes < near + EDGE // 2))
     inside = inside & (ids >= jnp.where(tile > 0, 0, ROWS))
     inside = inside & (ids < jnp.where(tile < lax.axis_size("tile") - 1, 3 * ROWS, 2 * ROWS))
@@ -178,10 +182,9 @@
 
 def join(z, even, own, odd):
     half, short = LANES // 2, EDGE // 2
-    level = lax.axis_index("level")
     from_even = lax.rem(lax.axis_index("tile"), 2) == 1
     mine = lane_ids((ROWS, LANES)) < half
-    shift = half + (half - short) * level - short * lax.rem(z, LANES // EDGE)
+    shift = half + (half - short) * y_half() - short * lax.rem(z, LANES // EDGE)
     shift = lax.rem(shift + LANES, LANES)
     left = [jnp.where(from_even, a, b) for a, b in zip(even, odd)]
     right = [jnp.where(from_even, b, a) for a, b in zip(even, odd)]
@@ -433,9 +436,10 @@
                 backward[offset + k] = value
                 return solved, value
 
-            carry = lax.fori_loop(0, depth, up, carry, unroll=GROUP)
+            carry = lax.fori_loop(0, depth, up, carry, unroll=4 * GROUP)
 
     ids = row_ids((ROWS, LANES))
+    sides_of = [[], []]
     for block in range(SLOTS // ROWS):
         high, low = own_zero, own_zero
         for slot in range(block * ROWS, min((block + 1) * ROWS, COUNT)):
@@ -444,17 +448,22 @@
                 pair = pair_add(pair, tuple(pltpu.roll(part, shift, 0) for part in pair))
             here = ids == slot - block * ROWS
             high, low = jnp.where(here, pair[0], high), jnp.where(here, pair[1], low)
-        gram_ref[block * ROWS : (block + 1) * ROWS] = high
-        gram_ref[SLOTS + block * ROWS : SLOTS + (block + 1) * ROWS] = low
+        sides_of[0].append(high)
+        sides_of[1].append(low)
     ones = jnp.ones((LANES, LANES), jnp.bfloat16)
 
     def lane_sum(part):
         return jnp.dot(part, ones, preferred_element_type=jnp.float32)
 
-    high, middle, low = (lane_sum(part) for part in split_three(gram_ref[:SLOTS]))
-    high, rest = two_sum(high, middle)
-    gram_ref[:SLOTS] = high
-    gram_ref[SLOTS:] = rest + (low + lane_sum(gram_ref[SLOTS:].astype(jnp.bfloat16)))
+    high, low = (jnp.concatenate(blocks, axis=0) for blocks in sides_of)
+    first, second, third = (lane_sum(part) for part in split_three(high))
+    high, rest = two_sum(first, second)
+    low = rest + (third + lane_sum(low.astype(jnp.bfloat16)))
+    quarter = lane_ids((ROWS, LANES)) // (LANES // 4)
+    tile = high[:ROWS]
+    for place, block in enumerate((high[ROWS:], low[:ROWS], low[ROWS:])):
+        tile = jnp.where(quarter == place + 1, block, tile)
+    gram_ref[...] = tile
 
 
 def terms_kernel(
@@ -535,36 +544,46 @@
 
 def combine_kernel(depth, terms_ref, *refs):
     gram_refs, (keep_ref, send_ref) = refs[:-2], refs[-2:]
+    half, width = LANES // 2, LANES // 4
     pairs = []
     for ref in gram_refs:
-        for start in range(0, ref.shape[0], 2 * SLOTS):
-            pairs.append((ref[start : start + SLOTS], ref[start + SLOTS : start + 2 * SLOTS]))
+        for start in range(0, ref.shape[0], ROWS):
+            tile = ref[start : start + ROWS]
+            pairs.append((tile, pltpu.roll(tile, half, 1)))
     while len(pairs) > 1:
         merged = [pair_add(pairs[i], pairs[i + 1]) for i in range(0, len(pairs) - 1, 2)]
         pairs = merged + pairs[2 * len(merged) :]
-    found = solve_small(*pairs[0])
+    lanes = lane_ids((ROWS, LANES))
+
+    def spread(part, block):
+        part = jnp.where(lanes // width == block, part, 0.0)
+        part = part + pltpu.roll(part, width, 1)
+        return part + pltpu.roll(part, half, 1)
+
+    found = solve_small(
+        *(jnp.concatenate([spread(part, 0), spread(part, 1)], axis=0) for part in pairs[0])
+    )
     core = lax.rem(lax.axis_index("probe"), 2)
-    width = LANES // 4
-    first_lanes = lane_ids((ROWS, LANES)) % (2 * width) < width
+    first_lanes = lanes % half < width
     pairs_deep = depth // 2
 
     def step(z, unused):
-        for half in range(2):
+        for which in range(2):
             def total(k):
                 value = found[0] * terms_ref[0, k]
                 for j in range(1, ITERS):
                     value = value + found[j] * terms_ref[j, k]
                 return value
 
-            one = total(half * depth + z)
-            two = total(half * depth + pairs_deep + z)
+            one = total(which * depth + z)
+            two = total(which * depth + pairs_deep + z)
             low = jnp.where(first_lanes, one, pltpu.roll(two, width, 1))
             high = jnp.where(first_lanes, pltpu.roll(one, LANES - width, 1), two)
-            keep_ref[half, z] = jnp.where(core == 0, low, high)
-            send_ref[half, z] = jnp.where(core == 0, high, low)
+            keep_ref[which, z] = jnp.where(core == 0, low, high)
+            send_ref[which, z] = jnp.where(core == 0, high, low)
         return unused
 
-    lax.fori_loop(0, pairs_deep, step, 0, unroll=2)
+    lax.fori_loop(0, pairs_deep, step, 0, unroll=GROUP)
 
 
 def observed_kernel(
@@ -586,9 +605,10 @@
         return jnp.where(in_low, value[..., :LANES], value[..., LANES:])
 
     def take(value):
-        return jnp.where(even, value, pltpu.roll(value, width, 1))[:, :width]
+        return jnp.where(even, value, pltpu.roll(value, width, 1))
 
     far_edge = far_ref[far_ref.shape[0] - 1]
+    factors, parts = [], []
     for z in range(depth):
         value = observed_ref[z]
         mine = half(value)
@@ -611,23 +631,29 @@
             - half(y_sides)
             - VERTICAL * (above + below)
         )
-        factor_ref[z] = take(kappa * (0.5 / probes))
-        data_ref[z] = take(kappa * (2.0 * mine * k_observed))
-
-
-def gradient_kernel(depth, trace_a_ref, trace_b_ref, factor_ref, data_ref, out_ref):
+        factors.append(take(kappa * (0.5 / probes)))
+        parts.append(take(kappa * (2.0 * mine * k_observed)))
+    first_lanes = lane_ids((ROWS, LANES)) < width
+    for ref, values in ((factor_ref, factors), (data_ref, parts)):
+        for z in range(depth // 2):
+            ref[z] = jnp.where(first_lanes, values[z], pltpu.roll(values[depth // 2 + z], width, 1))
+
+
+def gradient_kernel(
+    depth, trace_a_ref, trace_b_ref, straight_ref, factor_ref, data_ref, out_ref
+):
     width = LANES // 2
     square = (LANES, LANES)
     lane = lane_ids(square)
     source = (width // 2) * (lane // width) + (lane % width) // 2 + width * (lane % 2)
     chosen = jnp.where(row_ids(square) == source, 1.0, 0.0).astype(jnp.bfloat16)
-    traces = pick((trace_a_ref[...] + trace_b_ref[...]).reshape(-1, LANES), chosen)
-    traces = traces.reshape(depth // 2, ROWS, LANES)
+    stays = lax.axis_index("level") == 0
+    traces = trace_a_ref[...] + jnp.where(stays, straight_ref[...], trace_b_ref[...])
+    traces = pick(traces.reshape(-1, LANES), chosen).reshape(traces.shape)
+    values = factor_ref[...] * traces - data_ref[...]
     for z in range(depth // 2):
-        out_ref[z] = factor_ref[z] * traces[z, :, :width] - data_ref[z]
-        later = depth // 2 + z
-        second = pltpu.roll(traces[z], width, 1)[:, :width]
-        out_ref[later] = factor_ref[later] * second - data_ref[later]
+        out_ref[z] = values[z, :, :width]
+        out_ref[depth // 2 + z] = pltpu.roll(values[z], width, 1)[:, :width]
 
 
 def whole(count):
@@ -684,9 +710,10 @@
     )
 
     quarter = jax.ShapeDtypeStruct((depth, ROWS, columns // probes), f32)
+    paired = jax.ShapeDtypeStruct((depth // 2, ROWS, LANES), f32)
     factor, data = pl.pallas_call(
         functools.partial(observed_kernel, depth, probes),
-        out_shape=(quarter, quarter),
+        out_shape=(paired, paired),
         in_specs=whole(5),
         out_specs=tuple(whole(2)),
         compiler_params=params,
@@ -723,7 +750,7 @@
             fields,
             own_part,
             own_part,
-            jax.ShapeDtypeStruct((2 * SLOTS, LANES), f32),
+            jax.ShapeDtypeStruct((ROWS, LANES), f32),
         ),
         in_specs=whole(9),
         out_specs=tuple(whole(5)),
@@ -760,14 +787,20 @@
         name="terms",
     )(basis, images, near_signs, near_k_signs, far_signs, far_k_signs)
 
-    both = jnp.concatenate([gram, lax.ppermute(gram, "level", [(0, 1), (1, 0)])], axis=0)
     if tile_count in (2, 4):
-        partials = [both] + [
-            lax.ppermute(both, "tile", [(i, i ^ k) for i in range(tile_count)])
-            for k in range(1, tile_count)
+        group = [gram] + [
+            lax.ppermute(
+                gram,
+                ("tile", "level"),
+                swaps([(i, i ^ k) for i in range(2 * tile_count) if i < i ^ k]),
+            )
+            for k in (1, 2, 3)
         ]
+        partials = [jnp.concatenate(group, axis=0)]
+        if tile_count == 4:
+            partials.append(lax.ppermute(partials[0], "tile", swaps([(0, 2), (1, 3)])))
     else:
-        partials = [lax.all_gather(both, "tile", axis=0, tiled=True)]
+        partials = [lax.all_gather(gram, ("tile", "level"), axis=0, tiled=True)]
     piece = jax.ShapeDtypeStruct((2, depth // 2, ROWS, LANES), f32)
     keep, send = pl.pallas_call(
         functools.partial(combine_kernel, depth),
@@ -778,30 +811,34 @@
         name="combine",
     )(terms, *partials)
 
-    summed = keep + lax.ppermute(send, "probe", [(0, 1), (1, 0), (2, 3), (3, 2)])
-    half = lax.axis_index("probe") // 2
-    straight = lax.dynamic_index_in_dim(summed, half, 0, keepdims=False)
-    turned = lax.dynamic_index_in_dim(summed, 1 - half, 0, keepdims=False)
-
-    def routes(flip):
-        pairs = []
-        for x in range(2):
-            for core in range(2):
-                for level in range(2):
-                    target = x if not flip else 1 - x
-                    pairs.append(((2 * x + core) * 2 + level, (2 * level + core) * 2 + target))
-        return pairs
-
-    trace_a = lax.ppermute(straight, ("probe", "level"), routes(False))
-    trace_b = lax.ppermute(turned, ("probe", "level"), routes(True))
+    summed = keep + lax.ppermute(send, "probe", swaps([(0, 1), (2, 3)]))
+    level = lax.axis_index("level")
+    turned = lax.dynamic_index_in_dim(summed, 1 - level, 0, keepdims=False)
+    straight = lax.dynamic_index_in_dim(summed, level, 0, keepdims=False)
+
+    def device(x, core, level):
+        return (2 * x + core) * 2 + level
+
+    chips = [(x, core) for x in range(2) for core in range(2)]
+    trace_a = lax.ppermute(
+        turned,
+        ("probe", "level"),
+        [(device(x, core, 0), device(x, core, 1)) for x, core in chips]
+        + [(device(x, core, 1), device(1 - x, core, 0)) for x, core in chips],
+    )
+    trace_b = lax.ppermute(
+        straight,
+        ("probe", "level"),
+        [(device(x, core, 1), device(1 - x, core, 1)) for x, core in chips],
+    )
     return pl.pallas_call(
         functools.partial(gradient_kernel, depth),
         out_shape=quarter,
-        in_specs=whole(4),
+        in_specs=whole(5),
         out_specs=pl.BlockSpec(memory_space=pltpu.VMEM),
         compiler_params=params,
         name="gradient",
-    )(trace_a, trace_b, factor, data)
+    )(trace_a, trace_b, straight, factor, data)
 
 
 def solution(mesh):

time: 51.8 us -> 49.9 us (0.963)
  the two profiles are of different devices: /device:TPU:4 before, /device:TPU:20 now
where the time goes in v7:
time: 49.9 us; the launch traced here: 49.7 us
  waiting for transfers between devices  18.9 us (38%)
  Pallas kernels  16.2 us (32%)
  starting transfers between devices  14.4 us (29%)
    pallas_call x1, Pallas kernels, body(): pl.pallas_call(functools.partial(basis_kernel, depth), out_shape=(fields,...  9.29 us
    ppermute x1, waiting for transfers between devices, body(): lax.ppermute(cross_block, ('tile', 'level'), swaps([(2 * a + level, 2 * b...  3.64 us
    ppermute x3, starting transfers between devices, body(): lax.ppermute(gram, ('tile', 'level'), swaps([(i, i ^ k) for i in range(2...  3.55 us
    ppermute x1, waiting for transfers between devices, body(): partials.append(lax.ppermute(partials[0], 'tile', swaps([(0, 2), (1, 3)])))  3.2 us
    ppermute x3, waiting for transfers between devices, body(): lax.ppermute(gram, ('tile', 'level'), swaps([(i, i ^ k) for i in range(2...  3.1 us
    ppermute x1, waiting for transfers between devices, body(): own_far = lax.ppermute(cross_block, 'level', swaps([(0, 1)]))  2.78 us
    ppermute x1, waiting for transfers between devices, body(): lax.ppermute(straight, ('probe', 'level'), [(device(x, core, 1), device(1...  2.72 us
    ppermute x1, starting transfers between devices, body(): lax.ppermute(straight, ('probe', 'level'), [(device(x, core, 1), device(1...  2.43 us
  transfers between devices with their start and end apart: 14, of which 7 were waited for; matrix products, arithmetic and copies ran while one was open for 0% of the time, Pallas kernels for 7%

profile of v7, /device:TPU:20, one launch (start us, length us, event | category | flops | bytes accessed | tf_op | source)
XLA Modules:
  0.0 49.7 jit_solution(18289025152732105884)
XLA Ops:
  0.0 1.6 %pack.1 = (f32[68,8,128]{2,1,0:T(8,128)S(1)}, f32[55,8,128]{2,1,0:T(8,128)S(1)}, f32[55,8,128]{2,1,0:T(8,128)S(1)}, f32[52,8,128]{2,1,0:T(8,128)S(1)}) custom-call(s32[32,8,256]{2,1,0:T(8,128)} %bitcast.5, f32[32,8,256]{2,1,0:T(8,128)} %kappa_ref.1, f32[32,8,256]{2,1,0:T(8,128)} %observed_ref.1), custom_call_target="tpu_custom_call" | custom-call | tf_op jit(solution)/shard_map/pack/pallas_call | solution.py:677
  1.6 0.6 %collective-permute-start.2 = (f32[52,8,128]{2,1,0:T(8,128)S(1)}, f32[52,8,128]{2,1,0:T(8,128)S(1)}, u32[]{:S(2)}, u32[]{:S(2)}) collective-permute-start(f32[52,8,128]{2,1,0:T(8,128)S(1)} %get-tuple-element.26), channel_id=1, source_target_pairs={{0,1},{1,0},{2,3},{3,2},{4,5},{5,4},{6,7},{7,6},{8,9},{9,8},{10,11... | collective-permute-start | bytes 638984 | tf_op jit(solution)/shard_map/ppermute | solution.py:702
  2.2 1.6 %collective-permute-start = (f32[55,8,128]{2,1,0:T(8,128)S(1)}, f32[55,8,128]{2,1,0:T(8,128)S(1)}, u32[]{:S(2)}, u32[]{:S(2)}) collective-permute-start(f32[55,8,128]{2,1,0:T(8,128)S(1)} %get-tuple-element.24), channel_id=1, source_target_pairs={{0,2},{2,0},{4,6},{6,4},{1,3},{3,1},{5,7},{7,5},{8,10},{10,8},{12,... | collective-permute-start | bytes 675848 | tf_op jit(solution)/shard_map/ppermute | solution.py:703
  3.8 1.9 %collective-permute-start.1 = (f32[55,8,128]{2,1,0:T(8,128)S(1)}, f32[55,8,128]{2,1,0:T(8,128)S(1)}, u32[]{:S(2)}, u32[]{:S(2)}) collective-permute-start(f32[55,8,128]{2,1,0:T(8,128)S(1)} %get-tuple-element.25), channel_id=1, source_target_pairs={{2,4},{4,2},{3,5},{5,3},{10,12},{12,10},{11,13},{13,11},{18,20},{2... | collective-permute-start | bytes 675848 | tf_op jit(solution)/shard_map/ppermute | solution.py:704
  5.7 0.2 collective-permute-start.4
  5.9 2.8 %collective-permute-done.2.own_far_ref.far_ref = f32[52,8,128]{2,1,0:T(8,128)S(1)} collective-permute-done((f32[52,8,128]{2,1,0:T(8,128)S(1)}, f32[52,8,128]{2,1,0:T(8,128)S(1)}, u32[]{:S(2)}, u32[]{:S(2)}) %collective-permute-start.2) | collective-permute-done | bytes 213024 | tf_op jit(solution)/shard_map/ppermute | solution.py:702
  8.7 2.3 %collective-permute-start.5 = (f32[52,8,128]{2,1,0:T(8,128)S(1)}, f32[52,8,128]{2,1,0:T(8,128)S(1)}, u32[]{:S(2)}, u32[]{:S(2)}) collective-permute-start(f32[52,8,128]{2,1,0:T(8,128)S(1)} %collective-permute-done.2.own_far_ref.far_ref), channel_id=1, source_target_pairs={{2,4},{4,2},{3,5},{5,3},{10,12},{12,10},{11,13},{13,11},{18,20},{2... | collective-permute-start | bytes 638984 | tf_op jit(solution)/shard_map/ppermute | solution.py:705
  11.1 3.6 %collective-permute-done.4.even_far_ref = f32[52,8,128]{2,1,0:T(8,128)S(1)} collective-permute-done((f32[52,8,128]{2,1,0:T(8,128)S(1)}, f32[52,8,128]{2,1,0:T(8,128)S(1)}, u32[]{:S(2)}, u32[]{:S(2)}) %collective-permute-start.4) | collective-permute-done | bytes 213024 | tf_op jit(solution)/shard_map/ppermute | solution.py:706
  14.7 0.0 collective-permute-done.even_ref
  14.7 0.0 collective-permute-done.1.odd_ref
  14.8 0.1 collective-permute-start.3
  14.9 2.1 %collective-permute-done.5.odd_far_ref = f32[52,8,128]{2,1,0:T(8,128)S(1)} collective-permute-done((f32[52,8,128]{2,1,0:T(8,128)S(1)}, f32[52,8,128]{2,1,0:T(8,128)S(1)}, u32[]{:S(2)}, u32[]{:S(2)}) %collective-permute-start.5) | collective-permute-done | bytes 213024 | tf_op jit(solution)/shard_map/ppermute | solution.py:705
  16.9 0.1 collective-permute-start.6
  17.0 0.0 collective-permute-done.3.swapped_ref
  17.0 1.4 %near.1 = (f32[32,24,256]{2,1,0:T(8,128)S(1)}, f32[32,24,256]{2,1,0:T(8,128)S(1)}, f32[32,24,256]{2,1,0:T(8,128)S(1)}, f32[32,8,256]{2,1,0:T(8,128)S(1)}, f32[32,8,256]{2,1,0:T(8,128)S(1)}) custom-call(f32[68,8,128]{2,1,0:T(8,128)S(1)} %get-tuple-element.23.own_ref, f32[55,8,128]{2,1,0:T(8,128)S(1)} %collective-permute-done.even_ref, ...), custom_call_target="tpu_custom_call" | custom-call | tf_op jit(solution)/shard_map/near/pallas_call | solution.py:731
  18.4 0.0 collective-permute-done.6.swapped_far_ref
  18.4 9.3 %basis.1 = (f32[4,64,8,256]{3,2,1,0:T(8,128)S(1)}, f32[4,64,8,256]{3,2,1,0:T(8,128)S(1)}, f32[32,8,256]{2,1,0:T(8,128)S(1)}, f32[32,8,256]{2,1,0:T(8,128)S(1)}, f32[8,128]{1,0:T(8,128)S(1)}) custom-call(f32[32,24,256]{2,1,0:T(8,128)S(1)} %get-tuple-element.27.near_diag, f32[32,24,256]{2,1,0:T(8,128)S(1)} %get-tuple-element.28.near_lower, ...), custom_call_target="tpu_custom_call" | custom-call | tf_op jit(solution)/shard_map/basis/pallas_call | solution.py:746
  27.7 0.8 %collective-permute-start.9 = (f32[8,128]{1,0:T(8,128)S(1)}, f32[8,128]{1,0:T(8,128)S(1)}, u32[]{:S(2)}, u32[]{:S(2)}) collective-permute-start(f32[8,128]{1,0:T(8,128)S(1)} %get-tuple-element.36), channel_id=1, source_target_pairs={{0,3},{3,0},{1,2},{2,1},{4,7},{7,4},{5,6},{6,5},{8,11},{11,8},{9,1... | collective-permute-start | bytes 12296 | tf_op jit(solution)/shard_map/ppermute | solution.py:792
  28.5 2.2 %collective-permute-start.8 = (f32[8,128]{1,0:T(8,128)S(1)}, f32[8,128]{1,0:T(8,128)S(1)}, u32[]{:S(2)}, u32[]{:S(2)}) collective-permute-start(f32[8,128]{1,0:T(8,128)S(1)} %get-tuple-element.36), channel_id=1, source_target_pairs={{0,2},{2,0},{1,3},{3,1},{4,6},{6,4},{5,7},{7,5},{8,10},{10,8},{9,1... | collective-permute-start | bytes 12296 | tf_op jit(solution)/shard_map/ppermute | solution.py:792
  30.7 0.5 %collective-permute-start.7 = (f32[8,128]{1,0:T(8,128)S(1)}, f32[8,128]{1,0:T(8,128)S(1)}, u32[]{:S(2)}, u32[]{:S(2)}) collective-permute-start(f32[8,128]{1,0:T(8,128)S(1)} %get-tuple-element.36), channel_id=1, source_target_pairs={{0,1},{1,0},{2,3},{3,2},{4,5},{5,4},{6,7},{7,6},{8,9},{9,8},{10,11... | collective-permute-start | bytes 12296 | tf_op jit(solution)/shard_map/ppermute | solution.py:792
  31.2 3.1 %collective-permute-done.7 = f32[8,128]{1,0:T(8,128)S(1)} collective-permute-done((f32[8,128]{1,0:T(8,128)S(1)}, f32[8,128]{1,0:T(8,128)S(1)}, u32[]{:S(2)}, u32[]{:S(2)}) %collective-permute-start.7) | collective-permute-done | bytes 4128 | tf_op jit(solution)/shard_map/ppermute | solution.py:792
  34.3 0.0 collective-permute-done.8
  34.4 0.0 collective-permute-done.9
  34.4 0.1 collective-permute-start.10
  34.4 0.0 copy-start
  34.5 0.0 copy-start.1
  34.5 1.4 %terms.1.terms_ref = f32[4,64,8,128]{3,2,1,0:T(8,128)S(1)} custom-call(f32[4,64,8,256]{3,2,1,0:T(8,128)S(1)} %get-tuple-element.31.basis_ref, f32[4,64,8,256]{3,2,1,0:T(8,128)S(1)} %get-tuple-element.32.image_ref, f32[32,8,256]{2,1,0:T(8,128)S(1)} %get-tuple-element.30.near_signs, f32[32,8,256]{2,1,0:T(8,128)S(1)} %get-tuple-element.33.near_k_signs, ...), custom_call_target="tpu_custom_call" | custom-call | tf_op jit(solution)/shard_map/terms/pallas_call | solution.py:781
  35.9 3.2 %collective-permute-done.10.refs_1_ = f32[32,128]{1,0:T(8,128)S(1)} collective-permute-done((f32[32,128]{1,0:T(8,128)S(1)}, f32[32,128]{1,0:T(8,128)S(1)}, u32[]{:S(2)}, u32[]{:S(2)}) %collective-permute-start.10) | collective-permute-done | bytes 16416 | tf_op jit(solution)/shard_map/ppermute | solution.py:801
  39.1 0.6 %combine.1 = (f32[2,16,8,128]{3,2,1,0:T(8,128)S(1)}, f32[2,16,8,128]{3,2,1,0:T(8,128)S(1)}) custom-call(f32[4,64,8,128]{3,2,1,0:T(8,128)S(1)} %terms.1.terms_ref, f32[32,128]{1,0:T(8,128)S(1)} %constant_dynamic-update-slice_fusion.refs_0_, f32[32,128]{1,0:T(8,128)S(1)} %collective-permute-done.10.refs_1_), custom_call_target="tpu_custom_call" | custom-call | tf_op jit(solution)/shard_map/combine/pallas_call | solution.py:805
  39.7 0.1 collective-permute-start.11
  39.8 1.3 %collective-permute-done.11 = f32[2,16,8,128]{3,2,1,0:T(8,128)S(1)} collective-permute-done((f32[2,16,8,128]{3,2,1,0:T(8,128)S(1)}, f32[2,16,8,128]{3,2,1,0:T(8,128)S(1)}, u32[]{:S(2)}, u32[]{:S(2)}) %collective-permute-start.11) | collective-permute-done | bytes 131104 | tf_op jit(solution)/shard_map/ppermute | solution.py:814
  41.2 1.5 %collective-permute-start.12 = (f32[16,8,128]{2,1,0:T(8,128)S(1)}, f32[16,8,128]{2,1,0:T(8,128)S(1)}, u32[]{:S(2)}, u32[]{:S(2)}) collective-permute-start(f32[16,8,128]{2,1,0:T(8,128)S(1)} %get-tuple-element.42), channel_id=1, source_target_pairs={{0,1},{8,9},{16,17},{24,25},{1,16},{9,24},{17,0},{25,8},{2,3},{10,... | collective-permute-start | bytes 196616 | tf_op jit(solution)/shard_map/ppermute | solution.py:823
  42.7 2.4 %collective-permute-start.13 = (f32[16,8,128]{2,1,0:T(8,128)S(1)}, f32[16,8,128]{2,1,0:T(8,128)S(1)}, u32[]{:S(2)}, u32[]{:S(2)}) collective-permute-start(f32[16,8,128]{2,1,0:T(8,128)S(1)} %get-tuple-element.41.straight_ref), channel_id=1, source_target_pairs={{1,17},{9,25},{17,1},{25,9},{3,19},{11,27},{19,3},{27,11},{5,21},{... | collective-permute-start | bytes 196616 | tf_op jit(solution)/shard_map/ppermute | solution.py:829
  45.1 0.0 copy-done
  45.1 0.0 copy-done.1
  45.1 1.0 %observed.1 = (f32[16,8,128]{2,1,0:T(8,128)S(1)}, f32[16,8,128]{2,1,0:T(8,128)S(1)}) custom-call(f32[32,8,256]{2,1,0:T(8,128)S(1)} %copy-done, f32[32,8,256]{2,1,0:T(8,128)S(1)} %copy-done.1, f32[55,8,128]{2,1,0:T(8,128)S(1)} %collective-permute-done.even_ref, f32[55,8,128]{2,1,0:T(8,128)S(1)} %collective-permute-done.1.odd_ref, ...), custom_call_target="tpu_custom_call" | custom-call | tf_op jit(solution)/shard_map/observed/pallas_call | solution.py:714
  46.1 0.0 collective-permute-done.12.trace_a_ref
  46.1 2.7 %collective-permute-done.13.trace_b_ref = f32[16,8,128]{2,1,0:T(8,128)S(1)} collective-permute-done((f32[16,8,128]{2,1,0:T(8,128)S(1)}, f32[16,8,128]{2,1,0:T(8,128)S(1)}, u32[]{:S(2)}, u32[]{:S(2)}) %collective-permute-start.13) | collective-permute-done | bytes 65568 | tf_op jit(solution)/shard_map/ppermute | solution.py:829
  48.8 0.9 %gradient.1 = f32[32,8,64]{2,1,0:T(8,128)} custom-call(f32[16,8,128]{2,1,0:T(8,128)S(1)} %collective-permute-done.12.trace_a_ref, f32[16,8,128]{2,1,0:T(8,128)S(1)} %collective-permute-done.13.trace_b_ref, f32[16,8,128]{2,1,0:T(8,128)S(1)} %get-tuple-element.41.straight_ref, f32[16,8,128]{2,1,0:T(8,128)S(1)} %get-tuple-element.39.factor_ref, ...), custom_call_target="tpu_custom_call" | custom-call | tf_op jit(solution)/shard_map/gradient/pallas_call | solution.py:834
  (13 shorter events, 0.1 us)
Async XLA Ops:
  1.6 7.1 %collective-permute-start.2 = (f32[52,8,128]{2,1,0:T(8,128)S(1)}, f32[52,8,128]{2,1,0:T(8,128)S(1)}, u32[]{:S(2)}, u32[]{:S(2)}) collective-permute-start(f32[52,8,128]{2,1,0:T(8,128)S(1)} %get-tuple-element.26), channel_id=1, source_target_pairs={{0,1},{1,0},{2,3},{3,2},{4,5},{5,4},{6,7},{7,6},{8,9},{9,8},{10,11... | collective-permute-start | bytes 638984 | tf_op jit(solution)/shard_map/ppermute | solution.py:702
  2.2 12.5 %collective-permute-start = (f32[55,8,128]{2,1,0:T(8,128)S(1)}, f32[55,8,128]{2,1,0:T(8,128)S(1)}, u32[]{:S(2)}, u32[]{:S(2)}) collective-permute-start(f32[55,8,128]{2,1,0:T(8,128)S(1)} %get-tuple-element.24), channel_id=1, source_target_pairs={{0,2},{2,0},{4,6},{6,4},{1,3},{3,1},{5,7},{7,5},{8,10},{10,8},{12,... | collective-permute-start | bytes 675848 | tf_op jit(solution)/shard_map/ppermute | solution.py:703
  3.8 11.0 %collective-permute-start.1 = (f32[55,8,128]{2,1,0:T(8,128)S(1)}, f32[55,8,128]{2,1,0:T(8,128)S(1)}, u32[]{:S(2)}, u32[]{:S(2)}) collective-permute-start(f32[55,8,128]{2,1,0:T(8,128)S(1)} %get-tuple-element.25), channel_id=1, source_target_pairs={{2,4},{4,2},{3,5},{5,3},{10,12},{12,10},{11,13},{13,11},{18,20},{2... | collective-permute-start | bytes 675848 | tf_op jit(solution)/shard_map/ppermute | solution.py:704
  5.7 9.0 %collective-permute-start.4 = (f32[52,8,128]{2,1,0:T(8,128)S(1)}, f32[52,8,128]{2,1,0:T(8,128)S(1)}, u32[]{:S(2)}, u32[]{:S(2)}) collective-permute-start(f32[52,8,128]{2,1,0:T(8,128)S(1)} %get-tuple-element.26), channel_id=1, source_target_pairs={{0,3},{3,0},{1,2},{2,1},{4,7},{7,4},{5,6},{6,5},{8,11},{11,8},{9,1... | collective-permute-start | bytes 638984 | tf_op jit(solution)/shard_map/ppermute | solution.py:706
  8.7 8.2 %collective-permute-start.5 = (f32[52,8,128]{2,1,0:T(8,128)S(1)}, f32[52,8,128]{2,1,0:T(8,128)S(1)}, u32[]{:S(2)}, u32[]{:S(2)}) collective-permute-start(f32[52,8,128]{2,1,0:T(8,128)S(1)} %collective-permute-done.2.own_far_ref.far_ref), channel_id=1, source_target_pairs={{2,4},{4,2},{3,5},{5,3},{10,12},{12,10},{11,13},{13,11},{18,20},{2... | collective-permute-start | bytes 638984 | tf_op jit(solution)/shard_map/ppermute | solution.py:705
  14.8 2.2 %collective-permute-start.3 = (f32[51,8,128]{2,1,0:T(8,128)S(1)}, f32[51,8,128]{2,1,0:T(8,128)S(1)}, u32[]{:S(2)}, u32[]{:S(2)}) collective-permute-start(f32[51,8,128]{2,1,0:T(8,128)S(1)} %pad_maximum_fusion), channel_id=1, source_target_pairs={{0,8},{8,0},{16,24},{24,16},{1,9},{9,1},{17,25},{25,17},{2,10},{10... | collective-permute-start | bytes 626696 | tf_op jit(solution)/shard_map/ppermute | solution.py:725
  16.9 1.5 %collective-permute-start.6 = (f32[34,8,128]{2,1,0:T(8,128)S(1)}, f32[34,8,128]{2,1,0:T(8,128)S(1)}, u32[]{:S(2)}, u32[]{:S(2)}) collective-permute-start(f32[34,8,128]{2,1,0:T(8,128)S(1)} %pad_maximum_fusion.1), channel_id=1, source_target_pairs={{0,8},{8,0},{16,24},{24,16},{1,9},{9,1},{17,25},{25,17},{2,10},{10... | collective-permute-start | bytes 417800 | tf_op jit(solution)/shard_map/ppermute | solution.py:725
  27.7 6.7 %collective-permute-start.9 = (f32[8,128]{1,0:T(8,128)S(1)}, f32[8,128]{1,0:T(8,128)S(1)}, u32[]{:S(2)}, u32[]{:S(2)}) collective-permute-start(f32[8,128]{1,0:T(8,128)S(1)} %get-tuple-element.36), channel_id=1, source_target_pairs={{0,3},{3,0},{1,2},{2,1},{4,7},{7,4},{5,6},{6,5},{8,11},{11,8},{9,1... | collective-permute-start | bytes 12296 | tf_op jit(solution)/shard_map/ppermute | solution.py:792
  28.5 5.8 %collective-permute-start.8 = (f32[8,128]{1,0:T(8,128)S(1)}, f32[8,128]{1,0:T(8,128)S(1)}, u32[]{:S(2)}, u32[]{:S(2)}) collective-permute-start(f32[8,128]{1,0:T(8,128)S(1)} %get-tuple-element.36), channel_id=1, source_target_pairs={{0,2},{2,0},{1,3},{3,1},{4,6},{6,4},{5,7},{7,5},{8,10},{10,8},{9,1... | collective-permute-start | bytes 12296 | tf_op jit(solution)/shard_map/ppermute | solution.py:792
  30.7 3.6 %collective-permute-start.7 = (f32[8,128]{1,0:T(8,128)S(1)}, f32[8,128]{1,0:T(8,128)S(1)}, u32[]{:S(2)}, u32[]{:S(2)}) collective-permute-start(f32[8,128]{1,0:T(8,128)S(1)} %get-tuple-element.36), channel_id=1, source_target_pairs={{0,1},{1,0},{2,3},{3,2},{4,5},{5,4},{6,7},{7,6},{8,9},{9,8},{10,11... | collective-permute-start | bytes 12296 | tf_op jit(solution)/shard_map/ppermute | solution.py:792
  34.4 4.7 %collective-permute-start.10 = (f32[32,128]{1,0:T(8,128)S(1)}, f32[32,128]{1,0:T(8,128)S(1)}, u32[]{:S(2)}, u32[]{:S(2)}) collective-permute-start(f32[32,128]{1,0:T(8,128)S(1)} %constant_dynamic-update-slice_fusion.refs_0_), channel_id=1, source_target_pairs={{0,4},{4,0},{2,6},{6,2},{1,5},{5,1},{3,7},{7,3},{8,12},{12,8},{10,... | collective-permute-start | bytes 49160 | tf_op jit(solution)/shard_map/ppermute | solution.py:801
  34.4 10.7 %copy-start = (f32[32,8,256]{2,1,0:T(8,128)S(1)}, f32[32,8,256]{2,1,0:T(8,128)}, u32[]{:S(2)}) copy-start(f32[32,8,256]{2,1,0:T(8,128)} %kappa_ref.1) | copy-start | bytes 786436
  34.5 10.7 %copy-start.1 = (f32[32,8,256]{2,1,0:T(8,128)S(1)}, f32[32,8,256]{2,1,0:T(8,128)}, u32[]{:S(2)}) copy-start(f32[32,8,256]{2,1,0:T(8,128)} %observed_ref.1) | copy-start | bytes 786436
  39.7 1.4 %collective-permute-start.11 = (f32[2,16,8,128]{3,2,1,0:T(8,128)S(1)}, f32[2,16,8,128]{3,2,1,0:T(8,128)S(1)}, u32[]{:S(2)}, u32[]{:S(2)}) collective-permute-start(f32[2,16,8,128]{3,2,1,0:T(8,128)S(1)} %get-tuple-element.38), channel_id=1, source_target_pairs={{0,8},{8,0},{16,24},{24,16},{1,9},{9,1},{17,25},{25,17},{2,10},{10... | collective-permute-start | bytes 393224 | tf_op jit(solution)/shard_map/ppermute | solution.py:814
  41.2 4.9 %collective-permute-start.12 = (f32[16,8,128]{2,1,0:T(8,128)S(1)}, f32[16,8,128]{2,1,0:T(8,128)S(1)}, u32[]{:S(2)}, u32[]{:S(2)}) collective-permute-start(f32[16,8,128]{2,1,0:T(8,128)S(1)} %get-tuple-element.42), channel_id=1, source_target_pairs={{0,1},{8,9},{16,17},{24,25},{1,16},{9,24},{17,0},{25,8},{2,3},{10,... | collective-permute-start | bytes 196616 | tf_op jit(solution)/shard_map/ppermute | solution.py:823
  42.7 6.1 %collective-permute-start.13 = (f32[16,8,128]{2,1,0:T(8,128)S(1)}, f32[16,8,128]{2,1,0:T(8,128)S(1)}, u32[]{:S(2)}, u32[]{:S(2)}) collective-permute-start(f32[16,8,128]{2,1,0:T(8,128)S(1)} %get-tuple-element.41.straight_ref), channel_id=1, source_target_pairs={{1,17},{9,25},{17,1},{25,9},{3,19},{11,27},{19,3},{27,11},{5,21},{... | collective-permute-start | bytes 196616 | tf_op jit(solution)/shard_map/ppermute | solution.py:829

commit v8 on v7

--- a/solution.py
+++ b/solution.py
@@ -13,7 +13,7 @@
 ROWS = 8
 EDGE = 8
 GROUP = 8
-SHIFTS = (1.0, 0.0, -2.0)
+SHIFTS = (1.0, -1.0, 0.0)
 PAIRS = [(i, j) for j in range(ITERS) for i in range(j + 1)]
 COUNT = len(PAIRS) + ITERS
 SLOTS = 16
@@ -294,10 +294,12 @@
     sides,
     backward,
     sums,
+    masks,
 ):
     levels = 2 * depth
     mask = inside_mask()
     half_mask = 0.5 * mask
+    masks[...] = half_mask
     zero = jnp.zeros(mask.shape, jnp.float32)
     own_zero = jnp.zeros((ROWS, LANES), jnp.float32)
     mine = lane_ids((ROWS, LANES)) < LANES // 2
@@ -334,7 +336,7 @@
         return ratio, value, from_end
 
     start = (near_lower[depth - 1], near_forward[depth - 1], zero)
-    carry = lax.fori_loop(0, depth, start_down, start, unroll=GROUP)
+    carry = lax.fori_loop(0, depth, start_down, start, unroll=depth)
 
     def start_up_far(step, carry):
         k = depth - 1 - step
@@ -344,7 +346,7 @@
         backward[depth + k] = value
         return solved, value
 
-    solved, value = lax.fori_loop(0, depth, start_up_far, (zero, zero), unroll=GROUP)
+    solved, value = lax.fori_loop(0, depth, start_up_far, (zero, zero), unroll=depth)
 
     def start_up_near(step, carry):
         k = depth - 1 - step
@@ -356,7 +358,7 @@
         backward[k] = value
         return ratio, solved, value
 
-    lax.fori_loop(0, depth, start_up_near, (carry[2], solved, value), unroll=GROUP)
+    lax.fori_loop(0, depth, start_up_near, (carry[2], solved, value), unroll=depth)
 
     parts = (
         (0, near_diag, near_lower, lambda k: near_signs[k]),
@@ -372,7 +374,11 @@
             if index == 0:
                 value = solved
             elif SHIFTS[index - 1] == 0.0:
-                value = -solved
+                value = solved
+            elif SHIFTS[index - 1] == 1.0:
+                value = basis[k] - solved
+            elif SHIFTS[index - 1] == -1.0:
+                value = basis[k] + solved
             else:
                 value = SHIFTS[index - 1] * basis[k] - solved
             return solved, value
@@ -380,19 +386,20 @@
         solved, here = next_basis(0, zero)
         if not final:
             basis[0] = here
-        carry = (solved, zero, here, zero) + (own_zero,) * (2 * (index + 2))
+        carry = (solved, zero, here, zero)
+        slots = list(range(place, place + index + 1)) + [len(PAIRS) + index]
         for offset, half_diag, lower, sign_of in parts:
 
             def down(group, carry):
-                solved, above, here, value, *totals = carry
-                products = []
+                solved, above, here, value = carry
+                added = [None] * len(slots)
                 for step in range(group_size):
                     k = group * group_size + step
                     solved, below = next_basis(offset + k + 1, solved)
                     if not final:
                         basis[offset + k + 1] = below
                     side = beside(here)
-                    image = half_diag[k] * here - (above + below) - half_mask * side
+                    image = half_diag[k] * here - (above + below) - masks[...] * side
                     if not final:
                         value = lower[k] * (beside(image) + value)
                         forward[offset + k] = value
@@ -402,27 +409,17 @@
                     image_ref[index, offset + k] = my_image
                     factors = [(image_ref[other, offset + k], my_image) for other in range(index)]
                     factors += [(my_image, my_image), (my_basis, sign_of(k))]
-                    products.append(
-                        [a[:, :LANES] * b[:, :LANES] + a[:, LANES:] * b[:, LANES:] for a, b in factors]
-                    )
+                    for slot, (a, b) in enumerate(factors):
+                        product = a[:, :LANES] * b[:, :LANES] + a[:, LANES:] * b[:, LANES:]
+                        added[slot] = product if step % GROUP == 0 else added[slot] + product
+                        if step % GROUP == GROUP - 1:
+                            at = (offset + group * group_size + step) // GROUP
+                            sums[slots[slot], at] = added[slot]
                     above, here = here, below
-                for slot in range(index + 2):
-                    for four in range(0, group_size, 4):
-                        added = (products[four][slot] + products[four + 1][slot]) + (
-                            products[four + 2][slot] + products[four + 3][slot]
-                        )
-                        totals[2 * slot], rest = two_sum(totals[2 * slot], added)
-                        totals[2 * slot + 1] = totals[2 * slot + 1] + rest
-                return (solved, above, here, value, *totals)
+                return solved, above, here, value
 
             carry = lax.fori_loop(0, depth // group_size, down, carry)
-        totals = [jnp.where(mine, total, 0.0) for total in carry[4:]]
-        for slot in range(index + 1):
-            sums[2 * (place + slot)] = totals[2 * slot]
-            sums[2 * (place + slot) + 1] = totals[2 * slot + 1]
         place += index + 1
-        sums[2 * (len(PAIRS) + index)] = totals[2 * index + 2]
-        sums[2 * (len(PAIRS) + index) + 1] = totals[2 * index + 3]
         if final:
             break
         carry = (zero, zero)
@@ -443,7 +440,11 @@
     for block in range(SLOTS // ROWS):
         high, low = own_zero, own_zero
         for slot in range(block * ROWS, min((block + 1) * ROWS, COUNT)):
-            pair = (sums[2 * slot], sums[2 * slot + 1])
+            pair = (sums[slot, 0], own_zero)
+            for at in range(1, sums.shape[1]):
+                total, rest = two_sum(pair[0], sums[slot, at])
+                pair = (total, pair[1] + rest)
+            pair = tuple(jnp.where(mine, part, 0.0) for part in pair)
             for shift in (4, 2, 1):
                 pair = pair_add(pair, tuple(pltpu.roll(part, shift, 0) for part in pair))
             here = ids == slot - block * ROWS
@@ -640,7 +641,7 @@
 
 
 def gradient_kernel(
-    depth, trace_a_ref, trace_b_ref, straight_ref, factor_ref, data_ref, out_ref
+    depth, trace_b_ref, trace_a_ref, straight_ref, factor_ref, data_ref, out_ref
 ):
     width = LANES // 2
     square = (LANES, LANES)
@@ -763,7 +764,8 @@
             plain,
             plain,
             padded,
-            pltpu.VMEM((2 * SLOTS, ROWS, LANES), f32),
+            pltpu.VMEM((SLOTS, levels // GROUP, ROWS, LANES), f32),
+            pltpu.VMEM((3 * ROWS, 2 * LANES), f32),
         ],
         compiler_params=params,
         name="basis",
@@ -838,7 +840,7 @@
         out_specs=pl.BlockSpec(memory_space=pltpu.VMEM),
         compiler_params=params,
         name="gradient",
-    )(trace_a, trace_b, straight, factor, data)
+    )(trace_b, trace_a, straight, factor, data)
 
 
 def solution(mesh):

time: 49.9 us -> 49.6 us (level)
  transfers between devices with their start and end apart: 14 -> 14, of which waited for: 7 -> 7; matrix products, arithmetic and copies ran while one was open for 0% -> 0% of each run, Pallas kernels for 7% -> 8%
where the time goes in v8:
time: 49.6 us; the launch traced here: 49.4 us
  waiting for transfers between devices  18.8 us (38%)
  Pallas kernels  15.8 us (32%)
  starting transfers between devices  14.4 us (29%)
    pallas_call x1, Pallas kernels, body(): pl.pallas_call(functools.partial(basis_kernel, depth), out_shape=(fields,...  8.94 us
    ppermute x1, waiting for transfers between devices, body(): lax.ppermute(cross_block, ('tile', 'level'), swaps([(2 * a + level, 2 * b...  3.64 us
    ppermute x3, starting transfers between devices, body(): lax.ppermute(gram, ('tile', 'level'), swaps([(i, i ^ k) for i in range(2...  3.55 us
    ppermute x1, waiting for transfers between devices, body(): partials.append(lax.ppermute(partials[0], 'tile', swaps([(0, 2), (1, 3)])))  3.2 us
    ppermute x3, waiting for transfers between devices, body(): lax.ppermute(gram, ('tile', 'level'), swaps([(i, i ^ k) for i in range(2...  3.1 us
    ppermute x1, waiting for transfers between devices, body(): own_far = lax.ppermute(cross_block, 'level', swaps([(0, 1)]))  2.78 us
    ppermute x1, waiting for transfers between devices, body(): lax.ppermute(straight, ('probe', 'level'), [(device(x, core, 1), device(1...  2.72 us
    ppermute x1, starting transfers between devices, body(): lax.ppermute(straight, ('probe', 'level'), [(device(x, core, 1), device(1...  2.43 us
  transfers between devices with their start and end apart: 14, of which 7 were waited for; matrix products, arithmetic and copies ran while one was open for 0% of the time, Pallas kernels for 8%

profile of v8, /device:TPU:20, one launch (start us, length us, event | category | flops | bytes accessed | tf_op | source)
XLA Modules:
  0.0 49.4 jit_solution(11944077717670395346)
XLA Ops:
  0.0 1.6 %pack.1 = (f32[68,8,128]{2,1,0:T(8,128)S(1)}, f32[55,8,128]{2,1,0:T(8,128)S(1)}, f32[55,8,128]{2,1,0:T(8,128)S(1)}, f32[52,8,128]{2,1,0:T(8,128)S(1)}) custom-call(s32[32,8,256]{2,1,0:T(8,128)} %bitcast.5, f32[32,8,256]{2,1,0:T(8,128)} %kappa_ref.1, f32[32,8,256]{2,1,0:T(8,128)} %observed_ref.1), custom_call_target="tpu_custom_call" | custom-call | tf_op jit(solution)/shard_map/pack/pallas_call | solution.py:678
  1.6 0.6 %collective-permute-start.2 = (f32[52,8,128]{2,1,0:T(8,128)S(1)}, f32[52,8,128]{2,1,0:T(8,128)S(1)}, u32[]{:S(2)}, u32[]{:S(2)}) collective-permute-start(f32[52,8,128]{2,1,0:T(8,128)S(1)} %get-tuple-element.26), channel_id=1, source_target_pairs={{0,1},{1,0},{2,3},{3,2},{4,5},{5,4},{6,7},{7,6},{8,9},{9,8},{10,11... | collective-permute-start | bytes 638984 | tf_op jit(solution)/shard_map/ppermute | solution.py:703
  2.2 1.6 %collective-permute-start = (f32[55,8,128]{2,1,0:T(8,128)S(1)}, f32[55,8,128]{2,1,0:T(8,128)S(1)}, u32[]{:S(2)}, u32[]{:S(2)}) collective-permute-start(f32[55,8,128]{2,1,0:T(8,128)S(1)} %get-tuple-element.24), channel_id=1, source_target_pairs={{0,2},{2,0},{4,6},{6,4},{1,3},{3,1},{5,7},{7,5},{8,10},{10,8},{12,... | collective-permute-start | bytes 675848 | tf_op jit(solution)/shard_map/ppermute | solution.py:704
  3.8 1.9 %collective-permute-start.1 = (f32[55,8,128]{2,1,0:T(8,128)S(1)}, f32[55,8,128]{2,1,0:T(8,128)S(1)}, u32[]{:S(2)}, u32[]{:S(2)}) collective-permute-start(f32[55,8,128]{2,1,0:T(8,128)S(1)} %get-tuple-element.25), channel_id=1, source_target_pairs={{2,4},{4,2},{3,5},{5,3},{10,12},{12,10},{11,13},{13,11},{18,20},{2... | collective-permute-start | bytes 675848 | tf_op jit(solution)/shard_map/ppermute | solution.py:705
  5.7 0.2 collective-permute-start.4
  5.9 2.8 %collective-permute-done.2.own_far_ref.far_ref = f32[52,8,128]{2,1,0:T(8,128)S(1)} collective-permute-done((f32[52,8,128]{2,1,0:T(8,128)S(1)}, f32[52,8,128]{2,1,0:T(8,128)S(1)}, u32[]{:S(2)}, u32[]{:S(2)}) %collective-permute-start.2) | collective-permute-done | bytes 213024 | tf_op jit(solution)/shard_map/ppermute | solution.py:703
  8.7 2.3 %collective-permute-start.5 = (f32[52,8,128]{2,1,0:T(8,128)S(1)}, f32[52,8,128]{2,1,0:T(8,128)S(1)}, u32[]{:S(2)}, u32[]{:S(2)}) collective-permute-start(f32[52,8,128]{2,1,0:T(8,128)S(1)} %collective-permute-done.2.own_far_ref.far_ref), channel_id=1, source_target_pairs={{2,4},{4,2},{3,5},{5,3},{10,12},{12,10},{11,13},{13,11},{18,20},{2... | collective-permute-start | bytes 638984 | tf_op jit(solution)/shard_map/ppermute | solution.py:706
  11.1 3.6 %collective-permute-done.4.even_far_ref = f32[52,8,128]{2,1,0:T(8,128)S(1)} collective-permute-done((f32[52,8,128]{2,1,0:T(8,128)S(1)}, f32[52,8,128]{2,1,0:T(8,128)S(1)}, u32[]{:S(2)}, u32[]{:S(2)}) %collective-permute-start.4) | collective-permute-done | bytes 213024 | tf_op jit(solution)/shard_map/ppermute | solution.py:707
  14.7 0.0 collective-permute-done.even_ref
  14.7 0.0 collective-permute-done.1.odd_ref
  14.8 0.1 collective-permute-start.3
  14.9 2.1 %collective-permute-done.5.odd_far_ref = f32[52,8,128]{2,1,0:T(8,128)S(1)} collective-permute-done((f32[52,8,128]{2,1,0:T(8,128)S(1)}, f32[52,8,128]{2,1,0:T(8,128)S(1)}, u32[]{:S(2)}, u32[]{:S(2)}) %collective-permute-start.5) | collective-permute-done | bytes 213024 | tf_op jit(solution)/shard_map/ppermute | solution.py:706
  16.9 0.1 collective-permute-start.6
  17.0 0.0 collective-permute-done.3.swapped_ref
  17.0 1.4 %near.1 = (f32[32,24,256]{2,1,0:T(8,128)S(1)}, f32[32,24,256]{2,1,0:T(8,128)S(1)}, f32[32,24,256]{2,1,0:T(8,128)S(1)}, f32[32,8,256]{2,1,0:T(8,128)S(1)}, f32[32,8,256]{2,1,0:T(8,128)S(1)}) custom-call(f32[68,8,128]{2,1,0:T(8,128)S(1)} %get-tuple-element.23.own_ref, f32[55,8,128]{2,1,0:T(8,128)S(1)} %collective-permute-done.even_ref, ...), custom_call_target="tpu_custom_call" | custom-call | tf_op jit(solution)/shard_map/near/pallas_call | solution.py:732
  18.4 0.0 collective-permute-done.6.swapped_far_ref
  18.4 8.9 %basis.1 = (f32[4,64,8,256]{3,2,1,0:T(8,128)S(1)}, f32[4,64,8,256]{3,2,1,0:T(8,128)S(1)}, f32[32,8,256]{2,1,0:T(8,128)S(1)}, f32[32,8,256]{2,1,0:T(8,128)S(1)}, f32[8,128]{1,0:T(8,128)S(1)}) custom-call(f32[32,24,256]{2,1,0:T(8,128)S(1)} %get-tuple-element.27.near_diag, f32[32,24,256]{2,1,0:T(8,128)S(1)} %get-tuple-element.28.near_lower, ...), custom_call_target="tpu_custom_call" | custom-call | tf_op jit(solution)/shard_map/basis/pallas_call | solution.py:747
  27.3 0.8 %collective-permute-start.9 = (f32[8,128]{1,0:T(8,128)S(1)}, f32[8,128]{1,0:T(8,128)S(1)}, u32[]{:S(2)}, u32[]{:S(2)}) collective-permute-start(f32[8,128]{1,0:T(8,128)S(1)} %get-tuple-element.36), channel_id=1, source_target_pairs={{0,3},{3,0},{1,2},{2,1},{4,7},{7,4},{5,6},{6,5},{8,11},{11,8},{9,1... | collective-permute-start | bytes 12296 | tf_op jit(solution)/shard_map/ppermute | solution.py:794
  28.2 2.2 %collective-permute-start.8 = (f32[8,128]{1,0:T(8,128)S(1)}, f32[8,128]{1,0:T(8,128)S(1)}, u32[]{:S(2)}, u32[]{:S(2)}) collective-permute-start(f32[8,128]{1,0:T(8,128)S(1)} %get-tuple-element.36), channel_id=1, source_target_pairs={{0,2},{2,0},{1,3},{3,1},{4,6},{6,4},{5,7},{7,5},{8,10},{10,8},{9,1... | collective-permute-start | bytes 12296 | tf_op jit(solution)/shard_map/ppermute | solution.py:794
  30.4 0.5 %collective-permute-start.7 = (f32[8,128]{1,0:T(8,128)S(1)}, f32[8,128]{1,0:T(8,128)S(1)}, u32[]{:S(2)}, u32[]{:S(2)}) collective-permute-start(f32[8,128]{1,0:T(8,128)S(1)} %get-tuple-element.36), channel_id=1, source_target_pairs={{0,1},{1,0},{2,3},{3,2},{4,5},{5,4},{6,7},{7,6},{8,9},{9,8},{10,11... | collective-permute-start | bytes 12296 | tf_op jit(solution)/shard_map/ppermute | solution.py:794
  30.9 3.1 %collective-permute-done.7 = f32[8,128]{1,0:T(8,128)S(1)} collective-permute-done((f32[8,128]{1,0:T(8,128)S(1)}, f32[8,128]{1,0:T(8,128)S(1)}, u32[]{:S(2)}, u32[]{:S(2)}) %collective-permute-start.7) | collective-permute-done | bytes 4128 | tf_op jit(solution)/shard_map/ppermute | solution.py:794
  34.0 0.0 collective-permute-done.8
  34.0 0.0 collective-permute-done.9
  34.0 0.1 collective-permute-start.10
  34.1 0.0 copy-start
  34.1 0.0 copy-start.1
  34.1 1.4 %terms.1.terms_ref = f32[4,64,8,128]{3,2,1,0:T(8,128)S(1)} custom-call(f32[4,64,8,256]{3,2,1,0:T(8,128)S(1)} %get-tuple-element.31.basis_ref, f32[4,64,8,256]{3,2,1,0:T(8,128)S(1)} %get-tuple-element.32.image_ref, f32[32,8,256]{2,1,0:T(8,128)S(1)} %get-tuple-element.30.near_signs, f32[32,8,256]{2,1,0:T(8,128)S(1)} %get-tuple-element.33.near_k_signs, ...), custom_call_target="tpu_custom_call" | custom-call | tf_op jit(solution)/shard_map/terms/pallas_call | solution.py:783
  35.5 3.2 %collective-permute-done.10.refs_1_ = f32[32,128]{1,0:T(8,128)S(1)} collective-permute-done((f32[32,128]{1,0:T(8,128)S(1)}, f32[32,128]{1,0:T(8,128)S(1)}, u32[]{:S(2)}, u32[]{:S(2)}) %collective-permute-start.10) | collective-permute-done | bytes 16416 | tf_op jit(solution)/shard_map/ppermute | solution.py:803
  38.7 0.6 %combine.1 = (f32[2,16,8,128]{3,2,1,0:T(8,128)S(1)}, f32[2,16,8,128]{3,2,1,0:T(8,128)S(1)}) custom-call(f32[4,64,8,128]{3,2,1,0:T(8,128)S(1)} %terms.1.terms_ref, f32[32,128]{1,0:T(8,128)S(1)} %constant_dynamic-update-slice_fusion.refs_0_, f32[32,128]{1,0:T(8,128)S(1)} %collective-permute-done.10.refs_1_), custom_call_target="tpu_custom_call" | custom-call | tf_op jit(solution)/shard_map/combine/pallas_call | solution.py:807
  39.4 0.1 collective-permute-start.11
  39.5 1.3 %collective-permute-done.11 = f32[2,16,8,128]{3,2,1,0:T(8,128)S(1)} collective-permute-done((f32[2,16,8,128]{3,2,1,0:T(8,128)S(1)}, f32[2,16,8,128]{3,2,1,0:T(8,128)S(1)}, u32[]{:S(2)}, u32[]{:S(2)}) %collective-permute-start.11) | collective-permute-done | bytes 131104 | tf_op jit(solution)/shard_map/ppermute | solution.py:816
  40.8 1.5 %collective-permute-start.13 = (f32[16,8,128]{2,1,0:T(8,128)S(1)}, f32[16,8,128]{2,1,0:T(8,128)S(1)}, u32[]{:S(2)}, u32[]{:S(2)}) collective-permute-start(f32[16,8,128]{2,1,0:T(8,128)S(1)} %get-tuple-element.41), channel_id=1, source_target_pairs={{0,1},{8,9},{16,17},{24,25},{1,16},{9,24},{17,0},{25,8},{2,3},{10,... | collective-permute-start | bytes 196616 | tf_op jit(solution)/shard_map/ppermute | solution.py:825
  42.3 2.4 %collective-permute-start.12 = (f32[16,8,128]{2,1,0:T(8,128)S(1)}, f32[16,8,128]{2,1,0:T(8,128)S(1)}, u32[]{:S(2)}, u32[]{:S(2)}) collective-permute-start(f32[16,8,128]{2,1,0:T(8,128)S(1)} %get-tuple-element.42.straight_ref), channel_id=1, source_target_pairs={{1,17},{9,25},{17,1},{25,9},{3,19},{11,27},{19,3},{27,11},{5,21},{... | collective-permute-start | bytes 196616 | tf_op jit(solution)/shard_map/ppermute | solution.py:831
  44.8 0.0 copy-done
  44.8 0.0 copy-done.1
  44.8 1.0 %observed.1 = (f32[16,8,128]{2,1,0:T(8,128)S(1)}, f32[16,8,128]{2,1,0:T(8,128)S(1)}) custom-call(f32[32,8,256]{2,1,0:T(8,128)S(1)} %copy-done, f32[32,8,256]{2,1,0:T(8,128)S(1)} %copy-done.1, f32[55,8,128]{2,1,0:T(8,128)S(1)} %collective-permute-done.even_ref, f32[55,8,128]{2,1,0:T(8,128)S(1)} %collective-permute-done.1.odd_ref, ...), custom_call_target="tpu_custom_call" | custom-call | tf_op jit(solution)/shard_map/observed/pallas_call | solution.py:715
  45.8 0.0 collective-permute-done.13.trace_a_ref
  45.8 2.7 %collective-permute-done.12.trace_b_ref = f32[16,8,128]{2,1,0:T(8,128)S(1)} collective-permute-done((f32[16,8,128]{2,1,0:T(8,128)S(1)}, f32[16,8,128]{2,1,0:T(8,128)S(1)}, u32[]{:S(2)}, u32[]{:S(2)}) %collective-permute-start.12) | collective-permute-done | bytes 65568 | tf_op jit(solution)/shard_map/ppermute | solution.py:831
  48.5 0.9 %gradient.1 = f32[32,8,64]{2,1,0:T(8,128)} custom-call(f32[16,8,128]{2,1,0:T(8,128)S(1)} %collective-permute-done.12.trace_b_ref, f32[16,8,128]{2,1,0:T(8,128)S(1)} %collective-permute-done.13.trace_a_ref, f32[16,8,128]{2,1,0:T(8,128)S(1)} %get-tuple-element.42.straight_ref, f32[16,8,128]{2,1,0:T(8,128)S(1)} %get-tuple-element.39.factor_ref, ...), custom_call_target="tpu_custom_call" | custom-call | tf_op jit(solution)/shard_map/gradient/pallas_call | solution.py:836
  (13 shorter events, 0.1 us)
Async XLA Ops:
  1.6 7.1 %collective-permute-start.2 = (f32[52,8,128]{2,1,0:T(8,128)S(1)}, f32[52,8,128]{2,1,0:T(8,128)S(1)}, u32[]{:S(2)}, u32[]{:S(2)}) collective-permute-start(f32[52,8,128]{2,1,0:T(8,128)S(1)} %get-tuple-element.26), channel_id=1, source_target_pairs={{0,1},{1,0},{2,3},{3,2},{4,5},{5,4},{6,7},{7,6},{8,9},{9,8},{10,11... | collective-permute-start | bytes 638984 | tf_op jit(solution)/shard_map/ppermute | solution.py:703
  2.2 12.5 %collective-permute-start = (f32[55,8,128]{2,1,0:T(8,128)S(1)}, f32[55,8,128]{2,1,0:T(8,128)S(1)}, u32[]{:S(2)}, u32[]{:S(2)}) collective-permute-start(f32[55,8,128]{2,1,0:T(8,128)S(1)} %get-tuple-element.24), channel_id=1, source_target_pairs={{0,2},{2,0},{4,6},{6,4},{1,3},{3,1},{5,7},{7,5},{8,10},{10,8},{12,... | collective-permute-start | bytes 675848 | tf_op jit(solution)/shard_map/ppermute | solution.py:704
  3.8 11.0 %collective-permute-start.1 = (f32[55,8,128]{2,1,0:T(8,128)S(1)}, f32[55,8,128]{2,1,0:T(8,128)S(1)}, u32[]{:S(2)}, u32[]{:S(2)}) collective-permute-start(f32[55,8,128]{2,1,0:T(8,128)S(1)} %get-tuple-element.25), channel_id=1, source_target_pairs={{2,4},{4,2},{3,5},{5,3},{10,12},{12,10},{11,13},{13,11},{18,20},{2... | collective-permute-start | bytes 675848 | tf_op jit(solution)/shard_map/ppermute | solution.py:705
  5.7 9.0 %collective-permute-start.4 = (f32[52,8,128]{2,1,0:T(8,128)S(1)}, f32[52,8,128]{2,1,0:T(8,128)S(1)}, u32[]{:S(2)}, u32[]{:S(2)}) collective-permute-start(f32[52,8,128]{2,1,0:T(8,128)S(1)} %get-tuple-element.26), channel_id=1, source_target_pairs={{0,3},{3,0},{1,2},{2,1},{4,7},{7,4},{5,6},{6,5},{8,11},{11,8},{9,1... | collective-permute-start | bytes 638984 | tf_op jit(solution)/shard_map/ppermute | solution.py:707
  8.7 8.2 %collective-permute-start.5 = (f32[52,8,128]{2,1,0:T(8,128)S(1)}, f32[52,8,128]{2,1,0:T(8,128)S(1)}, u32[]{:S(2)}, u32[]{:S(2)}) collective-permute-start(f32[52,8,128]{2,1,0:T(8,128)S(1)} %collective-permute-done.2.own_far_ref.far_ref), channel_id=1, source_target_pairs={{2,4},{4,2},{3,5},{5,3},{10,12},{12,10},{11,13},{13,11},{18,20},{2... | collective-permute-start | bytes 638984 | tf_op jit(solution)/shard_map/ppermute | solution.py:706
  14.8 2.2 %collective-permute-start.3 = (f32[51,8,128]{2,1,0:T(8,128)S(1)}, f32[51,8,128]{2,1,0:T(8,128)S(1)}, u32[]{:S(2)}, u32[]{:S(2)}) collective-permute-start(f32[51,8,128]{2,1,0:T(8,128)S(1)} %pad_maximum_fusion), channel_id=1, source_target_pairs={{0,8},{8,0},{16,24},{24,16},{1,9},{9,1},{17,25},{25,17},{2,10},{10... | collective-permute-start | bytes 626696 | tf_op jit(solution)/shard_map/ppermute | solution.py:726
  16.9 1.5 %collective-permute-start.6 = (f32[34,8,128]{2,1,0:T(8,128)S(1)}, f32[34,8,128]{2,1,0:T(8,128)S(1)}, u32[]{:S(2)}, u32[]{:S(2)}) collective-permute-start(f32[34,8,128]{2,1,0:T(8,128)S(1)} %pad_maximum_fusion.1), channel_id=1, source_target_pairs={{0,8},{8,0},{16,24},{24,16},{1,9},{9,1},{17,25},{25,17},{2,10},{10... | collective-permute-start | bytes 417800 | tf_op jit(solution)/shard_map/ppermute | solution.py:726
  27.3 6.7 %collective-permute-start.9 = (f32[8,128]{1,0:T(8,128)S(1)}, f32[8,128]{1,0:T(8,128)S(1)}, u32[]{:S(2)}, u32[]{:S(2)}) collective-permute-start(f32[8,128]{1,0:T(8,128)S(1)} %get-tuple-element.36), channel_id=1, source_target_pairs={{0,3},{3,0},{1,2},{2,1},{4,7},{7,4},{5,6},{6,5},{8,11},{11,8},{9,1... | collective-permute-start | bytes 12296 | tf_op jit(solution)/shard_map/ppermute | solution.py:794
  28.2 5.8 %collective-permute-start.8 = (f32[8,128]{1,0:T(8,128)S(1)}, f32[8,128]{1,0:T(8,128)S(1)}, u32[]{:S(2)}, u32[]{:S(2)}) collective-permute-start(f32[8,128]{1,0:T(8,128)S(1)} %get-tuple-element.36), channel_id=1, source_target_pairs={{0,2},{2,0},{1,3},{3,1},{4,6},{6,4},{5,7},{7,5},{8,10},{10,8},{9,1... | collective-permute-start | bytes 12296 | tf_op jit(solution)/shard_map/ppermute | solution.py:794
  30.4 3.6 %collective-permute-start.7 = (f32[8,128]{1,0:T(8,128)S(1)}, f32[8,128]{1,0:T(8,128)S(1)}, u32[]{:S(2)}, u32[]{:S(2)}) collective-permute-start(f32[8,128]{1,0:T(8,128)S(1)} %get-tuple-element.36), channel_id=1, source_target_pairs={{0,1},{1,0},{2,3},{3,2},{4,5},{5,4},{6,7},{7,6},{8,9},{9,8},{10,11... | collective-permute-start | bytes 12296 | tf_op jit(solution)/shard_map/ppermute | solution.py:794
  34.0 4.7 %collective-permute-start.10 = (f32[32,128]{1,0:T(8,128)S(1)}, f32[32,128]{1,0:T(8,128)S(1)}, u32[]{:S(2)}, u32[]{:S(2)}) collective-permute-start(f32[32,128]{1,0:T(8,128)S(1)} %constant_dynamic-update-slice_fusion.refs_0_), channel_id=1, source_target_pairs={{0,4},{4,0},{2,6},{6,2},{1,5},{5,1},{3,7},{7,3},{8,12},{12,8},{10,... | collective-permute-start | bytes 49160 | tf_op jit(solution)/shard_map/ppermute | solution.py:803
  34.1 10.7 %copy-start = (f32[32,8,256]{2,1,0:T(8,128)S(1)}, f32[32,8,256]{2,1,0:T(8,128)}, u32[]{:S(2)}) copy-start(f32[32,8,256]{2,1,0:T(8,128)} %kappa_ref.1) | copy-start | bytes 786436
  34.1 10.7 %copy-start.1 = (f32[32,8,256]{2,1,0:T(8,128)S(1)}, f32[32,8,256]{2,1,0:T(8,128)}, u32[]{:S(2)}) copy-start(f32[32,8,256]{2,1,0:T(8,128)} %observed_ref.1) | copy-start | bytes 786436
  39.4 1.4 %collective-permute-start.11 = (f32[2,16,8,128]{3,2,1,0:T(8,128)S(1)}, f32[2,16,8,128]{3,2,1,0:T(8,128)S(1)}, u32[]{:S(2)}, u32[]{:S(2)}) collective-permute-start(f32[2,16,8,128]{3,2,1,0:T(8,128)S(1)} %get-tuple-element.38), channel_id=1, source_target_pairs={{0,8},{8,0},{16,24},{24,16},{1,9},{9,1},{17,25},{25,17},{2,10},{10... | collective-permute-start | bytes 393224 | tf_op jit(solution)/shard_map/ppermute | solution.py:816
  40.8 4.9 %collective-permute-start.13 = (f32[16,8,128]{2,1,0:T(8,128)S(1)}, f32[16,8,128]{2,1,0:T(8,128)S(1)}, u32[]{:S(2)}, u32[]{:S(2)}) collective-permute-start(f32[16,8,128]{2,1,0:T(8,128)S(1)} %get-tuple-element.41), channel_id=1, source_target_pairs={{0,1},{8,9},{16,17},{24,25},{1,16},{9,24},{17,0},{25,8},{2,3},{10,... | collective-permute-start | bytes 196616 | tf_op jit(solution)/shard_map/ppermute | solution.py:825
  42.3 6.1 %collective-permute-start.12 = (f32[16,8,128]{2,1,0:T(8,128)S(1)}, f32[16,8,128]{2,1,0:T(8,128)S(1)}, u32[]{:S(2)}, u32[]{:S(2)}) collective-permute-start(f32[16,8,128]{2,1,0:T(8,128)S(1)} %get-tuple-element.42.straight_ref), channel_id=1, source_target_pairs={{1,17},{9,25},{17,1},{25,9},{3,19},{11,27},{19,3},{27,11},{5,21},{... | collective-permute-start | bytes 196616 | tf_op jit(solution)/shard_map/ppermute | solution.py:831

commit v9 on v8

--- a/solution.py
+++ b/solution.py
@@ -698,17 +698,28 @@
     def swaps(pairs):
         return [way for a, b in pairs for way in ((a, b), (b, a))]
 
-    even_pairs = [(i, i + 1) for i in range(0, tile_count - 1, 2)]
-    odd_pairs = [(i, i + 1) for i in range(1, tile_count - 1, 2)]
+    def tile_swap(block, first, flip):
+        partner = dict(swaps([(i, i + 1) for i in range(first, tile_count - 1, 2)]))
+
+        def device(probe, tile, level):
+            return (probe * tile_count + tile) * 2 + level
+
+        ways = []
+        for probe in range(probes):
+            for tile in range(tile_count):
+                for level in range(2):
+                    if tile in partner:
+                        target = device(probe, partner[tile], level ^ flip)
+                    else:
+                        target = device(probe ^ 1, tile, level)
+                    ways.append((device(probe, tile, level), target))
+        return lax.ppermute(block, ("probe", "tile", "level"), ways)
+
     own_far = lax.ppermute(cross_block, "level", swaps([(0, 1)]))
-    even = lax.ppermute(even_block, "tile", swaps(even_pairs))
-    odd = lax.ppermute(odd_block, "tile", swaps(odd_pairs))
-    odd_far = lax.ppermute(own_far, "tile", swaps(odd_pairs))
-    even_far = lax.ppermute(
-        cross_block,
-        ("tile", "level"),
-        swaps([(2 * a + level, 2 * b + 1 - level) for a, b in even_pairs for level in range(2)]),
-    )
+    even = tile_swap(even_block, 0, 0)
+    odd = tile_swap(odd_block, 1, 0)
+    odd_far = tile_swap(own_far, 1, 0)
+    even_far = tile_swap(cross_block, 0, 1)
 
     quarter = jax.ShapeDtypeStruct((depth, ROWS, columns // probes), f32)
     paired = jax.ShapeDtypeStruct((depth // 2, ROWS, LANES), f32)
@@ -831,7 +842,8 @@
     trace_b = lax.ppermute(
         straight,
         ("probe", "level"),
-        [(device(x, core, 1), device(1 - x, core, 1)) for x, core in chips],
+        [(device(x, core, 1), device(1 - x, core, 1)) for x, core in chips]
+        + [(device(x, core, 0), device(x, 1 - core, 0)) for x, core in chips],
     )
     return pl.pallas_call(
         functools.partial(gradient_kernel, depth),

time: 49.6 us -> 48.2 us (0.972)
  the two profiles are of different devices: /device:TPU:20 before, /device:TPU:0 now
where the time goes in v9:
time: 48.2 us; the launch traced here: 48.1 us
  waiting for transfers between devices  17 us (35%)
  Pallas kernels  15.8 us (33%)
  starting transfers between devices  15 us (31%)
    pallas_call x1, Pallas kernels, body(): pl.pallas_call(functools.partial(basis_kernel, depth), out_shape=(fields,...  8.94 us
    ppermute x4, waiting for transfers between devices, tile_swap(): return lax.ppermute(block, ('probe', 'tile', 'level'), ways)  6.08 us
    ppermute x4, starting transfers between devices, tile_swap(): return lax.ppermute(block, ('probe', 'tile', 'level'), ways)  4.67 us
    ppermute x1, waiting for transfers between devices, body(): lax.ppermute(turned, ('probe', 'level'), [(device(x, core, 0), device(x,...  4.23 us
    ppermute x3, starting transfers between devices, body(): lax.ppermute(gram, ('tile', 'level'), swaps([(i, i ^ k) for i in range(2...  3.55 us
    ppermute x3, waiting for transfers between devices, body(): lax.ppermute(gram, ('tile', 'level'), swaps([(i, i ^ k) for i in range(2...  3.25 us
    ppermute x1, starting transfers between devices, body(): own_far = lax.ppermute(cross_block, 'level', swaps([(0, 1)]))  3.03 us
    ppermute x1, starting transfers between devices, body(): partials.append(lax.ppermute(partials[0], 'tile', swaps([(0, 2), (1, 3)])))  2.66 us
  transfers between devices with their start and end apart: 14, of which 7 were waited for; matrix products, arithmetic and copies ran while one was open for 0% of the time, Pallas kernels for 8%

profile of v9, /device:TPU:0, one launch (start us, length us, event | category | flops | bytes accessed | tf_op | source)
XLA Modules:
  0.0 48.1 jit_solution(14987105450068350901)
XLA Ops:
  0.0 1.6 %pack.1 = (f32[68,8,128]{2,1,0:T(8,128)S(1)}, f32[55,8,128]{2,1,0:T(8,128)S(1)}, f32[55,8,128]{2,1,0:T(8,128)S(1)}, f32[52,8,128]{2,1,0:T(8,128)S(1)}) custom-call(s32[32,8,256]{2,1,0:T(8,128)} %bitcast.5, f32[32,8,256]{2,1,0:T(8,128)} %kappa_ref.1, f32[32,8,256]{2,1,0:T(8,128)} %observed_ref.1), custom_call_target="tpu_custom_call" | custom-call | tf_op jit(solution)/shard_map/pack/pallas_call | solution.py:678
  1.6 3.0 %collective-permute-start.2 = (f32[52,8,128]{2,1,0:T(8,128)S(1)}, f32[52,8,128]{2,1,0:T(8,128)S(1)}, u32[]{:S(2)}, u32[]{:S(2)}) collective-permute-start(f32[52,8,128]{2,1,0:T(8,128)S(1)} %get-tuple-element.26), channel_id=1, source_target_pairs={{0,1},{1,0},{2,3},{3,2},{4,5},{5,4},{6,7},{7,6},{8,9},{9,8},{10,11... | collective-permute-start | bytes 638984 | tf_op jit(solution)/shard_map/ppermute | solution.py:718
  4.7 1.6 %collective-permute-start = (f32[55,8,128]{2,1,0:T(8,128)S(1)}, f32[55,8,128]{2,1,0:T(8,128)S(1)}, u32[]{:S(2)}, u32[]{:S(2)}) collective-permute-start(f32[55,8,128]{2,1,0:T(8,128)S(1)} %get-tuple-element.24), channel_id=1, source_target_pairs={{0,2},{1,3},{2,0},{3,1},{4,6},{5,7},{6,4},{7,5},{8,10},{9,11},{10,... | collective-permute-start | bytes 675848 | tf_op jit(solution)/shard_map/ppermute | solution.py:716
  6.2 0.0 collective-permute-start.1
  6.2 3.1 %collective-permute-start.4 = (f32[52,8,128]{2,1,0:T(8,128)S(1)}, f32[52,8,128]{2,1,0:T(8,128)S(1)}, u32[]{:S(2)}, u32[]{:S(2)}) collective-permute-start(f32[52,8,128]{2,1,0:T(8,128)S(1)} %get-tuple-element.26), channel_id=1, source_target_pairs={{0,3},{1,2},{2,1},{3,0},{4,7},{5,6},{6,5},{7,4},{8,11},{9,10},{10,... | collective-permute-start | bytes 638984 | tf_op jit(solution)/shard_map/ppermute | solution.py:716
  9.3 0.6 %collective-permute-done.2.own_far_ref.far_ref = f32[52,8,128]{2,1,0:T(8,128)S(1)} collective-permute-done((f32[52,8,128]{2,1,0:T(8,128)S(1)}, f32[52,8,128]{2,1,0:T(8,128)S(1)}, u32[]{:S(2)}, u32[]{:S(2)}) %collective-permute-start.2) | collective-permute-done | bytes 213024 | tf_op jit(solution)/shard_map/ppermute | solution.py:718
  9.9 0.0 collective-permute-start.5
  9.9 6.1 %collective-permute-done.4.even_far_ref = f32[52,8,128]{2,1,0:T(8,128)S(1)} collective-permute-done((f32[52,8,128]{2,1,0:T(8,128)S(1)}, f32[52,8,128]{2,1,0:T(8,128)S(1)}, u32[]{:S(2)}, u32[]{:S(2)}) %collective-permute-start.4) | collective-permute-done | bytes 213024 | tf_op jit(solution)/shard_map/ppermute | solution.py:716
  16.0 0.0 collective-permute-done.even_ref
  16.0 0.0 collective-permute-done.1.odd_ref
  16.1 0.1 collective-permute-start.3
  16.2 0.0 collective-permute-done.5.odd_far_ref
  16.2 0.5 %collective-permute-start.6 = (f32[34,8,128]{2,1,0:T(8,128)S(1)}, f32[34,8,128]{2,1,0:T(8,128)S(1)}, u32[]{:S(2)}, u32[]{:S(2)}) collective-permute-start(f32[34,8,128]{2,1,0:T(8,128)S(1)} %pad_maximum_fusion.1), channel_id=1, source_target_pairs={{0,8},{8,0},{16,24},{24,16},{1,9},{9,1},{17,25},{25,17},{2,10},{10... | collective-permute-start | bytes 417800 | tf_op jit(solution)/shard_map/ppermute | solution.py:737
  16.7 0.9 %collective-permute-done.3.swapped_ref = f32[51,8,128]{2,1,0:T(8,128)S(1)} collective-permute-done((f32[51,8,128]{2,1,0:T(8,128)S(1)}, f32[51,8,128]{2,1,0:T(8,128)S(1)}, u32[]{:S(2)}, u32[]{:S(2)}) %collective-permute-start.3) | collective-permute-done | bytes 208928 | tf_op jit(solution)/shard_map/ppermute | solution.py:737
  17.6 1.3 %near.1 = (f32[32,24,256]{2,1,0:T(8,128)S(1)}, f32[32,24,256]{2,1,0:T(8,128)S(1)}, f32[32,24,256]{2,1,0:T(8,128)S(1)}, f32[32,8,256]{2,1,0:T(8,128)S(1)}, f32[32,8,256]{2,1,0:T(8,128)S(1)}) custom-call(f32[68,8,128]{2,1,0:T(8,128)S(1)} %get-tuple-element.23.own_ref, f32[55,8,128]{2,1,0:T(8,128)S(1)} %collective-permute-done.even_ref, ...), custom_call_target="tpu_custom_call" | custom-call | tf_op jit(solution)/shard_map/near/pallas_call | solution.py:743
  18.9 0.0 collective-permute-done.6.swapped_far_ref
  18.9 8.9 %basis.1 = (f32[4,64,8,256]{3,2,1,0:T(8,128)S(1)}, f32[4,64,8,256]{3,2,1,0:T(8,128)S(1)}, f32[32,8,256]{2,1,0:T(8,128)S(1)}, f32[32,8,256]{2,1,0:T(8,128)S(1)}, f32[8,128]{1,0:T(8,128)S(1)}) custom-call(f32[32,24,256]{2,1,0:T(8,128)S(1)} %get-tuple-element.27.near_diag, f32[32,24,256]{2,1,0:T(8,128)S(1)} %get-tuple-element.28.near_lower, ...), custom_call_target="tpu_custom_call" | custom-call | tf_op jit(solution)/shard_map/basis/pallas_call | solution.py:758
  27.9 2.7 %collective-permute-start.9 = (f32[8,128]{1,0:T(8,128)S(1)}, f32[8,128]{1,0:T(8,128)S(1)}, u32[]{:S(2)}, u32[]{:S(2)}) collective-permute-start(f32[8,128]{1,0:T(8,128)S(1)} %get-tuple-element.36), channel_id=1, source_target_pairs={{0,3},{3,0},{1,2},{2,1},{4,7},{7,4},{5,6},{6,5},{8,11},{11,8},{9,1... | collective-permute-start | bytes 12296 | tf_op jit(solution)/shard_map/ppermute | solution.py:805
  30.6 0.4 collective-permute-start.8
  31.1 0.4 collective-permute-start.7
  31.4 3.2 %collective-permute-done.7 = f32[8,128]{1,0:T(8,128)S(1)} collective-permute-done((f32[8,128]{1,0:T(8,128)S(1)}, f32[8,128]{1,0:T(8,128)S(1)}, u32[]{:S(2)}, u32[]{:S(2)}) %collective-permute-start.7) | collective-permute-done | bytes 4128 | tf_op jit(solution)/shard_map/ppermute | solution.py:805
  34.7 0.0 collective-permute-done.8
  34.7 0.0 collective-permute-done.9
  34.7 2.7 %collective-permute-start.10 = (f32[32,128]{1,0:T(8,128)S(1)}, f32[32,128]{1,0:T(8,128)S(1)}, u32[]{:S(2)}, u32[]{:S(2)}) collective-permute-start(f32[32,128]{1,0:T(8,128)S(1)} %constant_dynamic-update-slice_fusion.refs_0_), channel_id=1, source_target_pairs={{0,4},{4,0},{2,6},{6,2},{1,5},{5,1},{3,7},{7,3},{8,12},{12,8},{10,... | collective-permute-start | bytes 49160 | tf_op jit(solution)/shard_map/ppermute | solution.py:814
  37.4 0.0 copy-start
  37.4 0.0 copy-start.1
  37.4 1.4 %terms.1.terms_ref = f32[4,64,8,128]{3,2,1,0:T(8,128)S(1)} custom-call(f32[4,64,8,256]{3,2,1,0:T(8,128)S(1)} %get-tuple-element.31.basis_ref, f32[4,64,8,256]{3,2,1,0:T(8,128)S(1)} %get-tuple-element.32.image_ref, f32[32,8,256]{2,1,0:T(8,128)S(1)} %get-tuple-element.30.near_signs, f32[32,8,256]{2,1,0:T(8,128)S(1)} %get-tuple-element.33.near_k_signs, ...), custom_call_target="tpu_custom_call" | custom-call | tf_op jit(solution)/shard_map/terms/pallas_call | solution.py:794
  38.8 0.6 %collective-permute-done.10.refs_1_ = f32[32,128]{1,0:T(8,128)S(1)} collective-permute-done((f32[32,128]{1,0:T(8,128)S(1)}, f32[32,128]{1,0:T(8,128)S(1)}, u32[]{:S(2)}, u32[]{:S(2)}) %collective-permute-start.10) | collective-permute-done | bytes 16416 | tf_op jit(solution)/shard_map/ppermute | solution.py:814
  39.4 0.6 %combine.1 = (f32[2,16,8,128]{3,2,1,0:T(8,128)S(1)}, f32[2,16,8,128]{3,2,1,0:T(8,128)S(1)}) custom-call(f32[4,64,8,128]{3,2,1,0:T(8,128)S(1)} %terms.1.terms_ref, f32[32,128]{1,0:T(8,128)S(1)} %constant_dynamic-update-slice_fusion.refs_0_, f32[32,128]{1,0:T(8,128)S(1)} %collective-permute-done.10.refs_1_), custom_call_target="tpu_custom_call" | custom-call | tf_op jit(solution)/shard_map/combine/pallas_call | solution.py:818
  40.1 0.1 collective-permute-start.11
  40.2 1.3 %collective-permute-done.11 = f32[2,16,8,128]{3,2,1,0:T(8,128)S(1)} collective-permute-done((f32[2,16,8,128]{3,2,1,0:T(8,128)S(1)}, f32[2,16,8,128]{3,2,1,0:T(8,128)S(1)}, u32[]{:S(2)}, u32[]{:S(2)}) %collective-permute-start.11) | collective-permute-done | bytes 131104 | tf_op jit(solution)/shard_map/ppermute | solution.py:827
  41.5 0.4 collective-permute-start.13
  41.9 0.0 collective-permute-start.12
  42.0 0.0 copy-done
  42.0 0.0 copy-done.1
  42.0 1.0 %observed.1 = (f32[16,8,128]{2,1,0:T(8,128)S(1)}, f32[16,8,128]{2,1,0:T(8,128)S(1)}) custom-call(f32[32,8,256]{2,1,0:T(8,128)S(1)} %copy-done, f32[32,8,256]{2,1,0:T(8,128)S(1)} %copy-done.1, f32[55,8,128]{2,1,0:T(8,128)S(1)} %collective-permute-done.even_ref, f32[55,8,128]{2,1,0:T(8,128)S(1)} %collective-permute-done.1.odd_ref, ...), custom_call_target="tpu_custom_call" | custom-call | tf_op jit(solution)/shard_map/observed/pallas_call | solution.py:726
  42.9 4.2 %collective-permute-done.13.trace_a_ref = f32[16,8,128]{2,1,0:T(8,128)S(1)} collective-permute-done((f32[16,8,128]{2,1,0:T(8,128)S(1)}, f32[16,8,128]{2,1,0:T(8,128)S(1)}, u32[]{:S(2)}, u32[]{:S(2)}) %collective-permute-start.13) | collective-permute-done | bytes 65568 | tf_op jit(solution)/shard_map/ppermute | solution.py:836
  47.2 0.0 collective-permute-done.12.trace_b_ref
  47.2 0.9 %gradient.1 = f32[32,8,64]{2,1,0:T(8,128)} custom-call(f32[16,8,128]{2,1,0:T(8,128)S(1)} %collective-permute-done.12.trace_b_ref, f32[16,8,128]{2,1,0:T(8,128)S(1)} %collective-permute-done.13.trace_a_ref, f32[16,8,128]{2,1,0:T(8,128)S(1)} %get-tuple-element.42.straight_ref, f32[16,8,128]{2,1,0:T(8,128)S(1)} %get-tuple-element.39.factor_ref, ...), custom_call_target="tpu_custom_call" | custom-call | tf_op jit(solution)/shard_map/gradient/pallas_call | solution.py:848
  (13 shorter events, 0.1 us)
Async XLA Ops:
  1.6 8.3 %collective-permute-start.2 = (f32[52,8,128]{2,1,0:T(8,128)S(1)}, f32[52,8,128]{2,1,0:T(8,128)S(1)}, u32[]{:S(2)}, u32[]{:S(2)}) collective-permute-start(f32[52,8,128]{2,1,0:T(8,128)S(1)} %get-tuple-element.26), channel_id=1, source_target_pairs={{0,1},{1,0},{2,3},{3,2},{4,5},{5,4},{6,7},{7,6},{8,9},{9,8},{10,11... | collective-permute-start | bytes 638984 | tf_op jit(solution)/shard_map/ppermute | solution.py:718
  4.7 11.3 %collective-permute-start = (f32[55,8,128]{2,1,0:T(8,128)S(1)}, f32[55,8,128]{2,1,0:T(8,128)S(1)}, u32[]{:S(2)}, u32[]{:S(2)}) collective-permute-start(f32[55,8,128]{2,1,0:T(8,128)S(1)} %get-tuple-element.24), channel_id=1, source_target_pairs={{0,2},{1,3},{2,0},{3,1},{4,6},{5,7},{6,4},{7,5},{8,10},{9,11},{10,... | collective-permute-start | bytes 675848 | tf_op jit(solution)/shard_map/ppermute | solution.py:716
  6.2 9.8 %collective-permute-start.1 = (f32[55,8,128]{2,1,0:T(8,128)S(1)}, f32[55,8,128]{2,1,0:T(8,128)S(1)}, u32[]{:S(2)}, u32[]{:S(2)}) collective-permute-start(f32[55,8,128]{2,1,0:T(8,128)S(1)} %get-tuple-element.25), channel_id=1, source_target_pairs={{0,8},{1,9},{2,4},{3,5},{4,2},{5,3},{6,14},{7,15},{8,0},{9,1},{10,... | collective-permute-start | bytes 675848 | tf_op jit(solution)/shard_map/ppermute | solution.py:716
  6.2 9.8 %collective-permute-start.4 = (f32[52,8,128]{2,1,0:T(8,128)S(1)}, f32[52,8,128]{2,1,0:T(8,128)S(1)}, u32[]{:S(2)}, u32[]{:S(2)}) collective-permute-start(f32[52,8,128]{2,1,0:T(8,128)S(1)} %get-tuple-element.26), channel_id=1, source_target_pairs={{0,3},{1,2},{2,1},{3,0},{4,7},{5,6},{6,5},{7,4},{8,11},{9,10},{10,... | collective-permute-start | bytes 638984 | tf_op jit(solution)/shard_map/ppermute | solution.py:716
  9.9 6.2 %collective-permute-start.5 = (f32[52,8,128]{2,1,0:T(8,128)S(1)}, f32[52,8,128]{2,1,0:T(8,128)S(1)}, u32[]{:S(2)}, u32[]{:S(2)}) collective-permute-start(f32[52,8,128]{2,1,0:T(8,128)S(1)} %collective-permute-done.2.own_far_ref.far_ref), channel_id=1, source_target_pairs={{0,8},{1,9},{2,4},{3,5},{4,2},{5,3},{6,14},{7,15},{8,0},{9,1},{10,... | collective-permute-start | bytes 638984 | tf_op jit(solution)/shard_map/ppermute | solution.py:716
  16.1 1.5 %collective-permute-start.3 = (f32[51,8,128]{2,1,0:T(8,128)S(1)}, f32[51,8,128]{2,1,0:T(8,128)S(1)}, u32[]{:S(2)}, u32[]{:S(2)}) collective-permute-start(f32[51,8,128]{2,1,0:T(8,128)S(1)} %pad_maximum_fusion), channel_id=1, source_target_pairs={{0,8},{8,0},{16,24},{24,16},{1,9},{9,1},{17,25},{25,17},{2,10},{10... | collective-permute-start | bytes 626696 | tf_op jit(solution)/shard_map/ppermute | solution.py:737
  16.2 2.7 %collective-permute-start.6 = (f32[34,8,128]{2,1,0:T(8,128)S(1)}, f32[34,8,128]{2,1,0:T(8,128)S(1)}, u32[]{:S(2)}, u32[]{:S(2)}) collective-permute-start(f32[34,8,128]{2,1,0:T(8,128)S(1)} %pad_maximum_fusion.1), channel_id=1, source_target_pairs={{0,8},{8,0},{16,24},{24,16},{1,9},{9,1},{17,25},{25,17},{2,10},{10... | collective-permute-start | bytes 417800 | tf_op jit(solution)/shard_map/ppermute | solution.py:737
  27.9 6.8 %collective-permute-start.9 = (f32[8,128]{1,0:T(8,128)S(1)}, f32[8,128]{1,0:T(8,128)S(1)}, u32[]{:S(2)}, u32[]{:S(2)}) collective-permute-start(f32[8,128]{1,0:T(8,128)S(1)} %get-tuple-element.36), channel_id=1, source_target_pairs={{0,3},{3,0},{1,2},{2,1},{4,7},{7,4},{5,6},{6,5},{8,11},{11,8},{9,1... | collective-permute-start | bytes 12296 | tf_op jit(solution)/shard_map/ppermute | solution.py:805
  30.6 4.1 %collective-permute-start.8 = (f32[8,128]{1,0:T(8,128)S(1)}, f32[8,128]{1,0:T(8,128)S(1)}, u32[]{:S(2)}, u32[]{:S(2)}) collective-permute-start(f32[8,128]{1,0:T(8,128)S(1)} %get-tuple-element.36), channel_id=1, source_target_pairs={{0,2},{2,0},{1,3},{3,1},{4,6},{6,4},{5,7},{7,5},{8,10},{10,8},{9,1... | collective-permute-start | bytes 12296 | tf_op jit(solution)/shard_map/ppermute | solution.py:805
  31.1 3.6 %collective-permute-start.7 = (f32[8,128]{1,0:T(8,128)S(1)}, f32[8,128]{1,0:T(8,128)S(1)}, u32[]{:S(2)}, u32[]{:S(2)}) collective-permute-start(f32[8,128]{1,0:T(8,128)S(1)} %get-tuple-element.36), channel_id=1, source_target_pairs={{0,1},{1,0},{2,3},{3,2},{4,5},{5,4},{6,7},{7,6},{8,9},{9,8},{10,11... | collective-permute-start | bytes 12296 | tf_op jit(solution)/shard_map/ppermute | solution.py:805
  34.7 4.7 %collective-permute-start.10 = (f32[32,128]{1,0:T(8,128)S(1)}, f32[32,128]{1,0:T(8,128)S(1)}, u32[]{:S(2)}, u32[]{:S(2)}) collective-permute-start(f32[32,128]{1,0:T(8,128)S(1)} %constant_dynamic-update-slice_fusion.refs_0_), channel_id=1, source_target_pairs={{0,4},{4,0},{2,6},{6,2},{1,5},{5,1},{3,7},{7,3},{8,12},{12,8},{10,... | collective-permute-start | bytes 49160 | tf_op jit(solution)/shard_map/ppermute | solution.py:814
  37.4 4.6 %copy-start = (f32[32,8,256]{2,1,0:T(8,128)S(1)}, f32[32,8,256]{2,1,0:T(8,128)}, u32[]{:S(2)}) copy-start(f32[32,8,256]{2,1,0:T(8,128)} %kappa_ref.1) | copy-start | bytes 786436
  37.4 4.6 %copy-start.1 = (f32[32,8,256]{2,1,0:T(8,128)S(1)}, f32[32,8,256]{2,1,0:T(8,128)}, u32[]{:S(2)}) copy-start(f32[32,8,256]{2,1,0:T(8,128)} %observed_ref.1) | copy-start | bytes 786436
  40.1 1.4 %collective-permute-start.11 = (f32[2,16,8,128]{3,2,1,0:T(8,128)S(1)}, f32[2,16,8,128]{3,2,1,0:T(8,128)S(1)}, u32[]{:S(2)}, u32[]{:S(2)}) collective-permute-start(f32[2,16,8,128]{3,2,1,0:T(8,128)S(1)} %get-tuple-element.38), channel_id=1, source_target_pairs={{0,8},{8,0},{16,24},{24,16},{1,9},{9,1},{17,25},{25,17},{2,10},{10... | collective-permute-start | bytes 393224 | tf_op jit(solution)/shard_map/ppermute | solution.py:827
  41.5 5.6 %collective-permute-start.13 = (f32[16,8,128]{2,1,0:T(8,128)S(1)}, f32[16,8,128]{2,1,0:T(8,128)S(1)}, u32[]{:S(2)}, u32[]{:S(2)}) collective-permute-start(f32[16,8,128]{2,1,0:T(8,128)S(1)} %get-tuple-element.41), channel_id=1, source_target_pairs={{0,1},{8,9},{16,17},{24,25},{1,16},{9,24},{17,0},{25,8},{2,3},{10,... | collective-permute-start | bytes 196616 | tf_op jit(solution)/shard_map/ppermute | solution.py:836
  41.9 5.2 %collective-permute-start.12 = (f32[16,8,128]{2,1,0:T(8,128)S(1)}, f32[16,8,128]{2,1,0:T(8,128)S(1)}, u32[]{:S(2)}, u32[]{:S(2)}) collective-permute-start(f32[16,8,128]{2,1,0:T(8,128)S(1)} %get-tuple-element.42.straight_ref), channel_id=1, source_target_pairs={{1,17},{9,25},{17,1},{25,9},{0,8},{8,0},{16,24},{24,16},{3,19},{11... | collective-permute-start | bytes 196616 | tf_op jit(solution)/shard_map/ppermute | solution.py:842

commit v10 on v9

--- a/solution.py
+++ b/solution.py
@@ -11,6 +11,7 @@
 VERTICAL = 2.0
 LANES = 128
 ROWS = 8
+HALO = ROWS - 1
 EDGE = 8
 GROUP = 8
 SHIFTS = (1.0, -1.0, 0.0)
@@ -90,6 +91,7 @@
     even_ref,
     odd_ref,
     cross_ref,
+    diagonal_ref,
     bits_ref,
     kappa_ref,
     observed_ref,
@@ -108,7 +110,6 @@
     in_first_core = lax.rem(lax.axis_index("probe"), 2) == 0
     per_tile = LANES // EDGE
     tiles = depth // per_tile
-    field = depth + tiles
     slot_ids = (lane_ids((ROWS, LANES)) % (LANES // 2)) // (EDGE // 2)
     same_columns, cross_columns = columns_of(y_half()), columns_of(1 - y_half())
 
@@ -122,28 +123,42 @@
             edges.append(packed)
         return [picked[z, :, :LANES] for z in range(depth)], edges
 
-    def write(refs, base, values):
-        for place, value in enumerate(values):
-            for ref in refs:
-                ref[base + place] = value
+    goes_up = lax.rem(lax.axis_index("tile"), 2) == 0
+
+    def write(ref, base, main, edges, up=None):
+        if up is not None:
+            main = [jnp.where(up, pltpu.roll(tile, HALO, 0), tile)[:HALO] for tile in main]
+        for tile in main + edges:
+            ref[base : base + tile.shape[0]] = tile
+            base += tile.shape[0]
+        return base
+
+    def halves(main, edges):
+        low = main[: depth // 2] + edges[: tiles // 2]
+        high = main[depth // 2 :] + edges[tiles // 2 :]
+        both = [jnp.where(in_first_core, a, b) for a, b in zip(low, high)]
+        return both[: depth // 2], both[depth // 2 :]
 
     copies[0].wait()
     signs = (2 * bits_ref[...] - 1).astype(jnp.float32).reshape(depth * ROWS, 2 * LANES)
     signs = signs.astype(jnp.bfloat16)
-    for refs, chosen in (((own_ref, even_ref, odd_ref), same_columns), ((cross_ref,), cross_columns)):
-        main, edges = blocks(jnp.dot(signs, chosen, preferred_element_type=jnp.float32))
-        write(refs, 0, main + edges)
+    same = blocks(jnp.dot(signs, same_columns, preferred_element_type=jnp.float32))
+    cross = blocks(jnp.dot(signs, cross_columns, preferred_element_type=jnp.float32))
+    own_base = write(own_ref, 0, *same)
+    even_base = write(even_ref, 0, *same, goes_up)
+    write(odd_ref, 0, *same, ~goes_up)
+    cross_base = write(cross_ref, 0, *cross)
+    write(diagonal_ref, 0, *cross, goes_up)
     copies[1].wait()
     kappa = kappa_ref[...].reshape(depth * ROWS, 2 * LANES)
-    for refs, chosen in (((even_ref, odd_ref), same_columns), ((cross_ref,), cross_columns)):
-        main, edges = blocks(pick(kappa, chosen))
-        if len(refs) == 2:
-            write((own_ref,), field, main + edges)
-        low = main[: depth // 2] + edges[: tiles // 2]
-        high = main[depth // 2 :] + edges[tiles // 2 :]
-        write(refs, field, [jnp.where(in_first_core, a, b) for a, b in zip(low, high)])
+    same = blocks(pick(kappa, same_columns))
+    write(own_ref, own_base, *same)
+    same, cross = halves(*same), halves(*blocks(pick(kappa, cross_columns)))
+    write(odd_ref, even_base, *same, ~goes_up)
+    cross_base = write(cross_ref, cross_base, *cross)
+    write(diagonal_ref, even_base, *cross, goes_up)
+    even_base = write(even_ref, even_base, *same, goes_up)
     copies[2].wait()
-    base = field + field // 2
     in_low = lax.axis_index("probe") < lax.axis_size("probe") // 2
 
     def half(value):
@@ -151,12 +166,9 @@
 
     top = half(observed_ref[:, ROWS - 1, :])
     bottom = half(observed_ref[:, 0, :])
-    goes_up = lax.rem(lax.axis_index("tile"), 2) == 0
-    for tile in range(depth // ROWS):
-        here = slice(tile * ROWS, (tile + 1) * ROWS)
-        even_ref[base + tile] = jnp.where(goes_up, top[here], bottom[here])
-        odd_ref[base + tile] = jnp.where(goes_up, bottom[here], top[here])
-    cross_ref[base] = jnp.where(first, half(observed_ref[depth - 1]), half(observed_ref[0]))
+    even_ref[even_base:] = jnp.where(goes_up, top, bottom)
+    odd_ref[even_base:] = jnp.where(goes_up, bottom, top)
+    cross_ref[cross_base:] = jnp.where(first, half(observed_ref[depth - 1]), half(observed_ref[0]))
 
 
 def beside(values):
@@ -203,28 +215,36 @@
     def place(z):
         return jnp.where(level == 0, z, depth - 1 - z)
 
-    def sign_level(z, unused):
-        pieces = [(ref[z], ref[depth + z // per_tile]) for ref in sign_pieces]
-        signs[place(z) + 1] = join(z, *pieces) * mask
-        return unused
-
-    lax.fori_loop(0, depth, sign_level, 0, unroll=per_tile)
+    def load(piece, count, z):
+        ref, base, height, side = piece
+        edge = base + height * count + ROWS * (z // per_tile)
+        main = ref[base + height * z : base + height * z + ROWS]
+        if side is not None:
+            main = jnp.where(side, pltpu.roll(main, 1, 0), main)
+        return main, ref[edge : edge + ROWS]
+
+    for z in range(depth):
+        signs[place(z) + 1] = join(z, *(load(piece, depth, z) for piece in sign_pieces)) * mask
     core = lax.rem(lax.axis_index("probe"), 2)
+    short = depth // 2
     for start, pieces in zip((core, 1 - core), kappa_pieces):
-        start = start * (depth // 2)
-
-        def kappa_level(step, unused, start=start, pieces=pieces):
-            z = start + step
+        for step in range(short):
+            z = start * short + step
             tiles = []
-            for ref, base, whole_field in pieces:
-                if whole_field:
-                    tiles.append((ref[base + z], ref[base + depth + z // per_tile]))
+            for piece in pieces:
+                if len(piece) == 2:
+                    ref, base = piece
+                    main = pl.multiple_of(base + ROWS * z, ROWS)
+                    edge = base + ROWS * (depth + start * (short // per_tile) + step // per_tile)
+                    edge = pl.multiple_of(edge, ROWS)
+                    tiles.append((ref[pl.ds(main, ROWS)], ref[pl.ds(edge, ROWS)]))
                 else:
-                    tiles.append((ref[base + step], ref[base + depth // 2 + step // per_tile]))
-            half_diag[place(z)] = 0.5 * join(z, *tiles) + (2.0 + VERTICAL)
-            return unused
-
-        lax.fori_loop(0, depth // 2, kappa_level, 0, unroll=per_tile)
+                    tiles.append(load(piece, short, step))
+            half_diag[place(z)] = 0.5 * join(step, *tiles) + (2.0 + VERTICAL)
+
+
+def from_above():
+    return lax.rem(lax.axis_index("tile"), 2) == 1
 
 
 OWN_ROWS = slice(ROWS, 2 * ROWS)
@@ -243,16 +263,23 @@
     k_signs,
     signs,
 ):
-    field = own_ref.shape[0] // 2
+    tiles = depth * EDGE // LANES
+    field, thin = ROWS * (depth + tiles), HALO * depth + ROWS * tiles
     mask = inside_mask()
     zero = jnp.zeros(mask.shape, jnp.float32)
     signs[0] = zero
     signs[depth + 1] = zero
+    above = from_above()
     kappa_pieces = (
-        ((even_ref, field, False), (own_ref, field, True), (odd_ref, field, False)),
-        ((swapped_ref, 0, False), (own_ref, field, True), (swapped_ref, field // 2, False)),
-    )
-    unpack(depth, signs, half_diag, mask, (even_ref, own_ref, odd_ref), kappa_pieces)
+        ((even_ref, thin, HALO, above), (own_ref, field), (odd_ref, thin, HALO, ~above)),
+        ((swapped_ref, 0, HALO, above), (own_ref, field), (swapped_ref, thin // 2, HALO, ~above)),
+    )
+    sign_pieces = (
+        (even_ref, 0, HALO, above),
+        (own_ref, 0, ROWS, None),
+        (odd_ref, 0, HALO, ~above),
+    )
+    unpack(depth, signs, half_diag, mask, sign_pieces, kappa_pieces)
 
     def down(k, carry):
         ratio, value = carry
@@ -303,7 +330,9 @@
     zero = jnp.zeros(mask.shape, jnp.float32)
     own_zero = jnp.zeros((ROWS, LANES), jnp.float32)
     mine = lane_ids((ROWS, LANES)) < LANES // 2
-    field = swapped_ref.shape[0] // 3 * 2
+    tiles = depth * EDGE // LANES
+    field, thin = ROWS * (depth + tiles), HALO * depth + ROWS * tiles
+    above = from_above()
     signs[0] = zero
     signs[0, OWN_ROWS] = near_signs[depth - 1]
     signs[depth + 1] = zero
@@ -311,14 +340,23 @@
     upper[levels] = zero
     basis[levels] = zero
     kappa_pieces = (
-        tuple((ref, field, False) for ref in (even_far_ref, own_far_ref, odd_far_ref)),
         (
-            (swapped_far_ref, 0, False),
-            (swapped_ref, field, False),
-            (swapped_far_ref, field // 2, False),
+            (even_far_ref, thin, HALO, above),
+            (own_far_ref, field, ROWS, None),
+            (odd_far_ref, field, ROWS, None),
         ),
-    )
-    unpack(depth, signs, far_diag, mask, (even_far_ref, own_far_ref, odd_far_ref), kappa_pieces)
+        (
+            (swapped_far_ref, 0, HALO, above),
+            (swapped_ref, thin, ROWS, None),
+            (swapped_far_ref, thin // 2, ROWS, None),
+        ),
+    )
+    sign_pieces = (
+        (even_far_ref, 0, HALO, above),
+        (own_far_ref, 0, ROWS, None),
+        (odd_far_ref, 0, ROWS, None),
+    )
+    unpack(depth, signs, far_diag, mask, sign_pieces, kappa_pieces)
 
     def start_down(k, carry):
         ratio, value, from_end = carry
@@ -599,7 +637,7 @@
     width = LANES // 2
     lanes = lane_ids((ROWS, 2 * LANES))
     ids = row_ids((ROWS, LANES))
-    base = even_ref.shape[0] - depth // ROWS
+    base = even_ref.shape[0] - depth
     from_even = lax.rem(tile, 2) == 1
 
     def half(value):
@@ -608,7 +646,7 @@
     def take(value):
         return jnp.where(even, value, pltpu.roll(value, width, 1))
 
-    far_edge = far_ref[far_ref.shape[0] - 1]
+    far_edge = far_ref[far_ref.shape[0] - ROWS :]
     factors, parts = [], []
     for z in range(depth):
         value = observed_ref[z]
@@ -616,8 +654,8 @@
         y_sides = jnp.where(lanes > 0, pltpu.roll(value, 1, 1), 0.0) + jnp.where(
             lanes < 2 * LANES - 1, pltpu.roll(value, 2 * LANES - 1, 1), 0.0
         )
-        first = even_ref[base + z // ROWS, z % ROWS : z % ROWS + 1, :]
-        second = odd_ref[base + z // ROWS, z % ROWS : z % ROWS + 1, :]
+        first = even_ref[base + z : base + z + 1]
+        second = odd_ref[base + z : base + z + 1]
         left, right = jnp.where(from_even, first, second), jnp.where(from_even, second, first)
         before = jnp.where(ids > 0, pltpu.roll(mine, 1, 0), jnp.where(tile > 0, left, 0.0))
         after = jnp.where(
@@ -669,17 +707,19 @@
     params = pltpu.CompilerParams(vmem_limit_bytes=24 * 1024 * 1024)
     f32 = jnp.float32
     tiles = depth * EDGE // LANES
-    field = depth + tiles
-    sent = field + field // 2
-    own_shape = jax.ShapeDtypeStruct((2 * field, ROWS, LANES), f32)
-    near_shape = jax.ShapeDtypeStruct((sent + depth // ROWS, ROWS, LANES), f32)
-    far_shape = jax.ShapeDtypeStruct((sent + 1, ROWS, LANES), f32)
-
-    own_block, even_block, odd_block, cross_block = pl.pallas_call(
+    field, thin = ROWS * (depth + tiles), HALO * depth + ROWS * tiles
+
+    def block(count):
+        return jax.ShapeDtypeStruct((count, LANES), f32)
+
+    near_shape = block(thin + thin // 2 + depth)
+    far_shape = block(field + field // 2 + ROWS)
+
+    own_block, even_block, odd_block, cross_block, diagonal_block = pl.pallas_call(
         functools.partial(pack_kernel, depth),
-        out_shape=(own_shape, near_shape, near_shape, far_shape),
+        out_shape=(block(2 * field), near_shape, near_shape, far_shape, block(thin + thin // 2)),
         in_specs=[pl.BlockSpec(memory_space=pltpu.HBM)] * 3,
-        out_specs=tuple(whole(4)),
+        out_specs=tuple(whole(5)),
         scratch_shapes=[
             pltpu.VMEM((depth, rows, columns), jnp.int32),
             pltpu.VMEM((depth, rows, columns), f32),
@@ -719,7 +759,7 @@
     even = tile_swap(even_block, 0, 0)
     odd = tile_swap(odd_block, 1, 0)
     odd_far = tile_swap(own_far, 1, 0)
-    even_far = tile_swap(cross_block, 0, 1)
+    even_far = tile_swap(diagonal_block, 0, 1)
 
     quarter = jax.ShapeDtypeStruct((depth, ROWS, columns // probes), f32)
     paired = jax.ShapeDtypeStruct((depth // 2, ROWS, LANES), f32)
@@ -733,10 +773,10 @@
     )(kappa_sq, observed, even, odd, own_far)
 
     def core_swap(*pieces):
-        kappa = jnp.concatenate([piece[field:sent] for piece in pieces], axis=0)
+        kappa = jnp.concatenate([piece[first : first + first // 2] for piece, first in pieces], axis=0)
         return lax.ppermute(kappa, "probe", swaps([(0, 1), (2, 3)]))
 
-    swapped = core_swap(even, odd, own_far)
+    swapped = core_swap((even, thin), (odd, thin), (own_far, field))
     levels = 2 * depth
     part = jax.ShapeDtypeStruct((depth, 3 * ROWS, 2 * LANES), f32)
     own_part = jax.ShapeDtypeStruct((depth, ROWS, 2 * LANES), f32)
@@ -750,7 +790,7 @@
         name="near",
     )(own_block, even, odd, swapped)
 
-    swapped_far = core_swap(even_far, odd_far)
+    swapped_far = core_swap((even_far, thin), (odd_far, field))
     padded = pltpu.VMEM((levels + 1, 3 * ROWS, 2 * LANES), f32)
     plain = pltpu.VMEM((levels, 3 * ROWS, 2 * LANES), f32)
     short = pltpu.VMEM((depth, 3 * ROWS, 2 * LANES), f32)

time: 48.2 us -> 46.7 us (0.969)
  waiting for transfers between devices: 17 us -> 14.6 us
  starting transfers between devices: 15 us -> 16.3 us
  Pallas kernels: 15.8 us -> 15.3 us
    ppermute x4, waiting for transfers between devices: 6.08 us -> 4.95 us  [tile_swap(): return lax.ppermute(block, ('probe', 'tile', 'level'), ways)]
    ppermute x1, waiting for transfers between devices: 4.23 us -> 3.63 us  [body(): lax.ppermute(turned, ('probe', 'level'), [(device(x, core, 0), device(x,...]
    ppermute x1, starting transfers between devices: 0.41 us -> 1 us  [body(): lax.ppermute(turned, ('probe', 'level'), [(device(x, core, 0), device(x,...]
  transfers between devices with their start and end apart: 14 -> 14, of which waited for: 7 -> 7; matrix products, arithmetic and copies ran while one was open for 0% -> 0% of each run, Pallas kernels for 8% -> 7%
where the time goes in v10:
time: 46.7 us; the launch traced here: 46.5 us
  starting transfers between devices  16.3 us (35%)
  Pallas kernels  15.3 us (33%)
  waiting for transfers between devices  14.6 us (31%)
    pallas_call x1, Pallas kernels, body(): pl.pallas_call(functools.partial(basis_kernel, depth), out_shape=(fields,...  8.89 us
    ppermute x4, waiting for transfers between devices, tile_swap(): return lax.ppermute(block, ('probe', 'tile', 'level'), ways)  4.95 us
    ppermute x4, starting transfers between devices, tile_swap(): return lax.ppermute(block, ('probe', 'tile', 'level'), ways)  4.66 us
    ppermute x3, starting transfers between devices, body(): lax.ppermute(gram, ('tile', 'level'), swaps([(i, i ^ k) for i in range(2...  3.92 us
    ppermute x1, waiting for transfers between devices, body(): lax.ppermute(turned, ('probe', 'level'), [(device(x, core, 0), device(x,...  3.63 us
    ppermute x1, starting transfers between devices, body(): partials.append(lax.ppermute(partials[0], 'tile', swaps([(0, 2), (1, 3)])))  3.04 us
    ppermute x1, starting transfers between devices, body(): own_far = lax.ppermute(cross_block, 'level', swaps([(0, 1)]))  3.03 us
    ppermute x3, waiting for transfers between devices, body(): lax.ppermute(gram, ('tile', 'level'), swaps([(i, i ^ k) for i in range(2...  2.89 us
  transfers between devices with their start and end apart: 14, of which 7 were waited for; matrix products, arithmetic and copies ran while one was open for 0% of the time, Pallas kernels for 7%

profile of v10, /device:TPU:0, one launch (start us, length us, event | category | flops | bytes accessed | tf_op | source)
XLA Modules:
  0.0 46.5 jit_solution(4155278344969590116)
XLA Ops:
  0.0 1.6 %pack.1 = (f32[544,128]{1,0:T(8,128)S(1)}, f32[392,128]{1,0:T(8,128)S(1)}, f32[392,128]{1,0:T(8,128)S(1)}, f32[416,128]{1,0:T(8,128)S(1)}, f32[360,128]{1,0:T(8,128)S(1)}) custom-call(s32[32,8,256]{2,1,0:T(8,128)} %bitcast.5, f32[32,8,256]{2,1,0:T(8,128)} %kappa_ref.1, f32[32,8,256]{2,1,0:T(8,128)} %observed_ref.1), custom_call_target="tpu_custom_call" | custom-call | tf_op jit(solution)/shard_map/pack/pallas_call | solution.py:718
  1.6 3.0 %collective-permute-start.2 = (f32[416,128]{1,0:T(8,128)S(1)}, f32[416,128]{1,0:T(8,128)S(1)}, u32[]{:S(2)}, u32[]{:S(2)}) collective-permute-start(f32[416,128]{1,0:T(8,128)S(1)} %get-tuple-element.27), channel_id=1, source_target_pairs={{0,1},{1,0},{2,3},{3,2},{4,5},{5,4},{6,7},{7,6},{8,9},{9,8},{10,11... | collective-permute-start | bytes 638984 | tf_op jit(solution)/shard_map/ppermute | solution.py:758
  4.7 1.6 %collective-permute-start = (f32[392,128]{1,0:T(8,128)S(1)}, f32[392,128]{1,0:T(8,128)S(1)}, u32[]{:S(2)}, u32[]{:S(2)}) collective-permute-start(f32[392,128]{1,0:T(8,128)S(1)} %get-tuple-element.25), channel_id=1, source_target_pairs={{0,2},{1,3},{2,0},{3,1},{4,6},{5,7},{6,4},{7,5},{8,10},{9,11},{10,... | collective-permute-start | bytes 602120 | tf_op jit(solution)/shard_map/ppermute | solution.py:756
  6.2 0.0 collective-permute-start.1
  6.2 3.1 %collective-permute-start.4 = (f32[360,128]{1,0:T(8,128)S(1)}, f32[360,128]{1,0:T(8,128)S(1)}, u32[]{:S(2)}, u32[]{:S(2)}) collective-permute-start(f32[360,128]{1,0:T(8,128)S(1)} %get-tuple-element.32), channel_id=1, source_target_pairs={{0,3},{1,2},{2,1},{3,0},{4,7},{5,6},{6,5},{7,4},{8,11},{9,10},{10,... | collective-permute-start | bytes 552968 | tf_op jit(solution)/shard_map/ppermute | solution.py:756
  9.3 0.6 %collective-permute-done.2.own_far_ref.far_ref = f32[416,128]{1,0:T(8,128)S(1)} collective-permute-done((f32[416,128]{1,0:T(8,128)S(1)}, f32[416,128]{1,0:T(8,128)S(1)}, u32[]{:S(2)}, u32[]{:S(2)}) %collective-permute-start.2) | collective-permute-done | bytes 213024 | tf_op jit(solution)/shard_map/ppermute | solution.py:758
  9.9 0.0 collective-permute-start.5
  9.9 4.9 %collective-permute-done.4.even_far_ref = f32[360,128]{1,0:T(8,128)S(1)} collective-permute-done((f32[360,128]{1,0:T(8,128)S(1)}, f32[360,128]{1,0:T(8,128)S(1)}, u32[]{:S(2)}, u32[]{:S(2)}) %collective-permute-start.4) | collective-permute-done | bytes 184352 | tf_op jit(solution)/shard_map/ppermute | solution.py:756
  14.9 0.0 collective-permute-done.even_ref
  14.9 0.0 collective-permute-done.1.odd_ref
  14.9 0.1 collective-permute-start.3
  15.0 0.0 collective-permute-done.5.odd_far_ref
  15.1 0.5 %collective-permute-start.6 = (f32[256,128]{1,0:T(8,128)S(1)}, f32[256,128]{1,0:T(8,128)S(1)}, u32[]{:S(2)}, u32[]{:S(2)}) collective-permute-start(f32[256,128]{1,0:T(8,128)S(1)} %pad_maximum_fusion.1), channel_id=1, source_target_pairs={{0,8},{8,0},{16,24},{24,16},{1,9},{9,1},{17,25},{25,17},{2,10},{10... | collective-permute-start | bytes 393224 | tf_op jit(solution)/shard_map/ppermute | solution.py:777
  15.6 0.8 %collective-permute-done.3.swapped_ref = f32[376,128]{1,0:T(8,128)S(1)} collective-permute-done((f32[376,128]{1,0:T(8,128)S(1)}, f32[376,128]{1,0:T(8,128)S(1)}, u32[]{:S(2)}, u32[]{:S(2)}) %collective-permute-start.3) | collective-permute-done | bytes 192544 | tf_op jit(solution)/shard_map/ppermute | solution.py:777
  16.4 0.9 %near.1 = (f32[32,24,256]{2,1,0:T(8,128)S(1)}, f32[32,24,256]{2,1,0:T(8,128)S(1)}, f32[32,24,256]{2,1,0:T(8,128)S(1)}, f32[32,8,256]{2,1,0:T(8,128)S(1)}, f32[32,8,256]{2,1,0:T(8,128)S(1)}) custom-call(f32[544,128]{1,0:T(8,128)S(1)} %get-tuple-element.24.own_ref, f32[392,128]{1,0:T(8,128)S(1)} %collective-permute-done.even_ref, ...), custom_call_target="tpu_custom_call" | custom-call | tf_op jit(solution)/shard_map/near/pallas_call | solution.py:783
  17.4 0.0 collective-permute-done.6.swapped_far_ref
  17.4 8.9 %basis.1 = (f32[4,64,8,256]{3,2,1,0:T(8,128)S(1)}, f32[4,64,8,256]{3,2,1,0:T(8,128)S(1)}, f32[32,8,256]{2,1,0:T(8,128)S(1)}, f32[32,8,256]{2,1,0:T(8,128)S(1)}, f32[8,128]{1,0:T(8,128)S(1)}) custom-call(f32[32,24,256]{2,1,0:T(8,128)S(1)} %get-tuple-element.28.near_diag, f32[32,24,256]{2,1,0:T(8,128)S(1)} %get-tuple-element.29.near_lower, ...), custom_call_target="tpu_custom_call" | custom-call | tf_op jit(solution)/shard_map/basis/pallas_call | solution.py:798
  26.3 3.1 %collective-permute-start.9 = (f32[8,128]{1,0:T(8,128)S(1)}, f32[8,128]{1,0:T(8,128)S(1)}, u32[]{:S(2)}, u32[]{:S(2)}) collective-permute-start(f32[8,128]{1,0:T(8,128)S(1)} %get-tuple-element.38), channel_id=1, source_target_pairs={{0,3},{3,0},{1,2},{2,1},{4,7},{7,4},{5,6},{6,5},{8,11},{11,8},{9,1... | collective-permute-start | bytes 12296 | tf_op jit(solution)/shard_map/ppermute | solution.py:845
  29.5 0.1 collective-permute-start.8
  29.5 0.7 %collective-permute-start.7 = (f32[8,128]{1,0:T(8,128)S(1)}, f32[8,128]{1,0:T(8,128)S(1)}, u32[]{:S(2)}, u32[]{:S(2)}) collective-permute-start(f32[8,128]{1,0:T(8,128)S(1)} %get-tuple-element.38), channel_id=1, source_target_pairs={{0,1},{1,0},{2,3},{3,2},{4,5},{5,4},{6,7},{7,6},{8,9},{9,8},{10,11... | collective-permute-start | bytes 12296 | tf_op jit(solution)/shard_map/ppermute | solution.py:845
  30.2 2.9 %collective-permute-done.7 = f32[8,128]{1,0:T(8,128)S(1)} collective-permute-done((f32[8,128]{1,0:T(8,128)S(1)}, f32[8,128]{1,0:T(8,128)S(1)}, u32[]{:S(2)}, u32[]{:S(2)}) %collective-permute-start.7) | collective-permute-done | bytes 4128 | tf_op jit(solution)/shard_map/ppermute | solution.py:845
  33.1 0.0 collective-permute-done.8
  33.1 0.0 collective-permute-done.9
  33.1 3.0 %collective-permute-start.10 = (f32[32,128]{1,0:T(8,128)S(1)}, f32[32,128]{1,0:T(8,128)S(1)}, u32[]{:S(2)}, u32[]{:S(2)}) collective-permute-start(f32[32,128]{1,0:T(8,128)S(1)} %constant_dynamic-update-slice_fusion.refs_0_), channel_id=1, source_target_pairs={{0,4},{4,0},{2,6},{6,2},{1,5},{5,1},{3,7},{7,3},{8,12},{12,8},{10,... | collective-permute-start | bytes 49160 | tf_op jit(solution)/shard_map/ppermute | solution.py:854
  36.2 0.0 copy-start
  36.2 0.0 copy-start.1
  36.2 1.4 %terms.1.terms_ref = f32[4,64,8,128]{3,2,1,0:T(8,128)S(1)} custom-call(f32[4,64,8,256]{3,2,1,0:T(8,128)S(1)} %get-tuple-element.33.basis_ref, f32[4,64,8,256]{3,2,1,0:T(8,128)S(1)} %get-tuple-element.34.image_ref, f32[32,8,256]{2,1,0:T(8,128)S(1)} %get-tuple-element.31.near_signs, f32[32,8,256]{2,1,0:T(8,128)S(1)} %get-tuple-element.35.near_k_signs, ...), custom_call_target="tpu_custom_call" | custom-call | tf_op jit(solution)/shard_map/terms/pallas_call | solution.py:834
  37.5 0.4 collective-permute-done.10.refs_1_
  37.9 0.6 %combine.1 = (f32[2,16,8,128]{3,2,1,0:T(8,128)S(1)}, f32[2,16,8,128]{3,2,1,0:T(8,128)S(1)}) custom-call(f32[4,64,8,128]{3,2,1,0:T(8,128)S(1)} %terms.1.terms_ref, f32[32,128]{1,0:T(8,128)S(1)} %constant_dynamic-update-slice_fusion.refs_0_, f32[32,128]{1,0:T(8,128)S(1)} %collective-permute-done.10.refs_1_), custom_call_target="tpu_custom_call" | custom-call | tf_op jit(solution)/shard_map/combine/pallas_call | solution.py:858
  38.6 0.1 collective-permute-start.11
  38.6 1.3 %collective-permute-done.11 = f32[2,16,8,128]{3,2,1,0:T(8,128)S(1)} collective-permute-done((f32[2,16,8,128]{3,2,1,0:T(8,128)S(1)}, f32[2,16,8,128]{3,2,1,0:T(8,128)S(1)}, u32[]{:S(2)}, u32[]{:S(2)}) %collective-permute-start.11) | collective-permute-done | bytes 131104 | tf_op jit(solution)/shard_map/ppermute | solution.py:867
  40.0 1.0 %collective-permute-start.13 = (f32[16,8,128]{2,1,0:T(8,128)S(1)}, f32[16,8,128]{2,1,0:T(8,128)S(1)}, u32[]{:S(2)}, u32[]{:S(2)}) collective-permute-start(f32[16,8,128]{2,1,0:T(8,128)S(1)} %get-tuple-element.43), channel_id=1, source_target_pairs={{0,1},{8,9},{16,17},{24,25},{1,16},{9,24},{17,0},{25,8},{2,3},{10,... | collective-permute-start | bytes 196616 | tf_op jit(solution)/shard_map/ppermute | solution.py:876
  41.0 0.0 collective-permute-start.12
  41.0 0.0 copy-done
  41.0 0.0 copy-done.1
  41.0 1.0 %observed.1 = (f32[16,8,128]{2,1,0:T(8,128)S(1)}, f32[16,8,128]{2,1,0:T(8,128)S(1)}) custom-call(f32[32,8,256]{2,1,0:T(8,128)S(1)} %copy-done, f32[32,8,256]{2,1,0:T(8,128)S(1)} %copy-done.1, f32[392,128]{1,0:T(8,128)S(1)} %collective-permute-done.even_ref, f32[392,128]{1,0:T(8,128)S(1)} %collective-permute-done.1.odd_ref, ...), custom_call_target="tpu_custom_call" | custom-call | tf_op jit(solution)/shard_map/observed/pallas_call | solution.py:766
  42.0 3.6 %collective-permute-done.13.trace_a_ref = f32[16,8,128]{2,1,0:T(8,128)S(1)} collective-permute-done((f32[16,8,128]{2,1,0:T(8,128)S(1)}, f32[16,8,128]{2,1,0:T(8,128)S(1)}, u32[]{:S(2)}, u32[]{:S(2)}) %collective-permute-start.13) | collective-permute-done | bytes 65568 | tf_op jit(solution)/shard_map/ppermute | solution.py:876
  45.6 0.0 collective-permute-done.12.trace_b_ref
  45.6 0.9 %gradient.1 = f32[32,8,64]{2,1,0:T(8,128)} custom-call(f32[16,8,128]{2,1,0:T(8,128)S(1)} %collective-permute-done.12.trace_b_ref, f32[16,8,128]{2,1,0:T(8,128)S(1)} %collective-permute-done.13.trace_a_ref, f32[16,8,128]{2,1,0:T(8,128)S(1)} %get-tuple-element.44.straight_ref, f32[16,8,128]{2,1,0:T(8,128)S(1)} %get-tuple-element.41.factor_ref, ...), custom_call_target="tpu_custom_call" | custom-call | tf_op jit(solution)/shard_map/gradient/pallas_call | solution.py:888
  (13 shorter events, 0.1 us)
Async XLA Ops:
  1.6 8.3 %collective-permute-start.2 = (f32[416,128]{1,0:T(8,128)S(1)}, f32[416,128]{1,0:T(8,128)S(1)}, u32[]{:S(2)}, u32[]{:S(2)}) collective-permute-start(f32[416,128]{1,0:T(8,128)S(1)} %get-tuple-element.27), channel_id=1, source_target_pairs={{0,1},{1,0},{2,3},{3,2},{4,5},{5,4},{6,7},{7,6},{8,9},{9,8},{10,11... | collective-permute-start | bytes 638984 | tf_op jit(solution)/shard_map/ppermute | solution.py:758
  4.7 10.2 %collective-permute-start = (f32[392,128]{1,0:T(8,128)S(1)}, f32[392,128]{1,0:T(8,128)S(1)}, u32[]{:S(2)}, u32[]{:S(2)}) collective-permute-start(f32[392,128]{1,0:T(8,128)S(1)} %get-tuple-element.25), channel_id=1, source_target_pairs={{0,2},{1,3},{2,0},{3,1},{4,6},{5,7},{6,4},{7,5},{8,10},{9,11},{10,... | collective-permute-start | bytes 602120 | tf_op jit(solution)/shard_map/ppermute | solution.py:756
  6.2 8.6 %collective-permute-start.1 = (f32[392,128]{1,0:T(8,128)S(1)}, f32[392,128]{1,0:T(8,128)S(1)}, u32[]{:S(2)}, u32[]{:S(2)}) collective-permute-start(f32[392,128]{1,0:T(8,128)S(1)} %get-tuple-element.26), channel_id=1, source_target_pairs={{0,8},{1,9},{2,4},{3,5},{4,2},{5,3},{6,14},{7,15},{8,0},{9,1},{10,... | collective-permute-start | bytes 602120 | tf_op jit(solution)/shard_map/ppermute | solution.py:756
  6.2 8.6 %collective-permute-start.4 = (f32[360,128]{1,0:T(8,128)S(1)}, f32[360,128]{1,0:T(8,128)S(1)}, u32[]{:S(2)}, u32[]{:S(2)}) collective-permute-start(f32[360,128]{1,0:T(8,128)S(1)} %get-tuple-element.32), channel_id=1, source_target_pairs={{0,3},{1,2},{2,1},{3,0},{4,7},{5,6},{6,5},{7,4},{8,11},{9,10},{10,... | collective-permute-start | bytes 552968 | tf_op jit(solution)/shard_map/ppermute | solution.py:756
  9.9 5.1 %collective-permute-start.5 = (f32[416,128]{1,0:T(8,128)S(1)}, f32[416,128]{1,0:T(8,128)S(1)}, u32[]{:S(2)}, u32[]{:S(2)}) collective-permute-start(f32[416,128]{1,0:T(8,128)S(1)} %collective-permute-done.2.own_far_ref.far_ref), channel_id=1, source_target_pairs={{0,8},{1,9},{2,4},{3,5},{4,2},{5,3},{6,14},{7,15},{8,0},{9,1},{10,... | collective-permute-start | bytes 638984 | tf_op jit(solution)/shard_map/ppermute | solution.py:756
  14.9 1.5 %collective-permute-start.3 = (f32[376,128]{1,0:T(8,128)S(1)}, f32[376,128]{1,0:T(8,128)S(1)}, u32[]{:S(2)}, u32[]{:S(2)}) collective-permute-start(f32[376,128]{1,0:T(8,128)S(1)} %pad_maximum_fusion), channel_id=1, source_target_pairs={{0,8},{8,0},{16,24},{24,16},{1,9},{9,1},{17,25},{25,17},{2,10},{10... | collective-permute-start | bytes 577544 | tf_op jit(solution)/shard_map/ppermute | solution.py:777
  15.1 2.3 %collective-permute-start.6 = (f32[256,128]{1,0:T(8,128)S(1)}, f32[256,128]{1,0:T(8,128)S(1)}, u32[]{:S(2)}, u32[]{:S(2)}) collective-permute-start(f32[256,128]{1,0:T(8,128)S(1)} %pad_maximum_fusion.1), channel_id=1, source_target_pairs={{0,8},{8,0},{16,24},{24,16},{1,9},{9,1},{17,25},{25,17},{2,10},{10... | collective-permute-start | bytes 393224 | tf_op jit(solution)/shard_map/ppermute | solution.py:777
  26.3 6.8 %collective-permute-start.9 = (f32[8,128]{1,0:T(8,128)S(1)}, f32[8,128]{1,0:T(8,128)S(1)}, u32[]{:S(2)}, u32[]{:S(2)}) collective-permute-start(f32[8,128]{1,0:T(8,128)S(1)} %get-tuple-element.38), channel_id=1, source_target_pairs={{0,3},{3,0},{1,2},{2,1},{4,7},{7,4},{5,6},{6,5},{8,11},{11,8},{9,1... | collective-permute-start | bytes 12296 | tf_op jit(solution)/shard_map/ppermute | solution.py:845
  29.5 3.7 %collective-permute-start.8 = (f32[8,128]{1,0:T(8,128)S(1)}, f32[8,128]{1,0:T(8,128)S(1)}, u32[]{:S(2)}, u32[]{:S(2)}) collective-permute-start(f32[8,128]{1,0:T(8,128)S(1)} %get-tuple-element.38), channel_id=1, source_target_pairs={{0,2},{2,0},{1,3},{3,1},{4,6},{6,4},{5,7},{7,5},{8,10},{10,8},{9,1... | collective-permute-start | bytes 12296 | tf_op jit(solution)/shard_map/ppermute | solution.py:845
  29.5 3.6 %collective-permute-start.7 = (f32[8,128]{1,0:T(8,128)S(1)}, f32[8,128]{1,0:T(8,128)S(1)}, u32[]{:S(2)}, u32[]{:S(2)}) collective-permute-start(f32[8,128]{1,0:T(8,128)S(1)} %get-tuple-element.38), channel_id=1, source_target_pairs={{0,1},{1,0},{2,3},{3,2},{4,5},{5,4},{6,7},{7,6},{8,9},{9,8},{10,11... | collective-permute-start | bytes 12296 | tf_op jit(solution)/shard_map/ppermute | solution.py:845
  33.1 4.8 %collective-permute-start.10 = (f32[32,128]{1,0:T(8,128)S(1)}, f32[32,128]{1,0:T(8,128)S(1)}, u32[]{:S(2)}, u32[]{:S(2)}) collective-permute-start(f32[32,128]{1,0:T(8,128)S(1)} %constant_dynamic-update-slice_fusion.refs_0_), channel_id=1, source_target_pairs={{0,4},{4,0},{2,6},{6,2},{1,5},{5,1},{3,7},{7,3},{8,12},{12,8},{10,... | collective-permute-start | bytes 49160 | tf_op jit(solution)/shard_map/ppermute | solution.py:854
  36.2 4.8 %copy-start = (f32[32,8,256]{2,1,0:T(8,128)S(1)}, f32[32,8,256]{2,1,0:T(8,128)}, u32[]{:S(2)}) copy-start(f32[32,8,256]{2,1,0:T(8,128)} %kappa_ref.1) | copy-start | bytes 786436
  36.2 4.8 %copy-start.1 = (f32[32,8,256]{2,1,0:T(8,128)S(1)}, f32[32,8,256]{2,1,0:T(8,128)}, u32[]{:S(2)}) copy-start(f32[32,8,256]{2,1,0:T(8,128)} %observed_ref.1) | copy-start | bytes 786436
  38.6 1.4 %collective-permute-start.11 = (f32[2,16,8,128]{3,2,1,0:T(8,128)S(1)}, f32[2,16,8,128]{3,2,1,0:T(8,128)S(1)}, u32[]{:S(2)}, u32[]{:S(2)}) collective-permute-start(f32[2,16,8,128]{3,2,1,0:T(8,128)S(1)} %get-tuple-element.40), channel_id=1, source_target_pairs={{0,8},{8,0},{16,24},{24,16},{1,9},{9,1},{17,25},{25,17},{2,10},{10... | collective-permute-start | bytes 393224 | tf_op jit(solution)/shard_map/ppermute | solution.py:867
  40.0 5.6 %collective-permute-start.13 = (f32[16,8,128]{2,1,0:T(8,128)S(1)}, f32[16,8,128]{2,1,0:T(8,128)S(1)}, u32[]{:S(2)}, u32[]{:S(2)}) collective-permute-start(f32[16,8,128]{2,1,0:T(8,128)S(1)} %get-tuple-element.43), channel_id=1, source_target_pairs={{0,1},{8,9},{16,17},{24,25},{1,16},{9,24},{17,0},{25,8},{2,3},{10,... | collective-permute-start | bytes 196616 | tf_op jit(solution)/shard_map/ppermute | solution.py:876
  41.0 4.6 %collective-permute-start.12 = (f32[16,8,128]{2,1,0:T(8,128)S(1)}, f32[16,8,128]{2,1,0:T(8,128)S(1)}, u32[]{:S(2)}, u32[]{:S(2)}) collective-permute-start(f32[16,8,128]{2,1,0:T(8,128)S(1)} %get-tuple-element.44.straight_ref), channel_id=1, source_target_pairs={{1,17},{9,25},{17,1},{25,9},{0,8},{8,0},{16,24},{24,16},{3,19},{11... | collective-permute-start | bytes 196616 | tf_op jit(solution)/shard_map/ppermute | solution.py:882

commit v11 on v10

--- a/solution.py
+++ b/solution.py
@@ -166,6 +166,14 @@
 
     top = half(observed_ref[:, ROWS - 1, :])
     bottom = half(observed_ref[:, 0, :])
+    width = LANES // 2
+    first_lanes = lane_ids((depth // 2, LANES)) < width
+
+    def quarters(value):
+        value = jnp.where(in_first_core, value, pltpu.roll(value, width, 1))
+        return jnp.where(first_lanes, value[: depth // 2], pltpu.roll(value[depth // 2 :], width, 1))
+
+    top, bottom = quarters(top), quarters(bottom)
     even_ref[even_base:] = jnp.where(goes_up, top, bottom)
     odd_ref[even_base:] = jnp.where(goes_up, bottom, top)
     cross_ref[cross_base:] = jnp.where(first, half(observed_ref[depth - 1]), half(observed_ref[0]))
@@ -637,7 +645,17 @@
     width = LANES // 2
     lanes = lane_ids((ROWS, 2 * LANES))
     ids = row_ids((ROWS, LANES))
-    base = even_ref.shape[0] - depth
+    base = even_ref.shape[0] - depth // 2
+
+    def rows_beside(ref):
+        packed = ref[base : base + depth // 2]
+        turned = pltpu.roll(packed, width, 1)
+        first_lanes = lane_ids(packed.shape) < width
+        return jnp.concatenate(
+            [jnp.where(first_lanes, packed, turned), jnp.where(first_lanes, turned, packed)], axis=0
+        )
+
+    even_rows, odd_rows = rows_beside(even_ref), rows_beside(odd_ref)
     from_even = lax.rem(tile, 2) == 1
 
     def half(value):
@@ -654,8 +672,7 @@
         y_sides = jnp.where(lanes > 0, pltpu.roll(value, 1, 1), 0.0) + jnp.where(
             lanes < 2 * LANES - 1, pltpu.roll(value, 2 * LANES - 1, 1), 0.0
         )
-        first = even_ref[base + z : base + z + 1]
-        second = odd_ref[base + z : base + z + 1]
+        first, second = even_rows[z : z + 1], odd_rows[z : z + 1]
         left, right = jnp.where(from_even, first, second), jnp.where(from_even, second, first)
         before = jnp.where(ids > 0, pltpu.roll(mine, 1, 0), jnp.where(tile > 0, left, 0.0))
         after = jnp.where(
@@ -712,7 +729,7 @@
     def block(count):
         return jax.ShapeDtypeStruct((count, LANES), f32)
 
-    near_shape = block(thin + thin // 2 + depth)
+    near_shape = block(thin + thin // 2 + depth // 2)
     far_shape = block(field + field // 2 + ROWS)
 
     own_block, even_block, odd_block, cross_block, diagonal_block = pl.pallas_call(

time: 46.7 us -> 47 us (level)
  no operation moved by 1% of the time
where the time goes in v11:
time: 47 us; the launch traced here: 46.8 us
  starting transfers between devices  16.3 us (35%)
  Pallas kernels  15.4 us (33%)
  waiting for transfers between devices  14.8 us (31%)
    pallas_call x1, Pallas kernels, body(): pl.pallas_call(functools.partial(basis_kernel, depth), out_shape=(fields,...  8.89 us
    ppermute x4, waiting for transfers between devices, tile_swap(): return lax.ppermute(block, ('probe', 'tile', 'level'), ways)  4.77 us
    ppermute x4, starting transfers between devices, tile_swap(): return lax.ppermute(block, ('probe', 'tile', 'level'), ways)  4.67 us
    ppermute x3, starting transfers between devices, body(): lax.ppermute(gram, ('tile', 'level'), swaps([(i, i ^ k) for i in range(2...  4.13 us
    ppermute x1, waiting for transfers between devices, body(): lax.ppermute(turned, ('probe', 'level'), [(device(x, core, 0), device(x,...  3.98 us
    ppermute x1, starting transfers between devices, body(): partials.append(lax.ppermute(partials[0], 'tile', swaps([(0, 2), (1, 3)])))  3.1 us
    ppermute x1, starting transfers between devices, body(): own_far = lax.ppermute(cross_block, 'level', swaps([(0, 1)]))  3.03 us
    ppermute x3, waiting for transfers between devices, body(): lax.ppermute(gram, ('tile', 'level'), swaps([(i, i ^ k) for i in range(2...  2.97 us
  transfers between devices with their start and end apart: 14, of which 7 were waited for; matrix products, arithmetic and copies ran while one was open for 0% of the time, Pallas kernels for 7%

profile of v11, /device:TPU:0, one launch (start us, length us, event | category | flops | bytes accessed | tf_op | source)
XLA Modules:
  0.0 46.8 jit_solution(6267724885728934507)
XLA Ops:
  0.0 1.7 %pack.1 = (f32[544,128]{1,0:T(8,128)S(1)}, f32[376,128]{1,0:T(8,128)S(1)}, f32[376,128]{1,0:T(8,128)S(1)}, f32[416,128]{1,0:T(8,128)S(1)}, f32[360,128]{1,0:T(8,128)S(1)}) custom-call(s32[32,8,256]{2,1,0:T(8,128)} %bitcast.5, f32[32,8,256]{2,1,0:T(8,128)} %kappa_ref.1, f32[32,8,256]{2,1,0:T(8,128)} %observed_ref.1), custom_call_target="tpu_custom_call" | custom-call | tf_op jit(solution)/shard_map/pack/pallas_call | solution.py:735
  1.7 3.0 %collective-permute-start.2 = (f32[416,128]{1,0:T(8,128)S(1)}, f32[416,128]{1,0:T(8,128)S(1)}, u32[]{:S(2)}, u32[]{:S(2)}) collective-permute-start(f32[416,128]{1,0:T(8,128)S(1)} %get-tuple-element.27), channel_id=1, source_target_pairs={{0,1},{1,0},{2,3},{3,2},{4,5},{5,4},{6,7},{7,6},{8,9},{9,8},{10,11... | collective-permute-start | bytes 638984 | tf_op jit(solution)/shard_map/ppermute | solution.py:775
  4.8 1.6 %collective-permute-start = (f32[376,128]{1,0:T(8,128)S(1)}, f32[376,128]{1,0:T(8,128)S(1)}, u32[]{:S(2)}, u32[]{:S(2)}) collective-permute-start(f32[376,128]{1,0:T(8,128)S(1)} %get-tuple-element.25), channel_id=1, source_target_pairs={{0,2},{1,3},{2,0},{3,1},{4,6},{5,7},{6,4},{7,5},{8,10},{9,11},{10,... | collective-permute-start | bytes 577544 | tf_op jit(solution)/shard_map/ppermute | solution.py:773
  6.4 0.0 collective-permute-start.1
  6.4 3.1 %collective-permute-start.4 = (f32[360,128]{1,0:T(8,128)S(1)}, f32[360,128]{1,0:T(8,128)S(1)}, u32[]{:S(2)}, u32[]{:S(2)}) collective-permute-start(f32[360,128]{1,0:T(8,128)S(1)} %get-tuple-element.32), channel_id=1, source_target_pairs={{0,3},{1,2},{2,1},{3,0},{4,7},{5,6},{6,5},{7,4},{8,11},{9,10},{10,... | collective-permute-start | bytes 552968 | tf_op jit(solution)/shard_map/ppermute | solution.py:773
  9.4 0.6 %collective-permute-done.2.own_far_ref.far_ref = f32[416,128]{1,0:T(8,128)S(1)} collective-permute-done((f32[416,128]{1,0:T(8,128)S(1)}, f32[416,128]{1,0:T(8,128)S(1)}, u32[]{:S(2)}, u32[]{:S(2)}) %collective-permute-start.2) | collective-permute-done | bytes 213024 | tf_op jit(solution)/shard_map/ppermute | solution.py:775
  10.0 0.0 collective-permute-start.5
  10.0 4.8 %collective-permute-done.4.even_far_ref = f32[360,128]{1,0:T(8,128)S(1)} collective-permute-done((f32[360,128]{1,0:T(8,128)S(1)}, f32[360,128]{1,0:T(8,128)S(1)}, u32[]{:S(2)}, u32[]{:S(2)}) %collective-permute-start.4) | collective-permute-done | bytes 184352 | tf_op jit(solution)/shard_map/ppermute | solution.py:773
  14.8 0.0 collective-permute-done.even_ref
  14.8 0.0 collective-permute-done.1.odd_ref
  14.9 0.1 collective-permute-start.3
  15.0 0.0 collective-permute-done.5.odd_far_ref
  15.0 0.5 %collective-permute-start.6 = (f32[256,128]{1,0:T(8,128)S(1)}, f32[256,128]{1,0:T(8,128)S(1)}, u32[]{:S(2)}, u32[]{:S(2)}) collective-permute-start(f32[256,128]{1,0:T(8,128)S(1)} %pad_maximum_fusion.1), channel_id=1, source_target_pairs={{0,8},{8,0},{16,24},{24,16},{1,9},{9,1},{17,25},{25,17},{2,10},{10... | collective-permute-start | bytes 393224 | tf_op jit(solution)/shard_map/ppermute | solution.py:794
  15.6 0.8 %collective-permute-done.3.swapped_ref = f32[376,128]{1,0:T(8,128)S(1)} collective-permute-done((f32[376,128]{1,0:T(8,128)S(1)}, f32[376,128]{1,0:T(8,128)S(1)}, u32[]{:S(2)}, u32[]{:S(2)}) %collective-permute-start.3) | collective-permute-done | bytes 192544 | tf_op jit(solution)/shard_map/ppermute | solution.py:794
  16.4 0.9 %near.1 = (f32[32,24,256]{2,1,0:T(8,128)S(1)}, f32[32,24,256]{2,1,0:T(8,128)S(1)}, f32[32,24,256]{2,1,0:T(8,128)S(1)}, f32[32,8,256]{2,1,0:T(8,128)S(1)}, f32[32,8,256]{2,1,0:T(8,128)S(1)}) custom-call(f32[544,128]{1,0:T(8,128)S(1)} %get-tuple-element.24.own_ref, f32[376,128]{1,0:T(8,128)S(1)} %collective-permute-done.even_ref, ...), custom_call_target="tpu_custom_call" | custom-call | tf_op jit(solution)/shard_map/near/pallas_call | solution.py:800
  17.3 0.0 collective-permute-done.6.swapped_far_ref
  17.4 8.9 %basis.1 = (f32[4,64,8,256]{3,2,1,0:T(8,128)S(1)}, f32[4,64,8,256]{3,2,1,0:T(8,128)S(1)}, f32[32,8,256]{2,1,0:T(8,128)S(1)}, f32[32,8,256]{2,1,0:T(8,128)S(1)}, f32[8,128]{1,0:T(8,128)S(1)}) custom-call(f32[32,24,256]{2,1,0:T(8,128)S(1)} %get-tuple-element.28.near_diag, f32[32,24,256]{2,1,0:T(8,128)S(1)} %get-tuple-element.29.near_lower, ...), custom_call_target="tpu_custom_call" | custom-call | tf_op jit(solution)/shard_map/basis/pallas_call | solution.py:815
  26.2 3.5 %collective-permute-start.9 = (f32[8,128]{1,0:T(8,128)S(1)}, f32[8,128]{1,0:T(8,128)S(1)}, u32[]{:S(2)}, u32[]{:S(2)}) collective-permute-start(f32[8,128]{1,0:T(8,128)S(1)} %get-tuple-element.38), channel_id=1, source_target_pairs={{0,3},{3,0},{1,2},{2,1},{4,7},{7,4},{5,6},{6,5},{8,11},{11,8},{9,1... | collective-permute-start | bytes 12296 | tf_op jit(solution)/shard_map/ppermute | solution.py:862
  29.7 0.0 collective-permute-start.8
  29.7 0.6 %collective-permute-start.7 = (f32[8,128]{1,0:T(8,128)S(1)}, f32[8,128]{1,0:T(8,128)S(1)}, u32[]{:S(2)}, u32[]{:S(2)}) collective-permute-start(f32[8,128]{1,0:T(8,128)S(1)} %get-tuple-element.38), channel_id=1, source_target_pairs={{0,1},{1,0},{2,3},{3,2},{4,5},{5,4},{6,7},{7,6},{8,9},{9,8},{10,11... | collective-permute-start | bytes 12296 | tf_op jit(solution)/shard_map/ppermute | solution.py:862
  30.4 3.0 %collective-permute-done.7 = f32[8,128]{1,0:T(8,128)S(1)} collective-permute-done((f32[8,128]{1,0:T(8,128)S(1)}, f32[8,128]{1,0:T(8,128)S(1)}, u32[]{:S(2)}, u32[]{:S(2)}) %collective-permute-start.7) | collective-permute-done | bytes 4128 | tf_op jit(solution)/shard_map/ppermute | solution.py:862
  33.3 0.0 collective-permute-done.8
  33.4 0.0 collective-permute-done.9
  33.4 3.1 %collective-permute-start.10 = (f32[32,128]{1,0:T(8,128)S(1)}, f32[32,128]{1,0:T(8,128)S(1)}, u32[]{:S(2)}, u32[]{:S(2)}) collective-permute-start(f32[32,128]{1,0:T(8,128)S(1)} %constant_dynamic-update-slice_fusion.refs_0_), channel_id=1, source_target_pairs={{0,4},{4,0},{2,6},{6,2},{1,5},{5,1},{3,7},{7,3},{8,12},{12,8},{10,... | collective-permute-start | bytes 49160 | tf_op jit(solution)/shard_map/ppermute | solution.py:871
  36.5 0.0 copy-start
  36.5 0.0 copy-start.1
  36.5 1.4 %terms.1.terms_ref = f32[4,64,8,128]{3,2,1,0:T(8,128)S(1)} custom-call(f32[4,64,8,256]{3,2,1,0:T(8,128)S(1)} %get-tuple-element.33.basis_ref, f32[4,64,8,256]{3,2,1,0:T(8,128)S(1)} %get-tuple-element.34.image_ref, f32[32,8,256]{2,1,0:T(8,128)S(1)} %get-tuple-element.31.near_signs, f32[32,8,256]{2,1,0:T(8,128)S(1)} %get-tuple-element.35.near_k_signs, ...), custom_call_target="tpu_custom_call" | custom-call | tf_op jit(solution)/shard_map/terms/pallas_call | solution.py:851
  37.8 0.4 collective-permute-done.10.refs_1_
  38.2 0.6 %combine.1 = (f32[2,16,8,128]{3,2,1,0:T(8,128)S(1)}, f32[2,16,8,128]{3,2,1,0:T(8,128)S(1)}) custom-call(f32[4,64,8,128]{3,2,1,0:T(8,128)S(1)} %terms.1.terms_ref, f32[32,128]{1,0:T(8,128)S(1)} %constant_dynamic-update-slice_fusion.refs_0_, f32[32,128]{1,0:T(8,128)S(1)} %collective-permute-done.10.refs_1_), custom_call_target="tpu_custom_call" | custom-call | tf_op jit(solution)/shard_map/combine/pallas_call | solution.py:875
  38.8 0.1 collective-permute-start.11
  38.9 1.3 %collective-permute-done.11 = f32[2,16,8,128]{3,2,1,0:T(8,128)S(1)} collective-permute-done((f32[2,16,8,128]{3,2,1,0:T(8,128)S(1)}, f32[2,16,8,128]{3,2,1,0:T(8,128)S(1)}, u32[]{:S(2)}, u32[]{:S(2)}) %collective-permute-start.11) | collective-permute-done | bytes 131104 | tf_op jit(solution)/shard_map/ppermute | solution.py:884
  40.3 0.6 %collective-permute-start.13 = (f32[16,8,128]{2,1,0:T(8,128)S(1)}, f32[16,8,128]{2,1,0:T(8,128)S(1)}, u32[]{:S(2)}, u32[]{:S(2)}) collective-permute-start(f32[16,8,128]{2,1,0:T(8,128)S(1)} %get-tuple-element.43), channel_id=1, source_target_pairs={{0,1},{8,9},{16,17},{24,25},{1,16},{9,24},{17,0},{25,8},{2,3},{10,... | collective-permute-start | bytes 196616 | tf_op jit(solution)/shard_map/ppermute | solution.py:893
  41.0 0.0 collective-permute-start.12
  41.0 0.0 copy-done
  41.0 0.0 copy-done.1
  41.0 1.0 %observed.1 = (f32[16,8,128]{2,1,0:T(8,128)S(1)}, f32[16,8,128]{2,1,0:T(8,128)S(1)}) custom-call(f32[32,8,256]{2,1,0:T(8,128)S(1)} %copy-done, f32[32,8,256]{2,1,0:T(8,128)S(1)} %copy-done.1, f32[376,128]{1,0:T(8,128)S(1)} %collective-permute-done.even_ref, f32[376,128]{1,0:T(8,128)S(1)} %collective-permute-done.1.odd_ref, ...), custom_call_target="tpu_custom_call" | custom-call | tf_op jit(solution)/shard_map/observed/pallas_call | solution.py:783
  41.9 4.0 %collective-permute-done.13.trace_a_ref = f32[16,8,128]{2,1,0:T(8,128)S(1)} collective-permute-done((f32[16,8,128]{2,1,0:T(8,128)S(1)}, f32[16,8,128]{2,1,0:T(8,128)S(1)}, u32[]{:S(2)}, u32[]{:S(2)}) %collective-permute-start.13) | collective-permute-done | bytes 65568 | tf_op jit(solution)/shard_map/ppermute | solution.py:893
  45.9 0.0 collective-permute-done.12.trace_b_ref
  45.9 0.9 %gradient.1 = f32[32,8,64]{2,1,0:T(8,128)} custom-call(f32[16,8,128]{2,1,0:T(8,128)S(1)} %collective-permute-done.12.trace_b_ref, f32[16,8,128]{2,1,0:T(8,128)S(1)} %collective-permute-done.13.trace_a_ref, f32[16,8,128]{2,1,0:T(8,128)S(1)} %get-tuple-element.44.straight_ref, f32[16,8,128]{2,1,0:T(8,128)S(1)} %get-tuple-element.41.factor_ref, ...), custom_call_target="tpu_custom_call" | custom-call | tf_op jit(solution)/shard_map/gradient/pallas_call | solution.py:905
  (13 shorter events, 0.1 us)
Async XLA Ops:
  1.7 8.3 %collective-permute-start.2 = (f32[416,128]{1,0:T(8,128)S(1)}, f32[416,128]{1,0:T(8,128)S(1)}, u32[]{:S(2)}, u32[]{:S(2)}) collective-permute-start(f32[416,128]{1,0:T(8,128)S(1)} %get-tuple-element.27), channel_id=1, source_target_pairs={{0,1},{1,0},{2,3},{3,2},{4,5},{5,4},{6,7},{7,6},{8,9},{9,8},{10,11... | collective-permute-start | bytes 638984 | tf_op jit(solution)/shard_map/ppermute | solution.py:775
  4.8 10.0 %collective-permute-start = (f32[376,128]{1,0:T(8,128)S(1)}, f32[376,128]{1,0:T(8,128)S(1)}, u32[]{:S(2)}, u32[]{:S(2)}) collective-permute-start(f32[376,128]{1,0:T(8,128)S(1)} %get-tuple-element.25), channel_id=1, source_target_pairs={{0,2},{1,3},{2,0},{3,1},{4,6},{5,7},{6,4},{7,5},{8,10},{9,11},{10,... | collective-permute-start | bytes 577544 | tf_op jit(solution)/shard_map/ppermute | solution.py:773
  6.4 8.5 %collective-permute-start.1 = (f32[376,128]{1,0:T(8,128)S(1)}, f32[376,128]{1,0:T(8,128)S(1)}, u32[]{:S(2)}, u32[]{:S(2)}) collective-permute-start(f32[376,128]{1,0:T(8,128)S(1)} %get-tuple-element.26), channel_id=1, source_target_pairs={{0,8},{1,9},{2,4},{3,5},{4,2},{5,3},{6,14},{7,15},{8,0},{9,1},{10,... | collective-permute-start | bytes 577544 | tf_op jit(solution)/shard_map/ppermute | solution.py:773
  6.4 8.4 %collective-permute-start.4 = (f32[360,128]{1,0:T(8,128)S(1)}, f32[360,128]{1,0:T(8,128)S(1)}, u32[]{:S(2)}, u32[]{:S(2)}) collective-permute-start(f32[360,128]{1,0:T(8,128)S(1)} %get-tuple-element.32), channel_id=1, source_target_pairs={{0,3},{1,2},{2,1},{3,0},{4,7},{5,6},{6,5},{7,4},{8,11},{9,10},{10,... | collective-permute-start | bytes 552968 | tf_op jit(solution)/shard_map/ppermute | solution.py:773
  10.0 4.9 %collective-permute-start.5 = (f32[416,128]{1,0:T(8,128)S(1)}, f32[416,128]{1,0:T(8,128)S(1)}, u32[]{:S(2)}, u32[]{:S(2)}) collective-permute-start(f32[416,128]{1,0:T(8,128)S(1)} %collective-permute-done.2.own_far_ref.far_ref), channel_id=1, source_target_pairs={{0,8},{1,9},{2,4},{3,5},{4,2},{5,3},{6,14},{7,15},{8,0},{9,1},{10,... | collective-permute-start | bytes 638984 | tf_op jit(solution)/shard_map/ppermute | solution.py:773
  14.9 1.5 %collective-permute-start.3 = (f32[376,128]{1,0:T(8,128)S(1)}, f32[376,128]{1,0:T(8,128)S(1)}, u32[]{:S(2)}, u32[]{:S(2)}) collective-permute-start(f32[376,128]{1,0:T(8,128)S(1)} %pad_maximum_fusion), channel_id=1, source_target_pairs={{0,8},{8,0},{16,24},{24,16},{1,9},{9,1},{17,25},{25,17},{2,10},{10... | collective-permute-start | bytes 577544 | tf_op jit(solution)/shard_map/ppermute | solution.py:794
  15.0 2.3 %collective-permute-start.6 = (f32[256,128]{1,0:T(8,128)S(1)}, f32[256,128]{1,0:T(8,128)S(1)}, u32[]{:S(2)}, u32[]{:S(2)}) collective-permute-start(f32[256,128]{1,0:T(8,128)S(1)} %pad_maximum_fusion.1), channel_id=1, source_target_pairs={{0,8},{8,0},{16,24},{24,16},{1,9},{9,1},{17,25},{25,17},{2,10},{10... | collective-permute-start | bytes 393224 | tf_op jit(solution)/shard_map/ppermute | solution.py:794
  26.2 7.1 %collective-permute-start.9 = (f32[8,128]{1,0:T(8,128)S(1)}, f32[8,128]{1,0:T(8,128)S(1)}, u32[]{:S(2)}, u32[]{:S(2)}) collective-permute-start(f32[8,128]{1,0:T(8,128)S(1)} %get-tuple-element.38), channel_id=1, source_target_pairs={{0,3},{3,0},{1,2},{2,1},{4,7},{7,4},{5,6},{6,5},{8,11},{11,8},{9,1... | collective-permute-start | bytes 12296 | tf_op jit(solution)/shard_map/ppermute | solution.py:862
  29.7 3.6 %collective-permute-start.8 = (f32[8,128]{1,0:T(8,128)S(1)}, f32[8,128]{1,0:T(8,128)S(1)}, u32[]{:S(2)}, u32[]{:S(2)}) collective-permute-start(f32[8,128]{1,0:T(8,128)S(1)} %get-tuple-element.38), channel_id=1, source_target_pairs={{0,2},{2,0},{1,3},{3,1},{4,6},{6,4},{5,7},{7,5},{8,10},{10,8},{9,1... | collective-permute-start | bytes 12296 | tf_op jit(solution)/shard_map/ppermute | solution.py:862
  29.7 3.6 %collective-permute-start.7 = (f32[8,128]{1,0:T(8,128)S(1)}, f32[8,128]{1,0:T(8,128)S(1)}, u32[]{:S(2)}, u32[]{:S(2)}) collective-permute-start(f32[8,128]{1,0:T(8,128)S(1)} %get-tuple-element.38), channel_id=1, source_target_pairs={{0,1},{1,0},{2,3},{3,2},{4,5},{5,4},{6,7},{7,6},{8,9},{9,8},{10,11... | collective-permute-start | bytes 12296 | tf_op jit(solution)/shard_map/ppermute | solution.py:862
  33.4 4.8 %collective-permute-start.10 = (f32[32,128]{1,0:T(8,128)S(1)}, f32[32,128]{1,0:T(8,128)S(1)}, u32[]{:S(2)}, u32[]{:S(2)}) collective-permute-start(f32[32,128]{1,0:T(8,128)S(1)} %constant_dynamic-update-slice_fusion.refs_0_), channel_id=1, source_target_pairs={{0,4},{4,0},{2,6},{6,2},{1,5},{5,1},{3,7},{7,3},{8,12},{12,8},{10,... | collective-permute-start | bytes 49160 | tf_op jit(solution)/shard_map/ppermute | solution.py:871
  36.5 4.5 %copy-start = (f32[32,8,256]{2,1,0:T(8,128)S(1)}, f32[32,8,256]{2,1,0:T(8,128)}, u32[]{:S(2)}) copy-start(f32[32,8,256]{2,1,0:T(8,128)} %kappa_ref.1) | copy-start | bytes 786436
  36.5 4.5 %copy-start.1 = (f32[32,8,256]{2,1,0:T(8,128)S(1)}, f32[32,8,256]{2,1,0:T(8,128)}, u32[]{:S(2)}) copy-start(f32[32,8,256]{2,1,0:T(8,128)} %observed_ref.1) | copy-start | bytes 786436
  38.8 1.4 %collective-permute-start.11 = (f32[2,16,8,128]{3,2,1,0:T(8,128)S(1)}, f32[2,16,8,128]{3,2,1,0:T(8,128)S(1)}, u32[]{:S(2)}, u32[]{:S(2)}) collective-permute-start(f32[2,16,8,128]{3,2,1,0:T(8,128)S(1)} %get-tuple-element.40), channel_id=1, source_target_pairs={{0,8},{8,0},{16,24},{24,16},{1,9},{9,1},{17,25},{25,17},{2,10},{10... | collective-permute-start | bytes 393224 | tf_op jit(solution)/shard_map/ppermute | solution.py:884
  40.3 5.6 %collective-permute-start.13 = (f32[16,8,128]{2,1,0:T(8,128)S(1)}, f32[16,8,128]{2,1,0:T(8,128)S(1)}, u32[]{:S(2)}, u32[]{:S(2)}) collective-permute-start(f32[16,8,128]{2,1,0:T(8,128)S(1)} %get-tuple-element.43), channel_id=1, source_target_pairs={{0,1},{8,9},{16,17},{24,25},{1,16},{9,24},{17,0},{25,8},{2,3},{10,... | collective-permute-start | bytes 196616 | tf_op jit(solution)/shard_map/ppermute | solution.py:893
  41.0 5.0 %collective-permute-start.12 = (f32[16,8,128]{2,1,0:T(8,128)S(1)}, f32[16,8,128]{2,1,0:T(8,128)S(1)}, u32[]{:S(2)}, u32[]{:S(2)}) collective-permute-start(f32[16,8,128]{2,1,0:T(8,128)S(1)} %get-tuple-element.44.straight_ref), channel_id=1, source_target_pairs={{1,17},{9,25},{17,1},{25,9},{0,8},{8,0},{16,24},{24,16},{3,19},{11... | collective-permute-start | bytes 196616 | tf_op jit(solution)/shard_map/ppermute | solution.py:899

commit v12 on v10

--- a/solution.py
+++ b/solution.py
@@ -293,7 +293,7 @@
         k_signs[k] = image[OWN_ROWS]
         return ratio, value
 
-    lax.fori_loop(0, depth, down, (zero, zero), unroll=GROUP)
+    lax.fori_loop(0, depth, down, (zero, zero), unroll=depth)
 
 
 def basis_kernel(
@@ -622,7 +622,7 @@
             send_ref[which, z] = jnp.where(core == 0, high, low)
         return unused
 
-    lax.fori_loop(0, pairs_deep, step, 0, unroll=GROUP)
+    lax.fori_loop(0, pairs_deep, step, 0, unroll=pairs_deep)
 
 
 def observed_kernel(

time: 46.7 us -> 46.6 us (level)
  no operation moved by 1% of the time
where the time goes in v12:
time: 46.6 us; the launch traced here: 46.5 us
  starting transfers between devices  16.3 us (35%)
  Pallas kernels  15.3 us (33%)
  waiting for transfers between devices  14.6 us (31%)
    pallas_call x1, Pallas kernels, body(): pl.pallas_call(functools.partial(basis_kernel, depth), out_shape=(fields,...  8.89 us
    ppermute x4, waiting for transfers between devices, tile_swap(): return lax.ppermute(block, ('probe', 'tile', 'level'), ways)  4.95 us
    ppermute x4, starting transfers between devices, tile_swap(): return lax.ppermute(block, ('probe', 'tile', 'level'), ways)  4.66 us
    ppermute x3, starting transfers between devices, body(): lax.ppermute(gram, ('tile', 'level'), swaps([(i, i ^ k) for i in range(2...  3.92 us
    ppermute x1, waiting for transfers between devices, body(): lax.ppermute(turned, ('probe', 'level'), [(device(x, core, 0), device(x,...  3.63 us
    ppermute x1, starting transfers between devices, body(): partials.append(lax.ppermute(partials[0], 'tile', swaps([(0, 2), (1, 3)])))  3.04 us
    ppermute x1, starting transfers between devices, body(): own_far = lax.ppermute(cross_block, 'level', swaps([(0, 1)]))  3.03 us
    ppermute x3, waiting for transfers between devices, body(): lax.ppermute(gram, ('tile', 'level'), swaps([(i, i ^ k) for i in range(2...  2.89 us
  transfers between devices with their start and end apart: 14, of which 7 were waited for; matrix products, arithmetic and copies ran while one was open for 0% of the time, Pallas kernels for 7%

profile of v12, /device:TPU:0, one launch (start us, length us, event | category | flops | bytes accessed | tf_op | source)
XLA Modules:
  0.0 46.5 jit_solution(13542592239718108619)
XLA Ops:
  0.0 1.6 %pack.1 = (f32[544,128]{1,0:T(8,128)S(1)}, f32[392,128]{1,0:T(8,128)S(1)}, f32[392,128]{1,0:T(8,128)S(1)}, f32[416,128]{1,0:T(8,128)S(1)}, f32[360,128]{1,0:T(8,128)S(1)}) custom-call(s32[32,8,256]{2,1,0:T(8,128)} %bitcast.5, f32[32,8,256]{2,1,0:T(8,128)} %kappa_ref.1, f32[32,8,256]{2,1,0:T(8,128)} %observed_ref.1), custom_call_target="tpu_custom_call" | custom-call | tf_op jit(solution)/shard_map/pack/pallas_call | solution.py:718
  1.6 3.0 %collective-permute-start.2 = (f32[416,128]{1,0:T(8,128)S(1)}, f32[416,128]{1,0:T(8,128)S(1)}, u32[]{:S(2)}, u32[]{:S(2)}) collective-permute-start(f32[416,128]{1,0:T(8,128)S(1)} %get-tuple-element.27), channel_id=1, source_target_pairs={{0,1},{1,0},{2,3},{3,2},{4,5},{5,4},{6,7},{7,6},{8,9},{9,8},{10,11... | collective-permute-start | bytes 638984 | tf_op jit(solution)/shard_map/ppermute | solution.py:758
  4.7 1.6 %collective-permute-start = (f32[392,128]{1,0:T(8,128)S(1)}, f32[392,128]{1,0:T(8,128)S(1)}, u32[]{:S(2)}, u32[]{:S(2)}) collective-permute-start(f32[392,128]{1,0:T(8,128)S(1)} %get-tuple-element.25), channel_id=1, source_target_pairs={{0,2},{1,3},{2,0},{3,1},{4,6},{5,7},{6,4},{7,5},{8,10},{9,11},{10,... | collective-permute-start | bytes 602120 | tf_op jit(solution)/shard_map/ppermute | solution.py:756
  6.2 0.0 collective-permute-start.1
  6.2 3.1 %collective-permute-start.4 = (f32[360,128]{1,0:T(8,128)S(1)}, f32[360,128]{1,0:T(8,128)S(1)}, u32[]{:S(2)}, u32[]{:S(2)}) collective-permute-start(f32[360,128]{1,0:T(8,128)S(1)} %get-tuple-element.32), channel_id=1, source_target_pairs={{0,3},{1,2},{2,1},{3,0},{4,7},{5,6},{6,5},{7,4},{8,11},{9,10},{10,... | collective-permute-start | bytes 552968 | tf_op jit(solution)/shard_map/ppermute | solution.py:756
  9.3 0.6 %collective-permute-done.2.own_far_ref.far_ref = f32[416,128]{1,0:T(8,128)S(1)} collective-permute-done((f32[416,128]{1,0:T(8,128)S(1)}, f32[416,128]{1,0:T(8,128)S(1)}, u32[]{:S(2)}, u32[]{:S(2)}) %collective-permute-start.2) | collective-permute-done | bytes 213024 | tf_op jit(solution)/shard_map/ppermute | solution.py:758
  9.9 0.0 collective-permute-start.5
  9.9 4.9 %collective-permute-done.4.even_far_ref = f32[360,128]{1,0:T(8,128)S(1)} collective-permute-done((f32[360,128]{1,0:T(8,128)S(1)}, f32[360,128]{1,0:T(8,128)S(1)}, u32[]{:S(2)}, u32[]{:S(2)}) %collective-permute-start.4) | collective-permute-done | bytes 184352 | tf_op jit(solution)/shard_map/ppermute | solution.py:756
  14.9 0.0 collective-permute-done.even_ref
  14.9 0.0 collective-permute-done.1.odd_ref
  14.9 0.1 collective-permute-start.3
  15.0 0.0 collective-permute-done.5.odd_far_ref
  15.1 0.5 %collective-permute-start.6 = (f32[256,128]{1,0:T(8,128)S(1)}, f32[256,128]{1,0:T(8,128)S(1)}, u32[]{:S(2)}, u32[]{:S(2)}) collective-permute-start(f32[256,128]{1,0:T(8,128)S(1)} %pad_maximum_fusion.1), channel_id=1, source_target_pairs={{0,8},{8,0},{16,24},{24,16},{1,9},{9,1},{17,25},{25,17},{2,10},{10... | collective-permute-start | bytes 393224 | tf_op jit(solution)/shard_map/ppermute | solution.py:777
  15.6 0.8 %collective-permute-done.3.swapped_ref = f32[376,128]{1,0:T(8,128)S(1)} collective-permute-done((f32[376,128]{1,0:T(8,128)S(1)}, f32[376,128]{1,0:T(8,128)S(1)}, u32[]{:S(2)}, u32[]{:S(2)}) %collective-permute-start.3) | collective-permute-done | bytes 192544 | tf_op jit(solution)/shard_map/ppermute | solution.py:777
  16.4 0.9 %near.1 = (f32[32,24,256]{2,1,0:T(8,128)S(1)}, f32[32,24,256]{2,1,0:T(8,128)S(1)}, f32[32,24,256]{2,1,0:T(8,128)S(1)}, f32[32,8,256]{2,1,0:T(8,128)S(1)}, f32[32,8,256]{2,1,0:T(8,128)S(1)}) custom-call(f32[544,128]{1,0:T(8,128)S(1)} %get-tuple-element.24.own_ref, f32[392,128]{1,0:T(8,128)S(1)} %collective-permute-done.even_ref, ...), custom_call_target="tpu_custom_call" | custom-call | tf_op jit(solution)/shard_map/near/pallas_call | solution.py:783
  17.4 0.0 collective-permute-done.6.swapped_far_ref
  17.4 8.9 %basis.1 = (f32[4,64,8,256]{3,2,1,0:T(8,128)S(1)}, f32[4,64,8,256]{3,2,1,0:T(8,128)S(1)}, f32[32,8,256]{2,1,0:T(8,128)S(1)}, f32[32,8,256]{2,1,0:T(8,128)S(1)}, f32[8,128]{1,0:T(8,128)S(1)}) custom-call(f32[32,24,256]{2,1,0:T(8,128)S(1)} %get-tuple-element.28.near_diag, f32[32,24,256]{2,1,0:T(8,128)S(1)} %get-tuple-element.29.near_lower, ...), custom_call_target="tpu_custom_call" | custom-call | tf_op jit(solution)/shard_map/basis/pallas_call | solution.py:798
  26.3 3.1 %collective-permute-start.9 = (f32[8,128]{1,0:T(8,128)S(1)}, f32[8,128]{1,0:T(8,128)S(1)}, u32[]{:S(2)}, u32[]{:S(2)}) collective-permute-start(f32[8,128]{1,0:T(8,128)S(1)} %get-tuple-element.38), channel_id=1, source_target_pairs={{0,3},{3,0},{1,2},{2,1},{4,7},{7,4},{5,6},{6,5},{8,11},{11,8},{9,1... | collective-permute-start | bytes 12296 | tf_op jit(solution)/shard_map/ppermute | solution.py:845
  29.5 0.1 collective-permute-start.8
  29.5 0.7 %collective-permute-start.7 = (f32[8,128]{1,0:T(8,128)S(1)}, f32[8,128]{1,0:T(8,128)S(1)}, u32[]{:S(2)}, u32[]{:S(2)}) collective-permute-start(f32[8,128]{1,0:T(8,128)S(1)} %get-tuple-element.38), channel_id=1, source_target_pairs={{0,1},{1,0},{2,3},{3,2},{4,5},{5,4},{6,7},{7,6},{8,9},{9,8},{10,11... | collective-permute-start | bytes 12296 | tf_op jit(solution)/shard_map/ppermute | solution.py:845
  30.2 2.9 %collective-permute-done.7 = f32[8,128]{1,0:T(8,128)S(1)} collective-permute-done((f32[8,128]{1,0:T(8,128)S(1)}, f32[8,128]{1,0:T(8,128)S(1)}, u32[]{:S(2)}, u32[]{:S(2)}) %collective-permute-start.7) | collective-permute-done | bytes 4128 | tf_op jit(solution)/shard_map/ppermute | solution.py:845
  33.1 0.0 collective-permute-done.8
  33.1 0.0 collective-permute-done.9
  33.1 3.0 %collective-permute-start.10 = (f32[32,128]{1,0:T(8,128)S(1)}, f32[32,128]{1,0:T(8,128)S(1)}, u32[]{:S(2)}, u32[]{:S(2)}) collective-permute-start(f32[32,128]{1,0:T(8,128)S(1)} %constant_dynamic-update-slice_fusion.refs_0_), channel_id=1, source_target_pairs={{0,4},{4,0},{2,6},{6,2},{1,5},{5,1},{3,7},{7,3},{8,12},{12,8},{10,... | collective-permute-start | bytes 49160 | tf_op jit(solution)/shard_map/ppermute | solution.py:854
  36.2 0.0 copy-start
  36.2 0.0 copy-start.1
  36.2 1.4 %terms.1.terms_ref = f32[4,64,8,128]{3,2,1,0:T(8,128)S(1)} custom-call(f32[4,64,8,256]{3,2,1,0:T(8,128)S(1)} %get-tuple-element.33.basis_ref, f32[4,64,8,256]{3,2,1,0:T(8,128)S(1)} %get-tuple-element.34.image_ref, f32[32,8,256]{2,1,0:T(8,128)S(1)} %get-tuple-element.31.near_signs, f32[32,8,256]{2,1,0:T(8,128)S(1)} %get-tuple-element.35.near_k_signs, ...), custom_call_target="tpu_custom_call" | custom-call | tf_op jit(solution)/shard_map/terms/pallas_call | solution.py:834
  37.5 0.4 collective-permute-done.10.refs_1_
  37.9 0.6 %combine.1 = (f32[2,16,8,128]{3,2,1,0:T(8,128)S(1)}, f32[2,16,8,128]{3,2,1,0:T(8,128)S(1)}) custom-call(f32[4,64,8,128]{3,2,1,0:T(8,128)S(1)} %terms.1.terms_ref, f32[32,128]{1,0:T(8,128)S(1)} %constant_dynamic-update-slice_fusion.refs_0_, f32[32,128]{1,0:T(8,128)S(1)} %collective-permute-done.10.refs_1_), custom_call_target="tpu_custom_call" | custom-call | tf_op jit(solution)/shard_map/combine/pallas_call | solution.py:858
  38.5 0.1 collective-permute-start.11
  38.6 1.3 %collective-permute-done.11 = f32[2,16,8,128]{3,2,1,0:T(8,128)S(1)} collective-permute-done((f32[2,16,8,128]{3,2,1,0:T(8,128)S(1)}, f32[2,16,8,128]{3,2,1,0:T(8,128)S(1)}, u32[]{:S(2)}, u32[]{:S(2)}) %collective-permute-start.11) | collective-permute-done | bytes 131104 | tf_op jit(solution)/shard_map/ppermute | solution.py:867
  39.9 1.0 %collective-permute-start.13 = (f32[16,8,128]{2,1,0:T(8,128)S(1)}, f32[16,8,128]{2,1,0:T(8,128)S(1)}, u32[]{:S(2)}, u32[]{:S(2)}) collective-permute-start(f32[16,8,128]{2,1,0:T(8,128)S(1)} %get-tuple-element.43), channel_id=1, source_target_pairs={{0,1},{8,9},{16,17},{24,25},{1,16},{9,24},{17,0},{25,8},{2,3},{10,... | collective-permute-start | bytes 196616 | tf_op jit(solution)/shard_map/ppermute | solution.py:876
  40.9 0.0 collective-permute-start.12
  40.9 0.0 copy-done
  40.9 0.0 copy-done.1
  40.9 1.0 %observed.1 = (f32[16,8,128]{2,1,0:T(8,128)S(1)}, f32[16,8,128]{2,1,0:T(8,128)S(1)}) custom-call(f32[32,8,256]{2,1,0:T(8,128)S(1)} %copy-done, f32[32,8,256]{2,1,0:T(8,128)S(1)} %copy-done.1, f32[392,128]{1,0:T(8,128)S(1)} %collective-permute-done.even_ref, f32[392,128]{1,0:T(8,128)S(1)} %collective-permute-done.1.odd_ref, ...), custom_call_target="tpu_custom_call" | custom-call | tf_op jit(solution)/shard_map/observed/pallas_call | solution.py:766
  41.9 3.6 %collective-permute-done.13.trace_a_ref = f32[16,8,128]{2,1,0:T(8,128)S(1)} collective-permute-done((f32[16,8,128]{2,1,0:T(8,128)S(1)}, f32[16,8,128]{2,1,0:T(8,128)S(1)}, u32[]{:S(2)}, u32[]{:S(2)}) %collective-permute-start.13) | collective-permute-done | bytes 65568 | tf_op jit(solution)/shard_map/ppermute | solution.py:876
  45.5 0.0 collective-permute-done.12.trace_b_ref
  45.5 0.9 %gradient.1 = f32[32,8,64]{2,1,0:T(8,128)} custom-call(f32[16,8,128]{2,1,0:T(8,128)S(1)} %collective-permute-done.12.trace_b_ref, f32[16,8,128]{2,1,0:T(8,128)S(1)} %collective-permute-done.13.trace_a_ref, f32[16,8,128]{2,1,0:T(8,128)S(1)} %get-tuple-element.44.straight_ref, f32[16,8,128]{2,1,0:T(8,128)S(1)} %get-tuple-element.41.factor_ref, ...), custom_call_target="tpu_custom_call" | custom-call | tf_op jit(solution)/shard_map/gradient/pallas_call | solution.py:888
  (13 shorter events, 0.1 us)
Async XLA Ops:
  1.6 8.3 %collective-permute-start.2 = (f32[416,128]{1,0:T(8,128)S(1)}, f32[416,128]{1,0:T(8,128)S(1)}, u32[]{:S(2)}, u32[]{:S(2)}) collective-permute-start(f32[416,128]{1,0:T(8,128)S(1)} %get-tuple-element.27), channel_id=1, source_target_pairs={{0,1},{1,0},{2,3},{3,2},{4,5},{5,4},{6,7},{7,6},{8,9},{9,8},{10,11... | collective-permute-start | bytes 638984 | tf_op jit(solution)/shard_map/ppermute | solution.py:758
  4.7 10.2 %collective-permute-start = (f32[392,128]{1,0:T(8,128)S(1)}, f32[392,128]{1,0:T(8,128)S(1)}, u32[]{:S(2)}, u32[]{:S(2)}) collective-permute-start(f32[392,128]{1,0:T(8,128)S(1)} %get-tuple-element.25), channel_id=1, source_target_pairs={{0,2},{1,3},{2,0},{3,1},{4,6},{5,7},{6,4},{7,5},{8,10},{9,11},{10,... | collective-permute-start | bytes 602120 | tf_op jit(solution)/shard_map/ppermute | solution.py:756
  6.2 8.6 %collective-permute-start.1 = (f32[392,128]{1,0:T(8,128)S(1)}, f32[392,128]{1,0:T(8,128)S(1)}, u32[]{:S(2)}, u32[]{:S(2)}) collective-permute-start(f32[392,128]{1,0:T(8,128)S(1)} %get-tuple-element.26), channel_id=1, source_target_pairs={{0,8},{1,9},{2,4},{3,5},{4,2},{5,3},{6,14},{7,15},{8,0},{9,1},{10,... | collective-permute-start | bytes 602120 | tf_op jit(solution)/shard_map/ppermute | solution.py:756
  6.2 8.6 %collective-permute-start.4 = (f32[360,128]{1,0:T(8,128)S(1)}, f32[360,128]{1,0:T(8,128)S(1)}, u32[]{:S(2)}, u32[]{:S(2)}) collective-permute-start(f32[360,128]{1,0:T(8,128)S(1)} %get-tuple-element.32), channel_id=1, source_target_pairs={{0,3},{1,2},{2,1},{3,0},{4,7},{5,6},{6,5},{7,4},{8,11},{9,10},{10,... | collective-permute-start | bytes 552968 | tf_op jit(solution)/shard_map/ppermute | solution.py:756
  9.9 5.1 %collective-permute-start.5 = (f32[416,128]{1,0:T(8,128)S(1)}, f32[416,128]{1,0:T(8,128)S(1)}, u32[]{:S(2)}, u32[]{:S(2)}) collective-permute-start(f32[416,128]{1,0:T(8,128)S(1)} %collective-permute-done.2.own_far_ref.far_ref), channel_id=1, source_target_pairs={{0,8},{1,9},{2,4},{3,5},{4,2},{5,3},{6,14},{7,15},{8,0},{9,1},{10,... | collective-permute-start | bytes 638984 | tf_op jit(solution)/shard_map/ppermute | solution.py:756
  14.9 1.5 %collective-permute-start.3 = (f32[376,128]{1,0:T(8,128)S(1)}, f32[376,128]{1,0:T(8,128)S(1)}, u32[]{:S(2)}, u32[]{:S(2)}) collective-permute-start(f32[376,128]{1,0:T(8,128)S(1)} %pad_maximum_fusion), channel_id=1, source_target_pairs={{0,8},{8,0},{16,24},{24,16},{1,9},{9,1},{17,25},{25,17},{2,10},{10... | collective-permute-start | bytes 577544 | tf_op jit(solution)/shard_map/ppermute | solution.py:777
  15.1 2.3 %collective-permute-start.6 = (f32[256,128]{1,0:T(8,128)S(1)}, f32[256,128]{1,0:T(8,128)S(1)}, u32[]{:S(2)}, u32[]{:S(2)}) collective-permute-start(f32[256,128]{1,0:T(8,128)S(1)} %pad_maximum_fusion.1), channel_id=1, source_target_pairs={{0,8},{8,0},{16,24},{24,16},{1,9},{9,1},{17,25},{25,17},{2,10},{10... | collective-permute-start | bytes 393224 | tf_op jit(solution)/shard_map/ppermute | solution.py:777
  26.3 6.8 %collective-permute-start.9 = (f32[8,128]{1,0:T(8,128)S(1)}, f32[8,128]{1,0:T(8,128)S(1)}, u32[]{:S(2)}, u32[]{:S(2)}) collective-permute-start(f32[8,128]{1,0:T(8,128)S(1)} %get-tuple-element.38), channel_id=1, source_target_pairs={{0,3},{3,0},{1,2},{2,1},{4,7},{7,4},{5,6},{6,5},{8,11},{11,8},{9,1... | collective-permute-start | bytes 12296 | tf_op jit(solution)/shard_map/ppermute | solution.py:845
  29.5 3.7 %collective-permute-start.8 = (f32[8,128]{1,0:T(8,128)S(1)}, f32[8,128]{1,0:T(8,128)S(1)}, u32[]{:S(2)}, u32[]{:S(2)}) collective-permute-start(f32[8,128]{1,0:T(8,128)S(1)} %get-tuple-element.38), channel_id=1, source_target_pairs={{0,2},{2,0},{1,3},{3,1},{4,6},{6,4},{5,7},{7,5},{8,10},{10,8},{9,1... | collective-permute-start | bytes 12296 | tf_op jit(solution)/shard_map/ppermute | solution.py:845
  29.5 3.6 %collective-permute-start.7 = (f32[8,128]{1,0:T(8,128)S(1)}, f32[8,128]{1,0:T(8,128)S(1)}, u32[]{:S(2)}, u32[]{:S(2)}) collective-permute-start(f32[8,128]{1,0:T(8,128)S(1)} %get-tuple-element.38), channel_id=1, source_target_pairs={{0,1},{1,0},{2,3},{3,2},{4,5},{5,4},{6,7},{7,6},{8,9},{9,8},{10,11... | collective-permute-start | bytes 12296 | tf_op jit(solution)/shard_map/ppermute | solution.py:845
  33.1 4.8 %collective-permute-start.10 = (f32[32,128]{1,0:T(8,128)S(1)}, f32[32,128]{1,0:T(8,128)S(1)}, u32[]{:S(2)}, u32[]{:S(2)}) collective-permute-start(f32[32,128]{1,0:T(8,128)S(1)} %constant_dynamic-update-slice_fusion.refs_0_), channel_id=1, source_target_pairs={{0,4},{4,0},{2,6},{6,2},{1,5},{5,1},{3,7},{7,3},{8,12},{12,8},{10,... | collective-permute-start | bytes 49160 | tf_op jit(solution)/shard_map/ppermute | solution.py:854
  36.2 4.8 %copy-start = (f32[32,8,256]{2,1,0:T(8,128)S(1)}, f32[32,8,256]{2,1,0:T(8,128)}, u32[]{:S(2)}) copy-start(f32[32,8,256]{2,1,0:T(8,128)} %kappa_ref.1) | copy-start | bytes 786436
  36.2 4.8 %copy-start.1 = (f32[32,8,256]{2,1,0:T(8,128)S(1)}, f32[32,8,256]{2,1,0:T(8,128)}, u32[]{:S(2)}) copy-start(f32[32,8,256]{2,1,0:T(8,128)} %observed_ref.1) | copy-start | bytes 786436
  38.5 1.4 %collective-permute-start.11 = (f32[2,16,8,128]{3,2,1,0:T(8,128)S(1)}, f32[2,16,8,128]{3,2,1,0:T(8,128)S(1)}, u32[]{:S(2)}, u32[]{:S(2)}) collective-permute-start(f32[2,16,8,128]{3,2,1,0:T(8,128)S(1)} %get-tuple-element.40), channel_id=1, source_target_pairs={{0,8},{8,0},{16,24},{24,16},{1,9},{9,1},{17,25},{25,17},{2,10},{10... | collective-permute-start | bytes 393224 | tf_op jit(solution)/shard_map/ppermute | solution.py:867
  39.9 5.6 %collective-permute-start.13 = (f32[16,8,128]{2,1,0:T(8,128)S(1)}, f32[16,8,128]{2,1,0:T(8,128)S(1)}, u32[]{:S(2)}, u32[]{:S(2)}) collective-permute-start(f32[16,8,128]{2,1,0:T(8,128)S(1)} %get-tuple-element.43), channel_id=1, source_target_pairs={{0,1},{8,9},{16,17},{24,25},{1,16},{9,24},{17,0},{25,8},{2,3},{10,... | collective-permute-start | bytes 196616 | tf_op jit(solution)/shard_map/ppermute | solution.py:876
  40.9 4.6 %collective-permute-start.12 = (f32[16,8,128]{2,1,0:T(8,128)S(1)}, f32[16,8,128]{2,1,0:T(8,128)S(1)}, u32[]{:S(2)}, u32[]{:S(2)}) collective-permute-start(f32[16,8,128]{2,1,0:T(8,128)S(1)} %get-tuple-element.44.straight_ref), channel_id=1, source_target_pairs={{1,17},{9,25},{17,1},{25,9},{0,8},{8,0},{16,24},{24,16},{3,19},{11... | collective-permute-start | bytes 196616 | tf_op jit(solution)/shard_map/ppermute | solution.py:882
